TPU v7x, 32 devices: a whole 2x2x4 slice. The times are simulated.
32 devices in a mesh: hst: 8 (over y, x, core), tp: 4 (over z).
Axes of the slice: x: 2, y: 2, z: 4, core: 2. Of those that a mesh axis runs over, the one named last changes fastest.
Arguments:
- ctx_q: bfloat16 [6144, 8192], P('hst', 'tp'), may hold values from -11.2 to 11.2
- ctx_kv: bfloat16 [2, 6144, 1024], P(None, 'hst'), may hold values from -4.5 to 4.5
- lengths: int32 [8], replicated, may hold values from 192 to 768, as said below
- query_q: bfloat16 [64, 8192], P('hst', 'tp'), may hold values from -11.2 to 11.2
- query_kv: bfloat16 [2, 64, 1024], P(None, 'hst'), may hold values from -4.5 to 4.5
- out_weight: bfloat16 [8192, 8192], P('tp', 'hst'), may hold values from -0.0625 to 0.0625
Outputs:
- context_out: bfloat16 [6144, 8192], P('hst', 'tp')
- query_out: bfloat16 [64, 8192], P(None, 'hst')
Inputs may be any that keep to these rules, and one draw needn't show every extreme that they name: lengths[0] is 768; blocks with index below three quarters of 8 are full, the last block holds 192 live positions.
All inputs are finite; a program needn't handle non-finite values.
Results may differ from a plain program's by a relative error of at most 0.012.
Values may be sent and summed in bfloat16 or wider, within the bound.
No kernel may reach another device: no remote copies, remote signals or barrier semaphores. Data moves between devices by JAX's collectives and lax.ppermute only.
A program may use at most 64 MiB of HBM per device.

v0:
```python
import jax
import jax.numpy as jnp
from jax import lax
from jax.sharding import PartitionSpec as P

H = 64
KVH = 8
HD = 128


MASKED = -1e30


def spread(value, axis, source):
    kept = jnp.where(lax.axis_index(axis) == source, value, 0).astype(value.dtype)
    return lax.psum(kept, axis)


def softmax_rows(query_rows, key_rows, allowed, score_scale):
    scores = (
        jnp.einsum("id,jd->ij", query_rows, key_rows, preferred_element_type=jnp.float32)
        * score_scale
    )
    scores = jnp.where(allowed, scores, MASKED)
    return scores


def per_device(ctx_q, ctx_kv, lengths, query_q, query_kv, out_weight):
    slab_rows = ctx_q.shape[0]
    local_heads = ctx_q.shape[1] // HD
    group_size = H // KVH
    kv_local = max(1, local_heads // group_size)
    per_kv = min(local_heads, group_size)
    score_scale = HD ** (-0.5)
    tp_index = lax.axis_index("tp")
    host_id = lax.axis_index("hst")
    kv_first = tp_index * local_heads // group_size
    own_kv = lax.dynamic_slice_in_dim(ctx_kv, kv_first * HD, kv_local * HD, 2)
    anchor = spread(own_kv, "hst", 0)
    own_len = lengths[host_id]
    first_len = lengths[0]
    row_ids = jnp.arange(slab_rows)
    own_ok = (row_ids[None, :] <= row_ids[:, None]) & (row_ids[None, :] < own_len)
    anchor_ok = (row_ids[None, :] < first_len) & (host_id > 0)
    allowed = jnp.concatenate([jnp.broadcast_to(anchor_ok, (slab_rows, slab_rows)), own_ok], 1)
    joined = jnp.concatenate([anchor, own_kv], 1)
    joined = joined.reshape(2, 2 * slab_rows, kv_local, HD).transpose(0, 2, 1, 3)
    head_queries = ctx_q.reshape(slab_rows, local_heads, HD).transpose(1, 0, 2)

    def encode_head(operands):
        query_rows, head_index = operands
        kv_index = head_index // per_kv
        scores = softmax_rows(query_rows, joined[0, kv_index], allowed, score_scale)
        peak = jnp.max(scores, axis=1, keepdims=True)
        expo = jnp.exp(scores - peak)
        probs = (expo / jnp.sum(expo, axis=1, keepdims=True)).astype(jnp.bfloat16)
        encoded = jnp.einsum(
            "ij,jd->id", probs, joined[1, kv_index], preferred_element_type=jnp.float32
        )
        return encoded.astype(jnp.bfloat16)

    encoded = lax.map(encode_head, (head_queries, jnp.arange(local_heads)))
    encoded = encoded.transpose(1, 0, 2).reshape(slab_rows, local_heads * HD)
    context_out = jnp.where((row_ids < own_len)[:, None], encoded, jnp.zeros_like(encoded))
    all_queries = lax.all_gather(query_q, "hst", axis=0, tiled=True)
    query_count = all_queries.shape[0]
    q_rows = query_q.shape[0]
    self_kv = lax.dynamic_slice_in_dim(query_kv, kv_first * HD, kv_local * HD, 2)
    source = jnp.concatenate([own_kv, self_kv], 1)
    source = source.reshape(2, slab_rows + q_rows, kv_local, HD).transpose(0, 2, 1, 3)
    query_ids = jnp.arange(query_count)
    context_ok = jnp.broadcast_to(row_ids[None, :] < own_len, (query_count, slab_rows))
    self_ok = (host_id * q_rows + jnp.arange(q_rows))[None, :] <= query_ids[:, None]
    seen_ok = jnp.concatenate([context_ok, self_ok], 1)
    query_heads = all_queries.reshape(query_count, local_heads, HD).transpose(1, 0, 2)

    def score_head(operands):
        query_rows, head_index = operands
        kv_index = head_index // per_kv
        scores = softmax_rows(query_rows, source[0, kv_index], seen_ok, score_scale)
        peak = jnp.max(scores, axis=1)
        expo = jnp.exp(scores - peak[:, None])
        denominator = jnp.sum(expo, axis=1)
        weighted = jnp.einsum(
            "ij,jd->id",
            expo.astype(jnp.bfloat16),
            source[1, kv_index],
            preferred_element_type=jnp.float32,
        )
        return (peak, denominator, weighted)

    maxima, totals, outputs = lax.map(score_head, (query_heads, jnp.arange(local_heads)))
    highest = lax.pmax(maxima, "hst")
    factor = jnp.exp(maxima - highest)
    denominator, summed = lax.psum((totals * factor, outputs * factor[..., None]), "hst")
    attended = (summed / denominator[..., None]).astype(jnp.bfloat16)
    attended = attended.transpose(1, 0, 2).reshape(query_count, local_heads * HD)
    partial_out = jnp.dot(attended, out_weight, preferred_element_type=jnp.float32)
    query_out = lax.psum(partial_out, "tp").astype(jnp.bfloat16)
    return (context_out, query_out)


def solution(mesh):
    return jax.shard_map(
        per_device,
        mesh=mesh,
        in_specs=(
            P("hst", "tp"),
            P(None, "hst", None),
            P(),
            P("hst", "tp"),
            P(None, "hst", None),
            P("tp", "hst"),
        ),
        out_specs=(P("hst", "tp"), P(None, "hst")),
        check_vma=False,
    )
```

profile of v0, /device:TPU:6, one launch (start us, length us, event | category | flops | bytes accessed | tf_op | source)
XLA Modules:
  0.0 431.2 jit_solution(7542648210469401064)
XLA Ops:
  15.3 3.6 copy.19
  22.4 8.3 %all_gather.3 = bf16[64,2048]{1,0:T(8,128)(2,1)S(1)} all-gather(bf16[8,2048]{1,0:T(8,128)(2,1)S(1)} %copy-done.1), channel_id=1, replica_groups=mesh['hst'=8,'tp'=4] {'hst'}, dimensions={0}, use_global_device_ids=true | all-gather | bytes 294912 | tf_op jit(solution)/shard_map/all_gather | solution.py:65
  30.9 103.1 %while.29 = (s32[]{:T(128)}, f32[16,64]{1,0:T(8,128)S(1)}, f32[16,64]{1,0:T(8,128)S(1)}, f32[16,64,128]{2,1,0:T(8,128)}, bf16[16,64,128]{2,1,0:T(8,128)(2,1)S(1)...) while((s32[]{:T(128)}, f32[16,64]{1,0:T(8,128)S(1)}, ...), condition=%wide.region_8.9_spmd, body=%wide.region_5.8_spmd.sunk | while | flops 25775508 | bytes 1103193 | solution.py:92
  134.0 12.0 %pmax.7 = f32[16,64]{1,0:T(8,128)S(1)} all-reduce(f32[16,64]{1,0:T(8,128)S(1)} %get-tuple-element.186), channel_id=1, replica_groups=mesh['hst'=8,'tp'=4] {'hst'}, use_global_device_ids=true, to_apply=%region_9.10 | all-reduce | flops 1024 | bytes 8192 | tf_op jit(solution)/shard_map/pmax | solution.py:93
  150.2 12.5 %psum.30 = f32[16,64]{1,0:T(8,128)S(1)} all-reduce(f32[16,64]{1,0:T(8,128)S(1)} %get-tuple-element.230), channel_id=1, replica_groups=mesh['hst'=8,'tp'=4] {'hst'}, use_global_device_ids=true, to_apply=%region_11.12 | all-reduce | flops 1024 | bytes 8192 | tf_op jit(solution)/shard_map/psum | solution.py:95
  163.3 4.6 %copy.9 = bf16[768,2048]{0,1:T(8,128)(2,1)} copy(bf16[768,2048]{1,0:T(8,128)(2,1)} %param.10) | data formatting | bytes 6291456 | tf_op args[0]
  170.5 33.4 %all-reduce.6.cloned.1.call-done = f32[16,64,128]{2,1,0:T(8,128)} async-done(((f32[16,64,128]{2,1,0:T(8,128)}), f32[16,64,128]{2,1,0:T(8,128)}) %all-reduce.6.cloned.1.call-update) | async-done | bytes 524304 | tf_op jit(solution)/shard_map/psum | solution.py:95
  203.8 3.2 fusion.30
  207.1 24.4 %all-reduce.7 = bf16[64,1024]{1,0:T(8,128)(2,1)} all-reduce(f32[64,1024]{1,0:T(8,128)S(1)} %fusion.30), channel_id=1, replica_groups=mesh['hst'=8,'tp'=4] {'tp'}, use_global_device_ids=true, to_apply=%region_12.13 | all-reduce | flops 65536 | bytes 393216 | tf_op jit(solution)/shard_map/psum | solution.py:99
  231.4 30.6 %all-reduce.4.cloned.1.call-done = bf16[2,768,256]{1,2,0:T(8,128)(2,1)} async-done(((bf16[2,768,256]{1,2,0:T(8,128)(2,1)}), bf16[2,768,256]{1,2,0:T(8,128)(2,1)}) %all-reduce.4.cloned.1.call-update) | async-done | bytes 786448 | tf_op jit(solution)/shard_map/psum | solution.py:16
  267.3 152.9 %while.28 = (s32[]{:T(128)}, bf16[16,768,128]{2,1,0:T(8,128)(2,1)}, bf16[16,768,128]{1,2,0:T(8,128)(2,1)}, s32[16]{0:T(128)S(1)}, bf16[2,2,1536,128]{3,2,1,0:T(8...) while((s32[]{:T(128)}, bf16[16,768,128]{2,1,0:T(8,128)(2,1)}, ...), condition=%wide.region_4.5_spmd, body=%wide.region_1.4_spmd.sunk | while | flops 613513728 | bytes 16531777 | solution.py:62
  270.7 2.7 fusion.53
  280.3 2.7 fusion.53
  289.8 2.7 fusion.53
  299.4 2.7 fusion.53
  302.9 2.7 fusion.55
  309.0 2.7 fusion.53
  318.5 2.7 fusion.53
  328.1 2.7 fusion.53
  337.6 2.7 fusion.53
  341.1 2.7 fusion.55
  347.2 2.7 fusion.53
  356.7 2.7 fusion.53
  366.3 2.7 fusion.53
  375.8 2.7 fusion.53
  379.3 2.7 fusion.55
  385.4 2.7 fusion.53
  388.9 2.7 fusion.55
  395.0 2.7 fusion.53
  404.5 2.7 fusion.53
  414.1 2.7 fusion.53
  420.2 4.2 bitcast_select_fusion
  (179 shorter events, 141.2 us)
Async XLA Ops:
  7.2 1.9 copy-start
  7.2 196.6 %all-reduce.6.cloned.1.call-start = ((), (), s32[]{:S(2)}) async-start(), calls=%async_computation.1 | async-start | bytes 1048576 | tf_op jit(solution)/shard_map/psum | solution.py:95
  10.0 11.0 %copy-start.2 = (s32[8]{0:T(128)S(1)}, s32[8]{0:T(128)}, u32[]{:S(2)}) copy-start(s32[8]{0:T(128)} %param.12) | copy-start | bytes 100
  10.0 12.3 %copy-start.1 = (bf16[8,2048]{1,0:T(8,128)(2,1)S(1)}, bf16[8,2048]{1,0:T(8,128)(2,1)}, u32[]{:S(2)}) copy-start(bf16[8,2048]{1,0:T(8,128)(2,1)} %param.13) | copy-start | bytes 98308
  148.1 114.0 %all-reduce.4.cloned.1.call-start = ((), (), s32[]{:S(2)}) async-start(), calls=%async_computation | async-start | bytes 1572864 | tf_op jit(solution)/shard_map/psum | solution.py:16
Sparse Core Ops, SparseCore 0:
  148.2 55.5 all-reduce.5
  207.3 54.7 all-reduce.3
where the time goes:
time: 438 us; the launch traced here: 431 us
  matrix products  137 us (31%)
  loops' own time  85.4 us (19%)
  waiting for transfers between devices  64 us (15%)
  blocking collectives  57.2 us (13%)
  local copies, waits for them, and re-layouts  41 us (9%)
  other arithmetic  32.3 us (7%)
  between operations  14.2 us (3%)
    dot_general x32, matrix products, softmax_rows(): jnp.einsum('id,jd->ij', query_rows, key_rows, preferred_element_type=jnp....  62.8 us
    another operation x1, loops' own time, per_device(): encoded = lax.map(encode_head, (head_queries, jnp.arange(local_heads)))  44.6 us
    dot_general x16, matrix products, encode_head(): jnp.einsum('ij,jd->id', probs, joined[1, kv_index], preferred_element_typ...  42.5 us
    another operation x1, loops' own time, per_device(): lax.map(score_head, (query_heads, jnp.arange(local_heads)))  40.8 us
    psum x1, waiting for transfers between devices, per_device(): lax.psum((totals * factor, outputs * factor[..., None]), 'hst')  33.4 us
    psum x1, waiting for transfers between devices, spread(): return lax.psum(kept, axis)  30.6 us
    dot_general x16, matrix products, score_head(): jnp.einsum('ij,jd->id', expo.astype(jnp.bfloat16), source[1, kv_index], p...  28.4 us
    psum x1, blocking collectives, per_device(): query_out = lax.psum(partial_out, 'tp').astype(jnp.bfloat16)  24.4 us
  transfers between devices with their start and end apart: 2, of which 2 were waited for; matrix products, arithmetic and copies ran while one was open for 3% of the time, Pallas kernels for 0%

commit v1 on v0

v1 whole, which is shorter than its diff:
```python
import functools

import jax
import jax.numpy as jnp
from jax import lax
from jax.experimental import pallas as pl
from jax.experimental.pallas import tpu as pltpu
from jax.sharding import PartitionSpec as P

H = 64
KVH = 8
HD = 128
MASKED = -1e30
LOG2E = 1.4426950408889634
SCALE2 = HD ** (-0.5) * LOG2E
TINY = 2.0 ** -90
BF = jnp.bfloat16
F32 = jnp.float32
VMEM = pl.BlockSpec(memory_space=pltpu.VMEM)
SMEM = pl.BlockSpec(memory_space=pltpu.SMEM)
ANY = pl.BlockSpec(memory_space=pl.ANY)


def params(mib=40):
    return pltpu.CompilerParams(vmem_limit_bytes=mib * 2**20)


def dot_t(a, b):
    return lax.dot_general(a, b, (((1,), (1,)), ((), ())), preferred_element_type=F32)


def dot(a, b):
    return lax.dot_general(a, b, (((1,), (0,)), ((), ())), preferred_element_type=F32)


def spread(value, axis, source):
    kept = jnp.where(lax.axis_index(axis) == source, value, 0).astype(value.dtype)
    return lax.psum(kept, axis)


def xor_pairs(size, bits, skip=()):
    return [(i, i ^ bits) for i in range(size) if (i ^ bits) not in skip]


def exchange(slots, axis, size, skip=()):
    return [slots[0]] + [
        lax.ppermute(slots[k], axis, xor_pairs(size, k, skip)) for k in range(1, size)
    ]


def pick_kernel(parts, group_size, local_heads, kv_ref, own_ref, *rest):
    piece_refs, sems = rest[: parts - 1], rest[parts - 1]
    width = own_ref.shape[2]
    rows = own_ref.shape[1]
    first = lax.axis_index("tp") * local_heads // group_size * HD
    cols = pl.ds(pl.multiple_of(first, HD), width)
    copies = [pltpu.make_async_copy(kv_ref.at[:, :, cols], own_ref, sems.at[0])]
    step = rows // parts
    for k in range(1, parts):
        copies.append(
            pltpu.make_async_copy(
                kv_ref.at[:, pl.ds(k * step, step), cols], piece_refs[k - 1], sems.at[k]
            )
        )
    for copy in copies:
        copy.start()
    for copy in copies:
        copy.wait()


def pick_kv(ctx_kv, kv_local, local_heads, parts):
    rows = ctx_kv.shape[1]
    width = kv_local * HD
    shapes = [jax.ShapeDtypeStruct((2, rows, width), BF)]
    shapes += [jax.ShapeDtypeStruct((2, rows // parts, width), BF)] * (parts - 1)
    return pl.pallas_call(
        functools.partial(pick_kernel, parts, H // KVH, local_heads),
        out_shape=shapes,
        in_specs=[ANY],
        out_specs=[ANY] * len(shapes),
        scratch_shapes=[pltpu.SemaphoreType.DMA((parts,))],
        compiler_params=params(),
        name="pick_kv",
    )(ctx_kv)


def fill_values(vaug, values):
    vaug[:, :HD] = values
    vaug[:, HD:] = jnp.ones_like(values)


def row_tile(slab):
    return 256 if slab % 256 == 0 else slab


def own_kernel(heads, q_ref, kv_ref, *rest):
    state_ref, vaug = rest[-2], rest[-1]
    slab = q_ref.shape[0]
    tile = row_tile(slab)

    @pl.when(pl.program_id(0) == 0)
    def _():
        fill_values(vaug, kv_ref[1])

    rows = lax.broadcasted_iota(jnp.int32, (tile, tile), 0)
    cols = lax.broadcasted_iota(jnp.int32, (tile, tile), 1)
    causal = cols <= rows
    tiles = [(h, r) for h in range(heads) for r in range(slab // tile)]

    def scores(at):
        h, r = tiles[at]
        query = q_ref[r * tile : (r + 1) * tile, h * HD : (h + 1) * HD]
        return dot_t(query, kv_ref[0, : (r + 1) * tile, :])

    current = scores(0)
    for at, (h, r) in enumerate(tiles):
        following = scores(at + 1) if at + 1 < len(tiles) else None
        expo = jnp.exp2(current * SCALE2)
        last = jnp.where(causal, expo[:, r * tile :], 0.0)
        expo = last if r == 0 else jnp.concatenate([expo[:, : r * tile], last], 1)
        total = dot(expo.astype(BF), vaug[: (r + 1) * tile, :])
        state_ref[r * tile : (r + 1) * tile, h * 2 * HD : (h + 1) * 2 * HD] = total.astype(BF)
        current = following


def own_part(ctx_q, own_kv, first, count, per_kv, after=()):
    slab = ctx_q.shape[0]
    heads = min(2, count)
    steps = count // heads
    kv = first // per_kv
    work = count * slab * (slab + row_tile(slab)) // 2
    return pl.pallas_call(
        functools.partial(own_kernel, heads),
        grid=(steps,),
        out_shape=jax.ShapeDtypeStruct((slab, count * 2 * HD), BF),
        in_specs=[
            pl.BlockSpec((slab, heads * HD), lambda i: (0, first // heads + i)),
            pl.BlockSpec((2, slab, HD), lambda i: (0, 0, kv)),
        ]
        + [ANY] * len(after),
        out_specs=pl.BlockSpec((slab, heads * 2 * HD), lambda i: (0, i)),
        scratch_shapes=[pltpu.VMEM((slab, 2 * HD), BF)],
        compiler_params=params(),
        cost_estimate=pl.CostEstimate(
            flops=work * HD * 8, bytes_accessed=count * slab * HD * 6, transcendentals=work
        ),
        name="context_own",
    )(ctx_q, own_kv, *after)


def anchor_kernel(heads, pieces, count_after, lengths_ref, q_ref, state_ref, kv_ref, *rest):
    piece_refs = rest[:pieces]
    out_ref, keys, vaug = rest[-3], rest[-2], rest[-1]
    slab = q_ref.shape[0]
    tile = row_tile(slab)
    host = lax.axis_index("hst")
    own_len = lengths_ref[host]
    step = slab // pieces

    @pl.when(pl.program_id(0) == 0)
    def _():
        for k in range(pieces):
            keys[k * step : (k + 1) * step, :] = piece_refs[k][0]
            vaug[k * step : (k + 1) * step, :HD] = piece_refs[k][1]
            vaug[k * step : (k + 1) * step, HD:] = jnp.ones((step, HD), BF)

    tiles = [(h, r) for h in range(heads) for r in range(slab // tile)]
    row_ids = lax.broadcasted_iota(jnp.int32, (tile, HD), 0)

    def query_of(at):
        h, r = tiles[at]
        return q_ref[r * tile : (r + 1) * tile, h * HD : (h + 1) * HD]

    def finish(at, total, worst):
        h, r = tiles[at]
        sums = total[:, HD:]
        inverse = 1.0 / sums
        live = row_ids < own_len - r * tile
        result = jnp.where(live, total[:, :HD] * inverse, 0.0)
        out_ref[r * tile : (r + 1) * tile, h * HD : (h + 1) * HD] = result.astype(BF)
        return jnp.minimum(worst, jnp.minimum(sums, inverse))

    def state_of(at):
        h, r = tiles[at]
        return state_ref[r * tile : (r + 1) * tile, h * 2 * HD : (h + 1) * 2 * HD].astype(F32)

    def check(worst):
        @pl.when(jnp.logical_not(jnp.min(worst) > TINY))
        def _():
            exact_block(heads, host, own_len, q_ref, kv_ref, keys, vaug, out_ref)

    @pl.when(host == 0)
    def _():
        worst = jnp.ones((tile, HD), F32)
        for at in range(len(tiles)):
            worst = finish(at, state_of(at), worst)
        check(worst)

    @pl.when(host > 0)
    def _():
        worst = jnp.ones((tile, HD), F32)
        current = dot_t(query_of(0), keys[...])
        for at in range(len(tiles)):
            following = dot_t(query_of(at + 1), keys[...]) if at + 1 < len(tiles) else None
            expo = jnp.exp2(current * SCALE2).astype(BF)
            total = dot(expo, vaug[...]) + state_of(at)
            worst = finish(at, total, worst)
            current = following
        check(worst)


def exact_block(heads, host, own_len, q_ref, kv_ref, keys, vaug, out_ref):
    slab = q_ref.shape[0]
    tile = 128

    def body(i, carry):
        h = i // (slab // tile)
        r = i % (slab // tile)
        at = pl.ds(pl.multiple_of(r * tile, tile), tile)
        lanes = pl.ds(pl.multiple_of(h * HD, HD), HD)
        query = q_ref[at, lanes]
        row_ids = lax.broadcasted_iota(jnp.int32, (tile, slab), 0) + r * tile
        key_ids = lax.broadcasted_iota(jnp.int32, (tile, slab), 1)
        own = dot_t(query, kv_ref[0]) * SCALE2
        own = jnp.where((key_ids <= row_ids) & (key_ids < own_len), own, MASKED)
        far = dot_t(query, keys[...]) * SCALE2
        far = jnp.where(host > 0, far, MASKED)
        peak = jnp.maximum(jnp.max(own, 1, keepdims=True), jnp.max(far, 1, keepdims=True))
        own = jnp.exp2(own - peak)
        far = jnp.where(host > 0, jnp.exp2(far - peak), 0.0)
        sums = jnp.sum(own, 1, keepdims=True) + jnp.sum(far, 1, keepdims=True)
        values = jnp.where(host > 0, vaug[:, :HD].astype(F32), 0.0).astype(BF)
        total = dot(own.astype(BF), kv_ref[1]) + dot(far.astype(BF), values)
        live = row_ids[:, :1] < own_len
        out_ref[at, lanes] = jnp.where(live, total / sums, 0.0).astype(BF)
        return carry

    lax.fori_loop(0, heads * (slab // tile), body, 0)


def anchor_part(lengths, ctx_q, state, state_first, own_kv, anchor, first, count, per_kv, out, after=()):
    slab, width = ctx_q.shape
    heads = min(2, count)
    kv = first // per_kv
    pieces = len(anchor)
    work = count * slab * slab
    extra = ([] if out is None else [out]) + list(after)
    aliases = {} if out is None else {4 + pieces: 0}
    return pl.pallas_call(
        functools.partial(anchor_kernel, heads, pieces, len(extra)),
        grid=(count // heads,),
        out_shape=jax.ShapeDtypeStruct((slab, width), BF),
        in_specs=[
            SMEM,
            pl.BlockSpec((slab, heads * HD), lambda i: (0, first // heads + i)),
            pl.BlockSpec((slab, heads * 2 * HD), lambda i: (0, (first - state_first) // heads + i)),
            pl.BlockSpec((2, slab, HD), lambda i: (0, 0, kv)),
        ]
        + [pl.BlockSpec((2, slab // pieces, HD), lambda i: (0, 0, kv))] * pieces
        + [ANY] * len(extra),
        out_specs=pl.BlockSpec((slab, heads * HD), lambda i: (0, first // heads + i)),
        scratch_shapes=[pltpu.VMEM((slab, HD), BF), pltpu.VMEM((slab, 2 * HD), BF)],
        input_output_aliases=aliases,
        compiler_params=params(),
        cost_estimate=pl.CostEstimate(
            flops=work * HD * 8, bytes_accessed=count * slab * HD * 8, transcendentals=work
        ),
        name="context_anchor",
    )(lengths, ctx_q, state, own_kv, *anchor, *extra)


def source_kernel(slots, per_kv, lengths_ref, kv_ref, self_ref, *rest):
    q_refs, out_refs = rest[:slots], rest[slots : 2 * slots]
    q_rows, width = q_refs[0].shape
    slab = kv_ref.shape[1]
    host = lax.axis_index("hst")
    own_len = lengths_ref[host]
    query_count = slots * q_rows
    rows = per_kv * query_count
    lane = lax.broadcasted_iota(jnp.int32, (query_count, HD), 1)
    place = lax.broadcasted_iota(jnp.int32, (query_count, HD), 0)
    query_ids = jnp.bitwise_xor(place // q_rows, host) * q_rows + place % q_rows
    self_ok = (host * q_rows + lane <= query_ids) & (lane < q_rows)
    self_ok = jnp.concatenate([self_ok] * per_kv, 0)
    stats = jnp.zeros((query_count, HD), F32)
    key_ids = lax.broadcasted_iota(jnp.int32, (rows, slab), 1)
    pad = jnp.zeros((HD - q_rows, HD), F32)
    for j in range(width // HD // per_kv):
        cols = slice(j * HD, (j + 1) * HD)
        parts = []
        for h in range(per_kv):
            at = (j * per_kv + h) * HD
            parts += [q_refs[k][:, at : at + HD].astype(F32) for k in range(slots)]
        queries = jnp.concatenate(parts, 0).astype(BF)
        self_keys = jnp.concatenate([self_ref[0, :, cols].astype(F32), pad], 0).astype(BF)
        self_values = jnp.concatenate([self_ref[1, :, cols].astype(F32), pad], 0).astype(BF)
        near = dot_t(queries, kv_ref[0, :, cols]) * SCALE2
        near = jnp.where(key_ids < own_len, near, MASKED)
        selves = dot_t(queries, self_keys) * SCALE2
        selves = jnp.where(self_ok, selves, MASKED)
        peak = jnp.maximum(jnp.max(near, 1, keepdims=True), jnp.max(selves, 1, keepdims=True))
        near = jnp.exp2(near - peak)
        selves = jnp.exp2(selves - peak)
        sums = jnp.sum(near, 1, keepdims=True) + jnp.sum(selves, 1, keepdims=True)
        total = dot(near.astype(BF), kv_ref[1, :, cols]) + dot(selves.astype(BF), self_values)
        total = total / sums
        level = peak + jnp.log2(sums)
        for h in range(per_kv):
            head = j * per_kv + h
            at = h * query_count
            stats = jnp.where(lane == head, level[at : at + query_count, :], stats)
            for k in range(slots):
                out_refs[k][:, head * HD : (head + 1) * HD] = total[
                    at + k * q_rows : at + (k + 1) * q_rows, :
                ].astype(BF)
    high = stats.astype(BF)
    left = stats - high.astype(F32)
    middle = left.astype(BF)
    low = (left - middle.astype(F32)).astype(BF)
    for k in range(slots):
        take = slice(k * q_rows, (k + 1) * q_rows)
        for at, part in enumerate((high, middle, low)):
            out_refs[k][:, width + at * HD : width + (at + 1) * HD] = part.astype(F32)[take].astype(BF)


def source_part(lengths, own_kv, self_kv, query_slots, per_kv, after=()):
    slots = len(query_slots)
    q_rows, width = query_slots[0].shape
    slab = own_kv.shape[1]
    work = slots * q_rows * (width // HD) * slab

    def body(*refs):
        count = 3 + slots
        return source_kernel(slots, per_kv, *refs[:count], *refs[count + len(after) :])

    return pl.pallas_call(
        body,
        out_shape=[jax.ShapeDtypeStruct((q_rows, width + 3 * HD), BF)] * slots,
        in_specs=[SMEM, VMEM, VMEM] + [VMEM] * slots + [ANY] * len(after),
        out_specs=[VMEM] * slots,
        compiler_params=params(),
        cost_estimate=pl.CostEstimate(flops=work * HD * 8, bytes_accessed=2**21, transcendentals=work),
        name="query_source",
    )(lengths, own_kv, self_kv, *query_slots, *after)


def merge_kernel(slots, *refs):
    in_refs, out_ref = refs[:slots], refs[-1]
    width = out_ref.shape[1]

    def level(ref):
        parts = [ref[:, width + i * HD : width + (i + 1) * HD].astype(F32) for i in range(3)]
        return parts[0] + parts[1] + parts[2]

    levels = [level(ref) for ref in in_refs]
    peak = functools.reduce(jnp.maximum, levels)
    weights = [jnp.exp2(x - peak) for x in levels]
    whole = functools.reduce(jnp.add, weights)
    weights = [w / whole for w in weights]
    for h in range(width // HD):
        cols = slice(h * HD, (h + 1) * HD)
        total = sum(weights[k][:, h : h + 1] * in_refs[k][:, cols].astype(F32) for k in range(slots))
        out_ref[:, cols] = total.astype(BF)


def merge_part(slots, after=()):
    q_rows, wide = slots[0].shape
    width = wide - 3 * HD
    return pl.pallas_call(
        functools.partial(merge_kernel, len(slots)),
        out_shape=jax.ShapeDtypeStruct((q_rows, width), BF),
        in_specs=[VMEM] * len(slots) + [ANY] * len(after),
        out_specs=VMEM,
        compiler_params=params(),
        name="query_merge",
    )(*slots, *after)


def project_kernel(slots, targets, w_ref, *rest):
    in_refs = rest[:slots]
    out_refs, attended, partial = rest[-2 - targets : -2], rest[-2], rest[-1]
    q_rows = in_refs[0].shape[0]

    @pl.when(pl.program_id(0) == 0)
    def _():
        rows = jnp.concatenate([ref[...].astype(F32) for ref in in_refs], 0)
        attended[...] = rows.astype(BF)

    partial[...] = dot(attended[...], w_ref[...])
    part = slots * q_rows // targets
    me = lax.axis_index("tp")
    for k in range(targets):
        start = pl.multiple_of(jnp.bitwise_xor(me, k) * part, part)
        out_refs[k][...] = partial[pl.ds(start, part), :].astype(BF)


def project_part(attended_slots, out_weight, targets, after=()):
    slots = len(attended_slots)
    q_rows, depth = attended_slots[0].shape
    columns = out_weight.shape[1]
    rows = slots * q_rows
    part = rows // targets
    tile = min(256, columns)
    return pl.pallas_call(
        functools.partial(project_kernel, slots, targets),
        grid=(columns // tile,),
        out_shape=[jax.ShapeDtypeStruct((part, columns), BF)] * targets,
        in_specs=[pl.BlockSpec((depth, tile), lambda i: (0, i))]
        + [pl.BlockSpec((q_rows, depth), lambda i: (0, 0))] * slots
        + [ANY] * len(after),
        out_specs=[pl.BlockSpec((part, tile), lambda i: (0, i))] * targets,
        scratch_shapes=[pltpu.VMEM((rows, depth), BF), pltpu.VMEM((rows, tile), F32)],
        compiler_params=params(),
        cost_estimate=pl.CostEstimate(
            flops=2 * rows * depth * columns, bytes_accessed=2 * depth * columns, transcendentals=0
        ),
        name="query_project",
    )(out_weight, *attended_slots, *after)


def arrange_kernel(slots, targets, *refs):
    in_refs, out_ref, rows_ref = refs[:targets], refs[-2], refs[-1]
    part = in_refs[0].shape[0]
    q_rows = part * targets // slots
    me = lax.axis_index("tp")
    host = lax.axis_index("hst")
    for k in range(targets):
        piece = in_refs[k][...].astype(F32)
        for i in range(part // q_rows):
            slot = jnp.bitwise_xor(me, k) * (part // q_rows) + i
            start = pl.multiple_of(jnp.bitwise_xor(slot, host) * q_rows, q_rows)
            rows_ref[pl.ds(start, q_rows), :] = piece[i * q_rows : (i + 1) * q_rows]
    out_ref[...] = rows_ref[...].astype(BF)


def arrange(parts, slots):
    targets = len(parts)
    part, columns = parts[0].shape
    return pl.pallas_call(
        functools.partial(arrange_kernel, slots, targets),
        out_shape=jax.ShapeDtypeStruct((part * targets, columns), BF),
        in_specs=[VMEM] * targets,
        out_specs=VMEM,
        scratch_shapes=[pltpu.VMEM((part * targets, columns), F32)],
        compiler_params=params(),
        name="query_arrange",
    )(*parts)


def general_queries(lengths, own_kv, self_kv, query_q, out_weight, per_kv):
    host_id = lax.axis_index("hst")
    local_heads = query_q.shape[1] // HD
    kv_local = own_kv.shape[2] // HD
    slab_rows = own_kv.shape[1]
    own_len = lengths[host_id]
    row_ids = jnp.arange(slab_rows)
    all_queries = lax.all_gather(query_q, "hst", axis=0, tiled=True)
    query_count = all_queries.shape[0]
    q_rows = query_q.shape[0]
    source = jnp.concatenate([own_kv, self_kv], 1)
    source = source.reshape(2, slab_rows + q_rows, kv_local, HD).transpose(0, 2, 1, 3)
    query_ids = jnp.arange(query_count)
    context_ok = jnp.broadcast_to(row_ids[None, :] < own_len, (query_count, slab_rows))
    self_ok = (host_id * q_rows + jnp.arange(q_rows))[None, :] <= query_ids[:, None]
    seen_ok = jnp.concatenate([context_ok, self_ok], 1)
    query_heads = all_queries.reshape(query_count, local_heads, HD).transpose(1, 0, 2)

    def score_head(operands):
        query_rows, head_index = operands
        kv_index = head_index // per_kv
        scores = dot_t(query_rows, source[0, kv_index]) * HD ** (-0.5)
        scores = jnp.where(seen_ok, scores, MASKED)
        peak = jnp.max(scores, axis=1)
        expo = jnp.exp(scores - peak[:, None])
        return peak, jnp.sum(expo, axis=1), dot(expo.astype(BF), source[1, kv_index])

    maxima, totals, outputs = lax.map(score_head, (query_heads, jnp.arange(local_heads)))
    factor = jnp.exp(maxima - lax.pmax(maxima, "hst"))
    denominator, summed = lax.psum((totals * factor, outputs * factor[..., None]), "hst")
    attended = (summed / denominator[..., None]).astype(BF)
    attended = attended.transpose(1, 0, 2).reshape(query_count, local_heads * HD)
    return lax.psum(dot(attended, out_weight), "tp").astype(BF)


def per_device(hosts, groups, ctx_q, ctx_kv, lengths, query_q, query_kv, out_weight):
    slab = ctx_q.shape[0]
    local_heads = ctx_q.shape[1] // HD
    group_size = H // KVH
    kv_local = max(1, local_heads // group_size)
    per_kv = min(local_heads, group_size)
    q_rows = query_q.shape[0]
    host = lax.axis_index("hst")
    kv_first = lax.axis_index("tp") * local_heads // group_size
    self_kv = lax.dynamic_slice_in_dim(query_kv, kv_first * HD, kv_local * HD, 2)

    tiled = slab % (16 * hosts) == 0 and hosts & (hosts - 1) == 0
    fast = tiled and q_rows % 8 == 0 and groups & (groups - 1) == 0
    fast = fast and (hosts * q_rows) % (16 * groups) == 0
    own_count = per_kv
    anchor_count = min(4, per_kv)

    if not fast:
        own_kv = pick_kv(ctx_kv, kv_local, local_heads, 1)[0]
        query_out = general_queries(lengths, own_kv, self_kv, query_q, out_weight, per_kv)
        anchor = [spread(own_kv, "hst", 0)]
        context_out = None
        for first in range(0, local_heads, own_count):
            state = own_part(ctx_q, own_kv, first, own_count, per_kv)
            context_out = anchor_part(
                lengths, ctx_q, state, first, own_kv, anchor, first, own_count, per_kv, context_out
            )
        return context_out, query_out

    query_slots = exchange([query_q] * hosts, "hst", hosts)
    own_kv, *pieces = pick_kv(ctx_kv, kv_local, local_heads, hosts)
    dealt = [lax.ppermute(pieces[k - 1], "hst", [(0, k)]) for k in range(1, hosts)]
    states = [own_part(ctx_q, own_kv, 0, own_count, per_kv)]
    mine = jnp.where(host == 0, own_kv[:, : slab // hosts], functools.reduce(jnp.add, dealt))
    anchor = exchange([mine] * hosts, "hst", hosts, skip=(0,))
    sources = source_part(lengths, own_kv, self_kv, query_slots, per_kv, after=(states[0],))
    landed = exchange(sources, "hst", hosts)
    for first in range(own_count, local_heads, own_count):
        states.append(own_part(ctx_q, own_kv, first, own_count, per_kv, after=(sources[0],)))
    merged = merge_part(landed, after=(states[-1],))
    attended = exchange([merged] * hosts, "hst", hosts)

    context_out = None
    shared = None
    firsts = list(range(0, local_heads, anchor_count))
    for at, first in enumerate(firsts):
        if at == 1:
            shared = project_part(attended, out_weight, groups, after=(context_out,))
            arrived = exchange(shared, "tp", groups)
        if at == len(firsts) - 1:
            total = functools.reduce(jnp.add, [x.astype(F32) for x in arrived]).astype(BF)
            pieces_out = exchange([total] * groups, "tp", groups)
        after = {0: (merged,), 1: (shared[0],) if shared else ()}.get(at, ())
        if at == len(firsts) - 1:
            after = (total,)
        context_out = anchor_part(
            lengths,
            ctx_q,
            states[first // own_count],
            first // own_count * own_count,
            own_kv,
            anchor,
            first,
            anchor_count,
            per_kv,
            context_out,
            after,
        )
    query_out = arrange(pieces_out, hosts)
    return context_out, query_out


def solution(mesh):
    hosts, groups = mesh.shape["hst"], mesh.shape["tp"]
    return jax.shard_map(
        functools.partial(per_device, hosts, groups),
        mesh=mesh,
        in_specs=(
            P("hst", "tp"),
            P(None, "hst", None),
            P(),
            P("hst", "tp"),
            P(None, "hst", None),
            P("tp", "hst"),
        ),
        out_specs=(P("hst", "tp"), P(None, "hst")),
        check_vma=False,
    )
```

time: 438 us -> 168 us (0.38); the launches traced: 431 us -> 167 us
  matrix products: 137 us -> 0 us
  Pallas kernels: 0 us -> 94.4 us
  loops' own time: 85.4 us -> 0 us
  waiting for transfers between devices: 64 us -> 0.11 us
  starting transfers between devices: 0.08 us -> 61.5 us
  blocking collectives: 57.2 us -> 0 us
  local copies, waits for them, and re-layouts: 41 us -> 8.51 us
  other arithmetic: 32.3 us -> 1.26 us
  between operations: 14.2 us -> 1.07 us
    dot_general x65 -> x0, matrix products: 137 us -> none  [the longest x32 62.8 us: softmax_rows(): jnp.einsum('id,jd->ij', query_rows, key_rows, preferred_element_type=jnp....]
    pallas_call x0 -> x11, Pallas kernels: none -> 94.4 us  [the longest x4 78.8 us: anchor_part(): pl.pallas_call(functools.partial(anchor_kernel, heads, pieces, len(extra)...]
    another operation x2 -> x0, loops' own time: 85.4 us -> none  [the longest x1 44.6 us: per_device(): encoded = lax.map(encode_head, (head_queries, jnp.arange(local_heads)))]
    psum x2 -> x0, waiting for transfers between devices: 64 us -> none  [the longest x1 33.4 us: per_device(): lax.psum((totals * factor, outputs * factor[..., None]), 'hst')]
    ppermute x0 -> x41, starting transfers between devices: none -> 61.5 us  [the longest x34 52.4 us: exchange(): lax.ppermute(slots[k], axis, xor_pairs(size, k, skip))]
    psum x2 -> x0, blocking collectives: 36.8 us -> none  [the longest x1 24.4 us: per_device(): query_out = lax.psum(partial_out, 'tp').astype(jnp.bfloat16)]
    dynamic_slice x33 -> x0, local copies, waits for them, and re-layouts: 21.2 us -> none  [the longest x32 20.2 us: per_device(): encoded = lax.map(encode_head, (head_queries, jnp.arange(local_heads)))]
    reduce_sum x32 -> x0, other arithmetic: 15.6 us -> none  [the longest x16 12.3 us: encode_head(): probs = (expo / jnp.sum(expo, axis=1, keepdims=True)).astype(jnp.bfloat16)]
  transfers between devices with their start and end apart: 2 -> 41, of which waited for: 2 -> 0; matrix products, arithmetic and copies ran while one was open for 3% -> 1% of each run, Pallas kernels for 0% -> 55%
where the time goes in v1:
time: 168 us; the launch traced here: 167 us
  Pallas kernels  94.4 us (56%)
  starting transfers between devices  61.5 us (37%)
  local copies, waits for them, and re-layouts  8.51 us (5%)
    pallas_call x4, Pallas kernels, anchor_part(): pl.pallas_call(functools.partial(anchor_kernel, heads, pieces, len(extra)...  78.8 us
    ppermute x34, starting transfers between devices, exchange(): lax.ppermute(slots[k], axis, xor_pairs(size, k, skip))  52.4 us
    pallas_call x2, Pallas kernels, own_part(): pl.pallas_call(functools.partial(own_kernel, heads), grid=(steps,), out_s...  9.48 us
    ppermute x7, starting transfers between devices, per_device(): lax.ppermute(pieces[k - 1], 'hst', [(0, k)])  9.04 us
    unnamed x34, local copies, waits for them, and re-layouts  8.51 us
  transfers between devices with their start and end apart: 41, of which 0 were waited for; matrix products, arithmetic and copies ran while one was open for 1% of the time, Pallas kernels for 55%

profile of v1, /device:TPU:6, one launch (start us, length us, event | category | flops | bytes accessed | tf_op | source)
XLA Modules:
  0.0 166.8 jit_solution(5570543745468682275)
XLA Ops:
  2.8 1.4 collective-permute-start.2
  4.5 1.9 %copy-done.10 = bf16[2,768,1024]{2,1,0:T(8,128)(2,1)S(1)} copy-done((bf16[2,768,1024]{2,1,0:T(8,128)(2,1)S(1)}, bf16[2,768,1024]{2,1,0:T(8,128)(2,1)}, u32[]{:S(2)}) %copy-start.10) | copy-done | bytes 3145752
  7.5 2.6 %collective-permute-start.6 = (bf16[8,2048]{1,0:T(8,128)(2,1)}, bf16[8,2048]{1,0:T(8,128)(2,1)S(1)}, u32[]{:S(2)}, u32[]{:S(2)}) collective-permute-start(bf16[8,2048]{1,0:T(8,128)(2,1)} %refs_3_.1), channel_id=1, source_target_pairs={{0,28},{4,24},{8,20},{12,16},{16,12},{20,8},{24,4},{28,0},{1,29},{... | collective-permute-start | bytes 98312 | tf_op jit(solution)/shard_map/ppermute | solution.py:47
  10.2 1.3 collective-permute-start.7
  12.8 4.7 %context_own.2.refs_11_.state_ref = bf16[768,2048]{1,0:T(8,128)(2,1)S(1)} custom-call(bf16[768,2048]{1,0:T(8,128)(2,1)S(1)} %copy-done.2, bf16[2,768,256]{2,1,0:T(8,128)(2,1)S(1)} %get-tuple-element.22.kv_ref.refs_1_), custom_call_target="tpu_custom_call" | custom-call | flops 3221225472 | bytes 4718592 | tf_op jit(solution)/shard_map/context_own/pallas_call | solution.py:132
  17.5 1.7 copy-done.3
  19.2 1.3 collective-permute-start.9
  20.5 1.3 collective-permute-start.10
  21.8 1.3 collective-permute-start.11
  24.4 1.3 collective-permute-start.13
  25.7 1.9 %copy-done.4 = bf16[768,2048]{1,0:T(8,128)(2,1)S(1)} copy-done((bf16[768,2048]{1,0:T(8,128)(2,1)S(1)}, bf16[768,2048]{1,0:T(8,128)(2,1)}, u32[]{:S(2)}) %copy-start.4) | copy-done | bytes 3145752
  28.7 2.4 %query_source.1 = (bf16[8,2432]{1,0:T(8,128)(2,1)S(1)}, bf16[8,2432]{1,0:T(8,128)(2,1)S(1)}, bf16[8,2432]{1,0:T(8,128)(2,1)S(1)}, bf16[8,2432]{1,0:T(8,128)(2,1)...) custom-call(s32[8]{0:T(128)S(1)} %copy-done.12, ...), custom_call_target="tpu_custom_call" | custom-call | flops 805306368 | bytes 2097152 | tf_op jit(solution)/shard_map/query_source/pallas_call | solution.py:336
  33.1 5.3 %collective-permute-start.24 = (bf16[8,2432]{1,0:T(8,128)(2,1)S(1)}, bf16[8,2432]{1,0:T(8,128)(2,1)S(1)}, u32[]{:S(2)}, u32[]{:S(2)}) collective-permute-start(bf16[8,2432]{1,0:T(8,128)(2,1)S(1)} %get-tuple-element.34), channel_id=1, source_target_pairs={{0,16},{4,20},{8,24},{12,28},{16,0},{20,4},{24,8},{28,12},{1,17},{... | collective-permute-start | bytes 116744 | tf_op jit(solution)/shard_map/ppermute | solution.py:47
  39.6 2.9 %collective-permute-start.26 = (bf16[8,2432]{1,0:T(8,128)(2,1)S(1)}, bf16[8,2432]{1,0:T(8,128)(2,1)S(1)}, u32[]{:S(2)}, u32[]{:S(2)}) collective-permute-start(bf16[8,2432]{1,0:T(8,128)(2,1)S(1)} %get-tuple-element.36), channel_id=1, source_target_pairs={{0,24},{4,28},{8,16},{12,20},{16,8},{20,12},{24,0},{28,4},{1,25},{... | collective-permute-start | bytes 116744 | tf_op jit(solution)/shard_map/ppermute | solution.py:47
  42.7 4.4 %collective-permute-start.20 = (bf16[2,96,256]{2,1,0:T(8,128)(2,1)S(1)}, bf16[2,96,256]{2,1,0:T(8,128)(2,1)S(1)}, u32[]{:S(2)}, u32[]{:S(2)}) collective-permute-start(bf16[2,96,256]{2,1,0:T(8,128)(2,1)S(1)} %add_select_fusion.rest_0_), channel_id=1, source_target_pairs={{0,28},{4,24},{8,20},{12,16},{16,12},{20,8},{24,4},{1,29},{5,25},{... | collective-permute-start | bytes 294920 | tf_op jit(solution)/shard_map/ppermute | solution.py:47
  47.1 1.3 collective-permute-start.19
  48.4 4.8 %context_own.3.refs_8_.state_ref = bf16[768,2048]{1,0:T(8,128)(2,1)S(1)} custom-call(bf16[768,2048]{1,0:T(8,128)(2,1)S(1)} %copy-done.2, bf16[2,768,256]{2,1,0:T(8,128)(2,1)S(1)} %copy-done.7, bf16[8,2432]{1,0:T(8,128)(2,1)S(1)} %get-tuple-element.23.rest_0_.refs_0_), custom_call_target="tpu_custom_call" | custom-call | flops 3221225472 | bytes 4718592 | tf_op jit(solution)/shard_map/context_own/pallas_call | solution.py:132
  54.3 2.8 %collective-permute-start.33 = (bf16[8,2048]{1,0:T(8,128)(2,1)S(1)}, bf16[8,2048]{1,0:T(8,128)(2,1)S(1)}, u32[]{:S(2)}, u32[]{:S(2)}) collective-permute-start(bf16[8,2048]{1,0:T(8,128)(2,1)S(1)} %query_merge.1.rest_8_.rest_0_), channel_id=1, source_target_pairs={{0,24},{4,28},{8,16},{12,20},{16,8},{20,12},{24,0},{28,4},{1,25},{... | collective-permute-start | bytes 98312 | tf_op jit(solution)/shard_map/ppermute | solution.py:47
  57.1 2.8 %collective-permute-start.18 = (bf16[2,96,256]{2,1,0:T(8,128)(2,1)S(1)}, bf16[2,96,256]{2,1,0:T(8,128)(2,1)S(1)}, u32[]{:S(2)}, u32[]{:S(2)}) collective-permute-start(bf16[2,96,256]{2,1,0:T(8,128)(2,1)S(1)} %add_select_fusion.rest_0_), channel_id=1, source_target_pairs={{0,20},{4,16},{8,28},{12,24},{16,4},{24,12},{28,8},{1,21},{5,17},{... | collective-permute-start | bytes 294920 | tf_op jit(solution)/shard_map/ppermute | solution.py:47
  60.0 2.6 %collective-permute-start.17 = (bf16[2,96,256]{2,1,0:T(8,128)(2,1)S(1)}, bf16[2,96,256]{2,1,0:T(8,128)(2,1)S(1)}, u32[]{:S(2)}, u32[]{:S(2)}) collective-permute-start(bf16[2,96,256]{2,1,0:T(8,128)(2,1)S(1)} %add_select_fusion.rest_0_), channel_id=1, source_target_pairs={{0,16},{4,20},{8,24},{12,28},{20,4},{24,8},{28,12},{1,17},{5,21},{... | collective-permute-start | bytes 294920 | tf_op jit(solution)/shard_map/ppermute | solution.py:47
  62.7 2.8 %collective-permute-start.16 = (bf16[2,96,256]{2,1,0:T(8,128)(2,1)S(1)}, bf16[2,96,256]{2,1,0:T(8,128)(2,1)S(1)}, u32[]{:S(2)}, u32[]{:S(2)}) collective-permute-start(bf16[2,96,256]{2,1,0:T(8,128)(2,1)S(1)} %add_select_fusion.rest_0_), channel_id=1, source_target_pairs={{0,12},{4,8},{8,4},{16,28},{20,24},{24,20},{28,16},{1,13},{5,9},{9... | collective-permute-start | bytes 294920 | tf_op jit(solution)/shard_map/ppermute | solution.py:47
  65.5 2.8 %collective-permute-start.15 = (bf16[2,96,256]{2,1,0:T(8,128)(2,1)S(1)}, bf16[2,96,256]{2,1,0:T(8,128)(2,1)S(1)}, u32[]{:S(2)}, u32[]{:S(2)}) collective-permute-start(bf16[2,96,256]{2,1,0:T(8,128)(2,1)S(1)} %add_select_fusion.rest_0_), channel_id=1, source_target_pairs={{0,8},{4,12},{12,4},{16,24},{20,28},{24,16},{28,20},{1,9},{5,13},{... | collective-permute-start | bytes 294920 | tf_op jit(solution)/shard_map/ppermute | solution.py:47
  68.3 2.1 %collective-permute-start.14 = (bf16[2,96,256]{2,1,0:T(8,128)(2,1)S(1)}, bf16[2,96,256]{2,1,0:T(8,128)(2,1)S(1)}, u32[]{:S(2)}, u32[]{:S(2)}) collective-permute-start(bf16[2,96,256]{2,1,0:T(8,128)(2,1)S(1)} %add_select_fusion.rest_0_), channel_id=1, source_target_pairs={{0,4},{8,12},{12,8},{16,20},{20,16},{24,28},{28,24},{1,5},{9,13},{... | collective-permute-start | bytes 294920 | tf_op jit(solution)/shard_map/ppermute | solution.py:47
  74.5 19.7 %context_anchor.4.rest_8_ = bf16[768,2048]{1,0:T(8,128)(2,1)} custom-call(s32[8]{0:T(128)S(1)} %copy-done.12, bf16[768,2048]{1,0:T(8,128)(2,1)S(1)} %copy-done.2, bf16[768,2048]{1,0:T(8,128)(2,1)S(1)} %copy-done.5, bf16[2,768,256]{2,1,0:T(8,128)(2,1)S(1)} %copy-done.8, bf16[2,96,256]{2,1,0:T(8,128)(2,1)S(1)} %add_select_fusion.rest_0_, ...), custom_call_target="tpu_custom_call" | custom-call | flops 2415919104 | bytes 3145728 | tf_op jit(solution)/shard_map/context_anchor/pallas_call | solution.py:249
  94.3 1.9 %copy-done.1 = bf16[768,2048]{1,0:T(8,128)(2,1)S(1)} copy-done((bf16[768,2048]{1,0:T(8,128)(2,1)S(1)}, bf16[768,2048]{1,0:T(8,128)(2,1)}, u32[]{:S(2)}) %copy-start.1) | copy-done | bytes 3145752
  96.2 1.9 %query_project.1 = (bf16[16,1024]{1,0:T(8,128)(2,1)S(1)}, bf16[16,1024]{1,0:T(8,128)(2,1)S(1)}, bf16[16,1024]{1,0:T(8,128)(2,1)S(1)}, bf16[16,1024]{1,0:T(8,128)(2,1)S(1)}) custom-call(bf16[2048,1024]{1,0:T(8,128)(2,1)S(1)} %copy-done.9, bf16[8,2048]{1,0:T(8,128)(2,1)S(1)} %query_merge.1.rest_8_.rest_0_, ...), custom_call_target="tpu_custom_call" | custom-call | flops 268435456 | bytes 4194304 | tf_op jit(solution)/shard_map/query_project/pallas_call | solution.py:404
  98.1 1.6 collective-permute-start.35
  99.7 2.6 %collective-permute-start.36 = (bf16[16,1024]{1,0:T(8,128)(2,1)S(1)}, bf16[16,1024]{1,0:T(8,128)(2,1)S(1)}, u32[]{:S(2)}, u32[]{:S(2)}) collective-permute-start(bf16[16,1024]{1,0:T(8,128)(2,1)S(1)} %get-tuple-element.40), channel_id=1, source_target_pairs={{0,2},{1,3},{2,0},{3,1},{4,6},{5,7},{6,4},{7,5},{8,10},{9,11},{10,... | collective-permute-start | bytes 98312 | tf_op jit(solution)/shard_map/ppermute | solution.py:47
  102.5 19.7 %context_anchor.5.rest_8_ = bf16[768,2048]{1,0:T(8,128)(2,1)} custom-call(s32[8]{0:T(128)S(1)} %copy-done.12, bf16[768,2048]{1,0:T(8,128)(2,1)S(1)} %copy-done.2, bf16[768,2048]{1,0:T(8,128)(2,1)S(1)} %copy-done.5, bf16[2,768,256]{2,1,0:T(8,128)(2,1)S(1)} %copy-done.8, ...), custom_call_target="tpu_custom_call", output_to_operand_aliasing={{}: (12, {})} | custom-call | flops 2415919104 | bytes 3145728 | tf_op jit(solution)/shard_map/context_anchor/pallas_call | solution.py:249
  122.2 19.7 %context_anchor.6.rest_8_ = bf16[768,2048]{1,0:T(8,128)(2,1)} custom-call(s32[8]{0:T(128)S(1)} %copy-done.12, bf16[768,2048]{1,0:T(8,128)(2,1)S(1)} %copy-done.2, bf16[768,2048]{1,0:T(8,128)(2,1)S(1)} %context_own.3.refs_8_.state_ref, bf16[2,768,256]{2,1,0:T(8,128)(2,1)S(1)} %copy-done.8, ...), custom_call_target="tpu_custom_call", output_to_operand_aliasing={{}: (12, {})} | custom-call | flops 2415919104 | bytes 3145728 | tf_op jit(solution)/shard_map/context_anchor/pallas_call | solution.py:249
  141.9 3.7 %collective-permute-start.40 = (bf16[16,1024]{1,0:T(8,128)(2,1)S(1)}, bf16[16,1024]{1,0:T(8,128)(2,1)S(1)}, u32[]{:S(2)}, u32[]{:S(2)}) collective-permute-start(bf16[16,1024]{1,0:T(8,128)(2,1)S(1)} %add_convert_fusion.rest_9_.refs_0_), channel_id=1, source_target_pairs={{0,3},{1,2},{2,1},{3,0},{4,7},{5,6},{6,5},{7,4},{8,11},{9,10},{10,... | collective-permute-start | bytes 98312 | tf_op jit(solution)/shard_map/ppermute | solution.py:47
  146.4 19.7 %context_anchor.7 = bf16[768,2048]{1,0:T(8,128)(2,1)} custom-call(s32[8]{0:T(128)S(1)} %copy-done.12, bf16[768,2048]{1,0:T(8,128)(2,1)S(1)} %copy-done.2, bf16[768,2048]{1,0:T(8,128)(2,1)S(1)} %context_own.3.refs_8_.state_ref, bf16[2,768,256]{2,1,0:T(8,128)(2,1)S(1)} %copy-done.8, ...), custom_call_target="tpu_custom_call", output_to_operand_aliasing={{}: (12, {})} | custom-call | flops 2415919104 | bytes 3145728 | tf_op jit(solution)/shard_map/context_anchor/pallas_call | solution.py:249
  (98 shorter events, 17.6 us)
Async XLA Ops:
  4.2 15.0 %collective-permute-start.1 = (bf16[8,2048]{1,0:T(8,128)(2,1)}, bf16[8,2048]{1,0:T(8,128)(2,1)S(1)}, u32[]{:S(2)}, u32[]{:S(2)}) collective-permute-start(bf16[8,2048]{1,0:T(8,128)(2,1)} %refs_3_.1), channel_id=1, source_target_pairs={{0,8},{4,12},{8,0},{12,4},{16,24},{20,28},{24,16},{28,20},{1,9},{5... | collective-permute-start | bytes 98312 | tf_op jit(solution)/shard_map/ppermute | solution.py:47
  7.3 13.2 %collective-permute-start = (bf16[8,2048]{1,0:T(8,128)(2,1)}, bf16[8,2048]{1,0:T(8,128)(2,1)S(1)}, u32[]{:S(2)}, u32[]{:S(2)}) collective-permute-start(bf16[8,2048]{1,0:T(8,128)(2,1)} %refs_3_.1), channel_id=1, source_target_pairs={{0,4},{4,0},{8,12},{12,8},{16,20},{20,16},{24,28},{28,24},{1,5},{5... | collective-permute-start | bytes 98312 | tf_op jit(solution)/shard_map/ppermute | solution.py:47
  7.5 14.3 %collective-permute-start.6 = (bf16[8,2048]{1,0:T(8,128)(2,1)}, bf16[8,2048]{1,0:T(8,128)(2,1)S(1)}, u32[]{:S(2)}, u32[]{:S(2)}) collective-permute-start(bf16[8,2048]{1,0:T(8,128)(2,1)} %refs_3_.1), channel_id=1, source_target_pairs={{0,28},{4,24},{8,20},{12,16},{16,12},{20,8},{24,4},{28,0},{1,29},{... | collective-permute-start | bytes 98312 | tf_op jit(solution)/shard_map/ppermute | solution.py:47
  10.2 12.9 %collective-permute-start.7 = (bf16[2,96,256]{2,1,0:T(8,128)(2,1)}, bf16[2,96,256]{2,1,0:T(8,128)(2,1)}, u32[]{:S(2)}, u32[]{:S(2)}) collective-permute-start(bf16[2,96,256]{2,1,0:T(8,128)(2,1)} %get-tuple-element.24), channel_id=1, source_target_pairs={{0,4},{1,5},{2,6},{3,7}} | collective-permute-start | bytes 294920 | tf_op jit(solution)/shard_map/ppermute | solution.py:516
  11.5 12.9 %collective-permute-start.8 = (bf16[2,96,256]{2,1,0:T(8,128)(2,1)}, bf16[2,96,256]{2,1,0:T(8,128)(2,1)}, u32[]{:S(2)}, u32[]{:S(2)}) collective-permute-start(bf16[2,96,256]{2,1,0:T(8,128)(2,1)} %get-tuple-element.25), channel_id=1, source_target_pairs={{0,8},{1,9},{2,10},{3,11}} | collective-permute-start | bytes 294920 | tf_op jit(solution)/shard_map/ppermute | solution.py:516
  19.2 12.0 %collective-permute-start.9 = (bf16[2,96,256]{2,1,0:T(8,128)(2,1)}, bf16[2,96,256]{2,1,0:T(8,128)(2,1)}, u32[]{:S(2)}, u32[]{:S(2)}) collective-permute-start(bf16[2,96,256]{2,1,0:T(8,128)(2,1)} %copy-done.16), channel_id=1, source_target_pairs={{0,12},{1,13},{2,14},{3,15}} | collective-permute-start | bytes 294920 | tf_op jit(solution)/shard_map/ppermute | solution.py:516
  20.5 10.8 %collective-permute-start.10 = (bf16[2,96,256]{2,1,0:T(8,128)(2,1)}, bf16[2,96,256]{2,1,0:T(8,128)(2,1)}, u32[]{:S(2)}, u32[]{:S(2)}) collective-permute-start(bf16[2,96,256]{2,1,0:T(8,128)(2,1)} %copy-done.15), channel_id=1, source_target_pairs={{0,16},{1,17},{2,18},{3,19}} | collective-permute-start | bytes 294920 | tf_op jit(solution)/shard_map/ppermute | solution.py:516
  21.8 10.1 %collective-permute-start.11 = (bf16[2,96,256]{2,1,0:T(8,128)(2,1)}, bf16[2,96,256]{2,1,0:T(8,128)(2,1)}, u32[]{:S(2)}, u32[]{:S(2)}) collective-permute-start(bf16[2,96,256]{2,1,0:T(8,128)(2,1)} %copy-done.14), channel_id=1, source_target_pairs={{0,20},{1,21},{2,22},{3,23}} | collective-permute-start | bytes 294920 | tf_op jit(solution)/shard_map/ppermute | solution.py:516
  23.1 10.0 %collective-permute-start.12 = (bf16[2,96,256]{2,1,0:T(8,128)(2,1)}, bf16[2,96,256]{2,1,0:T(8,128)(2,1)}, u32[]{:S(2)}, u32[]{:S(2)}) collective-permute-start(bf16[2,96,256]{2,1,0:T(8,128)(2,1)} %copy-done.13), channel_id=1, source_target_pairs={{0,24},{1,25},{2,26},{3,27}} | collective-permute-start | bytes 294920 | tf_op jit(solution)/shard_map/ppermute | solution.py:516
  24.4 14.0 %collective-permute-start.13 = (bf16[2,96,256]{2,1,0:T(8,128)(2,1)S(1)}, bf16[2,96,256]{2,1,0:T(8,128)(2,1)}, u32[]{:S(2)}, u32[]{:S(2)}) collective-permute-start(bf16[2,96,256]{2,1,0:T(8,128)(2,1)S(1)} %get-tuple-element.30), channel_id=1, source_target_pairs={{0,28},{1,29},{2,30},{3,31}} | collective-permute-start | bytes 294920 | tf_op jit(solution)/shard_map/ppermute | solution.py:516
  31.3 11.2 %collective-permute-start.22 = (bf16[8,2432]{1,0:T(8,128)(2,1)S(1)}, bf16[8,2432]{1,0:T(8,128)(2,1)S(1)}, u32[]{:S(2)}, u32[]{:S(2)}) collective-permute-start(bf16[8,2432]{1,0:T(8,128)(2,1)S(1)} %get-tuple-element.32), channel_id=1, source_target_pairs={{0,8},{4,12},{8,0},{12,4},{16,24},{20,28},{24,16},{28,20},{1,9},{5... | collective-permute-start | bytes 116744 | tf_op jit(solution)/shard_map/ppermute | solution.py:47
  31.9 10.8 %collective-permute-start.23 = (bf16[8,2432]{1,0:T(8,128)(2,1)S(1)}, bf16[8,2432]{1,0:T(8,128)(2,1)S(1)}, u32[]{:S(2)}, u32[]{:S(2)}) collective-permute-start(bf16[8,2432]{1,0:T(8,128)(2,1)S(1)} %get-tuple-element.33), channel_id=1, source_target_pairs={{0,12},{4,8},{8,4},{12,0},{16,28},{20,24},{24,20},{28,16},{1,13},{... | collective-permute-start | bytes 116744 | tf_op jit(solution)/shard_map/ppermute | solution.py:47
  33.1 13.9 %collective-permute-start.24 = (bf16[8,2432]{1,0:T(8,128)(2,1)S(1)}, bf16[8,2432]{1,0:T(8,128)(2,1)S(1)}, u32[]{:S(2)}, u32[]{:S(2)}) collective-permute-start(bf16[8,2432]{1,0:T(8,128)(2,1)S(1)} %get-tuple-element.34), channel_id=1, source_target_pairs={{0,16},{4,20},{8,24},{12,28},{16,0},{20,4},{24,8},{28,12},{1,17},{... | collective-permute-start | bytes 116744 | tf_op jit(solution)/shard_map/ppermute | solution.py:47
  38.4 14.8 %collective-permute-start.25 = (bf16[8,2432]{1,0:T(8,128)(2,1)S(1)}, bf16[8,2432]{1,0:T(8,128)(2,1)S(1)}, u32[]{:S(2)}, u32[]{:S(2)}) collective-permute-start(bf16[8,2432]{1,0:T(8,128)(2,1)S(1)} %get-tuple-element.35), channel_id=1, source_target_pairs={{0,20},{4,16},{8,28},{12,24},{16,4},{20,0},{24,12},{28,8},{1,21},{... | collective-permute-start | bytes 116744 | tf_op jit(solution)/shard_map/ppermute | solution.py:47
  39.6 13.5 %collective-permute-start.26 = (bf16[8,2432]{1,0:T(8,128)(2,1)S(1)}, bf16[8,2432]{1,0:T(8,128)(2,1)S(1)}, u32[]{:S(2)}, u32[]{:S(2)}) collective-permute-start(bf16[8,2432]{1,0:T(8,128)(2,1)S(1)} %get-tuple-element.36), channel_id=1, source_target_pairs={{0,24},{4,28},{8,16},{12,20},{16,8},{20,12},{24,0},{28,4},{1,25},{... | collective-permute-start | bytes 116744 | tf_op jit(solution)/shard_map/ppermute | solution.py:47
  42.5 10.7 %collective-permute-start.27 = (bf16[8,2432]{1,0:T(8,128)(2,1)S(1)}, bf16[8,2432]{1,0:T(8,128)(2,1)S(1)}, u32[]{:S(2)}, u32[]{:S(2)}) collective-permute-start(bf16[8,2432]{1,0:T(8,128)(2,1)S(1)} %get-tuple-element.37), channel_id=1, source_target_pairs={{0,28},{4,24},{8,20},{12,16},{16,12},{20,8},{24,4},{28,0},{1,29},{... | collective-permute-start | bytes 116744 | tf_op jit(solution)/shard_map/ppermute | solution.py:47
  42.7 22.8 %collective-permute-start.20 = (bf16[2,96,256]{2,1,0:T(8,128)(2,1)S(1)}, bf16[2,96,256]{2,1,0:T(8,128)(2,1)S(1)}, u32[]{:S(2)}, u32[]{:S(2)}) collective-permute-start(bf16[2,96,256]{2,1,0:T(8,128)(2,1)S(1)} %add_select_fusion.rest_0_), channel_id=1, source_target_pairs={{0,28},{4,24},{8,20},{12,16},{16,12},{20,8},{24,4},{1,29},{5,25},{... | collective-permute-start | bytes 294920 | tf_op jit(solution)/shard_map/ppermute | solution.py:47
  47.1 21.3 %collective-permute-start.19 = (bf16[2,96,256]{2,1,0:T(8,128)(2,1)S(1)}, bf16[2,96,256]{2,1,0:T(8,128)(2,1)S(1)}, u32[]{:S(2)}, u32[]{:S(2)}) collective-permute-start(bf16[2,96,256]{2,1,0:T(8,128)(2,1)S(1)} %add_select_fusion.rest_0_), channel_id=1, source_target_pairs={{0,24},{4,28},{8,16},{12,20},{16,8},{20,12},{28,4},{1,25},{5,29},{... | collective-permute-start | bytes 294920 | tf_op jit(solution)/shard_map/ppermute | solution.py:47
  57.1 13.3 %collective-permute-start.18 = (bf16[2,96,256]{2,1,0:T(8,128)(2,1)S(1)}, bf16[2,96,256]{2,1,0:T(8,128)(2,1)S(1)}, u32[]{:S(2)}, u32[]{:S(2)}) collective-permute-start(bf16[2,96,256]{2,1,0:T(8,128)(2,1)S(1)} %add_select_fusion.rest_0_), channel_id=1, source_target_pairs={{0,20},{4,16},{8,28},{12,24},{16,4},{24,12},{28,8},{1,21},{5,17},{... | collective-permute-start | bytes 294920 | tf_op jit(solution)/shard_map/ppermute | solution.py:47
  60.0 11.5 %collective-permute-start.17 = (bf16[2,96,256]{2,1,0:T(8,128)(2,1)S(1)}, bf16[2,96,256]{2,1,0:T(8,128)(2,1)S(1)}, u32[]{:S(2)}, u32[]{:S(2)}) collective-permute-start(bf16[2,96,256]{2,1,0:T(8,128)(2,1)S(1)} %add_select_fusion.rest_0_), channel_id=1, source_target_pairs={{0,16},{4,20},{8,24},{12,28},{20,4},{24,8},{28,12},{1,17},{5,21},{... | collective-permute-start | bytes 294920 | tf_op jit(solution)/shard_map/ppermute | solution.py:47
  62.7 10.0 %collective-permute-start.16 = (bf16[2,96,256]{2,1,0:T(8,128)(2,1)S(1)}, bf16[2,96,256]{2,1,0:T(8,128)(2,1)S(1)}, u32[]{:S(2)}, u32[]{:S(2)}) collective-permute-start(bf16[2,96,256]{2,1,0:T(8,128)(2,1)S(1)} %add_select_fusion.rest_0_), channel_id=1, source_target_pairs={{0,12},{4,8},{8,4},{16,28},{20,24},{24,20},{28,16},{1,13},{5,9},{9... | collective-permute-start | bytes 294920 | tf_op jit(solution)/shard_map/ppermute | solution.py:47
  70.5 23.7 %collective-permute-start.32 = (bf16[8,2048]{1,0:T(8,128)(2,1)S(1)}, bf16[8,2048]{1,0:T(8,128)(2,1)S(1)}, u32[]{:S(2)}, u32[]{:S(2)}) collective-permute-start(bf16[8,2048]{1,0:T(8,128)(2,1)S(1)} %query_merge.1.rest_8_.rest_0_), channel_id=1, source_target_pairs={{0,20},{4,16},{8,28},{12,24},{16,4},{20,0},{24,12},{28,8},{1,21},{... | collective-permute-start | bytes 98312 | tf_op jit(solution)/shard_map/ppermute | solution.py:47
  71.5 22.8 %collective-permute-start.31 = (bf16[8,2048]{1,0:T(8,128)(2,1)S(1)}, bf16[8,2048]{1,0:T(8,128)(2,1)S(1)}, u32[]{:S(2)}, u32[]{:S(2)}) collective-permute-start(bf16[8,2048]{1,0:T(8,128)(2,1)S(1)} %query_merge.1.rest_8_.rest_0_), channel_id=1, source_target_pairs={{0,16},{4,20},{8,24},{12,28},{16,0},{20,4},{24,8},{28,12},{1,17},{... | collective-permute-start | bytes 98312 | tf_op jit(solution)/shard_map/ppermute | solution.py:47
  72.7 21.6 %collective-permute-start.30 = (bf16[8,2048]{1,0:T(8,128)(2,1)S(1)}, bf16[8,2048]{1,0:T(8,128)(2,1)S(1)}, u32[]{:S(2)}, u32[]{:S(2)}) collective-permute-start(bf16[8,2048]{1,0:T(8,128)(2,1)S(1)} %query_merge.1.rest_8_.rest_0_), channel_id=1, source_target_pairs={{0,12},{4,8},{8,4},{12,0},{16,28},{20,24},{24,20},{28,16},{1,13},{... | collective-permute-start | bytes 98312 | tf_op jit(solution)/shard_map/ppermute | solution.py:47
  73.1 21.1 %collective-permute-start.29 = (bf16[8,2048]{1,0:T(8,128)(2,1)S(1)}, bf16[8,2048]{1,0:T(8,128)(2,1)S(1)}, u32[]{:S(2)}, u32[]{:S(2)}) collective-permute-start(bf16[8,2048]{1,0:T(8,128)(2,1)S(1)} %query_merge.1.rest_8_.rest_0_), channel_id=1, source_target_pairs={{0,8},{4,12},{8,0},{12,4},{16,24},{20,28},{24,16},{28,20},{1,9},{5... | collective-permute-start | bytes 98312 | tf_op jit(solution)/shard_map/ppermute | solution.py:47
  74.1 20.2 %collective-permute-start.28 = (bf16[8,2048]{1,0:T(8,128)(2,1)S(1)}, bf16[8,2048]{1,0:T(8,128)(2,1)S(1)}, u32[]{:S(2)}, u32[]{:S(2)}) collective-permute-start(bf16[8,2048]{1,0:T(8,128)(2,1)S(1)} %query_merge.1.rest_8_.rest_0_), channel_id=1, source_target_pairs={{0,4},{4,0},{8,12},{12,8},{16,20},{20,16},{24,28},{28,24},{1,5},{5... | collective-permute-start | bytes 98312 | tf_op jit(solution)/shard_map/ppermute | solution.py:47
  98.1 43.8 %collective-permute-start.35 = (bf16[16,1024]{1,0:T(8,128)(2,1)S(1)}, bf16[16,1024]{1,0:T(8,128)(2,1)S(1)}, u32[]{:S(2)}, u32[]{:S(2)}) collective-permute-start(bf16[16,1024]{1,0:T(8,128)(2,1)S(1)} %get-tuple-element.39), channel_id=1, source_target_pairs={{0,1},{1,0},{2,3},{3,2},{4,5},{5,4},{6,7},{7,6},{8,9},{9,8},{10,11... | collective-permute-start | bytes 98312 | tf_op jit(solution)/shard_map/ppermute | solution.py:47
  99.7 42.2 %collective-permute-start.36 = (bf16[16,1024]{1,0:T(8,128)(2,1)S(1)}, bf16[16,1024]{1,0:T(8,128)(2,1)S(1)}, u32[]{:S(2)}, u32[]{:S(2)}) collective-permute-start(bf16[16,1024]{1,0:T(8,128)(2,1)S(1)} %get-tuple-element.40), channel_id=1, source_target_pairs={{0,2},{1,3},{2,0},{3,1},{4,6},{5,7},{6,4},{7,5},{8,10},{9,11},{10,... | collective-permute-start | bytes 98312 | tf_op jit(solution)/shard_map/ppermute | solution.py:47
  102.3 39.6 %collective-permute-start.37 = (bf16[16,1024]{1,0:T(8,128)(2,1)S(1)}, bf16[16,1024]{1,0:T(8,128)(2,1)S(1)}, u32[]{:S(2)}, u32[]{:S(2)}) collective-permute-start(bf16[16,1024]{1,0:T(8,128)(2,1)S(1)} %get-tuple-element.41), channel_id=1, source_target_pairs={{0,3},{1,2},{2,1},{3,0},{4,7},{5,6},{6,5},{7,4},{8,11},{9,10},{10,... | collective-permute-start | bytes 98312 | tf_op jit(solution)/shard_map/ppermute | solution.py:47
  141.9 24.2 %collective-permute-start.40 = (bf16[16,1024]{1,0:T(8,128)(2,1)S(1)}, bf16[16,1024]{1,0:T(8,128)(2,1)S(1)}, u32[]{:S(2)}, u32[]{:S(2)}) collective-permute-start(bf16[16,1024]{1,0:T(8,128)(2,1)S(1)} %add_convert_fusion.rest_9_.refs_0_), channel_id=1, source_target_pairs={{0,3},{1,2},{2,1},{3,0},{4,7},{5,6},{6,5},{7,4},{8,11},{9,10},{10,... | collective-permute-start | bytes 98312 | tf_op jit(solution)/shard_map/ppermute | solution.py:47
  145.6 20.5 %collective-permute-start.39 = (bf16[16,1024]{1,0:T(8,128)(2,1)S(1)}, bf16[16,1024]{1,0:T(8,128)(2,1)S(1)}, u32[]{:S(2)}, u32[]{:S(2)}) collective-permute-start(bf16[16,1024]{1,0:T(8,128)(2,1)S(1)} %add_convert_fusion.rest_9_.refs_0_), channel_id=1, source_target_pairs={{0,2},{1,3},{2,0},{3,1},{4,6},{5,7},{6,4},{7,5},{8,10},{9,11},{10,... | collective-permute-start | bytes 98312 | tf_op jit(solution)/shard_map/ppermute | solution.py:47
  145.6 20.5 %collective-permute-start.38 = (bf16[16,1024]{1,0:T(8,128)(2,1)S(1)}, bf16[16,1024]{1,0:T(8,128)(2,1)S(1)}, u32[]{:S(2)}, u32[]{:S(2)}) collective-permute-start(bf16[16,1024]{1,0:T(8,128)(2,1)S(1)} %add_convert_fusion.rest_9_.refs_0_), channel_id=1, source_target_pairs={{0,1},{1,0},{2,3},{3,2},{4,5},{5,4},{6,7},{7,6},{8,9},{9,8},{10,11... | collective-permute-start | bytes 98312 | tf_op jit(solution)/shard_map/ppermute | solution.py:47
  (26 other events, 278.3 us)

commit v2 on v0

v2 whole, which is shorter than its diff:
```python
import functools

import jax
import jax.numpy as jnp
from jax import lax
from jax.experimental import pallas as pl
from jax.experimental.pallas import tpu as pltpu
from jax.sharding import PartitionSpec as P

H = 64
KVH = 8
HD = 128
MASKED = -1e30
LOG2E = 1.4426950408889634
SCALE2 = HD ** (-0.5) * LOG2E
TINY = 2.0 ** -90
BF = jnp.bfloat16
F32 = jnp.float32
VMEM = pl.BlockSpec(memory_space=pltpu.VMEM)
SMEM = pl.BlockSpec(memory_space=pltpu.SMEM)
ANY = pl.BlockSpec(memory_space=pl.ANY)
HBM = pl.BlockSpec(memory_space=pltpu.HBM)


def params(mib=20):
    return pltpu.CompilerParams(vmem_limit_bytes=mib * 2**20)


def dot_t(a, b):
    return lax.dot_general(a, b, (((1,), (1,)), ((), ())), preferred_element_type=F32)


def dot(a, b):
    return lax.dot_general(a, b, (((1,), (0,)), ((), ())), preferred_element_type=F32)


def spread(value, axis, source):
    kept = jnp.where(lax.axis_index(axis) == source, value, 0).astype(value.dtype)
    return lax.psum(kept, axis)


def swap(value, axis, size, even, odd):
    return lax.ppermute(value, axis, [(i, i ^ (odd if i & 1 else even)) for i in range(size)])


def pick_kernel(group_size, local_heads, kv_ref, query_ref, k_ref, v_ref, pay_ref, sems):
    slab, width = k_ref.shape
    first = lax.axis_index("tp") * local_heads // group_size * HD
    cols = pl.ds(pl.multiple_of(first, HD), width)
    moves = [
        pltpu.make_async_copy(kv_ref.at[1, :, cols], v_ref, sems.at[1]),
        pltpu.make_async_copy(kv_ref.at[0, :, cols], k_ref, sems.at[0]),
    ]
    for move in moves:
        move.start()
    if pay_ref is not None:
        blocks = [
            query_ref[:, i * width : (i + 1) * width].astype(F32)
            for i in range(query_ref.shape[1] // width)
        ]
        pay_ref[slab:, :] = jnp.concatenate(blocks, 0).astype(BF)
    moves[0].wait()
    if pay_ref is not None:
        pay_ref[:slab, :] = v_ref[...]
    moves[1].wait()


def pick(ctx_kv, query_q, kv_local, local_heads, share):
    rows = ctx_kv.shape[1]
    width = kv_local * HD
    shapes = [jax.ShapeDtypeStruct((rows, width), BF)] * 2
    kernel = functools.partial(pick_kernel, H // KVH, local_heads)
    if share:
        shapes.append(jax.ShapeDtypeStruct((rows + query_q.size // width, width), BF))
        body = kernel
    else:
        body = lambda kv, q, k, v, sems: kernel(kv, q, k, v, None, sems)
    return pl.pallas_call(
        body,
        out_shape=shapes,
        in_specs=[HBM, VMEM],
        out_specs=[VMEM] * len(shapes),
        scratch_shapes=[pltpu.SemaphoreType.DMA((2,))],
        compiler_params=params(52),
        name="pick_columns",
    )(ctx_kv, query_q)


def relay_call(kernel, name, shapes, inputs, after):
    return pl.pallas_call(
        kernel,
        out_shape=[jax.ShapeDtypeStruct(x, BF) for x in shapes],
        in_specs=[VMEM] * len(inputs) + [ANY] * len(after),
        out_specs=[VMEM] * len(shapes),
        compiler_params=params(),
        name=name,
    )(*inputs, *after)


def choose(condition, one, two):
    pl.when(condition)(one)
    pl.when(jnp.logical_not(condition))(two)


def copy_rows(target, at, source, start, rows):
    def run():
        target[at : at + rows, :] = source[start : start + rows, :]

    return run


def join_rows(low, target, at, known, landed, start, rows):
    def run(first, second):
        def body():
            target[at : at + rows, :] = first[start : start + rows, :]
            target[at + rows : at + 2 * rows, :] = second[start : start + rows, :]

        return body

    choose(low, run(known, landed), run(landed, known))


def first_relay(slab, cut, pay, own_k, landed, after):
    rows = pay.shape[0] - slab
    width = pay.shape[1]

    def kernel(pay_ref, k_ref, landed_ref, *rest):
        one_ref, two_ref = rest[-2:]
        even = bit(lax.axis_index("hst"), 0) == 0
        choose(even, copy_rows(one_ref, 0, k_ref, 0, cut), copy_rows(one_ref, 0, landed_ref, 0, cut))
        choose(
            even,
            copy_rows(two_ref, 0, k_ref, cut, slab - cut),
            copy_rows(two_ref, 0, landed_ref, cut, slab - cut),
        )
        join_rows(even, one_ref, cut, pay_ref, landed_ref, slab, rows)

    shapes = [(cut + 2 * rows, width), (slab - cut, width)]
    return relay_call(kernel, "relay_first", shapes, (pay, own_k, landed), after)


def second_relay(slab, cut, one, two, one_landed, two_landed, after):
    rows = one.shape[0] - cut
    width = one.shape[1]

    def kernel(one_ref, two_ref, one_landed_ref, two_landed_ref, *rest):
        back_ref, front_ref = rest[-2:]
        host = lax.axis_index("hst")
        source = host < 2
        choose(source, copy_rows(front_ref, 0, one_ref, 0, cut), copy_rows(front_ref, 0, one_landed_ref, 0, cut))
        left = slab - cut
        choose(source, copy_rows(back_ref, 0, two_ref, 0, left), copy_rows(back_ref, 0, two_landed_ref, 0, left))
        low = jnp.where(bit(host, 0) == 1, bit(host, 2), bit(host, 1)) == 0
        join_rows(low, front_ref, cut, one_ref, one_landed_ref, cut, rows)

    shapes = [(slab - cut, width), (cut + 2 * rows, width)]
    return relay_call(kernel, "relay_second", shapes, (one, two, one_landed, two_landed), after)


def third_relay(slab, cut, back, front, back_landed, front_landed, after):
    width = back.shape[1]

    def kernel(back_ref, front_ref, back_landed_ref, front_landed_ref, *rest):
        held_ref = rest[-1]
        host = lax.axis_index("hst")
        kept = (host <= 2) | (host == 5)
        choose(kept, copy_rows(held_ref, 0, front_ref, 0, cut), copy_rows(held_ref, 0, front_landed_ref, 0, cut))
        kept = (host < 2) | (host == 3) | (host == 4)
        left = slab - cut
        choose(kept, copy_rows(held_ref, cut, back_ref, 0, left), copy_rows(held_ref, cut, back_landed_ref, 0, left))

    return relay_call(kernel, "relay_third", [(slab, width)], (back, front, back_landed, front_landed), after)[0]


def bit(value, at):
    return (value >> at) & 1


def fill_values(vaug, values):
    for j in range(values.shape[1] // HD):
        vaug[:, 2 * j * HD : (2 * j + 1) * HD] = values[:, j * HD : (j + 1) * HD]
        vaug[:, (2 * j + 1) * HD : (2 * j + 2) * HD] = jnp.ones((values.shape[0], HD), BF)


def lanes(index, width):
    return pl.ds(pl.multiple_of(index * width, width), width)


def row_tile(slab):
    return 256 if slab % 256 == 0 else slab


def own_kernel(first, count, per_kv, q_ref, k_ref, v_ref, *rest):
    state_ref, vaug = rest[-2], rest[-1]
    slab = q_ref.shape[0]
    tile = row_tile(slab)
    heads = min(2, count)
    fill_values(vaug, v_ref)
    rows = lax.broadcasted_iota(jnp.int32, (tile, tile), 0)
    cols = lax.broadcasted_iota(jnp.int32, (tile, tile), 1)
    causal = cols <= rows
    chunks = slab // tile
    units = [(h, j) for h in range(heads) for j in range(chunks)]

    def body(i, carry):
        kv = lax.div(first + i * heads, per_kv)

        def scores(at):
            h, j = units[at]
            query = q_ref[j * tile :, lanes(first + i * heads + h, HD)]
            return dot_t(query, k_ref[j * tile : (j + 1) * tile, lanes(kv, HD)])

        current = scores(0)
        totals = [None] * chunks
        for at, (h, j) in enumerate(units):
            following = scores(at + 1) if at + 1 < len(units) else None
            expo = jnp.exp2(current * SCALE2)
            corner = jnp.where(causal, expo[:tile], 0.0)
            expo = corner if j == chunks - 1 else jnp.concatenate([corner, expo[tile:]], 0)
            part = dot(expo.astype(BF), vaug[j * tile : (j + 1) * tile, lanes(kv, 2 * HD)])
            for r in range(j, chunks):
                piece = part[(r - j) * tile : (r - j + 1) * tile]
                totals[r] = piece if j == 0 else totals[r] + piece
            state_ref[j * tile : (j + 1) * tile, lanes(i * heads + h, 2 * HD)] = totals[j].astype(BF)
            current = following
        return carry

    lax.fori_loop(0, count // heads, body, 0)


def own_part(ctx_q, own_k, own_v, first, count, per_kv, after=()):
    slab = ctx_q.shape[0]
    work = count * slab * (slab + row_tile(slab)) // 2
    return pl.pallas_call(
        functools.partial(own_kernel, first, count, per_kv),
        out_shape=jax.ShapeDtypeStruct((slab, count * 2 * HD), BF),
        in_specs=[VMEM] * 3 + [ANY] * len(after),
        out_specs=VMEM,
        scratch_shapes=[pltpu.VMEM((slab, 2 * own_v.shape[1]), BF)],
        compiler_params=params(),
        cost_estimate=pl.CostEstimate(
            flops=work * HD * 8, bytes_accessed=count * slab * HD * 6, transcendentals=work
        ),
        name="context_own",
    )(ctx_q, own_k, own_v, *after)


def anchor_kernel(first, count, base, per_kv, last, befores, *refs):
    lengths_ref, q_ref, state_ref, k_ref, v_ref, even_ref, odd_ref = refs[:7]
    earlier = refs[7 : 7 + len(befores)]
    if last:
        full_ref, out_ref, keys, vaug, sems = refs[-5:]
    else:
        out_ref, keys, vaug = refs[-3:]
    slab = q_ref.shape[0]
    heads = min(2, count)
    host = lax.axis_index("hst")
    own_len = lengths_ref[host]

    def hand_over(source, at, width, sem):
        return pltpu.make_async_copy(source, full_ref.at[:, at], sems.at[sem])

    moves = []
    for n, (start, width) in enumerate(befores):
        at = pl.ds(start * HD, width * HD)
        moves.append(hand_over(earlier[n], at, width, n))
    for move in moves:
        move.start()

    @pl.when(host % 2 == 0)
    def _():
        keys[...] = even_ref[...]
        fill_values(vaug, odd_ref)

    @pl.when(host % 2 == 1)
    def _():
        keys[...] = odd_ref[...]
        fill_values(vaug, even_ref)

    row_ids = lax.broadcasted_iota(jnp.int32, (slab, HD), 0)
    live = row_ids < own_len

    def result_move(i):
        cols = pl.ds(pl.multiple_of(i * heads * HD, heads * HD), heads * HD)
        target = pl.ds(pl.multiple_of((first + i * heads) * HD, heads * HD), heads * HD)
        return hand_over(out_ref.at[:, cols], target, heads, len(befores) + i)

    def body(i, carry):
        kv = lax.div(first + i * heads, per_kv)

        def scores(h):
            return dot_t(q_ref[:, lanes(first + i * heads + h, HD)], keys[:, lanes(kv, HD)])

        def state_of(h):
            return state_ref[:, lanes(first - base + i * heads + h, 2 * HD)].astype(F32)

        def finish(h, total, worst):
            sums = total[:, HD:]
            inverse = 1.0 / sums
            result = jnp.where(live, total[:, :HD] * inverse, 0.0)
            out_ref[:, lanes(i * heads + h, HD)] = result.astype(BF)
            return jnp.minimum(worst, jnp.minimum(sums, inverse))

        def check(worst):
            @pl.when(jnp.logical_not(jnp.min(worst) > TINY))
            def _():
                exact_block(first + i * heads, i * heads, heads, host, own_len, kv, q_ref, k_ref, v_ref, keys, vaug, out_ref)

        @pl.when(host == 0)
        def _():
            worst = jnp.ones((slab, HD), F32)
            for h in range(heads):
                worst = finish(h, state_of(h), worst)
            check(worst)

        @pl.when(host > 0)
        def _():
            worst = jnp.ones((slab, HD), F32)
            current = scores(0)
            for h in range(heads):
                following = scores(h + 1) if h + 1 < heads else None
                expo = jnp.exp2(current * SCALE2).astype(BF)
                total = dot(expo, vaug[:, lanes(kv, 2 * HD)]) + state_of(h)
                worst = finish(h, total, worst)
                current = following
            check(worst)

        if last:
            result_move(i).start()
        return carry

    lax.fori_loop(0, count // heads, body, 0)
    for move in moves:
        move.wait()
    if last:
        for i in range(count // heads):
            result_move(i).wait()


def exact_block(q_head, out_head, heads, host, own_len, kv, q_ref, k_ref, v_ref, keys, vaug, out_ref):
    slab = q_ref.shape[0]
    tile = 128

    def body(i, carry):
        h = lax.div(i, slab // tile)
        r = lax.rem(i, slab // tile)
        at = pl.ds(pl.multiple_of(r * tile, tile), tile)
        query = q_ref[at, lanes(q_head + h, HD)]
        row_ids = lax.broadcasted_iota(jnp.int32, (tile, slab), 0) + r * tile
        key_ids = lax.broadcasted_iota(jnp.int32, (tile, slab), 1)
        own = dot_t(query, k_ref[:, lanes(kv, HD)]) * SCALE2
        own = jnp.where((key_ids <= row_ids) & (key_ids < own_len), own, MASKED)
        far = dot_t(query, keys[:, lanes(kv, HD)]) * SCALE2
        far = jnp.where(host > 0, far, MASKED)
        peak = jnp.maximum(jnp.max(own, 1, keepdims=True), jnp.max(far, 1, keepdims=True))
        own = jnp.exp2(own - peak)
        far = jnp.where(host > 0, jnp.exp2(far - peak), 0.0)
        sums = jnp.sum(own, 1, keepdims=True) + jnp.sum(far, 1, keepdims=True)
        values = jnp.where(host > 0, vaug[:, lanes(2 * kv, HD)].astype(F32), 0.0).astype(BF)
        total = dot(own.astype(BF), v_ref[:, lanes(kv, HD)]) + dot(far.astype(BF), values)
        live = row_ids[:, :1] < own_len
        out_ref[at, lanes(out_head + h, HD)] = jnp.where(live, total / sums, 0.0).astype(BF)
        return carry

    lax.fori_loop(0, heads * (slab // tile), body, 0)


def anchor_part(lengths, ctx_q, state, base, own_k, own_v, anchor, first, count, per_kv, befores=None, after=()):
    slab, width = ctx_q.shape
    work = count * slab * slab
    last = befores is not None
    heads = min(2, count)
    earlier = list(befores.values()) if last else []
    places = tuple((at, x.shape[1] // HD) for at, x in befores.items()) if last else ()
    results = jax.ShapeDtypeStruct((slab, count * HD), BF)
    scratch = [pltpu.VMEM((slab, own_k.shape[1]), BF), pltpu.VMEM((slab, 2 * own_k.shape[1]), BF)]
    if last:
        scratch = [pltpu.VMEM(results.shape, BF)] + scratch
        scratch += [pltpu.SemaphoreType.DMA((len(earlier) + count // heads,))]
        results = jax.ShapeDtypeStruct((slab, width), BF)
    return pl.pallas_call(
        functools.partial(anchor_kernel, first, count, base, per_kv, last, places),
        out_shape=results,
        in_specs=[SMEM] + [VMEM] * (6 + len(earlier)) + [ANY] * len(after),
        out_specs=ANY if last else VMEM,
        scratch_shapes=scratch,
        compiler_params=params(),
        cost_estimate=pl.CostEstimate(
            flops=work * HD * 8, bytes_accessed=count * slab * HD * 8, transcendentals=work
        ),
        name="context_anchor",
    )(lengths, ctx_q, state, own_k, own_v, *anchor, *earlier, *after)


def write_level(ref, width, level):
    for at in range(3):
        part = level.astype(BF)
        ref[:, width + at * HD : width + (at + 1) * HD] = part
        level = level - part.astype(F32)


def read_level(ref, width):
    parts = [ref[:, width + i * HD : width + (i + 1) * HD].astype(F32) for i in range(3)]
    return parts[0] + parts[1] + parts[2]


def source_kernel(cut, per_kv, q_rows, group_size, lengths_ref, k_ref, v_ref, self_ref, known_ref, landed_ref, *rest):
    out_ref, q_all = rest[-2], rest[-1]
    slab, columns = k_ref.shape
    width = per_kv * columns
    half = known_ref.shape[0] - cut
    quarter = half // 2
    query_count = out_ref.shape[1]
    slots = query_count // q_rows
    host = lax.axis_index("hst")
    own_len = lengths_ref[host]
    rows = per_kv * query_count
    odd = bit(host, 0) == 1
    low = jnp.where(odd, bit(host, 1), bit(host, 2)) == 0

    def place(lower, upper, spread_out):
        middle = (2, 1) if spread_out else (1, 2)
        for ref, (one, two) in ((lower, (0, middle[0])), (upper, (middle[1], 3))):
            q_all[one * quarter : (one + 1) * quarter, :] = ref[cut : cut + quarter, :]
            q_all[two * quarter : (two + 1) * quarter, :] = ref[cut + quarter :, :]

    for is_low, is_odd in ((False, False), (False, True), (True, False), (True, True)):
        @pl.when((low == is_low) & (odd == is_odd))
        def _():
            pair = (known_ref, landed_ref) if is_low else (landed_ref, known_ref)
            place(*pair, is_odd)

    first = lax.axis_index("tp") * (width // HD) // group_size * HD
    own_cols = pl.ds(pl.multiple_of(first, HD), columns)
    selves_kv = [self_ref[i, :, own_cols].astype(F32) for i in range(2)]
    lane = lax.broadcasted_iota(jnp.int32, (query_count, HD), 1)
    query_ids = lax.broadcasted_iota(jnp.int32, (query_count, HD), 0)
    self_ok = (host * q_rows + lane <= query_ids) & (lane < q_rows)
    self_ok = jnp.concatenate([self_ok] * per_kv, 0)
    key_ids = lax.broadcasted_iota(jnp.int32, (rows, slab), 1)
    pad = jnp.zeros((HD - q_rows, HD), F32)
    heads_wide = columns // HD
    q_lanes = [q_all[:, i * HD : (i + 1) * HD].astype(F32) for i in range(heads_wide)]
    stride = width // columns * q_rows
    for j in range(columns // HD):
        cols = slice(j * HD, (j + 1) * HD)
        parts = []
        for h in range(per_kv):
            block, lanes = divmod(j * per_kv + h, heads_wide)
            starts = [k * stride + block * q_rows for k in range(slots)]
            parts += [q_lanes[lanes][at : at + q_rows] for at in starts]
        queries = jnp.concatenate(parts, 0).astype(BF)
        self_keys = jnp.concatenate([selves_kv[0][:, cols], pad], 0).astype(BF)
        self_values = jnp.concatenate([selves_kv[1][:, cols], pad], 0).astype(BF)
        near = dot_t(queries, k_ref[:, cols]) * SCALE2
        near = jnp.where(key_ids < own_len, near, MASKED)
        selves = dot_t(queries, self_keys) * SCALE2
        selves = jnp.where(self_ok, selves, MASKED)
        peak = jnp.maximum(jnp.max(near, 1, keepdims=True), jnp.max(selves, 1, keepdims=True))
        near = jnp.exp2(near - peak)
        selves = jnp.exp2(selves - peak)
        sums = jnp.sum(near, 1, keepdims=True) + jnp.sum(selves, 1, keepdims=True)
        total = dot(near.astype(BF), v_ref[:, cols]) + dot(selves.astype(BF), self_values)
        total = total / sums
        level = peak + jnp.log2(sums)
        stats = jnp.zeros((query_count, HD), F32)
        for h in range(per_kv):
            at = h * query_count
            stats = jnp.where(lane == h, level[at : at + query_count, :], stats)
            out_ref[j, :, h * HD : (h + 1) * HD] = total[at : at + query_count, :].astype(BF)
        write_level(out_ref.at[j], per_kv * HD, stats)


def source_part(lengths, own_k, own_v, query_kv, known, landed, cut, q_rows, count, per_kv, after=()):
    slab, columns = own_k.shape
    width = per_kv * columns
    work = count * (width // HD) * slab
    return pl.pallas_call(
        functools.partial(source_kernel, cut, per_kv, q_rows, H // KVH),
        out_shape=jax.ShapeDtypeStruct((columns // HD, count, (per_kv + 3) * HD), BF),
        in_specs=[SMEM] + [VMEM] * 5 + [ANY] * len(after),
        out_specs=VMEM,
        scratch_shapes=[pltpu.VMEM((count * width // columns, columns), BF)],
        compiler_params=params(),
        cost_estimate=pl.CostEstimate(flops=work * HD * 8, bytes_accessed=2**21, transcendentals=work),
        name="query_source",
    )(lengths, own_k, own_v, query_kv, known, landed, *after)


def merged(refs, width):
    levels = [read_level(ref, width) for ref in refs]
    peak = jnp.maximum(*levels)
    weights = [jnp.exp2(x - peak) for x in levels]
    whole = weights[0] + weights[1]
    return [w / whole for w in weights], peak + jnp.log2(whole)


def blend(shares, refs, h):
    cols = slice(h * HD, (h + 1) * HD)
    return sum(w[:, h : h + 1] * ref[:, cols].astype(F32) for w, ref in zip(shares, refs))


def merge_kernel(groups, *refs):
    ones, twos, outs = refs[:groups], refs[groups : 2 * groups], refs[-groups:]
    for pair in zip(ones, twos, outs):
        out_ref = pair[2]
        width = out_ref.shape[1] - 3 * HD
        shares, level = merged(pair[:2], width)
        write_level(out_ref, width, level)
        for h in range(width // HD):
            out_ref[:, h * HD : (h + 1) * HD] = blend(shares, pair[:2], h).astype(BF)


def merge_part(ones, twos, after=()):
    stacked = len(ones) == 1
    groups = ones[0].shape[0] if stacked else len(ones)
    shape = ones[0].shape[-2:]

    def body(*refs):
        if stacked:
            refs = [refs[n].at[j] for n in range(2) for j in range(groups)] + list(refs[2:])
        merge_kernel(groups, *refs)

    return pl.pallas_call(
        body,
        out_shape=[jax.ShapeDtypeStruct(shape, BF)] * groups,
        in_specs=[VMEM] * (2 * len(ones)) + [ANY] * len(after),
        out_specs=[VMEM] * groups,
        compiler_params=params(),
        name="query_merge",
    )(*ones, *twos, *after)


def project_kernel(groups, w_ref, *rest):
    ones, twos = rest[:groups], rest[groups : 2 * groups]
    out_ref, attended = rest[-2], rest[-1]
    width = ones[0].shape[1] - 3 * HD

    @pl.when(pl.program_id(0) == 0)
    def _():
        for j, pair in enumerate(zip(ones, twos)):
            shares, _ = merged(pair, width)
            for h in range(width // HD):
                at = j * width + h * HD
                attended[:, at : at + HD] = blend(shares, pair, h).astype(BF)

    out_ref[...] = dot(attended[...], w_ref[...]).astype(BF)


def project_part(ones, twos, out_weight, after=()):
    rows, wide = ones[0].shape
    depth, columns = out_weight.shape
    tile = min(256, columns)
    return pl.pallas_call(
        functools.partial(project_kernel, len(ones)),
        grid=(columns // tile,),
        out_shape=jax.ShapeDtypeStruct((rows, columns), BF),
        in_specs=[pl.BlockSpec((depth, tile), lambda i: (0, i))]
        + [pl.BlockSpec((rows, wide), lambda i: (0, 0))] * (2 * len(ones))
        + [ANY] * len(after),
        out_specs=pl.BlockSpec((rows, tile), lambda i: (0, i)),
        scratch_shapes=[pltpu.VMEM((rows, depth), BF)],
        compiler_params=params(),
        cost_estimate=pl.CostEstimate(
            flops=2 * rows * depth * columns, bytes_accessed=2 * depth * columns, transcendentals=0
        ),
        name="query_project",
    )(out_weight, *ones, *twos, *after)


def general_queries(lengths, own_k, own_v, self_kv, query_q, out_weight, per_kv):
    own_kv = jnp.stack([own_k, own_v], 0)
    host_id = lax.axis_index("hst")
    local_heads = query_q.shape[1] // HD
    kv_local = own_kv.shape[2] // HD
    slab_rows = own_kv.shape[1]
    own_len = lengths[host_id]
    row_ids = jnp.arange(slab_rows)
    all_queries = lax.all_gather(query_q, "hst", axis=0, tiled=True)
    query_count = all_queries.shape[0]
    q_rows = query_q.shape[0]
    source = jnp.concatenate([own_kv, self_kv], 1)
    source = source.reshape(2, slab_rows + q_rows, kv_local, HD).transpose(0, 2, 1, 3)
    query_ids = jnp.arange(query_count)
    context_ok = jnp.broadcast_to(row_ids[None, :] < own_len, (query_count, slab_rows))
    self_ok = (host_id * q_rows + jnp.arange(q_rows))[None, :] <= query_ids[:, None]
    seen_ok = jnp.concatenate([context_ok, self_ok], 1)
    query_heads = all_queries.reshape(query_count, local_heads, HD).transpose(1, 0, 2)

    def score_head(operands):
        query_rows, head_index = operands
        kv_index = head_index // per_kv
        scores = dot_t(query_rows, source[0, kv_index]) * HD ** (-0.5)
        scores = jnp.where(seen_ok, scores, MASKED)
        peak = jnp.max(scores, axis=1)
        expo = jnp.exp(scores - peak[:, None])
        return peak, jnp.sum(expo, axis=1), dot(expo.astype(BF), source[1, kv_index])

    maxima, totals, outputs = lax.map(score_head, (query_heads, jnp.arange(local_heads)))
    factor = jnp.exp(maxima - lax.pmax(maxima, "hst"))
    denominator, summed = lax.psum((totals * factor, outputs * factor[..., None]), "hst")
    attended = (summed / denominator[..., None]).astype(BF)
    attended = attended.transpose(1, 0, 2).reshape(query_count, local_heads * HD)
    return lax.psum(dot(attended, out_weight), "tp").astype(BF)


def per_device(hosts, groups, ctx_q, ctx_kv, lengths, query_q, query_kv, out_weight):
    slab = ctx_q.shape[0]
    local_heads = ctx_q.shape[1] // HD
    group_size = H // KVH
    kv_local = max(1, local_heads // group_size)
    per_kv = min(local_heads, group_size)
    q_rows = query_q.shape[0]
    host = lax.axis_index("hst")
    fast = hosts == 8 and groups & (groups - 1) == 0
    fast = fast and q_rows == 8 and local_heads == 16 and per_kv == 8

    if not fast:
        kv_first = lax.axis_index("tp") * local_heads // group_size
        self_kv = lax.dynamic_slice_in_dim(query_kv, kv_first * HD, kv_local * HD, 2)
        own_k, own_v = pick(ctx_kv, query_q, kv_local, local_heads, False)
        query_out = general_queries(lengths, own_k, own_v, self_kv, query_q, out_weight, per_kv)
        k, v = spread(jnp.stack([own_k, own_v]), "hst", 0)
        anchor = jnp.where(host % 2 == 0, k, v), jnp.where(host % 2 == 0, v, k)
        state = own_part(ctx_q, own_k, own_v, 0, local_heads, per_kv)
        context_out = anchor_part(
            lengths, ctx_q, state, 0, own_k, own_v, anchor, 0, local_heads, per_kv, {}
        )
        return context_out, query_out

    states = {}

    def own(first, count, after=()):
        states[first] = own_part(ctx_q, own_k, own_v, first, count, per_kv, after)
        return states[first]

    cut = slab * 3 // 8
    own_k, own_v, pay = pick(ctx_kv, query_q, kv_local, local_heads, True)
    landed = swap(pay, "hst", hosts, 1, 1)
    done = own(0, 2)
    one, two = first_relay(slab, cut, pay, own_k, landed, (done,))
    one_landed = swap(one, "hst", hosts, 2, 4)
    two_landed = swap(two, "hst", hosts, 4, 2)
    done = own(2, 8, (one,))
    back, front = second_relay(slab, cut, one, two, one_landed, two_landed, (done,))
    back_landed = swap(back, "hst", hosts, 2, 4)
    front_landed = swap(front, "hst", hosts, 4, 2)
    done = own(10, 6, (front,))
    held = third_relay(slab, cut, back, front, back_landed, front_landed, (done,))
    other = swap(held, "hst", hosts, 1, 1)
    source = source_part(
        lengths, own_k, own_v, query_kv, front, front_landed, cut, q_rows, hosts * q_rows, per_kv, (held,)
    )
    results = {}

    def anchors(first, count, after, last=False):
        base = max(x for x in states if x <= first)
        results[first] = anchor_part(
            lengths, ctx_q, states[base], base, own_k, own_v, (held, other),
            first, count, per_kv, dict(results) if last else None, after,
        )
        return results[first]

    landed = swap(source, "hst", hosts, 1, 1)
    done = anchors(0, 2, (source,))
    sources = merge_part([source], [landed], (done,))
    landed = [swap(sources[0], "hst", hosts, 2, 4), swap(sources[1], "hst", hosts, 4, 2)]
    done = anchors(2, 4, (sources[0],))
    sources = merge_part(sources, landed, (done,))
    landed = [swap(sources[0], "hst", hosts, 4, 2), swap(sources[1], "hst", hosts, 2, 4)]
    done = anchors(6, 4, (sources[0],))
    terms = project_part(sources, landed, out_weight, (done,))
    shares = [(12, 4, True), (10, 2, False)]
    step = 1
    while step < groups:
        landed = swap(terms, "tp", groups, step, step)
        if shares:
            first, count, last = shares.pop()
            done = anchors(first, count, (terms,), last)
            if not last:
                landed, _ = lax.optimization_barrier((landed, done))
        terms = (terms.astype(F32) + landed.astype(F32)).astype(BF)
        step *= 2
    for first, count, last in reversed(shares):
        done = anchors(first, count, (), last)
    return done, terms


def solution(mesh):
    hosts, groups = mesh.shape["hst"], mesh.shape["tp"]
    return jax.shard_map(
        functools.partial(per_device, hosts, groups),
        mesh=mesh,
        in_specs=(
            P("hst", "tp"),
            P(None, "hst", None),
            P(),
            P("hst", "tp"),
            P(None, "hst", None),
            P("tp", "hst"),
        ),
        out_specs=(P("hst", "tp"), P(None, "hst")),
        check_vma=False,
    )
```

time: 438 us -> 115 us (0.26); the launches traced: 431 us -> 114 us
  matrix products: 137 us -> 0 us
  Pallas kernels: 0 us -> 93.7 us
  loops' own time: 85.4 us -> 0 us
  blocking collectives: 57.2 us -> 0 us
  waiting for transfers between devices: 64 us -> 7.27 us
  local copies, waits for them, and re-layouts: 41 us -> 0.92 us
  other arithmetic: 32.3 us -> 0.73 us
  between operations: 14.2 us -> 0.89 us
  starting transfers between devices: 0.08 us -> 10.4 us
    dot_general x65 -> x0, matrix products: 137 us -> none  [the longest x32 62.8 us: softmax_rows(): jnp.einsum('id,jd->ij', query_rows, key_rows, preferred_element_type=jnp....]
    pallas_call x0 -> x16, Pallas kernels: none -> 93.7 us  [the longest x5 77.9 us: anchor_part(): pl.pallas_call(functools.partial(anchor_kernel, first, count, base, per_k...]
    another operation x2 -> x0, loops' own time: 85.4 us -> none  [the longest x1 44.6 us: per_device(): encoded = lax.map(encode_head, (head_queries, jnp.arange(local_heads)))]
    psum x2 -> x0, waiting for transfers between devices: 64 us -> none  [the longest x1 33.4 us: per_device(): lax.psum((totals * factor, outputs * factor[..., None]), 'hst')]
    psum x2 -> x0, blocking collectives: 36.8 us -> none  [the longest x1 24.4 us: per_device(): query_out = lax.psum(partial_out, 'tp').astype(jnp.bfloat16)]
    dynamic_slice x34 -> x0, local copies, waits for them, and re-layouts: 21.9 us -> none  [the longest x32 20.2 us: per_device(): encoded = lax.map(encode_head, (head_queries, jnp.arange(local_heads)))]
    reduce_sum x32 -> x0, other arithmetic: 15.6 us -> none  [the longest x16 12.3 us: encode_head(): probs = (expo / jnp.sum(expo, axis=1, keepdims=True)).astype(jnp.bfloat16)]
    pmax x1 -> x0, blocking collectives: 12 us -> none  [per_device(): highest = lax.pmax(maxima, 'hst')]
  transfers between devices with their start and end apart: 2 -> 13, of which waited for: 2 -> 4; matrix products, arithmetic and copies ran while one was open for 3% -> 0% of each run, Pallas kernels for 0% -> 79%
where the time goes in v2:
time: 115 us; the launch traced here: 114 us
  Pallas kernels  93.7 us (81%)
  starting transfers between devices  10.4 us (9%)
  waiting for transfers between devices  7.27 us (6%)
    pallas_call x5, Pallas kernels, anchor_part(): pl.pallas_call(functools.partial(anchor_kernel, first, count, base, per_k...  77.9 us
    ppermute x13, starting transfers between devices, swap(): lax.ppermute(value, axis, [(i, i ^ (odd if i & 1 else even)) for i in ran...  10.4 us
    pallas_call x3, Pallas kernels, own_part(): pl.pallas_call(functools.partial(own_kernel, first, count, per_kv), out_s...  9.05 us
    ppermute x13, waiting for transfers between devices, swap(): lax.ppermute(value, axis, [(i, i ^ (odd if i & 1 else even)) for i in ran...  7.27 us
    pallas_call x1, Pallas kernels, source_part(): pl.pallas_call(functools.partial(source_kernel, cut, per_kv, q_rows, H //...  2.43 us
  transfers between devices with their start and end apart: 13, of which 4 were waited for; matrix products, arithmetic and copies ran while one was open for 0% of the time, Pallas kernels for 79%

profile of v2, /device:TPU:6, one launch (start us, length us, event | category | flops | bytes accessed | tf_op | source)
XLA Modules:
  0.0 113.8 jit_solution(15636469240218248946)
XLA Ops:
  0.6 0.9 copy-done.2
  1.5 1.2 %pick_columns.1 = (bf16[768,256]{1,0:T(8,128)(2,1)S(1)}, bf16[768,256]{1,0:T(8,128)(2,1)S(1)}, bf16[832,256]{1,0:T(8,128)(2,1)S(1)}) custom-call(bf16[2,768,1024]{2,1,0:T(8,128)(2,1)} %kv_ref.1, bf16[8,2048]{1,0:T(8,128)(2,1)S(1)} %copy-done.2), custom_call_target="tpu_custom_call" | custom-call | tf_op jit(solution)/shard_map/pick_columns/pallas_call | solution.py:78
  2.7 0.1 collective-permute-start
  2.8 1.1 context_own.3.rest_0_.refs_2_
  3.9 0.6 collective-permute-done.landed_ref
  4.6 0.6 collective-permute-start.1
  5.2 0.1 collective-permute-start.2
  5.3 4.5 %context_own.4.rest_0_.refs_2_ = bf16[768,2048]{1,0:T(8,128)(2,1)S(1)} custom-call(bf16[768,2048]{1,0:T(8,128)(2,1)S(1)} %copy-done, bf16[768,256]{1,0:T(8,128)(2,1)S(1)} %get-tuple-element.14.k_ref.refs_3_, bf16[768,256]{1,0:T(8,128)(2,1)S(1)} %get-tuple-element.15.v_ref.refs_4_, bf16[416,256]{1,0:T(8,128)(2,1)S(1)} %get-tuple-element.17.rest_0_.one_ref), custom_call_target="tpu_custom_call" | custom-call | flops 3221225472 | bytes 4718592 | tf_op jit(solution)/shard_map/context_own/pallas_call | solution.py:234
  9.8 2.8 %collective-permute-done.1.one_landed_ref = bf16[416,256]{1,0:T(8,128)(2,1)S(1)} collective-permute-done((bf16[416,256]{1,0:T(8,128)(2,1)S(1)}, bf16[416,256]{1,0:T(8,128)(2,1)S(1)}, u32[]{:S(2)}, u32[]{:S(2)}) %collective-permute-start.1) | collective-permute-done | bytes 213024 | tf_op jit(solution)/shard_map/ppermute | solution.py:43
  12.6 0.5 collective-permute-start.4
  13.1 0.4 collective-permute-start.3
  13.5 3.4 %context_own.5.rest_0_.refs_2_ = bf16[768,1536]{1,0:T(8,128)(2,1)S(1)} custom-call(bf16[768,2048]{1,0:T(8,128)(2,1)S(1)} %copy-done, bf16[768,256]{1,0:T(8,128)(2,1)S(1)} %get-tuple-element.14.k_ref.refs_3_, bf16[768,256]{1,0:T(8,128)(2,1)S(1)} %get-tuple-element.15.v_ref.refs_4_, bf16[544,256]{1,0:T(8,128)(2,1)S(1)} %get-tuple-element.19.rest_0_.front_ref.known_ref), custom_call_target="tpu_custom_call" | custom-call | flops 2415919104 | bytes 3538944 | tf_op jit(solution)/shard_map/context_own/pallas_call | solution.py:234
  17.0 3.8 %collective-permute-done.3.back_landed_ref = bf16[480,256]{1,0:T(8,128)(2,1)S(1)} collective-permute-done((bf16[480,256]{1,0:T(8,128)(2,1)S(1)}, bf16[480,256]{1,0:T(8,128)(2,1)S(1)}, u32[]{:S(2)}, u32[]{:S(2)}) %collective-permute-start.3) | collective-permute-done | bytes 245792 | tf_op jit(solution)/shard_map/ppermute | solution.py:43
  20.8 0.1 collective-permute-done.4.front_landed_ref.landed_ref
  20.9 0.1 collective-permute-start.5
  21.0 2.4 %query_source.1.refs_7_.refs_0_ = bf16[2,64,1408]{2,1,0:T(8,128)(2,1)S(1)} custom-call(s32[8]{0:T(128)S(1)} %copy-done.3, bf16[768,256]{1,0:T(8,128)(2,1)S(1)} %get-tuple-element.14.k_ref.refs_3_, bf16[768,256]{1,0:T(8,128)(2,1)S(1)} %get-tuple-element.15.v_ref.refs_4_, bf16[2,8,1024]{2,1,0:T(8,128)(2,1)S(1)} %copy-done.4, ...), custom_call_target="tpu_custom_call" | custom-call | flops 805306368 | bytes 2097152 | tf_op jit(solution)/shard_map/query_source/pallas_call | solution.py:478
  23.4 0.5 collective-permute-start.6
  24.0 9.8 %context_anchor.5.refs_2_.refs_7_ = bf16[768,256]{1,0:T(8,128)(2,1)S(1)} custom-call(s32[8]{0:T(128)S(1)} %copy-done.3, bf16[768,2048]{1,0:T(8,128)(2,1)S(1)} %copy-done, bf16[768,512]{1,0:T(8,128)(2,1)S(1)} %context_own.3.rest_0_.refs_2_, bf16[768,256]{1,0:T(8,128)(2,1)S(1)} %get-tuple-element.14.k_ref.refs_3_, ...), custom_call_target="tpu_custom_call" | custom-call | flops 1207959552 | bytes 1572864 | tf_op jit(solution)/shard_map/context_anchor/pallas_call | solution.py:381
  33.8 0.4 query_merge.2
  34.1 1.1 collective-permute-start.8
  35.3 0.4 collective-permute-start.7
  35.7 19.2 %context_anchor.6.refs_4_.refs_8_ = bf16[768,512]{1,0:T(8,128)(2,1)S(1)} custom-call(s32[8]{0:T(128)S(1)} %copy-done.3, bf16[768,2048]{1,0:T(8,128)(2,1)S(1)} %copy-done, bf16[768,2048]{1,0:T(8,128)(2,1)S(1)} %context_own.4.rest_0_.refs_2_, bf16[768,256]{1,0:T(8,128)(2,1)S(1)} %get-tuple-element.14.k_ref.refs_3_, ...), custom_call_target="tpu_custom_call" | custom-call | flops 2415919104 | bytes 3145728 | tf_op jit(solution)/shard_map/context_anchor/pallas_call | solution.py:381
  54.9 0.4 query_merge.3
  55.3 1.7 %collective-permute-start.10 = (bf16[64,1408]{1,0:T(8,128)(2,1)S(1)}, bf16[64,1408]{1,0:T(8,128)(2,1)S(1)}, u32[]{:S(2)}, u32[]{:S(2)}) collective-permute-start(bf16[64,1408]{1,0:T(8,128)(2,1)S(1)} %get-tuple-element.24.rest_1_), channel_id=1, source_target_pairs={{0,8},{4,20},{8,0},{12,28},{16,24},{20,4},{24,16},{28,12},{1,9},{5... | collective-permute-start | bytes 540680 | tf_op jit(solution)/shard_map/ppermute | solution.py:43
  57.0 0.4 collective-permute-start.9
  57.4 19.0 %context_anchor.7.rest_4_.refs_9_ = bf16[768,512]{1,0:T(8,128)(2,1)S(1)} custom-call(s32[8]{0:T(128)S(1)} %copy-done.3, bf16[768,2048]{1,0:T(8,128)(2,1)S(1)} %copy-done, bf16[768,2048]{1,0:T(8,128)(2,1)S(1)} %context_own.4.rest_0_.refs_2_, bf16[768,256]{1,0:T(8,128)(2,1)S(1)} %get-tuple-element.14.k_ref.refs_3_, ...), custom_call_target="tpu_custom_call" | custom-call | flops 2415919104 | bytes 3145728 | tf_op jit(solution)/shard_map/context_anchor/pallas_call | solution.py:381
  76.5 2.2 %query_project.1.refs_7_ = bf16[64,1024]{1,0:T(8,128)(2,1)S(1)} custom-call(bf16[2048,1024]{1,0:T(8,128)(2,1)S(1)} %copy-done.1, bf16[64,1408]{1,0:T(8,128)(2,1)S(1)} %get-tuple-element.23.refs_7_.rest_0_, bf16[64,1408]{1,0:T(8,128)(2,1)S(1)} %get-tuple-element.24.rest_1_, bf16[64,1408]{1,0:T(8,128)(2,1)S(1)} %collective-permute-done.9.rest_2_, ...), custom_call_target="tpu_custom_call" | custom-call | flops 268435456 | bytes 4194304 | tf_op jit(solution)/shard_map/query_project/pallas_call | solution.py:554
  78.7 1.8 %collective-permute-start.11 = (bf16[64,1024]{1,0:T(8,128)(2,1)S(1)}, bf16[64,1024]{1,0:T(8,128)(2,1)S(1)}, u32[]{:S(2)}, u32[]{:S(2)}) collective-permute-start(bf16[64,1024]{1,0:T(8,128)(2,1)S(1)} %query_project.1.refs_7_), channel_id=1, source_target_pairs={{0,1},{1,0},{2,3},{3,2},{4,5},{5,4},{6,7},{7,6},{8,9},{9,8},{10,11... | collective-permute-start | bytes 393224 | tf_op jit(solution)/shard_map/ppermute | solution.py:43
  80.5 9.8 %context_anchor.8.refs_10_ = bf16[768,256]{1,0:T(8,128)(2,1)S(1)} custom-call(s32[8]{0:T(128)S(1)} %copy-done.3, bf16[768,2048]{1,0:T(8,128)(2,1)S(1)} %copy-done, bf16[768,1536]{1,0:T(8,128)(2,1)S(1)} %context_own.5.rest_0_.refs_2_, bf16[768,256]{1,0:T(8,128)(2,1)S(1)} %get-tuple-element.14.k_ref.refs_3_, ...), custom_call_target="tpu_custom_call" | custom-call | flops 1207959552 | bytes 1572864 | tf_op jit(solution)/shard_map/context_anchor/pallas_call | solution.py:381
  90.4 2.7 %collective-permute-start.12 = (bf16[64,1024]{1,0:T(8,128)(2,1)S(1)}, bf16[64,1024]{1,0:T(8,128)(2,1)S(1)}, u32[]{:S(2)}, u32[]{:S(2)}) collective-permute-start(bf16[64,1024]{1,0:T(8,128)(2,1)S(1)} %add_convert_fusion.1.refs_11_), channel_id=1, source_target_pairs={{0,2},{1,3},{2,0},{3,1},{4,6},{5,7},{6,4},{7,5},{8,10},{9,11},{10,... | collective-permute-start | bytes 393224 | tf_op jit(solution)/shard_map/ppermute | solution.py:43
  93.0 20.1 %context_anchor.9 = bf16[768,2048]{1,0:T(8,128)(2,1)} custom-call(s32[8]{0:T(128)S(1)} %copy-done.3, bf16[768,2048]{1,0:T(8,128)(2,1)S(1)} %copy-done, bf16[768,1536]{1,0:T(8,128)(2,1)S(1)} %context_own.5.rest_0_.refs_2_, bf16[768,256]{1,0:T(8,128)(2,1)S(1)} %get-tuple-element.14.k_ref.refs_3_, bf16[768,256]{1,0:T(8,128)(2,1)S(1)} %get-tuple-element.15.v_ref.refs_4_, ...), custom_call_target="tpu_custom_call" | custom-call | flops 2415919104 | bytes 3145728 | tf_op jit(solution)/shard_map/context_anchor/pallas_call | solution.py:381
  113.2 0.7 add_convert_fusion
  (22 shorter events, 0.2 us)
Async XLA Ops:
  0.6 2.2 %copy-start = (bf16[768,2048]{1,0:T(8,128)(2,1)S(1)}, bf16[768,2048]{1,0:T(8,128)(2,1)}, u32[]{:S(2)}) copy-start(bf16[768,2048]{1,0:T(8,128)(2,1)} %refs_1_.9) | copy-start | bytes 9437188
  0.6 0.9 copy-start.2
  2.7 1.8 %collective-permute-start = (bf16[832,256]{1,0:T(8,128)(2,1)S(1)}, bf16[832,256]{1,0:T(8,128)(2,1)S(1)}, u32[]{:S(2)}, u32[]{:S(2)}) collective-permute-start(bf16[832,256]{1,0:T(8,128)(2,1)S(1)} %get-tuple-element.16.pay_ref), channel_id=1, source_target_pairs={{0,4},{4,0},{8,12},{12,8},{16,20},{20,16},{24,28},{28,24},{1,5},{5... | collective-permute-start | bytes 1277960 | tf_op jit(solution)/shard_map/ppermute | solution.py:43
  4.6 7.9 %collective-permute-start.1 = (bf16[416,256]{1,0:T(8,128)(2,1)S(1)}, bf16[416,256]{1,0:T(8,128)(2,1)S(1)}, u32[]{:S(2)}, u32[]{:S(2)}) collective-permute-start(bf16[416,256]{1,0:T(8,128)(2,1)S(1)} %get-tuple-element.17.rest_0_.one_ref), channel_id=1, source_target_pairs={{0,8},{4,20},{8,0},{12,28},{16,24},{20,4},{24,16},{28,12},{1,9},{5... | collective-permute-start | bytes 638984 | tf_op jit(solution)/shard_map/ppermute | solution.py:43
  5.2 7.3 %collective-permute-start.2 = (bf16[480,256]{1,0:T(8,128)(2,1)S(1)}, bf16[480,256]{1,0:T(8,128)(2,1)S(1)}, u32[]{:S(2)}, u32[]{:S(2)}) collective-permute-start(bf16[480,256]{1,0:T(8,128)(2,1)S(1)} %get-tuple-element.18.two_ref), channel_id=1, source_target_pairs={{0,16},{4,12},{8,24},{12,4},{16,0},{20,28},{24,8},{28,20},{1,17},{... | collective-permute-start | bytes 737288 | tf_op jit(solution)/shard_map/ppermute | solution.py:43
  12.6 8.2 %collective-permute-start.4 = (bf16[544,256]{1,0:T(8,128)(2,1)S(1)}, bf16[544,256]{1,0:T(8,128)(2,1)S(1)}, u32[]{:S(2)}, u32[]{:S(2)}) collective-permute-start(bf16[544,256]{1,0:T(8,128)(2,1)S(1)} %get-tuple-element.19.rest_0_.front_ref.known_ref), channel_id=1, source_target_pairs={{0,16},{4,12},{8,24},{12,4},{16,0},{20,28},{24,8},{28,20},{1,17},{... | collective-permute-start | bytes 835592 | tf_op jit(solution)/shard_map/ppermute | solution.py:43
  13.1 7.6 %collective-permute-start.3 = (bf16[480,256]{1,0:T(8,128)(2,1)S(1)}, bf16[480,256]{1,0:T(8,128)(2,1)S(1)}, u32[]{:S(2)}, u32[]{:S(2)}) collective-permute-start(bf16[480,256]{1,0:T(8,128)(2,1)S(1)} %get-tuple-element.20.back_ref), channel_id=1, source_target_pairs={{0,8},{4,20},{8,0},{12,28},{16,24},{20,4},{24,16},{28,12},{1,9},{5... | collective-permute-start | bytes 737288 | tf_op jit(solution)/shard_map/ppermute | solution.py:43
  17.0 4.0 %copy-start.3 = (s32[8]{0:T(128)S(1)}, s32[8]{0:T(128)}, u32[]{:S(2)}) copy-start(s32[8]{0:T(128)} %refs_0_.9) | copy-start | bytes 100
  17.0 4.0 %copy-start.4 = (bf16[2,8,1024]{2,1,0:T(8,128)(2,1)S(1)}, bf16[2,8,1024]{2,1,0:T(8,128)(2,1)}, u32[]{:S(2)}) copy-start(bf16[2,8,1024]{2,1,0:T(8,128)(2,1)} %self_ref.1) | copy-start | bytes 98308
  20.9 3.1 %collective-permute-start.5 = (bf16[768,256]{1,0:T(8,128)(2,1)S(1)}, bf16[768,256]{1,0:T(8,128)(2,1)S(1)}, u32[]{:S(2)}, u32[]{:S(2)}) collective-permute-start(bf16[768,256]{1,0:T(8,128)(2,1)S(1)} %relay_third.1.rest_0_.refs_5_), channel_id=1, source_target_pairs={{0,4},{4,0},{8,12},{12,8},{16,20},{20,16},{24,28},{28,24},{1,5},{5... | collective-permute-start | bytes 1179656 | tf_op jit(solution)/shard_map/ppermute | solution.py:43
  23.4 10.3 %collective-permute-start.6 = (bf16[2,64,1408]{2,1,0:T(8,128)(2,1)S(1)}, bf16[2,64,1408]{2,1,0:T(8,128)(2,1)S(1)}, u32[]{:S(2)}, u32[]{:S(2)}) collective-permute-start(bf16[2,64,1408]{2,1,0:T(8,128)(2,1)S(1)} %query_source.1.refs_7_.refs_0_), channel_id=1, source_target_pairs={{0,4},{4,0},{8,12},{12,8},{16,20},{20,16},{24,28},{28,24},{1,5},{5... | collective-permute-start | bytes 1081352 | tf_op jit(solution)/shard_map/ppermute | solution.py:43
  34.1 20.7 %collective-permute-start.8 = (bf16[64,1408]{1,0:T(8,128)(2,1)S(1)}, bf16[64,1408]{1,0:T(8,128)(2,1)S(1)}, u32[]{:S(2)}, u32[]{:S(2)}) collective-permute-start(bf16[64,1408]{1,0:T(8,128)(2,1)S(1)} %get-tuple-element.22.refs_1_), channel_id=1, source_target_pairs={{0,16},{4,12},{8,24},{12,4},{16,0},{20,28},{24,8},{28,20},{1,17},{... | collective-permute-start | bytes 540680 | tf_op jit(solution)/shard_map/ppermute | solution.py:43
  35.3 19.6 %collective-permute-start.7 = (bf16[64,1408]{1,0:T(8,128)(2,1)S(1)}, bf16[64,1408]{1,0:T(8,128)(2,1)S(1)}, u32[]{:S(2)}, u32[]{:S(2)}) collective-permute-start(bf16[64,1408]{1,0:T(8,128)(2,1)S(1)} %get-tuple-element.21.refs_7_.refs_0_), channel_id=1, source_target_pairs={{0,8},{4,20},{8,0},{12,28},{16,24},{20,4},{24,16},{28,12},{1,9},{5... | collective-permute-start | bytes 540680 | tf_op jit(solution)/shard_map/ppermute | solution.py:43
  55.3 21.2 %collective-permute-start.10 = (bf16[64,1408]{1,0:T(8,128)(2,1)S(1)}, bf16[64,1408]{1,0:T(8,128)(2,1)S(1)}, u32[]{:S(2)}, u32[]{:S(2)}) collective-permute-start(bf16[64,1408]{1,0:T(8,128)(2,1)S(1)} %get-tuple-element.24.rest_1_), channel_id=1, source_target_pairs={{0,8},{4,20},{8,0},{12,28},{16,24},{20,4},{24,16},{28,12},{1,9},{5... | collective-permute-start | bytes 540680 | tf_op jit(solution)/shard_map/ppermute | solution.py:43
  57.0 19.5 %copy-start.1 = (bf16[2048,1024]{1,0:T(8,128)(2,1)S(1)}, bf16[2048,1024]{1,0:T(8,128)(2,1)}, u32[]{:S(2)}) copy-start(bf16[2048,1024]{1,0:T(8,128)(2,1)} %w_ref.1) | copy-start | bytes 12582916
  57.0 19.5 %collective-permute-start.9 = (bf16[64,1408]{1,0:T(8,128)(2,1)S(1)}, bf16[64,1408]{1,0:T(8,128)(2,1)S(1)}, u32[]{:S(2)}, u32[]{:S(2)}) collective-permute-start(bf16[64,1408]{1,0:T(8,128)(2,1)S(1)} %get-tuple-element.23.refs_7_.rest_0_), channel_id=1, source_target_pairs={{0,16},{4,12},{8,24},{12,4},{16,0},{20,28},{24,8},{28,20},{1,17},{... | collective-permute-start | bytes 540680 | tf_op jit(solution)/shard_map/ppermute | solution.py:43
  78.7 11.6 %collective-permute-start.11 = (bf16[64,1024]{1,0:T(8,128)(2,1)S(1)}, bf16[64,1024]{1,0:T(8,128)(2,1)S(1)}, u32[]{:S(2)}, u32[]{:S(2)}) collective-permute-start(bf16[64,1024]{1,0:T(8,128)(2,1)S(1)} %query_project.1.refs_7_), channel_id=1, source_target_pairs={{0,1},{1,0},{2,3},{3,2},{4,5},{5,4},{6,7},{7,6},{8,9},{9,8},{10,11... | collective-permute-start | bytes 393224 | tf_op jit(solution)/shard_map/ppermute | solution.py:43
  90.4 22.8 %collective-permute-start.12 = (bf16[64,1024]{1,0:T(8,128)(2,1)S(1)}, bf16[64,1024]{1,0:T(8,128)(2,1)S(1)}, u32[]{:S(2)}, u32[]{:S(2)}) collective-permute-start(bf16[64,1024]{1,0:T(8,128)(2,1)S(1)} %add_convert_fusion.1.refs_11_), channel_id=1, source_target_pairs={{0,2},{1,3},{2,0},{3,1},{4,6},{5,7},{6,4},{7,5},{8,10},{9,11},{10,... | collective-permute-start | bytes 393224 | tf_op jit(solution)/shard_map/ppermute | solution.py:43

commit v3 on v2

--- a/solution.py
+++ b/solution.py
@@ -43,50 +43,36 @@
     return lax.ppermute(value, axis, [(i, i ^ (odd if i & 1 else even)) for i in range(size)])
 
 
-def pick_kernel(group_size, local_heads, kv_ref, query_ref, k_ref, v_ref, pay_ref, sems):
-    slab, width = k_ref.shape
+def pick_kernel(group_size, local_heads, kv_ref, k_ref, v_ref, sems):
     first = lax.axis_index("tp") * local_heads // group_size * HD
-    cols = pl.ds(pl.multiple_of(first, HD), width)
+    cols = pl.ds(pl.multiple_of(first, HD), k_ref.shape[1])
     moves = [
         pltpu.make_async_copy(kv_ref.at[1, :, cols], v_ref, sems.at[1]),
         pltpu.make_async_copy(kv_ref.at[0, :, cols], k_ref, sems.at[0]),
     ]
     for move in moves:
         move.start()
-    if pay_ref is not None:
-        blocks = [
-            query_ref[:, i * width : (i + 1) * width].astype(F32)
-            for i in range(query_ref.shape[1] // width)
-        ]
-        pay_ref[slab:, :] = jnp.concatenate(blocks, 0).astype(BF)
-    moves[0].wait()
-    if pay_ref is not None:
-        pay_ref[:slab, :] = v_ref[...]
-    moves[1].wait()
-
-
-def pick(ctx_kv, query_q, kv_local, local_heads, share):
-    rows = ctx_kv.shape[1]
-    width = kv_local * HD
-    shapes = [jax.ShapeDtypeStruct((rows, width), BF)] * 2
-    kernel = functools.partial(pick_kernel, H // KVH, local_heads)
-    if share:
-        shapes.append(jax.ShapeDtypeStruct((rows + query_q.size // width, width), BF))
-        body = kernel
-    else:
-        body = lambda kv, q, k, v, sems: kernel(kv, q, k, v, None, sems)
+    for move in moves:
+        move.wait()
+
+
+def pick(ctx_kv, kv_local, local_heads):
     return pl.pallas_call(
-        body,
-        out_shape=shapes,
-        in_specs=[HBM, VMEM],
-        out_specs=[VMEM] * len(shapes),
+        functools.partial(pick_kernel, H // KVH, local_heads),
+        out_shape=[jax.ShapeDtypeStruct((ctx_kv.shape[1], kv_local * HD), BF)] * 2,
+        in_specs=[HBM],
+        out_specs=[VMEM] * 2,
         scratch_shapes=[pltpu.SemaphoreType.DMA((2,))],
         compiler_params=params(52),
         name="pick_columns",
-    )(ctx_kv, query_q)
-
-
-def relay_call(kernel, name, shapes, inputs, after):
+    )(ctx_kv)
+
+
+def bit(value, at):
+    return (value >> at) & 1
+
+
+def small_call(kernel, name, shapes, inputs, after=()):
     return pl.pallas_call(
         kernel,
         out_shape=[jax.ShapeDtypeStruct(x, BF) for x in shapes],
@@ -102,78 +88,44 @@
     pl.when(jnp.logical_not(condition))(two)
 
 
-def copy_rows(target, at, source, start, rows):
-    def run():
-        target[at : at + rows, :] = source[start : start + rows, :]
-
-    return run
-
-
-def join_rows(low, target, at, known, landed, start, rows):
-    def run(first, second):
-        def body():
-            target[at : at + rows, :] = first[start : start + rows, :]
-            target[at + rows : at + 2 * rows, :] = second[start : start + rows, :]
-
-        return body
-
-    choose(low, run(known, landed), run(landed, known))
-
-
-def first_relay(slab, cut, pay, own_k, landed, after):
-    rows = pay.shape[0] - slab
-    width = pay.shape[1]
-
-    def kernel(pay_ref, k_ref, landed_ref, *rest):
-        one_ref, two_ref = rest[-2:]
-        even = bit(lax.axis_index("hst"), 0) == 0
-        choose(even, copy_rows(one_ref, 0, k_ref, 0, cut), copy_rows(one_ref, 0, landed_ref, 0, cut))
-        choose(
-            even,
-            copy_rows(two_ref, 0, k_ref, cut, slab - cut),
-            copy_rows(two_ref, 0, landed_ref, cut, slab - cut),
-        )
-        join_rows(even, one_ref, cut, pay_ref, landed_ref, slab, rows)
-
-    shapes = [(cut + 2 * rows, width), (slab - cut, width)]
-    return relay_call(kernel, "relay_first", shapes, (pay, own_k, landed), after)
-
-
-def second_relay(slab, cut, one, two, one_landed, two_landed, after):
-    rows = one.shape[0] - cut
-    width = one.shape[1]
-
-    def kernel(one_ref, two_ref, one_landed_ref, two_landed_ref, *rest):
-        back_ref, front_ref = rest[-2:]
-        host = lax.axis_index("hst")
-        source = host < 2
-        choose(source, copy_rows(front_ref, 0, one_ref, 0, cut), copy_rows(front_ref, 0, one_landed_ref, 0, cut))
-        left = slab - cut
-        choose(source, copy_rows(back_ref, 0, two_ref, 0, left), copy_rows(back_ref, 0, two_landed_ref, 0, left))
-        low = jnp.where(bit(host, 0) == 1, bit(host, 2), bit(host, 1)) == 0
-        join_rows(low, front_ref, cut, one_ref, one_landed_ref, cut, rows)
-
-    shapes = [(slab - cut, width), (cut + 2 * rows, width)]
-    return relay_call(kernel, "relay_second", shapes, (one, two, one_landed, two_landed), after)
-
-
-def third_relay(slab, cut, back, front, back_landed, front_landed, after):
-    width = back.shape[1]
-
-    def kernel(back_ref, front_ref, back_landed_ref, front_landed_ref, *rest):
-        held_ref = rest[-1]
-        host = lax.axis_index("hst")
-        kept = (host <= 2) | (host == 5)
-        choose(kept, copy_rows(held_ref, 0, front_ref, 0, cut), copy_rows(held_ref, 0, front_landed_ref, 0, cut))
-        kept = (host < 2) | (host == 3) | (host == 4)
-        left = slab - cut
-        choose(kept, copy_rows(held_ref, cut, back_ref, 0, left), copy_rows(held_ref, cut, back_landed_ref, 0, left))
-
-    return relay_call(kernel, "relay_third", [(slab, width)], (back, front, back_landed, front_landed), after)[0]
-
-
-def bit(value, at):
-    return (value >> at) & 1
+def relay(keep_of, one, two, after):
+    def kernel(one_ref, two_ref, *rest):
+        out_ref = rest[-1]
+
+        def take(ref):
+            def run():
+                out_ref[...] = ref[...]
+
+            return run
+
+        choose(keep_of(lax.axis_index("hst")), take(one_ref), take(two_ref))
+
+    return small_call(kernel, "anchor_relay", [one.shape], (one, two), after)[0]
+
+
+def join(low_of, known, landed, after):
+    rows, width = known.shape
+
+    def kernel(known_ref, landed_ref, *rest):
+        out_ref = rest[-1]
+
+        def put(first, second):
+            def run():
+                both = jnp.concatenate([first[...].astype(F32), second[...].astype(F32)], 0)
+                out_ref[...] = both.astype(BF)
+
+            return run
+
+        choose(low_of(lax.axis_index("hst")), put(known_ref, landed_ref), put(landed_ref, known_ref))
+
+    return small_call(kernel, "query_join", [(2 * rows, width)], (known, landed), after)[0]
+
+
+def add_part(one, two, after=()):
+    def kernel(one_ref, two_ref, *rest):
+        rest[-1][...] = (one_ref[...].astype(F32) + two_ref[...].astype(F32)).astype(BF)
+
+    return small_call(kernel, "query_sum", [one.shape], (one, two), after)[0]
 
 
 def fill_values(vaug, values):
@@ -214,14 +166,21 @@
         totals = [None] * chunks
         for at, (h, j) in enumerate(units):
             following = scores(at + 1) if at + 1 < len(units) else None
-            expo = jnp.exp2(current * SCALE2)
-            corner = jnp.where(causal, expo[:tile], 0.0)
-            expo = corner if j == chunks - 1 else jnp.concatenate([corner, expo[tile:]], 0)
-            part = dot(expo.astype(BF), vaug[j * tile : (j + 1) * tile, lanes(kv, 2 * HD)])
+            corner = jnp.where(causal, current[:tile], MASKED)
+            masked = corner if j == chunks - 1 else jnp.concatenate([corner, current[tile:]], 0)
+            if j == 0:
+                peak = jnp.max(masked, axis=1, keepdims=True) * SCALE2
+                shift = jnp.broadcast_to(peak, (slab, HD)).astype(BF)
+                state_ref[:, pl.ds(pl.multiple_of((i * heads + h) * 3 * HD + 2 * HD, HD), HD)] = shift
+                shift = shift.astype(F32)
+            shifts = jnp.concatenate([shift[j * tile :]] * (tile // HD), 1)
+            expo = jnp.exp2((masked * SCALE2 - shifts).astype(BF))
+            part = dot(expo, vaug[j * tile : (j + 1) * tile, lanes(kv, 2 * HD)])
             for r in range(j, chunks):
                 piece = part[(r - j) * tile : (r - j + 1) * tile]
                 totals[r] = piece if j == 0 else totals[r] + piece
-            state_ref[j * tile : (j + 1) * tile, lanes(i * heads + h, 2 * HD)] = totals[j].astype(BF)
+            cols = pl.ds(pl.multiple_of((i * heads + h) * 3 * HD, HD), 2 * HD)
+            state_ref[j * tile : (j + 1) * tile, cols] = totals[j].astype(BF)
             current = following
         return carry
 
@@ -233,7 +192,7 @@
     work = count * slab * (slab + row_tile(slab)) // 2
     return pl.pallas_call(
         functools.partial(own_kernel, first, count, per_kv),
-        out_shape=jax.ShapeDtypeStruct((slab, count * 2 * HD), BF),
+        out_shape=jax.ShapeDtypeStruct((slab, count * 3 * HD), BF),
         in_specs=[VMEM] * 3 + [ANY] * len(after),
         out_specs=VMEM,
         scratch_shapes=[pltpu.VMEM((slab, 2 * own_v.shape[1]), BF)],
@@ -291,8 +250,9 @@
         def scores(h):
             return dot_t(q_ref[:, lanes(first + i * heads + h, HD)], keys[:, lanes(kv, HD)])
 
-        def state_of(h):
-            return state_ref[:, lanes(first - base + i * heads + h, 2 * HD)].astype(F32)
+        def state_of(h, at, width):
+            start = (first - base + i * heads + h) * 3 * HD + at
+            return state_ref[:, pl.ds(pl.multiple_of(start, HD), width)].astype(F32)
 
         def finish(h, total, worst):
             sums = total[:, HD:]
@@ -310,7 +270,7 @@
         def _():
             worst = jnp.ones((slab, HD), F32)
             for h in range(heads):
-                worst = finish(h, state_of(h), worst)
+                worst = finish(h, state_of(h, 0, 2 * HD), worst)
             check(worst)
 
         @pl.when(host > 0)
@@ -319,8 +279,9 @@
             current = scores(0)
             for h in range(heads):
                 following = scores(h + 1) if h + 1 < heads else None
-                expo = jnp.exp2(current * SCALE2).astype(BF)
-                total = dot(expo, vaug[:, lanes(kv, 2 * HD)]) + state_of(h)
+                shifts = jnp.concatenate([state_of(h, 2 * HD, HD)] * (slab // HD), 1)
+                expo = jnp.exp2((current * SCALE2 - shifts).astype(BF))
+                total = dot(expo, vaug[:, lanes(kv, 2 * HD)]) + state_of(h, 0, 2 * HD)
                 worst = finish(h, total, worst)
                 current = following
             check(worst)
@@ -404,14 +365,12 @@
     return parts[0] + parts[1] + parts[2]
 
 
-def source_kernel(cut, per_kv, q_rows, group_size, lengths_ref, k_ref, v_ref, self_ref, known_ref, landed_ref, *rest):
-    out_ref, q_all = rest[-2], rest[-1]
+def source_kernel(per_kv, q_rows, group_size, lengths_ref, k_ref, v_ref, self_ref, known_ref, landed_ref, *rest):
+    keep_ref, send_ref, q_all = rest[-3:]
     slab, columns = k_ref.shape
     width = per_kv * columns
-    half = known_ref.shape[0] - cut
-    quarter = half // 2
-    query_count = out_ref.shape[1]
-    slots = query_count // q_rows
+    quarter = known_ref.shape[0] // 2
+    query_count = 4 * quarter
     host = lax.axis_index("hst")
     own_len = lengths_ref[host]
     rows = per_kv * query_count
@@ -421,8 +380,8 @@
     def place(lower, upper, spread_out):
         middle = (2, 1) if spread_out else (1, 2)
         for ref, (one, two) in ((lower, (0, middle[0])), (upper, (middle[1], 3))):
-            q_all[one * quarter : (one + 1) * quarter, :] = ref[cut : cut + quarter, :]
-            q_all[two * quarter : (two + 1) * quarter, :] = ref[cut + quarter :, :]
+            q_all[one * quarter : (one + 1) * quarter, :] = ref[:quarter, :]
+            q_all[two * quarter : (two + 1) * quarter, :] = ref[quarter:, :]
 
     for is_low, is_odd in ((False, False), (False, True), (True, False), (True, True)):
         @pl.when((low == is_low) & (odd == is_odd))
@@ -439,17 +398,10 @@
     self_ok = jnp.concatenate([self_ok] * per_kv, 0)
     key_ids = lax.broadcasted_iota(jnp.int32, (rows, slab), 1)
     pad = jnp.zeros((HD - q_rows, HD), F32)
-    heads_wide = columns // HD
-    q_lanes = [q_all[:, i * HD : (i + 1) * HD].astype(F32) for i in range(heads_wide)]
-    stride = width // columns * q_rows
     for j in range(columns // HD):
         cols = slice(j * HD, (j + 1) * HD)
-        parts = []
-        for h in range(per_kv):
-            block, lanes = divmod(j * per_kv + h, heads_wide)
-            starts = [k * stride + block * q_rows for k in range(slots)]
-            parts += [q_lanes[lanes][at : at + q_rows] for at in starts]
-        queries = jnp.concatenate(parts, 0).astype(BF)
+        parts = [q_all[:, (j * per_kv + h) * HD : (j * per_kv + h + 1) * HD] for h in range(per_kv)]
+        queries = jnp.concatenate(parts, 0)
         self_keys = jnp.concatenate([selves_kv[0][:, cols], pad], 0).astype(BF)
         self_values = jnp.concatenate([selves_kv[1][:, cols], pad], 0).astype(BF)
         near = dot_t(queries, k_ref[:, cols]) * SCALE2
@@ -465,22 +417,31 @@
         level = peak + jnp.log2(sums)
         stats = jnp.zeros((query_count, HD), F32)
         for h in range(per_kv):
-            at = h * query_count
-            stats = jnp.where(lane == h, level[at : at + query_count, :], stats)
-            out_ref[j, :, h * HD : (h + 1) * HD] = total[at : at + query_count, :].astype(BF)
-        write_level(out_ref.at[j], per_kv * HD, stats)
-
-
-def source_part(lengths, own_k, own_v, query_kv, known, landed, cut, q_rows, count, per_kv, after=()):
+            stats = jnp.where(lane == h, level[h * query_count : (h + 1) * query_count, :], stats)
+
+        def put(out_ref):
+            def run():
+                for h in range(per_kv):
+                    part = total[h * query_count : (h + 1) * query_count, :]
+                    out_ref[:, h * HD : (h + 1) * HD] = part.astype(BF)
+                write_level(out_ref, per_kv * HD, stats)
+
+            return run
+
+        choose(odd if j else jnp.logical_not(odd), put(keep_ref), put(send_ref))
+
+
+def source_part(lengths, own_k, own_v, query_kv, known, landed, q_rows, per_kv, after=()):
     slab, columns = own_k.shape
     width = per_kv * columns
+    count = 2 * known.shape[0]
     work = count * (width // HD) * slab
     return pl.pallas_call(
-        functools.partial(source_kernel, cut, per_kv, q_rows, H // KVH),
-        out_shape=jax.ShapeDtypeStruct((columns // HD, count, (per_kv + 3) * HD), BF),
+        functools.partial(source_kernel, per_kv, q_rows, H // KVH),
+        out_shape=[jax.ShapeDtypeStruct((count, (per_kv + 3) * HD), BF)] * 2,
         in_specs=[SMEM] + [VMEM] * 5 + [ANY] * len(after),
-        out_specs=VMEM,
-        scratch_shapes=[pltpu.VMEM((count * width // columns, columns), BF)],
+        out_specs=[VMEM] * 2,
+        scratch_shapes=[pltpu.VMEM((count, width), BF)],
         compiler_params=params(),
         cost_estimate=pl.CostEstimate(flops=work * HD * 8, bytes_accessed=2**21, transcendentals=work),
         name="query_source",
@@ -500,72 +461,51 @@
     return sum(w[:, h : h + 1] * ref[:, cols].astype(F32) for w, ref in zip(shares, refs))
 
 
-def merge_kernel(groups, *refs):
-    ones, twos, outs = refs[:groups], refs[groups : 2 * groups], refs[-groups:]
-    for pair in zip(ones, twos, outs):
-        out_ref = pair[2]
-        width = out_ref.shape[1] - 3 * HD
-        shares, level = merged(pair[:2], width)
-        write_level(out_ref, width, level)
+def merge_part(one, two, last, after=()):
+    rows, wide = one.shape
+    width = wide - 3 * HD
+
+    def kernel(one_ref, two_ref, *rest):
+        out_ref = rest[-1]
+        shares, level = merged((one_ref, two_ref), width)
+        if not last:
+            write_level(out_ref, width, level)
         for h in range(width // HD):
-            out_ref[:, h * HD : (h + 1) * HD] = blend(shares, pair[:2], h).astype(BF)
-
-
-def merge_part(ones, twos, after=()):
-    stacked = len(ones) == 1
-    groups = ones[0].shape[0] if stacked else len(ones)
-    shape = ones[0].shape[-2:]
-
-    def body(*refs):
-        if stacked:
-            refs = [refs[n].at[j] for n in range(2) for j in range(groups)] + list(refs[2:])
-        merge_kernel(groups, *refs)
+            out_ref[:, h * HD : (h + 1) * HD] = blend(shares, (one_ref, two_ref), h).astype(BF)
+
+    return small_call(kernel, "query_merge", [(rows, width if last else wide)], (one, two), after)[0]
+
+
+def project_part(own, other, out_weight, after=()):
+    rows, half = own.shape
+    depth, columns = out_weight.shape
+
+    def kernel(w_ref, own_ref, other_ref, *rest):
+        out_ref, attended = rest[-2:]
+
+        def put(first, second):
+            def run():
+                attended[:, :half] = first[...]
+                attended[:, half:] = second[...]
+
+            return run
+
+        even = bit(lax.axis_index("hst"), 0) == 0
+        choose(even, put(own_ref, other_ref), put(other_ref, own_ref))
+        out_ref[...] = dot(attended[...], w_ref[...]).astype(BF)
 
     return pl.pallas_call(
-        body,
-        out_shape=[jax.ShapeDtypeStruct(shape, BF)] * groups,
-        in_specs=[VMEM] * (2 * len(ones)) + [ANY] * len(after),
-        out_specs=[VMEM] * groups,
-        compiler_params=params(),
-        name="query_merge",
-    )(*ones, *twos, *after)
-
-
-def project_kernel(groups, w_ref, *rest):
-    ones, twos = rest[:groups], rest[groups : 2 * groups]
-    out_ref, attended = rest[-2], rest[-1]
-    width = ones[0].shape[1] - 3 * HD
-
-    @pl.when(pl.program_id(0) == 0)
-    def _():
-        for j, pair in enumerate(zip(ones, twos)):
-            shares, _ = merged(pair, width)
-            for h in range(width // HD):
-                at = j * width + h * HD
-                attended[:, at : at + HD] = blend(shares, pair, h).astype(BF)
-
-    out_ref[...] = dot(attended[...], w_ref[...]).astype(BF)
-
-
-def project_part(ones, twos, out_weight, after=()):
-    rows, wide = ones[0].shape
-    depth, columns = out_weight.shape
-    tile = min(256, columns)
-    return pl.pallas_call(
-        functools.partial(project_kernel, len(ones)),
-        grid=(columns // tile,),
+        kernel,
         out_shape=jax.ShapeDtypeStruct((rows, columns), BF),
-        in_specs=[pl.BlockSpec((depth, tile), lambda i: (0, i))]
-        + [pl.BlockSpec((rows, wide), lambda i: (0, 0))] * (2 * len(ones))
-        + [ANY] * len(after),
-        out_specs=pl.BlockSpec((rows, tile), lambda i: (0, i)),
+        in_specs=[VMEM] * 3 + [ANY] * len(after),
+        out_specs=VMEM,
         scratch_shapes=[pltpu.VMEM((rows, depth), BF)],
         compiler_params=params(),
         cost_estimate=pl.CostEstimate(
             flops=2 * rows * depth * columns, bytes_accessed=2 * depth * columns, transcendentals=0
         ),
         name="query_project",
-    )(out_weight, *ones, *twos, *after)
+    )(out_weight, own, other, *after)
 
 
 def general_queries(lengths, own_k, own_v, self_kv, query_q, out_weight, per_kv):
@@ -618,7 +558,7 @@
     if not fast:
         kv_first = lax.axis_index("tp") * local_heads // group_size
         self_kv = lax.dynamic_slice_in_dim(query_kv, kv_first * HD, kv_local * HD, 2)
-        own_k, own_v = pick(ctx_kv, query_q, kv_local, local_heads, False)
+        own_k, own_v = pick(ctx_kv, kv_local, local_heads)
         query_out = general_queries(lengths, own_k, own_v, self_kv, query_q, out_weight, per_kv)
         k, v = spread(jnp.stack([own_k, own_v]), "hst", 0)
         anchor = jnp.where(host % 2 == 0, k, v), jnp.where(host % 2 == 0, v, k)
@@ -634,23 +574,35 @@
         states[first] = own_part(ctx_q, own_k, own_v, first, count, per_kv, after)
         return states[first]
 
-    cut = slab * 3 // 8
-    own_k, own_v, pay = pick(ctx_kv, query_q, kv_local, local_heads, True)
-    landed = swap(pay, "hst", hosts, 1, 1)
-    done = own(0, 2)
-    one, two = first_relay(slab, cut, pay, own_k, landed, (done,))
-    one_landed = swap(one, "hst", hosts, 2, 4)
-    two_landed = swap(two, "hst", hosts, 4, 2)
-    done = own(2, 8, (one,))
-    back, front = second_relay(slab, cut, one, two, one_landed, two_landed, (done,))
-    back_landed = swap(back, "hst", hosts, 2, 4)
-    front_landed = swap(front, "hst", hosts, 4, 2)
-    done = own(10, 6, (front,))
-    held = third_relay(slab, cut, back, front, back_landed, front_landed, (done,))
+    along = ((2, 4), (4, 2))
+
+    def near_low(h):
+        return jnp.where(bit(h, 0) == 1, bit(h, 2), bit(h, 1)) == 0
+
+    landed = swap(query_q, "hst", hosts, 1, 1)
+    own_k, own_v = pick(ctx_kv, kv_local, local_heads)
+    value_landed = swap(own_v, "hst", hosts, 1, 1)
+    queries = join(lambda h: bit(h, 0) == 0, query_q, landed, (own_v,))
+    landed = swap(queries, "hst", hosts, *along[0])
+    done = own(0, 2, (queries,))
+    held = relay(lambda h: bit(h, 0) == 0, own_k, value_landed, (done,))
+    held_landed = swap(held, "hst", hosts, *along[0])
+    done = own(2, 2, (held,))
+    queries = join(near_low, queries, landed, (done,))
+    landed = swap(queries, "hst", hosts, *along[1])
+    done = own(4, 4, (queries,))
+    keep, send = source_part(lengths, own_k, own_v, query_kv, queries, landed, q_rows, per_kv, (done,))
+    landed = swap(send, "hst", hosts, 1, 1)
+    done = own(8, 2, (keep,))
+    held = relay(lambda h: h < 2, held, held_landed, (done,))
+    held_landed = swap(held, "hst", hosts, *along[1])
+    source = merge_part(keep, landed, False, (held,))
+    landed = swap(source, "hst", hosts, *along[0])
+    done = own(10, 6, (source,))
+    source = merge_part(source, landed, False, (done,))
+    landed = swap(source, "hst", hosts, *along[1])
+    held = relay(lambda h: (h <= 2) | (h == 5), held, held_landed, (source,))
     other = swap(held, "hst", hosts, 1, 1)
-    source = source_part(
-        lengths, own_k, own_v, query_kv, front, front_landed, cut, q_rows, hosts * q_rows, per_kv, (held,)
-    )
     results = {}
 
     def anchors(first, count, after, last=False):
@@ -661,25 +613,22 @@
         )
         return results[first]
 
+    done = anchors(0, 2, (held,))
+    done = anchors(2, 2, (done,))
+    source = merge_part(source, landed, True, (done,))
     landed = swap(source, "hst", hosts, 1, 1)
-    done = anchors(0, 2, (source,))
-    sources = merge_part([source], [landed], (done,))
-    landed = [swap(sources[0], "hst", hosts, 2, 4), swap(sources[1], "hst", hosts, 4, 2)]
-    done = anchors(2, 4, (sources[0],))
-    sources = merge_part(sources, landed, (done,))
-    landed = [swap(sources[0], "hst", hosts, 4, 2), swap(sources[1], "hst", hosts, 2, 4)]
-    done = anchors(6, 4, (sources[0],))
-    terms = project_part(sources, landed, out_weight, (done,))
-    shares = [(12, 4, True), (10, 2, False)]
+    done = anchors(4, 2, (source,))
+    terms = project_part(source, landed, out_weight, (done,))
+    shares = [(10, 6, True), (8, 2, False), (6, 2, False)]
     step = 1
     while step < groups:
         landed = swap(terms, "tp", groups, step, step)
-        if shares:
+        while shares:
             first, count, last = shares.pop()
-            done = anchors(first, count, (terms,), last)
-            if not last:
-                landed, _ = lax.optimization_barrier((landed, done))
-        terms = (terms.astype(F32) + landed.astype(F32)).astype(BF)
+            done = anchors(first, count, (terms, done), last)
+            if last or (first == 8 and step == 1):
+                break
+        terms = add_part(terms, landed, () if last else (done,))
         step *= 2
     for first, count, last in reversed(shares):
         done = anchors(first, count, (), last)

time: 115 us -> 120 us (1.043)
  the two profiles are of different devices: /device:TPU:6 before, /device:TPU:2 now
where the time goes in v3:
time: 120 us
  Pallas kernels  96.2 us (80%)
  starting transfers between devices  12.7 us (11%)
  waiting for transfers between devices  10.3 us (9%)
    pallas_call x6, Pallas kernels, anchor_part(): pl.pallas_call(functools.partial(anchor_kernel, first, count, base, per_k...  79.4 us
    ppermute x13, starting transfers between devices, swap(): lax.ppermute(value, axis, [(i, i ^ (odd if i & 1 else even)) for i in ran...  12.7 us
    ppermute x13, waiting for transfers between devices, swap(): lax.ppermute(value, axis, [(i, i ^ (odd if i & 1 else even)) for i in ran...  10.3 us
    pallas_call x5, Pallas kernels, own_part(): pl.pallas_call(functools.partial(own_kernel, first, count, per_kv), out_s...  10.2 us
    pallas_call x1, Pallas kernels, source_part(): pl.pallas_call(functools.partial(source_kernel, per_kv, q_rows, H // KVH)...  2.86 us
  transfers between devices with their start and end apart: 13, of which 5 were waited for; matrix products, arithmetic and copies ran while one was open for 0% of the time, Pallas kernels for 77%

profile of v3, /device:TPU:2, one launch (start us, length us, event | category | flops | bytes accessed | tf_op | source)
XLA Modules:
  0.0 120.2 jit_solution(10092199070074387592)
XLA Ops:
  0.6 1.3 %pick_columns.1 = (bf16[768,256]{1,0:T(8,128)(2,1)S(1)}, bf16[768,256]{1,0:T(8,128)(2,1)S(1)}) custom-call(bf16[2,768,1024]{2,1,0:T(8,128)(2,1)} %kv_ref.1), custom_call_target="tpu_custom_call" | custom-call | tf_op jit(solution)/shard_map/pick_columns/pallas_call | solution.py:60
  2.0 0.5 collective-permute-start
  2.5 1.3 %collective-permute-done.landed_ref = bf16[8,2048]{1,0:T(8,128)(2,1)S(1)} collective-permute-done((bf16[8,2048]{1,0:T(8,128)(2,1)S(1)}, bf16[8,2048]{1,0:T(8,128)(2,1)S(1)}, u32[]{:S(2)}, u32[]{:S(2)}) %collective-permute-start) | collective-permute-done | bytes 32800 | tf_op jit(solution)/shard_map/ppermute | solution.py:43
  3.8 1.2 %context_own.5.rest_0_.refs_2_ = bf16[768,768]{1,0:T(8,128)(2,1)S(1)} custom-call(bf16[768,2048]{1,0:T(8,128)(2,1)S(1)} %copy-done, bf16[768,256]{1,0:T(8,128)(2,1)S(1)} %get-tuple-element.6.k_ref.one_ref.refs_3_, bf16[768,256]{1,0:T(8,128)(2,1)S(1)} %get-tuple-element.7.rest_0_.v_ref.refs_4_, bf16[16,2048]{1,0:T(8,128)(2,1)S(1)} %query_join.2.rest_0_.known_ref), custom_call_target="tpu_custom_call" | custom-call | flops 805306368 | bytes 1179648 | tf_op jit(solution)/shard_map/context_own/pallas_call | solution.py:193
  5.1 0.1 collective-permute-start.5
  5.2 2.0 %collective-permute-start.1 = (bf16[16,2048]{1,0:T(8,128)(2,1)S(1)}, bf16[16,2048]{1,0:T(8,128)(2,1)S(1)}, u32[]{:S(2)}, u32[]{:S(2)}) collective-permute-start(bf16[16,2048]{1,0:T(8,128)(2,1)S(1)} %query_join.2.rest_0_.known_ref), channel_id=1, source_target_pairs={{0,8},{4,20},{8,0},{12,28},{16,24},{20,4},{24,16},{28,12},{1,9},{5... | collective-permute-start | bytes 196616 | tf_op jit(solution)/shard_map/ppermute | solution.py:43
  7.2 1.2 %context_own.6.rest_0_.refs_2_ = bf16[768,768]{1,0:T(8,128)(2,1)S(1)} custom-call(bf16[768,2048]{1,0:T(8,128)(2,1)S(1)} %copy-done, bf16[768,256]{1,0:T(8,128)(2,1)S(1)} %get-tuple-element.6.k_ref.one_ref.refs_3_, bf16[768,256]{1,0:T(8,128)(2,1)S(1)} %get-tuple-element.7.rest_0_.v_ref.refs_4_, bf16[768,256]{1,0:T(8,128)(2,1)S(1)} %anchor_relay.3.rest_0_.one_ref), custom_call_target="tpu_custom_call" | custom-call | flops 805306368 | bytes 1179648 | tf_op jit(solution)/shard_map/context_own/pallas_call | solution.py:193
  8.4 5.2 %collective-permute-done.1.landed_ref = bf16[16,2048]{1,0:T(8,128)(2,1)S(1)} collective-permute-done((bf16[16,2048]{1,0:T(8,128)(2,1)S(1)}, bf16[16,2048]{1,0:T(8,128)(2,1)S(1)}, u32[]{:S(2)}, u32[]{:S(2)}) %collective-permute-start.1) | collective-permute-done | bytes 65568 | tf_op jit(solution)/shard_map/ppermute | solution.py:43
  13.7 1.6 %collective-permute-start.3 = (bf16[32,2048]{1,0:T(8,128)(2,1)S(1)}, bf16[32,2048]{1,0:T(8,128)(2,1)S(1)}, u32[]{:S(2)}, u32[]{:S(2)}) collective-permute-start(bf16[32,2048]{1,0:T(8,128)(2,1)S(1)} %query_join.3.rest_0_.known_ref), channel_id=1, source_target_pairs={{0,16},{4,12},{8,24},{12,4},{16,0},{20,28},{24,8},{28,20},{1,17},{... | collective-permute-start | bytes 393224 | tf_op jit(solution)/shard_map/ppermute | solution.py:43
  15.3 2.6 %context_own.7.rest_0_.refs_2_ = bf16[768,1536]{1,0:T(8,128)(2,1)S(1)} custom-call(bf16[768,2048]{1,0:T(8,128)(2,1)S(1)} %copy-done, bf16[768,256]{1,0:T(8,128)(2,1)S(1)} %get-tuple-element.6.k_ref.one_ref.refs_3_, bf16[768,256]{1,0:T(8,128)(2,1)S(1)} %get-tuple-element.7.rest_0_.v_ref.refs_4_, bf16[32,2048]{1,0:T(8,128)(2,1)S(1)} %query_join.3.rest_0_.known_ref), custom_call_target="tpu_custom_call" | custom-call | flops 1610612736 | bytes 2359296 | tf_op jit(solution)/shard_map/context_own/pallas_call | solution.py:193
  17.9 0.8 collective-permute-done.3.landed_ref
  18.7 2.9 %query_source.1 = (bf16[64,1408]{1,0:T(8,128)(2,1)S(1)}, bf16[64,1408]{1,0:T(8,128)(2,1)S(1)}) custom-call(s32[8]{0:T(128)S(1)} %copy-done.4, bf16[768,256]{1,0:T(8,128)(2,1)S(1)} %get-tuple-element.6.k_ref.one_ref.refs_3_, bf16[768,256]{1,0:T(8,128)(2,1)S(1)} %get-tuple-element.7.rest_0_.v_ref.refs_4_, bf16[2,8,1024]{2,1,0:T(8,128)(2,1)S(1)} %copy-done.2, ...), custom_call_target="tpu_custom_call" | custom-call | flops 805306368 | bytes 2097152 | tf_op jit(solution)/shard_map/query_source/pallas_call | solution.py:439
  21.7 1.2 %context_own.8.rest_0_.refs_2_ = bf16[768,768]{1,0:T(8,128)(2,1)S(1)} custom-call(bf16[768,2048]{1,0:T(8,128)(2,1)S(1)} %copy-done, bf16[768,256]{1,0:T(8,128)(2,1)S(1)} %get-tuple-element.6.k_ref.one_ref.refs_3_, bf16[768,256]{1,0:T(8,128)(2,1)S(1)} %get-tuple-element.7.rest_0_.v_ref.refs_4_, bf16[64,1408]{1,0:T(8,128)(2,1)S(1)} %get-tuple-element.8.rest_0_.one_ref), custom_call_target="tpu_custom_call" | custom-call | flops 805306368 | bytes 1179648 | tf_op jit(solution)/shard_map/context_own/pallas_call | solution.py:193
  23.0 1.6 %collective-permute-start.6 = (bf16[768,256]{1,0:T(8,128)(2,1)S(1)}, bf16[768,256]{1,0:T(8,128)(2,1)S(1)}, u32[]{:S(2)}, u32[]{:S(2)}) collective-permute-start(bf16[768,256]{1,0:T(8,128)(2,1)S(1)} %anchor_relay.4.rest_0_.one_ref), channel_id=1, source_target_pairs={{0,16},{4,12},{8,24},{12,4},{16,0},{20,28},{24,8},{28,20},{1,17},{... | collective-permute-start | bytes 1179656 | tf_op jit(solution)/shard_map/ppermute | solution.py:43
  24.5 0.2 query_merge.3.rest_0_.one_ref
  24.8 0.6 collective-permute-start.7
  25.4 3.9 %context_own.9.rest_0_.refs_2_ = bf16[768,2304]{1,0:T(8,128)(2,1)S(1)} custom-call(bf16[768,2048]{1,0:T(8,128)(2,1)S(1)} %copy-done, bf16[768,256]{1,0:T(8,128)(2,1)S(1)} %get-tuple-element.6.k_ref.one_ref.refs_3_, bf16[768,256]{1,0:T(8,128)(2,1)S(1)} %get-tuple-element.7.rest_0_.v_ref.refs_4_, bf16[64,1408]{1,0:T(8,128)(2,1)S(1)} %query_merge.3.rest_0_.one_ref), custom_call_target="tpu_custom_call" | custom-call | flops 2415919104 | bytes 3538944 | tf_op jit(solution)/shard_map/context_own/pallas_call | solution.py:193
  29.3 2.9 %collective-permute-done.7.two_ref = bf16[64,1408]{1,0:T(8,128)(2,1)S(1)} collective-permute-done((bf16[64,1408]{1,0:T(8,128)(2,1)S(1)}, bf16[64,1408]{1,0:T(8,128)(2,1)S(1)}, u32[]{:S(2)}, u32[]{:S(2)}) %collective-permute-start.7) | collective-permute-done | bytes 180256 | tf_op jit(solution)/shard_map/ppermute | solution.py:43
  32.3 0.2 query_merge.4.rest_0_.one_ref
  32.5 0.1 collective-permute-done.6.two_ref
  32.7 1.7 %collective-permute-start.9 = (bf16[64,1408]{1,0:T(8,128)(2,1)S(1)}, bf16[64,1408]{1,0:T(8,128)(2,1)S(1)}, u32[]{:S(2)}, u32[]{:S(2)}) collective-permute-start(bf16[64,1408]{1,0:T(8,128)(2,1)S(1)} %query_merge.4.rest_0_.one_ref), channel_id=1, source_target_pairs={{0,16},{4,12},{8,24},{12,4},{16,0},{20,28},{24,8},{28,20},{1,17},{... | collective-permute-start | bytes 540680 | tf_op jit(solution)/shard_map/ppermute | solution.py:43
  34.4 10.1 %context_anchor.6.refs_7_ = bf16[768,256]{1,0:T(8,128)(2,1)S(1)} custom-call(s32[8]{0:T(128)S(1)} %copy-done.4, bf16[768,2048]{1,0:T(8,128)(2,1)S(1)} %copy-done, bf16[768,768]{1,0:T(8,128)(2,1)S(1)} %context_own.5.rest_0_.refs_2_, bf16[768,256]{1,0:T(8,128)(2,1)S(1)} %get-tuple-element.6.k_ref.one_ref.refs_3_, ...), custom_call_target="tpu_custom_call" | custom-call | flops 1207959552 | bytes 1572864 | tf_op jit(solution)/shard_map/context_anchor/pallas_call | solution.py:342
  44.5 9.9 %context_anchor.7.rest_0_.refs_8_ = bf16[768,256]{1,0:T(8,128)(2,1)S(1)} custom-call(s32[8]{0:T(128)S(1)} %copy-done.4, bf16[768,2048]{1,0:T(8,128)(2,1)S(1)} %copy-done, bf16[768,768]{1,0:T(8,128)(2,1)S(1)} %context_own.6.rest_0_.refs_2_, bf16[768,256]{1,0:T(8,128)(2,1)S(1)} %get-tuple-element.6.k_ref.one_ref.refs_3_, ...), custom_call_target="tpu_custom_call" | custom-call | flops 1207959552 | bytes 1572864 | tf_op jit(solution)/shard_map/context_anchor/pallas_call | solution.py:342
  54.4 0.2 query_merge.5.refs_7_.own_ref
  54.7 9.9 %context_anchor.8.rest_0_.refs_8_.refs_9_ = bf16[768,256]{1,0:T(8,128)(2,1)S(1)} custom-call(s32[8]{0:T(128)S(1)} %copy-done.4, bf16[768,2048]{1,0:T(8,128)(2,1)S(1)} %copy-done, bf16[768,1536]{1,0:T(8,128)(2,1)S(1)} %context_own.7.rest_0_.refs_2_, bf16[768,256]{1,0:T(8,128)(2,1)S(1)} %get-tuple-element.6.k_ref.one_ref.refs_3_, ...), custom_call_target="tpu_custom_call" | custom-call | flops 1207959552 | bytes 1572864 | tf_op jit(solution)/shard_map/context_anchor/pallas_call | solution.py:342
  64.7 0.9 query_project.1.refs_7_.one_ref
  65.6 1.8 %collective-permute-start.11 = (bf16[64,1024]{1,0:T(8,128)(2,1)S(1)}, bf16[64,1024]{1,0:T(8,128)(2,1)S(1)}, u32[]{:S(2)}, u32[]{:S(2)}) collective-permute-start(bf16[64,1024]{1,0:T(8,128)(2,1)S(1)} %query_project.1.refs_7_.one_ref), channel_id=1, source_target_pairs={{0,1},{1,0},{2,3},{3,2},{4,5},{5,4},{6,7},{7,6},{8,9},{9,8},{10,11... | collective-permute-start | bytes 393224 | tf_op jit(solution)/shard_map/ppermute | solution.py:43
  67.3 9.9 %context_anchor.9.refs_8_.refs_10_ = bf16[768,256]{1,0:T(8,128)(2,1)S(1)} custom-call(s32[8]{0:T(128)S(1)} %copy-done.4, bf16[768,2048]{1,0:T(8,128)(2,1)S(1)} %copy-done, bf16[768,1536]{1,0:T(8,128)(2,1)S(1)} %context_own.7.rest_0_.refs_2_, bf16[768,256]{1,0:T(8,128)(2,1)S(1)} %get-tuple-element.6.k_ref.one_ref.refs_3_, ...), custom_call_target="tpu_custom_call" | custom-call | flops 1207959552 | bytes 1572864 | tf_op jit(solution)/shard_map/context_anchor/pallas_call | solution.py:342
  77.3 10.2 %context_anchor.10.rest_0_.refs_11_.refs_13_ = bf16[768,256]{1,0:T(8,128)(2,1)S(1)} custom-call(s32[8]{0:T(128)S(1)} %copy-done.4, bf16[768,2048]{1,0:T(8,128)(2,1)S(1)} %copy-done, bf16[768,768]{1,0:T(8,128)(2,1)S(1)} %context_own.8.rest_0_.refs_2_, bf16[768,256]{1,0:T(8,128)(2,1)S(1)} %get-tuple-element.6.k_ref.one_ref.refs_3_, ...), custom_call_target="tpu_custom_call" | custom-call | flops 1207959552 | bytes 1572864 | tf_op jit(solution)/shard_map/context_anchor/pallas_call | solution.py:342
  87.5 2.6 %collective-permute-start.12 = (bf16[64,1024]{1,0:T(8,128)(2,1)S(1)}, bf16[64,1024]{1,0:T(8,128)(2,1)S(1)}, u32[]{:S(2)}, u32[]{:S(2)}) collective-permute-start(bf16[64,1024]{1,0:T(8,128)(2,1)S(1)} %query_sum.2.refs_12_.one_ref), channel_id=1, source_target_pairs={{0,2},{1,3},{2,0},{3,1},{4,6},{5,7},{6,4},{7,5},{8,10},{9,11},{10,... | collective-permute-start | bytes 393224 | tf_op jit(solution)/shard_map/ppermute | solution.py:43
  90.1 29.4 %context_anchor.11 = bf16[768,2048]{1,0:T(8,128)(2,1)} custom-call(s32[8]{0:T(128)S(1)} %copy-done.4, bf16[768,2048]{1,0:T(8,128)(2,1)S(1)} %copy-done, bf16[768,2304]{1,0:T(8,128)(2,1)S(1)} %context_own.9.rest_0_.refs_2_, bf16[768,256]{1,0:T(8,128)(2,1)S(1)} %get-tuple-element.6.k_ref.one_ref.refs_3_, ...), custom_call_target="tpu_custom_call" | custom-call | flops 3623878656 | bytes 4718592 | tf_op jit(solution)/shard_map/context_anchor/pallas_call | solution.py:342
  119.6 0.7 query_sum.3
  (28 shorter events, 0.5 us)
Async XLA Ops:
  0.6 1.4 %copy-start.3 = (bf16[8,2048]{1,0:T(8,128)(2,1)S(1)}, bf16[8,2048]{1,0:T(8,128)(2,1)}, u32[]{:S(2)}) copy-start(bf16[8,2048]{1,0:T(8,128)(2,1)} %known_ref.1) | copy-start | bytes 98308
  0.6 3.2 %copy-start = (bf16[768,2048]{1,0:T(8,128)(2,1)S(1)}, bf16[768,2048]{1,0:T(8,128)(2,1)}, u32[]{:S(2)}) copy-start(bf16[768,2048]{1,0:T(8,128)(2,1)} %refs_1_.11) | copy-start | bytes 9437188
  2.0 3.1 %collective-permute-start.2 = (bf16[768,256]{1,0:T(8,128)(2,1)S(1)}, bf16[768,256]{1,0:T(8,128)(2,1)S(1)}, u32[]{:S(2)}, u32[]{:S(2)}) collective-permute-start(bf16[768,256]{1,0:T(8,128)(2,1)S(1)} %get-tuple-element.7.rest_0_.v_ref.refs_4_), channel_id=1, source_target_pairs={{0,4},{4,0},{8,12},{12,8},{16,20},{20,16},{24,28},{28,24},{1,5},{5... | collective-permute-start | bytes 1179656 | tf_op jit(solution)/shard_map/ppermute | solution.py:43
  2.0 1.7 %collective-permute-start = (bf16[8,2048]{1,0:T(8,128)(2,1)S(1)}, bf16[8,2048]{1,0:T(8,128)(2,1)S(1)}, u32[]{:S(2)}, u32[]{:S(2)}) collective-permute-start(bf16[8,2048]{1,0:T(8,128)(2,1)S(1)} %copy-done.3), channel_id=1, source_target_pairs={{0,4},{4,0},{8,12},{12,8},{16,20},{20,16},{24,28},{28,24},{1,5},{5... | collective-permute-start | bytes 98312 | tf_op jit(solution)/shard_map/ppermute | solution.py:43
  5.1 17.8 %collective-permute-start.5 = (bf16[768,256]{1,0:T(8,128)(2,1)S(1)}, bf16[768,256]{1,0:T(8,128)(2,1)S(1)}, u32[]{:S(2)}, u32[]{:S(2)}) collective-permute-start(bf16[768,256]{1,0:T(8,128)(2,1)S(1)} %anchor_relay.3.rest_0_.one_ref), channel_id=1, source_target_pairs={{0,8},{4,20},{8,0},{12,28},{16,24},{20,4},{24,16},{28,12},{1,9},{5... | collective-permute-start | bytes 1179656 | tf_op jit(solution)/shard_map/ppermute | solution.py:43
  5.2 8.5 %collective-permute-start.1 = (bf16[16,2048]{1,0:T(8,128)(2,1)S(1)}, bf16[16,2048]{1,0:T(8,128)(2,1)S(1)}, u32[]{:S(2)}, u32[]{:S(2)}) collective-permute-start(bf16[16,2048]{1,0:T(8,128)(2,1)S(1)} %query_join.2.rest_0_.known_ref), channel_id=1, source_target_pairs={{0,8},{4,20},{8,0},{12,28},{16,24},{20,4},{24,16},{28,12},{1,9},{5... | collective-permute-start | bytes 196616 | tf_op jit(solution)/shard_map/ppermute | solution.py:43
  13.7 5.1 %copy-start.2 = (bf16[2,8,1024]{2,1,0:T(8,128)(2,1)S(1)}, bf16[2,8,1024]{2,1,0:T(8,128)(2,1)}, u32[]{:S(2)}) copy-start(bf16[2,8,1024]{2,1,0:T(8,128)(2,1)} %self_ref.1) | copy-start | bytes 98308
  13.7 5.1 %copy-start.4 = (s32[8]{0:T(128)S(1)}, s32[8]{0:T(128)}, u32[]{:S(2)}) copy-start(s32[8]{0:T(128)} %refs_0_.11) | copy-start | bytes 100
  13.7 5.0 %collective-permute-start.3 = (bf16[32,2048]{1,0:T(8,128)(2,1)S(1)}, bf16[32,2048]{1,0:T(8,128)(2,1)S(1)}, u32[]{:S(2)}, u32[]{:S(2)}) collective-permute-start(bf16[32,2048]{1,0:T(8,128)(2,1)S(1)} %query_join.3.rest_0_.known_ref), channel_id=1, source_target_pairs={{0,16},{4,12},{8,24},{12,4},{16,0},{20,28},{24,8},{28,20},{1,17},{... | collective-permute-start | bytes 393224 | tf_op jit(solution)/shard_map/ppermute | solution.py:43
  21.6 3.0 %collective-permute-start.4 = (bf16[64,1408]{1,0:T(8,128)(2,1)S(1)}, bf16[64,1408]{1,0:T(8,128)(2,1)S(1)}, u32[]{:S(2)}, u32[]{:S(2)}) collective-permute-start(bf16[64,1408]{1,0:T(8,128)(2,1)S(1)} %get-tuple-element.9), channel_id=1, source_target_pairs={{0,4},{4,0},{8,12},{12,8},{16,20},{20,16},{24,28},{28,24},{1,5},{5... | collective-permute-start | bytes 540680 | tf_op jit(solution)/shard_map/ppermute | solution.py:43
  23.0 9.7 %collective-permute-start.6 = (bf16[768,256]{1,0:T(8,128)(2,1)S(1)}, bf16[768,256]{1,0:T(8,128)(2,1)S(1)}, u32[]{:S(2)}, u32[]{:S(2)}) collective-permute-start(bf16[768,256]{1,0:T(8,128)(2,1)S(1)} %anchor_relay.4.rest_0_.one_ref), channel_id=1, source_target_pairs={{0,16},{4,12},{8,24},{12,4},{16,0},{20,28},{24,8},{28,20},{1,17},{... | collective-permute-start | bytes 1179656 | tf_op jit(solution)/shard_map/ppermute | solution.py:43
  24.8 7.5 %collective-permute-start.7 = (bf16[64,1408]{1,0:T(8,128)(2,1)S(1)}, bf16[64,1408]{1,0:T(8,128)(2,1)S(1)}, u32[]{:S(2)}, u32[]{:S(2)}) collective-permute-start(bf16[64,1408]{1,0:T(8,128)(2,1)S(1)} %query_merge.3.rest_0_.one_ref), channel_id=1, source_target_pairs={{0,8},{4,20},{8,0},{12,28},{16,24},{20,4},{24,16},{28,12},{1,9},{5... | collective-permute-start | bytes 540680 | tf_op jit(solution)/shard_map/ppermute | solution.py:43
  32.6 1.8 %collective-permute-start.8 = (bf16[768,256]{1,0:T(8,128)(2,1)S(1)}, bf16[768,256]{1,0:T(8,128)(2,1)S(1)}, u32[]{:S(2)}, u32[]{:S(2)}) collective-permute-start(bf16[768,256]{1,0:T(8,128)(2,1)S(1)} %anchor_relay.5.refs_5_.refs_7_), channel_id=1, source_target_pairs={{0,4},{4,0},{8,12},{12,8},{16,20},{20,16},{24,28},{28,24},{1,5},{5... | collective-permute-start | bytes 1179656 | tf_op jit(solution)/shard_map/ppermute | solution.py:43
  32.7 21.7 %collective-permute-start.9 = (bf16[64,1408]{1,0:T(8,128)(2,1)S(1)}, bf16[64,1408]{1,0:T(8,128)(2,1)S(1)}, u32[]{:S(2)}, u32[]{:S(2)}) collective-permute-start(bf16[64,1408]{1,0:T(8,128)(2,1)S(1)} %query_merge.4.rest_0_.one_ref), channel_id=1, source_target_pairs={{0,16},{4,12},{8,24},{12,4},{16,0},{20,28},{24,8},{28,20},{1,17},{... | collective-permute-start | bytes 540680 | tf_op jit(solution)/shard_map/ppermute | solution.py:43
  54.7 10.0 %copy-start.1 = (bf16[2048,1024]{1,0:T(8,128)(2,1)S(1)}, bf16[2048,1024]{1,0:T(8,128)(2,1)}, u32[]{:S(2)}) copy-start(bf16[2048,1024]{1,0:T(8,128)(2,1)} %w_ref.1) | copy-start | bytes 12582916
  54.7 10.0 %collective-permute-start.10 = (bf16[64,1024]{1,0:T(8,128)(2,1)S(1)}, bf16[64,1024]{1,0:T(8,128)(2,1)S(1)}, u32[]{:S(2)}, u32[]{:S(2)}) collective-permute-start(bf16[64,1024]{1,0:T(8,128)(2,1)S(1)} %query_merge.5.refs_7_.own_ref), channel_id=1, source_target_pairs={{0,4},{4,0},{8,12},{12,8},{16,20},{20,16},{24,28},{28,24},{1,5},{5... | collective-permute-start | bytes 393224 | tf_op jit(solution)/shard_map/ppermute | solution.py:43
  65.6 21.8 %collective-permute-start.11 = (bf16[64,1024]{1,0:T(8,128)(2,1)S(1)}, bf16[64,1024]{1,0:T(8,128)(2,1)S(1)}, u32[]{:S(2)}, u32[]{:S(2)}) collective-permute-start(bf16[64,1024]{1,0:T(8,128)(2,1)S(1)} %query_project.1.refs_7_.one_ref), channel_id=1, source_target_pairs={{0,1},{1,0},{2,3},{3,2},{4,5},{5,4},{6,7},{7,6},{8,9},{9,8},{10,11... | collective-permute-start | bytes 393224 | tf_op jit(solution)/shard_map/ppermute | solution.py:43
  87.5 32.1 %collective-permute-start.12 = (bf16[64,1024]{1,0:T(8,128)(2,1)S(1)}, bf16[64,1024]{1,0:T(8,128)(2,1)S(1)}, u32[]{:S(2)}, u32[]{:S(2)}) collective-permute-start(bf16[64,1024]{1,0:T(8,128)(2,1)S(1)} %query_sum.2.refs_12_.one_ref), channel_id=1, source_target_pairs={{0,2},{1,3},{2,0},{3,1},{4,6},{5,7},{6,4},{7,5},{8,10},{9,11},{10,... | collective-permute-start | bytes 393224 | tf_op jit(solution)/shard_map/ppermute | solution.py:43

commit v4 on v3

--- a/solution.py
+++ b/solution.py
@@ -88,37 +88,59 @@
     pl.when(jnp.logical_not(condition))(two)
 
 
-def relay(keep_of, one, two, after):
+def take_rows(target, source, rows, cols=slice(None)):
+    def run():
+        target[:rows, :] = source[:rows, cols]
+
+    return run
+
+
+def first_payloads(own_k, value_landed, query_q, query_landed, after):
+    slab, columns = own_k.shape
+    q_rows, width = query_q.shape
+
+    def kernel(k_ref, v_ref, own_ref, landed_ref, *rest):
+        out_refs = rest[-(columns // HD) :]
+        even = bit(lax.axis_index("hst"), 0) == 0
+        for j, out_ref in enumerate(out_refs):
+            cols = slice(j * HD, (j + 1) * HD)
+            choose(even, take_rows(out_ref, k_ref, slab, cols), take_rows(out_ref, v_ref, slab, cols))
+
+        def put(first, second):
+            def run():
+                both = jnp.concatenate([first[...].astype(F32), second[...].astype(F32)], 0).astype(BF)
+                for h in range(width // HD):
+                    at = slab + 2 * q_rows * h
+                    out_refs[0][at : at + 2 * q_rows, :] = both[:, h * HD : (h + 1) * HD]
+
+            return run
+
+        choose(even, put(own_ref, landed_ref), put(landed_ref, own_ref))
+
+    shapes = [(slab, HD)] * (columns // HD)
+    shapes[0] = (slab + 2 * q_rows * width // HD, HD)
+    return small_call(kernel, "payload_first", shapes, (own_k, value_landed, query_q, query_landed), after)
+
+
+def relay(keep_of, one, two, slab, low_of=None, after=()):
+    rows = one.shape[0] - slab if low_of is not None else 0
+
     def kernel(one_ref, two_ref, *rest):
         out_ref = rest[-1]
-
-        def take(ref):
-            def run():
-                out_ref[...] = ref[...]
-
-            return run
-
-        choose(keep_of(lax.axis_index("hst")), take(one_ref), take(two_ref))
-
-    return small_call(kernel, "anchor_relay", [one.shape], (one, two), after)[0]
-
-
-def join(low_of, known, landed, after):
-    rows, width = known.shape
-
-    def kernel(known_ref, landed_ref, *rest):
-        out_ref = rest[-1]
+        host = lax.axis_index("hst")
+        choose(keep_of(host), take_rows(out_ref, one_ref, slab), take_rows(out_ref, two_ref, slab))
 
         def put(first, second):
             def run():
-                both = jnp.concatenate([first[...].astype(F32), second[...].astype(F32)], 0)
-                out_ref[...] = both.astype(BF)
+                out_ref[slab : slab + rows, :] = first[slab:, :]
+                out_ref[slab + rows :, :] = second[slab:, :]
 
             return run
 
-        choose(low_of(lax.axis_index("hst")), put(known_ref, landed_ref), put(landed_ref, known_ref))
-
-    return small_call(kernel, "query_join", [(2 * rows, width)], (known, landed), after)[0]
+        if rows:
+            choose(low_of(host), put(one_ref, two_ref), put(two_ref, one_ref))
+
+    return small_call(kernel, "payload_relay", [(slab + 2 * rows, HD)], (one, two), after)[0]
 
 
 def add_part(one, two, after=()):
@@ -142,14 +164,19 @@
     return 256 if slab % 256 == 0 else slab
 
 
+def body_size(count, most):
+    return max(x for x in range(1, most + 1) if count % x == 0)
+
+
 def own_kernel(first, count, per_kv, q_ref, k_ref, v_ref, *rest):
     state_ref, vaug = rest[-2], rest[-1]
     slab = q_ref.shape[0]
     tile = row_tile(slab)
-    heads = min(2, count)
+    half = tile // 2
+    heads = body_size(count, 4)
     fill_values(vaug, v_ref)
-    rows = lax.broadcasted_iota(jnp.int32, (tile, tile), 0)
-    cols = lax.broadcasted_iota(jnp.int32, (tile, tile), 1)
+    rows = lax.broadcasted_iota(jnp.int32, (half, half), 0)
+    cols = lax.broadcasted_iota(jnp.int32, (half, half), 1)
     causal = cols <= rows
     chunks = slab // tile
     units = [(h, j) for h in range(heads) for j in range(chunks)]
@@ -162,25 +189,24 @@
             query = q_ref[j * tile :, lanes(first + i * heads + h, HD)]
             return dot_t(query, k_ref[j * tile : (j + 1) * tile, lanes(kv, HD)])
 
+        def power(x):
+            return jnp.exp2(x * SCALE2).astype(BF)
+
+        def corner(x):
+            return jnp.where(causal, jnp.exp2(x * SCALE2), 0.0).astype(BF)
+
         current = scores(0)
         totals = [None] * chunks
         for at, (h, j) in enumerate(units):
             following = scores(at + 1) if at + 1 < len(units) else None
-            corner = jnp.where(causal, current[:tile], MASKED)
-            masked = corner if j == chunks - 1 else jnp.concatenate([corner, current[tile:]], 0)
-            if j == 0:
-                peak = jnp.max(masked, axis=1, keepdims=True) * SCALE2
-                shift = jnp.broadcast_to(peak, (slab, HD)).astype(BF)
-                state_ref[:, pl.ds(pl.multiple_of((i * heads + h) * 3 * HD + 2 * HD, HD), HD)] = shift
-                shift = shift.astype(F32)
-            shifts = jnp.concatenate([shift[j * tile :]] * (tile // HD), 1)
-            expo = jnp.exp2((masked * SCALE2 - shifts).astype(BF))
-            part = dot(expo, vaug[j * tile : (j + 1) * tile, lanes(kv, 2 * HD)])
+            top = jnp.concatenate([corner(current[:half, :half]), jnp.zeros((half, half), BF)], 1)
+            low = jnp.concatenate([power(current[half:tile, :half]), corner(current[half:tile, half:])], 1)
+            expo = [top, low] if j == chunks - 1 else [top, low, power(current[tile:])]
+            part = dot(jnp.concatenate(expo, 0), vaug[j * tile : (j + 1) * tile, lanes(kv, 2 * HD)])
             for r in range(j, chunks):
                 piece = part[(r - j) * tile : (r - j + 1) * tile]
                 totals[r] = piece if j == 0 else totals[r] + piece
-            cols = pl.ds(pl.multiple_of((i * heads + h) * 3 * HD, HD), 2 * HD)
-            state_ref[j * tile : (j + 1) * tile, cols] = totals[j].astype(BF)
+            state_ref[j * tile : (j + 1) * tile, lanes(i * heads + h, 2 * HD)] = totals[j]
             current = following
         return carry
 
@@ -192,7 +218,7 @@
     work = count * slab * (slab + row_tile(slab)) // 2
     return pl.pallas_call(
         functools.partial(own_kernel, first, count, per_kv),
-        out_shape=jax.ShapeDtypeStruct((slab, count * 3 * HD), BF),
+        out_shape=jax.ShapeDtypeStruct((slab, count * 2 * HD), F32),
         in_specs=[VMEM] * 3 + [ANY] * len(after),
         out_specs=VMEM,
         scratch_shapes=[pltpu.VMEM((slab, 2 * own_v.shape[1]), BF)],
@@ -212,17 +238,16 @@
     else:
         out_ref, keys, vaug = refs[-3:]
     slab = q_ref.shape[0]
-    heads = min(2, count)
+    heads = body_size(count, 2 if last else 4)
+    kv = first // per_kv
     host = lax.axis_index("hst")
     own_len = lengths_ref[host]
 
-    def hand_over(source, at, width, sem):
-        return pltpu.make_async_copy(source, full_ref.at[:, at], sems.at[sem])
-
-    moves = []
-    for n, (start, width) in enumerate(befores):
-        at = pl.ds(start * HD, width * HD)
-        moves.append(hand_over(earlier[n], at, width, n))
+    def hand_over(source, start, width, sem):
+        target = full_ref.at[:, pl.ds(start * HD, width * HD)]
+        return pltpu.make_async_copy(source, target, sems.at[sem])
+
+    moves = [hand_over(earlier[n], *place, n) for n, place in enumerate(befores)]
     for move in moves:
         move.start()
 
@@ -236,41 +261,34 @@
         keys[...] = odd_ref[...]
         fill_values(vaug, even_ref)
 
-    row_ids = lax.broadcasted_iota(jnp.int32, (slab, HD), 0)
-    live = row_ids < own_len
-
-    def result_move(i):
-        cols = pl.ds(pl.multiple_of(i * heads * HD, heads * HD), heads * HD)
-        target = pl.ds(pl.multiple_of((first + i * heads) * HD, heads * HD), heads * HD)
-        return hand_over(out_ref.at[:, cols], target, heads, len(befores) + i)
-
-    def body(i, carry):
-        kv = lax.div(first + i * heads, per_kv)
+    def part(start):
+        def query_of(h):
+            at = (first + start + h) * HD
+            return q_ref[:, at : at + HD]
 
         def scores(h):
-            return dot_t(q_ref[:, lanes(first + i * heads + h, HD)], keys[:, lanes(kv, HD)])
-
-        def state_of(h, at, width):
-            start = (first - base + i * heads + h) * 3 * HD + at
-            return state_ref[:, pl.ds(pl.multiple_of(start, HD), width)].astype(F32)
+            return dot_t(query_of(h), keys[...])
+
+        def state_of(h):
+            at = (first - base + start + h) * 2 * HD
+            return state_ref[:, at : at + 2 * HD]
 
         def finish(h, total, worst):
             sums = total[:, HD:]
-            inverse = 1.0 / sums
-            result = jnp.where(live, total[:, :HD] * inverse, 0.0)
-            out_ref[:, lanes(i * heads + h, HD)] = result.astype(BF)
+            inverse = pl.reciprocal(sums, approx=True)
+            out_ref[:, (start + h) * HD : (start + h + 1) * HD] = (total[:, :HD] * inverse).astype(BF)
             return jnp.minimum(worst, jnp.minimum(sums, inverse))
 
         def check(worst):
             @pl.when(jnp.logical_not(jnp.min(worst) > TINY))
             def _():
-                exact_block(first + i * heads, i * heads, heads, host, own_len, kv, q_ref, k_ref, v_ref, keys, vaug, out_ref)
+                exact_block(first + start, start, heads, host, own_len, kv, q_ref, k_ref, v_ref, keys, vaug, out_ref)
 
         @pl.when(host == 0)
         def _():
             worst = jnp.ones((slab, HD), F32)
             for h in range(heads):
-                worst = finish(h, state_of(h, 0, 2 * HD), worst)
+                worst = finish(h, state_of(h), worst)
             check(worst)
 
         @pl.when(host > 0)
@@ -279,23 +297,30 @@
             current = scores(0)
             for h in range(heads):
                 following = scores(h + 1) if h + 1 < heads else None
-                shifts = jnp.concatenate([state_of(h, 2 * HD, HD)] * (slab // HD), 1)
-                expo = jnp.exp2((current * SCALE2 - shifts).astype(BF))
-                total = dot(expo, vaug[:, lanes(kv, 2 * HD)]) + state_of(h, 0, 2 * HD)
+                expo = jnp.exp2(current * SCALE2).astype(BF)
+                total = dot(expo, vaug[...]) + state_of(h)
                 worst = finish(h, total, worst)
                 current = following
             check(worst)
 
+        @pl.when(own_len < slab)
+        def _():
+            row_ids = lax.broadcasted_iota(jnp.int32, (slab, HD), 0)
+            for h in range(start, start + heads):
+                cols = slice(h * HD, (h + 1) * HD)
+                kept = jnp.where(row_ids < own_len, out_ref[:, cols].astype(F32), 0.0)
+                out_ref[:, cols] = kept.astype(BF)
+
         if last:
-            result_move(i).start()
-        return carry
-
-    lax.fori_loop(0, count // heads, body, 0)
+            source = out_ref.at[:, start * HD : (start + heads) * HD]
+            move = hand_over(source, first + start, heads, len(befores) + start // heads)
+            move.start()
+            moves.append(move)
+
+    for start in range(0, count, heads):
+        part(start)
     for move in moves:
         move.wait()
-    if last:
-        for i in range(count // heads):
-            result_move(i).wait()
 
 
 def exact_block(q_head, out_head, heads, host, own_len, kv, q_ref, k_ref, v_ref, keys, vaug, out_ref):
@@ -309,16 +334,16 @@
         query = q_ref[at, lanes(q_head + h, HD)]
         row_ids = lax.broadcasted_iota(jnp.int32, (tile, slab), 0) + r * tile
         key_ids = lax.broadcasted_iota(jnp.int32, (tile, slab), 1)
-        own = dot_t(query, k_ref[:, lanes(kv, HD)]) * SCALE2
+        own = dot_t(query, k_ref[:, kv * HD : (kv + 1) * HD]) * SCALE2
         own = jnp.where((key_ids <= row_ids) & (key_ids < own_len), own, MASKED)
-        far = dot_t(query, keys[:, lanes(kv, HD)]) * SCALE2
+        far = dot_t(query, keys[...]) * SCALE2
         far = jnp.where(host > 0, far, MASKED)
         peak = jnp.maximum(jnp.max(own, 1, keepdims=True), jnp.max(far, 1, keepdims=True))
         own = jnp.exp2(own - peak)
         far = jnp.where(host > 0, jnp.exp2(far - peak), 0.0)
         sums = jnp.sum(own, 1, keepdims=True) + jnp.sum(far, 1, keepdims=True)
-        values = jnp.where(host > 0, vaug[:, lanes(2 * kv, HD)].astype(F32), 0.0).astype(BF)
-        total = dot(own.astype(BF), v_ref[:, lanes(kv, HD)]) + dot(far.astype(BF), values)
+        values = jnp.where(host > 0, vaug[:, :HD].astype(F32), 0.0).astype(BF)
+        total = dot(own.astype(BF), v_ref[:, kv * HD : (kv + 1) * HD]) + dot(far.astype(BF), values)
         live = row_ids[:, :1] < own_len
         out_ref[at, lanes(out_head + h, HD)] = jnp.where(live, total / sums, 0.0).astype(BF)
         return carry
@@ -330,14 +355,13 @@
     slab, width = ctx_q.shape
     work = count * slab * slab
     last = befores is not None
-    heads = min(2, count)
     earlier = list(befores.values()) if last else []
     places = tuple((at, x.shape[1] // HD) for at, x in befores.items()) if last else ()
     results = jax.ShapeDtypeStruct((slab, count * HD), BF)
-    scratch = [pltpu.VMEM((slab, own_k.shape[1]), BF), pltpu.VMEM((slab, 2 * own_k.shape[1]), BF)]
+    scratch = [pltpu.VMEM((slab, HD), BF), pltpu.VMEM((slab, 2 * HD), BF)]
     if last:
         scratch = [pltpu.VMEM(results.shape, BF)] + scratch
-        scratch += [pltpu.SemaphoreType.DMA((len(earlier) + count // heads,))]
+        scratch += [pltpu.SemaphoreType.DMA((len(earlier) + count,))]
         results = jax.ShapeDtypeStruct((slab, width), BF)
     return pl.pallas_call(
         functools.partial(anchor_kernel, first, count, base, per_kv, last, places),
@@ -369,8 +393,9 @@
     keep_ref, send_ref, q_all = rest[-3:]
     slab, columns = k_ref.shape
     width = per_kv * columns
-    quarter = known_ref.shape[0] // 2
-    query_count = 4 * quarter
+    query_count = 8 * q_rows
+    block = 2 * q_rows
+    quarter = block * width // HD
     host = lax.axis_index("hst")
     own_len = lengths_ref[host]
     rows = per_kv * query_count
@@ -379,9 +404,12 @@
 
     def place(lower, upper, spread_out):
         middle = (2, 1) if spread_out else (1, 2)
-        for ref, (one, two) in ((lower, (0, middle[0])), (upper, (middle[1], 3))):
-            q_all[one * quarter : (one + 1) * quarter, :] = ref[:quarter, :]
-            q_all[two * quarter : (two + 1) * quarter, :] = ref[quarter:, :]
+        for ref, chips in ((lower, (0, middle[0])), (upper, (middle[1], 3))):
+            for n, chip in enumerate(chips):
+                for h in range(width // HD):
+                    at = slab + n * quarter + h * block
+                    to = h * query_count + chip * block
+                    q_all[to : to + block, :] = ref[at : at + block, :]
 
     for is_low, is_odd in ((False, False), (False, True), (True, False), (True, True)):
         @pl.when((low == is_low) & (odd == is_odd))
@@ -400,8 +428,7 @@
     pad = jnp.zeros((HD - q_rows, HD), F32)
     for j in range(columns // HD):
         cols = slice(j * HD, (j + 1) * HD)
-        parts = [q_all[:, (j * per_kv + h) * HD : (j * per_kv + h + 1) * HD] for h in range(per_kv)]
-        queries = jnp.concatenate(parts, 0)
+        queries = q_all[j * rows : (j + 1) * rows, :]
         self_keys = jnp.concatenate([selves_kv[0][:, cols], pad], 0).astype(BF)
         self_values = jnp.concatenate([selves_kv[1][:, cols], pad], 0).astype(BF)
         near = dot_t(queries, k_ref[:, cols]) * SCALE2
@@ -434,14 +461,14 @@
 def source_part(lengths, own_k, own_v, query_kv, known, landed, q_rows, per_kv, after=()):
     slab, columns = own_k.shape
     width = per_kv * columns
-    count = 2 * known.shape[0]
+    count = 8 * q_rows
     work = count * (width // HD) * slab
     return pl.pallas_call(
         functools.partial(source_kernel, per_kv, q_rows, H // KVH),
         out_shape=[jax.ShapeDtypeStruct((count, (per_kv + 3) * HD), BF)] * 2,
         in_specs=[SMEM] + [VMEM] * 5 + [ANY] * len(after),
         out_specs=[VMEM] * 2,
-        scratch_shapes=[pltpu.VMEM((count, width), BF)],
+        scratch_shapes=[pltpu.VMEM((count * width // HD, HD), BF)],
         compiler_params=params(),
         cost_estimate=pl.CostEstimate(flops=work * HD * 8, bytes_accessed=2**21, transcendentals=work),
         name="query_source",
@@ -563,10 +590,15 @@
         k, v = spread(jnp.stack([own_k, own_v]), "hst", 0)
         anchor = jnp.where(host % 2 == 0, k, v), jnp.where(host % 2 == 0, v, k)
         state = own_part(ctx_q, own_k, own_v, 0, local_heads, per_kv)
-        context_out = anchor_part(
-            lengths, ctx_q, state, 0, own_k, own_v, anchor, 0, local_heads, per_kv, {}
-        )
-        return context_out, query_out
+        results = {}
+        for first in range(0, local_heads, per_kv):
+            cols = slice(first // per_kv * HD, (first // per_kv + 1) * HD)
+            last = first + per_kv == local_heads
+            results[first] = anchor_part(
+                lengths, ctx_q, state, 0, own_k, own_v, [x[:, cols] for x in anchor],
+                first, per_kv, per_kv, dict(results) if last else None,
+            )
+        return results[first], query_out
 
     states = {}
 
@@ -576,58 +608,64 @@
 
     along = ((2, 4), (4, 2))
 
+    def source_first(h):
+        return h < 2
+
+    def done_early(h):
+        return (h <= 2) | (h == 5)
+
     def near_low(h):
         return jnp.where(bit(h, 0) == 1, bit(h, 2), bit(h, 1)) == 0
 
-    landed = swap(query_q, "hst", hosts, 1, 1)
+    query_landed = swap(query_q, "hst", hosts, 1, 1)
     own_k, own_v = pick(ctx_kv, kv_local, local_heads)
-    value_landed = swap(own_v, "hst", hosts, 1, 1)
-    queries = join(lambda h: bit(h, 0) == 0, query_q, landed, (own_v,))
-    landed = swap(queries, "hst", hosts, *along[0])
-    done = own(0, 2, (queries,))
-    held = relay(lambda h: bit(h, 0) == 0, own_k, value_landed, (done,))
-    held_landed = swap(held, "hst", hosts, *along[0])
-    done = own(2, 2, (held,))
-    queries = join(near_low, queries, landed, (done,))
-    landed = swap(queries, "hst", hosts, *along[1])
-    done = own(4, 4, (queries,))
-    keep, send = source_part(lengths, own_k, own_v, query_kv, queries, landed, q_rows, per_kv, (done,))
+    landed = swap(own_v, "hst", hosts, 1, 1)
+    done = own(0, 2)
+    one, two = first_payloads(own_k, landed, query_q, query_landed, (done,))
+    one_landed = swap(one, "hst", hosts, *along[0])
+    two_landed = swap(two, "hst", hosts, *along[0])
+    done = own(2, 6, (one,))
+    one = relay(source_first, one, one_landed, slab, near_low, (done,))
+    one_landed = swap(one, "hst", hosts, *along[1])
+    done = own(8, 8, (one,))
+    two = relay(source_first, two, two_landed, slab, None, (done,))
+    two_landed = swap(two, "hst", hosts, *along[1])
+    held = relay(done_early, one, one_landed, slab, None, (two,))
+    anchor = held, swap(held, "hst", hosts, 1, 1)
+    keep, send = source_part(lengths, own_k, own_v, query_kv, one, one_landed, q_rows, per_kv, (held,))
     landed = swap(send, "hst", hosts, 1, 1)
-    done = own(8, 2, (keep,))
-    held = relay(lambda h: h < 2, held, held_landed, (done,))
-    held_landed = swap(held, "hst", hosts, *along[1])
-    source = merge_part(keep, landed, False, (held,))
-    landed = swap(source, "hst", hosts, *along[0])
-    done = own(10, 6, (source,))
-    source = merge_part(source, landed, False, (done,))
-    landed = swap(source, "hst", hosts, *along[1])
-    held = relay(lambda h: (h <= 2) | (h == 5), held, held_landed, (source,))
-    other = swap(held, "hst", hosts, 1, 1)
     results = {}
 
     def anchors(first, count, after, last=False):
         base = max(x for x in states if x <= first)
         results[first] = anchor_part(
-            lengths, ctx_q, states[base], base, own_k, own_v, (held, other),
+            lengths, ctx_q, states[base], base, own_k, own_v, anchor,
             first, count, per_kv, dict(results) if last else None, after,
         )
         return results[first]
 
-    done = anchors(0, 2, (held,))
-    done = anchors(2, 2, (done,))
+    done = anchors(0, 2, (keep,))
+    source = merge_part(keep, landed, False, (done,))
+    landed = swap(source, "hst", hosts, *along[0])
+    done = anchors(2, 3, (source,))
+    source = merge_part(source, landed, False, (done,))
+    landed = swap(source, "hst", hosts, *along[1])
+    held = relay(done_early, two, two_landed, slab, None, (source,))
+    other = swap(held, "hst", hosts, 1, 1)
+    done = anchors(5, 3, (held,))
+    anchor = held, other
     source = merge_part(source, landed, True, (done,))
     landed = swap(source, "hst", hosts, 1, 1)
-    done = anchors(4, 2, (source,))
+    done = anchors(8, 1, (source,))
     terms = project_part(source, landed, out_weight, (done,))
-    shares = [(10, 6, True), (8, 2, False), (6, 2, False)]
+    shares = [(12, 4, True), (9, 3, False)]
     step = 1
     while step < groups:
         landed = swap(terms, "tp", groups, step, step)
-        while shares:
+        last = False
+        if shares:
             first, count, last = shares.pop()
-            done = anchors(first, count, (terms, done), last)
-            if last or (first == 8 and step == 1):
-                break
+            done = anchors(first, count, (terms,), last)
         terms = add_part(terms, landed, () if last else (done,))
         step *= 2
     for first, count, last in reversed(shares):

time: 120 us -> 111 us (0.925)
  the two profiles are of different devices: /device:TPU:2 before, /device:TPU:6 now
where the time goes in v4:
time: 111 us; the launch traced here: 110 us
  Pallas kernels  92.9 us (84%)
  starting transfers between devices  9.84 us (9%)
  waiting for transfers between devices  5.99 us (5%)
    pallas_call x6, Pallas kernels, anchor_part(): pl.pallas_call(functools.partial(anchor_kernel, first, count, base, per_k...  78.1 us
    ppermute x14, starting transfers between devices, swap(): lax.ppermute(value, axis, [(i, i ^ (odd if i & 1 else even)) for i in ran...  9.84 us
    pallas_call x3, Pallas kernels, own_part(): pl.pallas_call(functools.partial(own_kernel, first, count, per_kv), out_s...  8.19 us
    ppermute x14, waiting for transfers between devices, swap(): lax.ppermute(value, axis, [(i, i ^ (odd if i & 1 else even)) for i in ran...  5.99 us
    pallas_call x1, Pallas kernels, source_part(): pl.pallas_call(functools.partial(source_kernel, per_kv, q_rows, H // KVH)...  2.86 us
  transfers between devices with their start and end apart: 14, of which 4 were waited for; matrix products, arithmetic and copies ran while one was open for 0% of the time, Pallas kernels for 82%

profile of v4, /device:TPU:6, one launch (start us, length us, event | category | flops | bytes accessed | tf_op | source)
XLA Modules:
  0.0 109.9 jit_solution(10093296241640739382)
XLA Ops:
  0.6 1.3 %pick_columns.1 = (bf16[768,256]{1,0:T(8,128)(2,1)S(1)}, bf16[768,256]{1,0:T(8,128)(2,1)S(1)}) custom-call(bf16[2,768,1024]{2,1,0:T(8,128)(2,1)} %kv_ref.1), custom_call_target="tpu_custom_call" | custom-call | tf_op jit(solution)/shard_map/pick_columns/pallas_call | solution.py:60
  2.0 0.5 collective-permute-start.1
  2.5 0.2 copy-done
  2.8 1.1 %context_own.3.rest_0_.refs_2_ = f32[768,512]{1,0:T(8,128)S(1)} custom-call(bf16[768,2048]{1,0:T(8,128)(2,1)S(1)} %copy-done, bf16[768,256]{1,0:T(8,128)(2,1)S(1)} %get-tuple-element.8.k_ref.refs_3_, bf16[768,256]{1,0:T(8,128)(2,1)S(1)} %get-tuple-element.9.v_ref.refs_4_), custom_call_target="tpu_custom_call" | custom-call | flops 805306368 | bytes 1179648 | tf_op jit(solution)/shard_map/context_own/pallas_call | solution.py:219
  3.9 0.1 collective-permute-done.1.landed_ref
  4.1 0.6 collective-permute-start.2
  4.7 3.1 %context_own.4.rest_0_.refs_2_ = f32[768,1536]{1,0:T(8,128)S(1)} custom-call(bf16[768,2048]{1,0:T(8,128)(2,1)S(1)} %copy-done, bf16[768,256]{1,0:T(8,128)(2,1)S(1)} %get-tuple-element.8.k_ref.refs_3_, bf16[768,256]{1,0:T(8,128)(2,1)S(1)} %get-tuple-element.9.v_ref.refs_4_, bf16[1024,128]{1,0:T(8,128)(2,1)S(1)} %get-tuple-element.10.rest_0_.one_ref), custom_call_target="tpu_custom_call" | custom-call | flops 2415919104 | bytes 3538944 | tf_op jit(solution)/shard_map/context_own/pallas_call | solution.py:219
  7.8 2.7 %collective-permute-done.2.two_ref = bf16[1024,128]{1,0:T(8,128)(2,1)S(1)} collective-permute-done((bf16[1024,128]{1,0:T(8,128)(2,1)S(1)}, bf16[1024,128]{1,0:T(8,128)(2,1)S(1)}, u32[]{:S(2)}, u32[]{:S(2)}) %collective-permute-start.2) | collective-permute-done | bytes 262176 | tf_op jit(solution)/shard_map/ppermute | solution.py:43
  10.6 0.6 collective-permute-start.5
  11.2 0.1 collective-permute-start.3
  11.3 4.0 %context_own.5.rest_0_.refs_2_ = f32[768,2048]{1,0:T(8,128)S(1)} custom-call(bf16[768,2048]{1,0:T(8,128)(2,1)S(1)} %copy-done, bf16[768,256]{1,0:T(8,128)(2,1)S(1)} %get-tuple-element.8.k_ref.refs_3_, bf16[768,256]{1,0:T(8,128)(2,1)S(1)} %get-tuple-element.9.v_ref.refs_4_, bf16[1280,128]{1,0:T(8,128)(2,1)S(1)} %payload_relay.4.rest_0_.one_ref.known_ref), custom_call_target="tpu_custom_call" | custom-call | flops 3221225472 | bytes 4718592 | tf_op jit(solution)/shard_map/context_own/pallas_call | solution.py:219
  15.2 2.9 %collective-permute-done.3.two_ref = bf16[768,128]{1,0:T(8,128)(2,1)S(1)} collective-permute-done((bf16[768,128]{1,0:T(8,128)(2,1)S(1)}, bf16[768,128]{1,0:T(8,128)(2,1)S(1)}, u32[]{:S(2)}, u32[]{:S(2)}) %collective-permute-start.3) | collective-permute-done | bytes 196640 | tf_op jit(solution)/shard_map/ppermute | solution.py:43
  18.2 0.2 collective-permute-done.5.two_ref.landed_ref
  18.5 2.9 %query_source.1 = (bf16[64,1408]{1,0:T(8,128)(2,1)S(1)}, bf16[64,1408]{1,0:T(8,128)(2,1)S(1)}) custom-call(s32[8]{0:T(128)S(1)} %copy-done.3, bf16[768,256]{1,0:T(8,128)(2,1)S(1)} %get-tuple-element.8.k_ref.refs_3_, bf16[768,256]{1,0:T(8,128)(2,1)S(1)} %get-tuple-element.9.v_ref.refs_4_, bf16[2,8,1024]{2,1,0:T(8,128)(2,1)S(1)} %copy-done.4, ...), custom_call_target="tpu_custom_call" | custom-call | flops 805306368 | bytes 2097152 | tf_op jit(solution)/shard_map/query_source/pallas_call | solution.py:466
  21.4 0.5 collective-permute-start.6
  21.9 0.3 collective-permute-start.4
  22.3 9.8 %context_anchor.6.rest_0_.refs_7_ = bf16[768,256]{1,0:T(8,128)(2,1)S(1)} custom-call(s32[8]{0:T(128)S(1)} %copy-done.3, bf16[768,2048]{1,0:T(8,128)(2,1)S(1)} %copy-done, f32[768,512]{1,0:T(8,128)S(1)} %context_own.3.rest_0_.refs_2_, bf16[768,256]{1,0:T(8,128)(2,1)S(1)} %get-tuple-element.8.k_ref.refs_3_, ...), custom_call_target="tpu_custom_call" | custom-call | flops 1207959552 | bytes 1572864 | tf_op jit(solution)/shard_map/context_anchor/pallas_call | solution.py:366
  32.0 0.2 query_merge.3.refs_7_.one_ref
  32.3 1.6 %collective-permute-start.8 = (bf16[64,1408]{1,0:T(8,128)(2,1)S(1)}, bf16[64,1408]{1,0:T(8,128)(2,1)S(1)}, u32[]{:S(2)}, u32[]{:S(2)}) collective-permute-start(bf16[64,1408]{1,0:T(8,128)(2,1)S(1)} %query_merge.3.refs_7_.one_ref), channel_id=1, source_target_pairs={{0,8},{4,20},{8,0},{12,28},{16,24},{20,4},{24,16},{28,12},{1,9},{5... | collective-permute-start | bytes 540680 | tf_op jit(solution)/shard_map/ppermute | solution.py:43
  33.9 14.4 %context_anchor.7.rest_0_.refs_8_ = bf16[768,384]{1,0:T(8,128)(2,1)S(1)} custom-call(s32[8]{0:T(128)S(1)} %copy-done.3, bf16[768,2048]{1,0:T(8,128)(2,1)S(1)} %copy-done, f32[768,1536]{1,0:T(8,128)S(1)} %context_own.4.rest_0_.refs_2_, bf16[768,256]{1,0:T(8,128)(2,1)S(1)} %get-tuple-element.8.k_ref.refs_3_, ...), custom_call_target="tpu_custom_call" | custom-call | flops 1811939328 | bytes 2359296 | tf_op jit(solution)/shard_map/context_anchor/pallas_call | solution.py:366
  48.3 0.2 query_merge.4.rest_0_.one_ref
  48.6 0.5 collective-permute-start.10
  49.2 14.2 %context_anchor.8.rest_0_.refs_9_ = bf16[768,384]{1,0:T(8,128)(2,1)S(1)} custom-call(s32[8]{0:T(128)S(1)} %copy-done.3, bf16[768,2048]{1,0:T(8,128)(2,1)S(1)} %copy-done, f32[768,1536]{1,0:T(8,128)S(1)} %context_own.4.rest_0_.refs_2_, bf16[768,256]{1,0:T(8,128)(2,1)S(1)} %get-tuple-element.8.k_ref.refs_3_, ...), custom_call_target="tpu_custom_call" | custom-call | flops 1811939328 | bytes 2359296 | tf_op jit(solution)/shard_map/context_anchor/pallas_call | solution.py:366
  63.4 0.2 query_merge.5.refs_7_.own_ref
  63.7 0.6 collective-permute-start.11
  64.3 5.4 %context_anchor.9.rest_0_.refs_10_ = bf16[768,128]{1,0:T(8,128)(2,1)S(1)} custom-call(s32[8]{0:T(128)S(1)} %copy-done.3, bf16[768,2048]{1,0:T(8,128)(2,1)S(1)} %copy-done, f32[768,2048]{1,0:T(8,128)S(1)} %context_own.5.rest_0_.refs_2_, bf16[768,256]{1,0:T(8,128)(2,1)S(1)} %get-tuple-element.8.k_ref.refs_3_, ...), custom_call_target="tpu_custom_call" | custom-call | flops 603979776 | bytes 786432 | tf_op jit(solution)/shard_map/context_anchor/pallas_call | solution.py:366
  69.7 0.9 query_project.1.refs_7_.one_ref
  70.6 1.6 %collective-permute-start.12 = (bf16[64,1024]{1,0:T(8,128)(2,1)S(1)}, bf16[64,1024]{1,0:T(8,128)(2,1)S(1)}, u32[]{:S(2)}, u32[]{:S(2)}) collective-permute-start(bf16[64,1024]{1,0:T(8,128)(2,1)S(1)} %query_project.1.refs_7_.one_ref), channel_id=1, source_target_pairs={{0,1},{1,0},{2,3},{3,2},{4,5},{5,4},{6,7},{7,6},{8,9},{9,8},{10,11... | collective-permute-start | bytes 393224 | tf_op jit(solution)/shard_map/ppermute | solution.py:43
  72.2 14.5 %context_anchor.10.rest_0_.refs_11_ = bf16[768,384]{1,0:T(8,128)(2,1)S(1)} custom-call(s32[8]{0:T(128)S(1)} %copy-done.3, bf16[768,2048]{1,0:T(8,128)(2,1)S(1)} %copy-done, f32[768,2048]{1,0:T(8,128)S(1)} %context_own.5.rest_0_.refs_2_, bf16[768,256]{1,0:T(8,128)(2,1)S(1)} %get-tuple-element.8.k_ref.refs_3_, ...), custom_call_target="tpu_custom_call" | custom-call | flops 1811939328 | bytes 2359296 | tf_op jit(solution)/shard_map/context_anchor/pallas_call | solution.py:366
  86.8 2.7 %collective-permute-start.13 = (bf16[64,1024]{1,0:T(8,128)(2,1)S(1)}, bf16[64,1024]{1,0:T(8,128)(2,1)S(1)}, u32[]{:S(2)}, u32[]{:S(2)}) collective-permute-start(bf16[64,1024]{1,0:T(8,128)(2,1)S(1)} %query_sum.2.refs_12_.one_ref), channel_id=1, source_target_pairs={{0,2},{1,3},{2,0},{3,1},{4,6},{5,7},{6,4},{7,5},{8,10},{9,11},{10,... | collective-permute-start | bytes 393224 | tf_op jit(solution)/shard_map/ppermute | solution.py:43
  89.4 19.8 %context_anchor.11 = bf16[768,2048]{1,0:T(8,128)(2,1)} custom-call(s32[8]{0:T(128)S(1)} %copy-done.3, bf16[768,2048]{1,0:T(8,128)(2,1)S(1)} %copy-done, f32[768,2048]{1,0:T(8,128)S(1)} %context_own.5.rest_0_.refs_2_, bf16[768,256]{1,0:T(8,128)(2,1)S(1)} %get-tuple-element.8.k_ref.refs_3_, bf16[768,256]{1,0:T(8,128)(2,1)S(1)} %get-tuple-element.9.v_ref.refs_4_, ...), custom_call_target="tpu_custom_call" | custom-call | flops 2415919104 | bytes 3145728 | tf_op jit(solution)/shard_map/context_anchor/pallas_call | solution.py:366
  109.2 0.7 query_sum.3
  (28 shorter events, 0.5 us)
Async XLA Ops:
  0.6 2.1 %copy-start = (bf16[768,2048]{1,0:T(8,128)(2,1)S(1)}, bf16[768,2048]{1,0:T(8,128)(2,1)}, u32[]{:S(2)}) copy-start(bf16[768,2048]{1,0:T(8,128)(2,1)} %refs_1_.11) | copy-start | bytes 9437188
  1.9 2.1 %copy-start.2 = (bf16[8,2048]{1,0:T(8,128)(2,1)S(1)}, bf16[8,2048]{1,0:T(8,128)(2,1)}, u32[]{:S(2)}) copy-start(bf16[8,2048]{1,0:T(8,128)(2,1)} %own_ref.1) | copy-start | bytes 98308
  2.0 2.0 %collective-permute-start = (bf16[768,256]{1,0:T(8,128)(2,1)S(1)}, bf16[768,256]{1,0:T(8,128)(2,1)S(1)}, u32[]{:S(2)}, u32[]{:S(2)}) collective-permute-start(bf16[768,256]{1,0:T(8,128)(2,1)S(1)} %get-tuple-element.9.v_ref.refs_4_), channel_id=1, source_target_pairs={{0,4},{4,0},{8,12},{12,8},{16,20},{20,16},{24,28},{28,24},{1,5},{5... | collective-permute-start | bytes 1179656 | tf_op jit(solution)/shard_map/ppermute | solution.py:43
  2.0 2.0 %collective-permute-start.1 = (bf16[8,2048]{1,0:T(8,128)(2,1)}, bf16[8,2048]{1,0:T(8,128)(2,1)S(1)}, u32[]{:S(2)}, u32[]{:S(2)}) collective-permute-start(bf16[8,2048]{1,0:T(8,128)(2,1)} %own_ref.1), channel_id=1, source_target_pairs={{0,4},{4,0},{8,12},{12,8},{16,20},{20,16},{24,28},{28,24},{1,5},{5... | collective-permute-start | bytes 98312 | tf_op jit(solution)/shard_map/ppermute | solution.py:43
  4.1 6.4 %collective-permute-start.2 = (bf16[1024,128]{1,0:T(8,128)(2,1)S(1)}, bf16[1024,128]{1,0:T(8,128)(2,1)S(1)}, u32[]{:S(2)}, u32[]{:S(2)}) collective-permute-start(bf16[1024,128]{1,0:T(8,128)(2,1)S(1)} %get-tuple-element.10.rest_0_.one_ref), channel_id=1, source_target_pairs={{0,8},{4,20},{8,0},{12,28},{16,24},{20,4},{24,16},{28,12},{1,9},{5... | collective-permute-start | bytes 786440 | tf_op jit(solution)/shard_map/ppermute | solution.py:43
  10.6 7.8 %collective-permute-start.5 = (bf16[1280,128]{1,0:T(8,128)(2,1)S(1)}, bf16[1280,128]{1,0:T(8,128)(2,1)S(1)}, u32[]{:S(2)}, u32[]{:S(2)}) collective-permute-start(bf16[1280,128]{1,0:T(8,128)(2,1)S(1)} %payload_relay.4.rest_0_.one_ref.known_ref), channel_id=1, source_target_pairs={{0,16},{4,12},{8,24},{12,4},{16,0},{20,28},{24,8},{28,20},{1,17},{... | collective-permute-start | bytes 983048 | tf_op jit(solution)/shard_map/ppermute | solution.py:43
  11.2 7.0 %collective-permute-start.3 = (bf16[768,128]{1,0:T(8,128)(2,1)S(1)}, bf16[768,128]{1,0:T(8,128)(2,1)S(1)}, u32[]{:S(2)}, u32[]{:S(2)}) collective-permute-start(bf16[768,128]{1,0:T(8,128)(2,1)S(1)} %get-tuple-element.11.one_ref), channel_id=1, source_target_pairs={{0,8},{4,20},{8,0},{12,28},{16,24},{20,4},{24,16},{28,12},{1,9},{5... | collective-permute-start | bytes 589832 | tf_op jit(solution)/shard_map/ppermute | solution.py:43
  15.2 3.3 %copy-start.3 = (s32[8]{0:T(128)S(1)}, s32[8]{0:T(128)}, u32[]{:S(2)}) copy-start(s32[8]{0:T(128)} %refs_0_.11) | copy-start | bytes 100
  15.2 3.3 %copy-start.4 = (bf16[2,8,1024]{2,1,0:T(8,128)(2,1)S(1)}, bf16[2,8,1024]{2,1,0:T(8,128)(2,1)}, u32[]{:S(2)}) copy-start(bf16[2,8,1024]{2,1,0:T(8,128)(2,1)} %self_ref.1) | copy-start | bytes 98308
  18.4 3.8 %collective-permute-start.7 = (bf16[768,128]{1,0:T(8,128)(2,1)S(1)}, bf16[768,128]{1,0:T(8,128)(2,1)S(1)}, u32[]{:S(2)}, u32[]{:S(2)}) collective-permute-start(bf16[768,128]{1,0:T(8,128)(2,1)S(1)} %payload_relay.6.rest_0_.refs_5_), channel_id=1, source_target_pairs={{0,4},{4,0},{8,12},{12,8},{16,20},{20,16},{24,28},{28,24},{1,5},{5... | collective-permute-start | bytes 589832 | tf_op jit(solution)/shard_map/ppermute | solution.py:43
  21.4 10.7 %collective-permute-start.6 = (bf16[64,1408]{1,0:T(8,128)(2,1)S(1)}, bf16[64,1408]{1,0:T(8,128)(2,1)S(1)}, u32[]{:S(2)}, u32[]{:S(2)}) collective-permute-start(bf16[64,1408]{1,0:T(8,128)(2,1)S(1)} %get-tuple-element.13), channel_id=1, source_target_pairs={{0,4},{4,0},{8,12},{12,8},{16,20},{20,16},{24,28},{28,24},{1,5},{5... | collective-permute-start | bytes 540680 | tf_op jit(solution)/shard_map/ppermute | solution.py:43
  21.9 27.2 %collective-permute-start.4 = (bf16[768,128]{1,0:T(8,128)(2,1)S(1)}, bf16[768,128]{1,0:T(8,128)(2,1)S(1)}, u32[]{:S(2)}, u32[]{:S(2)}) collective-permute-start(bf16[768,128]{1,0:T(8,128)(2,1)S(1)} %payload_relay.5.rest_0_.one_ref), channel_id=1, source_target_pairs={{0,16},{4,12},{8,24},{12,4},{16,0},{20,28},{24,8},{28,20},{1,17},{... | collective-permute-start | bytes 589832 | tf_op jit(solution)/shard_map/ppermute | solution.py:43
  32.3 16.0 %collective-permute-start.8 = (bf16[64,1408]{1,0:T(8,128)(2,1)S(1)}, bf16[64,1408]{1,0:T(8,128)(2,1)S(1)}, u32[]{:S(2)}, u32[]{:S(2)}) collective-permute-start(bf16[64,1408]{1,0:T(8,128)(2,1)S(1)} %query_merge.3.refs_7_.one_ref), channel_id=1, source_target_pairs={{0,8},{4,20},{8,0},{12,28},{16,24},{20,4},{24,16},{28,12},{1,9},{5... | collective-permute-start | bytes 540680 | tf_op jit(solution)/shard_map/ppermute | solution.py:43
  48.6 14.9 %collective-permute-start.10 = (bf16[64,1408]{1,0:T(8,128)(2,1)S(1)}, bf16[64,1408]{1,0:T(8,128)(2,1)S(1)}, u32[]{:S(2)}, u32[]{:S(2)}) collective-permute-start(bf16[64,1408]{1,0:T(8,128)(2,1)S(1)} %query_merge.4.rest_0_.one_ref), channel_id=1, source_target_pairs={{0,16},{4,12},{8,24},{12,4},{16,0},{20,28},{24,8},{28,20},{1,17},{... | collective-permute-start | bytes 540680 | tf_op jit(solution)/shard_map/ppermute | solution.py:43
  49.1 15.1 %collective-permute-start.9 = (bf16[768,128]{1,0:T(8,128)(2,1)S(1)}, bf16[768,128]{1,0:T(8,128)(2,1)S(1)}, u32[]{:S(2)}, u32[]{:S(2)}) collective-permute-start(bf16[768,128]{1,0:T(8,128)(2,1)S(1)} %payload_relay.7.refs_7_.refs_5_), channel_id=1, source_target_pairs={{0,4},{4,0},{8,12},{12,8},{16,20},{20,16},{24,28},{28,24},{1,5},{5... | collective-permute-start | bytes 589832 | tf_op jit(solution)/shard_map/ppermute | solution.py:43
  63.7 6.0 %copy-start.1 = (bf16[2048,1024]{1,0:T(8,128)(2,1)S(1)}, bf16[2048,1024]{1,0:T(8,128)(2,1)}, u32[]{:S(2)}) copy-start(bf16[2048,1024]{1,0:T(8,128)(2,1)} %w_ref.1) | copy-start | bytes 12582916
  63.7 6.0 %collective-permute-start.11 = (bf16[64,1024]{1,0:T(8,128)(2,1)S(1)}, bf16[64,1024]{1,0:T(8,128)(2,1)S(1)}, u32[]{:S(2)}, u32[]{:S(2)}) collective-permute-start(bf16[64,1024]{1,0:T(8,128)(2,1)S(1)} %query_merge.5.refs_7_.own_ref), channel_id=1, source_target_pairs={{0,4},{4,0},{8,12},{12,8},{16,20},{20,16},{24,28},{28,24},{1,5},{5... | collective-permute-start | bytes 393224 | tf_op jit(solution)/shard_map/ppermute | solution.py:43
  70.6 16.1 %collective-permute-start.12 = (bf16[64,1024]{1,0:T(8,128)(2,1)S(1)}, bf16[64,1024]{1,0:T(8,128)(2,1)S(1)}, u32[]{:S(2)}, u32[]{:S(2)}) collective-permute-start(bf16[64,1024]{1,0:T(8,128)(2,1)S(1)} %query_project.1.refs_7_.one_ref), channel_id=1, source_target_pairs={{0,1},{1,0},{2,3},{3,2},{4,5},{5,4},{6,7},{7,6},{8,9},{9,8},{10,11... | collective-permute-start | bytes 393224 | tf_op jit(solution)/shard_map/ppermute | solution.py:43
  86.8 22.5 %collective-permute-start.13 = (bf16[64,1024]{1,0:T(8,128)(2,1)S(1)}, bf16[64,1024]{1,0:T(8,128)(2,1)S(1)}, u32[]{:S(2)}, u32[]{:S(2)}) collective-permute-start(bf16[64,1024]{1,0:T(8,128)(2,1)S(1)} %query_sum.2.refs_12_.one_ref), channel_id=1, source_target_pairs={{0,2},{1,3},{2,0},{3,1},{4,6},{5,7},{6,4},{7,5},{8,10},{9,11},{10,... | collective-permute-start | bytes 393224 | tf_op jit(solution)/shard_map/ppermute | solution.py:43

commit v5 on v4

--- a/solution.py
+++ b/solution.py
@@ -95,52 +95,35 @@
     return run
 
 
-def first_payloads(own_k, value_landed, query_q, query_landed, after):
-    slab, columns = own_k.shape
-    q_rows, width = query_q.shape
-
-    def kernel(k_ref, v_ref, own_ref, landed_ref, *rest):
-        out_refs = rest[-(columns // HD) :]
-        even = bit(lax.axis_index("hst"), 0) == 0
-        for j, out_ref in enumerate(out_refs):
-            cols = slice(j * HD, (j + 1) * HD)
-            choose(even, take_rows(out_ref, k_ref, slab, cols), take_rows(out_ref, v_ref, slab, cols))
+def join(low_of, known, landed, after=()):
+    rows, width = known.shape
+
+    def kernel(known_ref, landed_ref, *rest):
+        out_ref = rest[-1]
 
         def put(first, second):
             def run():
-                both = jnp.concatenate([first[...].astype(F32), second[...].astype(F32)], 0).astype(BF)
-                for h in range(width // HD):
-                    at = slab + 2 * q_rows * h
-                    out_refs[0][at : at + 2 * q_rows, :] = both[:, h * HD : (h + 1) * HD]
+                both = jnp.concatenate([first[...].astype(F32), second[...].astype(F32)], 0)
+                out_ref[...] = both.astype(BF)
 
             return run
 
-        choose(even, put(own_ref, landed_ref), put(landed_ref, own_ref))
-
-    shapes = [(slab, HD)] * (columns // HD)
-    shapes[0] = (slab + 2 * q_rows * width // HD, HD)
-    return small_call(kernel, "payload_first", shapes, (own_k, value_landed, query_q, query_landed), after)
-
-
-def relay(keep_of, one, two, slab, low_of=None, after=()):
-    rows = one.shape[0] - slab if low_of is not None else 0
+        choose(low_of(lax.axis_index("hst")), put(known_ref, landed_ref), put(landed_ref, known_ref))
+
+    return small_call(kernel, "query_join", [(2 * rows, width)], (known, landed), after)[0]
+
+
+def relay(keep_of, one, two, after=(), split=1):
+    slab, columns = one.shape
+    width = columns // split
 
     def kernel(one_ref, two_ref, *rest):
-        out_ref = rest[-1]
-        host = lax.axis_index("hst")
-        choose(keep_of(host), take_rows(out_ref, one_ref, slab), take_rows(out_ref, two_ref, slab))
-
-        def put(first, second):
-            def run():
-                out_ref[slab : slab + rows, :] = first[slab:, :]
-                out_ref[slab + rows :, :] = second[slab:, :]
-
-            return run
-
-        if rows:
-            choose(low_of(host), put(one_ref, two_ref), put(two_ref, one_ref))
-
-    return small_call(kernel, "payload_relay", [(slab + 2 * rows, HD)], (one, two), after)[0]
+        keep = keep_of(lax.axis_index("hst"))
+        for j, out_ref in enumerate(rest[-split:]):
+            cols = slice(j * width, (j + 1) * width)
+            choose(keep, take_rows(out_ref, one_ref, slab, cols), take_rows(out_ref, two_ref, slab, cols))
+
+    return small_call(kernel, "anchor_relay", [(slab, width)] * split, (one, two), after)
 
 
 def add_part(one, two, after=()):
@@ -377,25 +360,31 @@
     )(lengths, ctx_q, state, own_k, own_v, *anchor, *earlier, *after)
 
 
+PART = 16
+
+
 def write_level(ref, width, level):
+    lane = lax.broadcasted_iota(jnp.int32, level.shape, 1)
+    parts = []
     for at in range(3):
-        part = level.astype(BF)
-        ref[:, width + at * HD : width + (at + 1) * HD] = part
-        level = level - part.astype(F32)
+        part = level.astype(BF).astype(F32)
+        parts.append(part if at == 0 else pltpu.roll(part, at * PART, 1))
+        level = level - part
+    packed = jnp.where(lane < PART, parts[0], jnp.where(lane < 2 * PART, parts[1], parts[2]))
+    ref[:, width : width + HD] = packed.astype(BF)
 
 
 def read_level(ref, width):
-    parts = [ref[:, width + i * HD : width + (i + 1) * HD].astype(F32) for i in range(3)]
-    return parts[0] + parts[1] + parts[2]
+    packed = ref[:, width : width + HD].astype(F32)
+    return packed + pltpu.roll(packed, HD - PART, 1) + pltpu.roll(packed, HD - 2 * PART, 1)
 
 
 def source_kernel(per_kv, q_rows, group_size, lengths_ref, k_ref, v_ref, self_ref, known_ref, landed_ref, *rest):
-    keep_ref, send_ref, q_all = rest[-3:]
+    keep_ref, send_ref, q_all, vaug = rest[-4:]
     slab, columns = k_ref.shape
     width = per_kv * columns
     query_count = 8 * q_rows
     block = 2 * q_rows
-    quarter = block * width // HD
     host = lax.axis_index("hst")
     own_len = lengths_ref[host]
     rows = per_kv * query_count
@@ -407,9 +396,8 @@
         for ref, chips in ((lower, (0, middle[0])), (upper, (middle[1], 3))):
             for n, chip in enumerate(chips):
                 for h in range(width // HD):
-                    at = slab + n * quarter + h * block
                     to = h * query_count + chip * block
-                    q_all[to : to + block, :] = ref[at : at + block, :]
+                    q_all[to : to + block, :] = ref[n * block : (n + 1) * block, h * HD : (h + 1) * HD]
 
     for is_low, is_odd in ((False, False), (False, True), (True, False), (True, True)):
         @pl.when((low == is_low) & (odd == is_odd))
@@ -424,24 +412,24 @@
     query_ids = lax.broadcasted_iota(jnp.int32, (query_count, HD), 0)
     self_ok = (host * q_rows + lane <= query_ids) & (lane < q_rows)
     self_ok = jnp.concatenate([self_ok] * per_kv, 0)
-    key_ids = lax.broadcasted_iota(jnp.int32, (rows, slab), 1)
     pad = jnp.zeros((HD - q_rows, HD), F32)
+    key_rows = lax.broadcasted_iota(jnp.int32, (slab, HD), 0)
+    ones = jnp.where(key_rows < own_len, 1.0, 0.0).astype(BF)
     for j in range(columns // HD):
+        values = v_ref[:, j * HD : (j + 1) * HD].astype(F32)
+        vaug[:, 2 * j * HD : (2 * j + 1) * HD] = jnp.where(key_rows < own_len, values, 0.0).astype(BF)
+        vaug[:, (2 * j + 1) * HD : (2 * j + 2) * HD] = ones
+
+    def operands(j):
         cols = slice(j * HD, (j + 1) * HD)
         queries = q_all[j * rows : (j + 1) * rows, :]
         self_keys = jnp.concatenate([selves_kv[0][:, cols], pad], 0).astype(BF)
         self_values = jnp.concatenate([selves_kv[1][:, cols], pad], 0).astype(BF)
         near = dot_t(queries, k_ref[:, cols]) * SCALE2
-        near = jnp.where(key_ids < own_len, near, MASKED)
-        selves = dot_t(queries, self_keys) * SCALE2
-        selves = jnp.where(self_ok, selves, MASKED)
-        peak = jnp.maximum(jnp.max(near, 1, keepdims=True), jnp.max(selves, 1, keepdims=True))
-        near = jnp.exp2(near - peak)
-        selves = jnp.exp2(selves - peak)
-        sums = jnp.sum(near, 1, keepdims=True) + jnp.sum(selves, 1, keepdims=True)
-        total = dot(near.astype(BF), v_ref[:, cols]) + dot(selves.astype(BF), self_values)
-        total = total / sums
-        level = peak + jnp.log2(sums)
+        selves = jnp.where(self_ok, dot_t(queries, self_keys) * SCALE2, MASKED)
+        return near, selves, jnp.concatenate([self_values, jnp.ones((HD, HD), BF)], 1)
+
+    def store(j, total, level):
         stats = jnp.zeros((query_count, HD), F32)
         for h in range(per_kv):
             stats = jnp.where(lane == h, level[h * query_count : (h + 1) * query_count, :], stats)
@@ -456,6 +444,33 @@
             return run
 
         choose(odd if j else jnp.logical_not(odd), put(keep_ref), put(send_ref))
+
+    worst = jnp.ones((rows, HD), F32)
+    found = []
+    for j in range(columns // HD):
+        near, selves, self_values = operands(j)
+        near = jnp.exp2(near).astype(BF)
+        selves = jnp.exp2(selves).astype(BF)
+        total = dot(near, vaug[:, 2 * j * HD : (2 * j + 2) * HD]) + dot(selves, self_values)
+        sums = total[:, HD:]
+        inverse = 1.0 / sums
+        worst = jnp.minimum(worst, jnp.minimum(sums, inverse))
+        found.append((total[:, :HD] * inverse, jnp.log2(sums)))
+    for j, result in enumerate(found):
+        store(j, *result)
+
+    @pl.when(jnp.logical_not(jnp.min(worst) > TINY))
+    def _():
+        key_ids = lax.broadcasted_iota(jnp.int32, (rows, slab), 1)
+        for j in range(columns // HD):
+            near, selves, self_values = operands(j)
+            near = jnp.where(key_ids < own_len, near, MASKED)
+            peak = jnp.maximum(jnp.max(near, 1, keepdims=True), jnp.max(selves, 1, keepdims=True))
+            near = jnp.exp2(near - peak).astype(BF)
+            selves = jnp.exp2(selves - peak).astype(BF)
+            total = dot(near, vaug[:, 2 * j * HD : (2 * j + 2) * HD]) + dot(selves, self_values)
+            sums = total[:, HD:]
+            store(j, total[:, :HD] / sums, peak + jnp.log2(sums))
 
 
 def source_part(lengths, own_k, own_v, query_kv, known, landed, q_rows, per_kv, after=()):
@@ -465,10 +480,10 @@
     work = count * (width // HD) * slab
     return pl.pallas_call(
         functools.partial(source_kernel, per_kv, q_rows, H // KVH),
-        out_shape=[jax.ShapeDtypeStruct((count, (per_kv + 3) * HD), BF)] * 2,
+        out_shape=[jax.ShapeDtypeStruct((count, (per_kv + 1) * HD), BF)] * 2,
         in_specs=[SMEM] + [VMEM] * 5 + [ANY] * len(after),
         out_specs=[VMEM] * 2,
-        scratch_shapes=[pltpu.VMEM((count * width // HD, HD), BF)],
+        scratch_shapes=[pltpu.VMEM((count * width // HD, HD), BF), pltpu.VMEM((slab, 2 * columns), BF)],
         compiler_params=params(),
         cost_estimate=pl.CostEstimate(flops=work * HD * 8, bytes_accessed=2**21, transcendentals=work),
         name="query_source",
@@ -490,7 +505,7 @@
 
 def merge_part(one, two, last, after=()):
     rows, wide = one.shape
-    width = wide - 3 * HD
+    width = wide - HD
 
     def kernel(one_ref, two_ref, *rest):
         out_ref = rest[-1]
@@ -608,6 +623,9 @@
 
     along = ((2, 4), (4, 2))
 
+    def is_even(h):
+        return bit(h, 0) == 0
+
     def source_first(h):
         return h < 2
 
@@ -617,59 +635,65 @@
     def near_low(h):
         return jnp.where(bit(h, 0) == 1, bit(h, 2), bit(h, 1)) == 0
 
-    query_landed = swap(query_q, "hst", hosts, 1, 1)
+    landed = swap(query_q, "hst", hosts, 1, 1)
     own_k, own_v = pick(ctx_kv, kv_local, local_heads)
-    landed = swap(own_v, "hst", hosts, 1, 1)
-    done = own(0, 2)
-    one, two = first_payloads(own_k, landed, query_q, query_landed, (done,))
-    one_landed = swap(one, "hst", hosts, *along[0])
-    two_landed = swap(two, "hst", hosts, *along[0])
-    done = own(2, 6, (one,))
-    one = relay(source_first, one, one_landed, slab, near_low, (done,))
-    one_landed = swap(one, "hst", hosts, *along[1])
-    done = own(8, 8, (one,))
-    two = relay(source_first, two, two_landed, slab, None, (done,))
-    two_landed = swap(two, "hst", hosts, *along[1])
-    held = relay(done_early, one, one_landed, slab, None, (two,))
-    anchor = held, swap(held, "hst", hosts, 1, 1)
-    keep, send = source_part(lengths, own_k, own_v, query_kv, one, one_landed, q_rows, per_kv, (held,))
+    value_landed = swap(own_v, "hst", hosts, 1, 1)
+    queries = join(is_even, query_q, landed, (own_v,))
+    landed = swap(queries, "hst", hosts, *along[0])
+    done = own(0, 2, (queries,))
+    (held,) = relay(is_even, own_k, value_landed, (done,))
+    held_landed = swap(held, "hst", hosts, *along[0])
+    queries = join(near_low, queries, landed, (held,))
+    landed = swap(queries, "hst", hosts, *along[1])
+    done = own(2, 6, (queries,))
+    keep, send = source_part(lengths, own_k, own_v, query_kv, queries, landed, q_rows, per_kv, (done,))
     landed = swap(send, "hst", hosts, 1, 1)
+    done = own(8, 4, (keep,))
+    parts = relay(source_first, held, held_landed, (done,), kv_local)
+    parts_landed = [swap(x, "hst", hosts, *along[1]) for x in parts]
+    source = merge_part(keep, landed, False, (parts[-1],))
+    landed = swap(source, "hst", hosts, *along[0])
+    done = own(12, 4, (source,))
+    anchor = {}
+
+    def complete(kv, after):
+        (held,) = relay(done_early, parts[kv], parts_landed[kv], after)
+        anchor[kv] = held, swap(held, "hst", hosts, 1, 1)
+        return held
+
+    source = merge_part(source, landed, False, (done,))
+    landed = swap(source, "hst", hosts, *along[1])
+    done = complete(0, (source,))
     results = {}
 
     def anchors(first, count, after, last=False):
         base = max(x for x in states if x <= first)
         results[first] = anchor_part(
-            lengths, ctx_q, states[base], base, own_k, own_v, anchor,
+            lengths, ctx_q, states[base], base, own_k, own_v, anchor[first // per_kv],
             first, count, per_kv, dict(results) if last else None, after,
         )
         return results[first]
 
-    done = anchors(0, 2, (keep,))
-    source = merge_part(keep, landed, False, (done,))
-    landed = swap(source, "hst", hosts, *along[0])
-    done = anchors(2, 3, (source,))
-    source = merge_part(source, landed, False, (done,))
-    landed = swap(source, "hst", hosts, *along[1])
-    held = relay(done_early, two, two_landed, slab, None, (source,))
-    other = swap(held, "hst", hosts, 1, 1)
-    done = anchors(5, 3, (held,))
-    anchor = held, other
+    done = anchors(0, 2, (done,))
+    done = anchors(2, 2, (done,))
     source = merge_part(source, landed, True, (done,))
     landed = swap(source, "hst", hosts, 1, 1)
-    done = anchors(8, 1, (source,))
+    done = complete(1, (source,))
+    done = anchors(4, 2, (done,))
     terms = project_part(source, landed, out_weight, (done,))
-    shares = [(12, 4, True), (9, 3, False)]
+    shares = [[(12, 4, True)], [(6, 2, False), (8, 4, False)]]
     step = 1
     while step < groups:
         landed = swap(terms, "tp", groups, step, step)
         last = False
-        if shares:
-            first, count, last = shares.pop()
-            done = anchors(first, count, (terms,), last)
+        done = terms
+        for first, count, last in shares.pop() if shares else ():
+            done = anchors(first, count, (terms, done), last)
         terms = add_part(terms, landed, () if last else (done,))
         step *= 2
-    for first, count, last in reversed(shares):
-        done = anchors(first, count, (), last)
+    for group in reversed(shares):
+        for first, count, last in group:
+            done = anchors(first, count, (), last)
     return done, terms
 
 

time: 111 us -> 116 us (1.045)
  Pallas kernels: 92.9 us -> 95.3 us
  starting transfers between devices: 9.84 us -> 12 us
  waiting for transfers between devices: 5.99 us -> 7.26 us
    pallas_call x1, Pallas kernels: 2.86 us -> 5.16 us  [source_part(): pl.pallas_call(functools.partial(source_kernel, per_kv, q_rows, H // KVH)...]
    ppermute x14 -> x15, starting transfers between devices: 9.84 us -> 12 us  [swap(): lax.ppermute(value, axis, [(i, i ^ (odd if i & 1 else even)) for i in ran...]
    ppermute x14 -> x15, waiting for transfers between devices: 5.99 us -> 7.26 us  [swap(): lax.ppermute(value, axis, [(i, i ^ (odd if i & 1 else even)) for i in ran...]
    pallas_call x3 -> x4, Pallas kernels: 8.19 us -> 8.1 us  [own_part(): pl.pallas_call(functools.partial(own_kernel, first, count, per_kv), out_s...]
  transfers between devices with their start and end apart: 14 -> 15, of which waited for: 4 -> 4; matrix products, arithmetic and copies ran while one was open for 0% -> 0% of each run, Pallas kernels for 82% -> 81%
where the time goes in v5:
time: 116 us
  Pallas kernels  95.3 us (82%)
  starting transfers between devices  12 us (10%)
  waiting for transfers between devices  7.26 us (6%)
    pallas_call x6, Pallas kernels, anchor_part(): pl.pallas_call(functools.partial(anchor_kernel, first, count, base, per_k...  77.6 us
    ppermute x15, starting transfers between devices, swap(): lax.ppermute(value, axis, [(i, i ^ (odd if i & 1 else even)) for i in ran...  12 us
    pallas_call x4, Pallas kernels, own_part(): pl.pallas_call(functools.partial(own_kernel, first, count, per_kv), out_s...  8.1 us
    ppermute x15, waiting for transfers between devices, swap(): lax.ppermute(value, axis, [(i, i ^ (odd if i & 1 else even)) for i in ran...  7.26 us
    pallas_call x1, Pallas kernels, source_part(): pl.pallas_call(functools.partial(source_kernel, per_kv, q_rows, H // KVH)...  5.16 us
  transfers between devices with their start and end apart: 15, of which 4 were waited for; matrix products, arithmetic and copies ran while one was open for 0% of the time, Pallas kernels for 81%

profile of v5, /device:TPU:6, one launch (start us, length us, event | category | flops | bytes accessed | tf_op | source)
XLA Modules:
  0.0 115.6 jit_solution(709452032066954590)
XLA Ops:
  0.6 1.3 %pick_columns.1 = (bf16[768,256]{1,0:T(8,128)(2,1)S(1)}, bf16[768,256]{1,0:T(8,128)(2,1)S(1)}) custom-call(bf16[2,768,1024]{2,1,0:T(8,128)(2,1)} %kv_ref.1), custom_call_target="tpu_custom_call" | custom-call | tf_op jit(solution)/shard_map/pick_columns/pallas_call | solution.py:60
  2.0 0.5 collective-permute-start
  2.5 1.3 %collective-permute-done.landed_ref = bf16[8,2048]{1,0:T(8,128)(2,1)S(1)} collective-permute-done((bf16[8,2048]{1,0:T(8,128)(2,1)S(1)}, bf16[8,2048]{1,0:T(8,128)(2,1)S(1)}, u32[]{:S(2)}, u32[]{:S(2)}) %collective-permute-start) | collective-permute-done | bytes 32800 | tf_op jit(solution)/shard_map/ppermute | solution.py:43
  3.8 0.5 collective-permute-start.1
  4.3 1.1 context_own.4.rest_0_.refs_2_
  5.5 1.6 %collective-permute-start.5 = (bf16[768,256]{1,0:T(8,128)(2,1)S(1)}, bf16[768,256]{1,0:T(8,128)(2,1)S(1)}, u32[]{:S(2)}, u32[]{:S(2)}) collective-permute-start(bf16[768,256]{1,0:T(8,128)(2,1)S(1)} %anchor_relay.4.rest_0_.one_ref), channel_id=1, source_target_pairs={{0,8},{4,20},{8,0},{12,28},{16,24},{20,4},{24,16},{28,12},{1,9},{5... | collective-permute-start | bytes 1179656 | tf_op jit(solution)/shard_map/ppermute | solution.py:43
  7.1 1.0 collective-permute-done.1.landed_ref
  8.1 0.6 collective-permute-start.3
  8.7 3.1 %context_own.5.rest_0_.refs_2_ = f32[768,1536]{1,0:T(8,128)S(1)} custom-call(bf16[768,2048]{1,0:T(8,128)(2,1)S(1)} %copy-done, bf16[768,256]{1,0:T(8,128)(2,1)S(1)} %get-tuple-element.8.k_ref.one_ref.refs_3_, bf16[768,256]{1,0:T(8,128)(2,1)S(1)} %get-tuple-element.9.rest_0_.v_ref.refs_4_, bf16[32,2048]{1,0:T(8,128)(2,1)S(1)} %query_join.3.rest_0_.known_ref), custom_call_target="tpu_custom_call" | custom-call | flops 2415919104 | bytes 3538944 | tf_op jit(solution)/shard_map/context_own/pallas_call | solution.py:202
  11.8 1.8 %collective-permute-done.3.landed_ref = bf16[32,2048]{1,0:T(8,128)(2,1)S(1)} collective-permute-done((bf16[32,2048]{1,0:T(8,128)(2,1)S(1)}, bf16[32,2048]{1,0:T(8,128)(2,1)S(1)}, u32[]{:S(2)}, u32[]{:S(2)}) %collective-permute-start.3) | collective-permute-done | bytes 131104 | tf_op jit(solution)/shard_map/ppermute | solution.py:43
  13.6 5.2 %query_source.1 = (bf16[64,1152]{1,0:T(8,128)(2,1)S(1)}, bf16[64,1152]{1,0:T(8,128)(2,1)S(1)}) custom-call(s32[8]{0:T(128)S(1)} %copy-done.4, bf16[768,256]{1,0:T(8,128)(2,1)S(1)} %get-tuple-element.8.k_ref.one_ref.refs_3_, bf16[768,256]{1,0:T(8,128)(2,1)S(1)} %get-tuple-element.9.rest_0_.v_ref.refs_4_, bf16[2,8,1024]{2,1,0:T(8,128)(2,1)S(1)} %copy-done.2, ...), custom_call_target="tpu_custom_call" | custom-call | flops 805306368 | bytes 2097152 | tf_op jit(solution)/shard_map/query_source/pallas_call | solution.py:481
  18.9 1.9 %context_own.6.rest_0_.refs_2_ = f32[768,1024]{1,0:T(8,128)S(1)} custom-call(bf16[768,2048]{1,0:T(8,128)(2,1)S(1)} %copy-done, bf16[768,256]{1,0:T(8,128)(2,1)S(1)} %get-tuple-element.8.k_ref.one_ref.refs_3_, bf16[768,256]{1,0:T(8,128)(2,1)S(1)} %get-tuple-element.9.rest_0_.v_ref.refs_4_, bf16[64,1152]{1,0:T(8,128)(2,1)S(1)} %get-tuple-element.10.rest_0_.one_ref), custom_call_target="tpu_custom_call" | custom-call | flops 1610612736 | bytes 2359296 | tf_op jit(solution)/shard_map/context_own/pallas_call | solution.py:202
  20.8 0.3 anchor_relay.5
  21.1 1.6 %collective-permute-start.9 = (bf16[768,128]{1,0:T(8,128)(2,1)S(1)}, bf16[768,128]{1,0:T(8,128)(2,1)S(1)}, u32[]{:S(2)}, u32[]{:S(2)}) collective-permute-start(bf16[768,128]{1,0:T(8,128)(2,1)S(1)} %get-tuple-element.13.one_ref), channel_id=1, source_target_pairs={{0,16},{4,12},{8,24},{12,4},{16,0},{20,28},{24,8},{28,20},{1,17},{... | collective-permute-start | bytes 589832 | tf_op jit(solution)/shard_map/ppermute | solution.py:43
  22.7 0.3 query_merge.3.rest_0_.one_ref
  23.1 1.9 %context_own.7.rest_0_.refs_2_ = f32[768,1024]{1,0:T(8,128)S(1)} custom-call(bf16[768,2048]{1,0:T(8,128)(2,1)S(1)} %copy-done, bf16[768,256]{1,0:T(8,128)(2,1)S(1)} %get-tuple-element.8.k_ref.one_ref.refs_3_, bf16[768,256]{1,0:T(8,128)(2,1)S(1)} %get-tuple-element.9.rest_0_.v_ref.refs_4_, bf16[64,1152]{1,0:T(8,128)(2,1)S(1)} %query_merge.3.rest_0_.one_ref), custom_call_target="tpu_custom_call" | custom-call | flops 1610612736 | bytes 2359296 | tf_op jit(solution)/shard_map/context_own/pallas_call | solution.py:202
  25.0 3.2 %collective-permute-done.7.two_ref = bf16[64,1152]{1,0:T(8,128)(2,1)S(1)} collective-permute-done((bf16[64,1152]{1,0:T(8,128)(2,1)S(1)}, bf16[64,1152]{1,0:T(8,128)(2,1)S(1)}, u32[]{:S(2)}, u32[]{:S(2)}) %collective-permute-start.7) | collective-permute-done | bytes 147488 | tf_op jit(solution)/shard_map/ppermute | solution.py:43
  28.2 0.3 query_merge.4.rest_0_.one_ref
  28.7 1.4 %collective-permute-start.6 = (bf16[768,128]{1,0:T(8,128)(2,1)S(1)}, bf16[768,128]{1,0:T(8,128)(2,1)S(1)}, u32[]{:S(2)}, u32[]{:S(2)}) collective-permute-start(bf16[768,128]{1,0:T(8,128)(2,1)S(1)} %get-tuple-element.12.rest_0_.one_ref), channel_id=1, source_target_pairs={{0,16},{4,12},{8,24},{12,4},{16,0},{20,28},{24,8},{28,20},{1,17},{... | collective-permute-start | bytes 589832 | tf_op jit(solution)/shard_map/ppermute | solution.py:43
  30.0 0.7 collective-permute-start.8
  30.7 9.8 %context_anchor.6.refs_7_ = bf16[768,256]{1,0:T(8,128)(2,1)S(1)} custom-call(s32[8]{0:T(128)S(1)} %copy-done.4, bf16[768,2048]{1,0:T(8,128)(2,1)S(1)} %copy-done, f32[768,512]{1,0:T(8,128)S(1)} %context_own.4.rest_0_.refs_2_, bf16[768,256]{1,0:T(8,128)(2,1)S(1)} %get-tuple-element.8.k_ref.one_ref.refs_3_, ...), custom_call_target="tpu_custom_call" | custom-call | flops 1207959552 | bytes 1572864 | tf_op jit(solution)/shard_map/context_anchor/pallas_call | solution.py:349
  40.5 9.8 %context_anchor.7.rest_0_.refs_8_ = bf16[768,256]{1,0:T(8,128)(2,1)S(1)} custom-call(s32[8]{0:T(128)S(1)} %copy-done.4, bf16[768,2048]{1,0:T(8,128)(2,1)S(1)} %copy-done, f32[768,1536]{1,0:T(8,128)S(1)} %context_own.5.rest_0_.refs_2_, bf16[768,256]{1,0:T(8,128)(2,1)S(1)} %get-tuple-element.8.k_ref.one_ref.refs_3_, ...), custom_call_target="tpu_custom_call" | custom-call | flops 1207959552 | bytes 1572864 | tf_op jit(solution)/shard_map/context_anchor/pallas_call | solution.py:349
  50.3 0.3 query_merge.5.rest_0_.own_ref
  50.8 0.5 collective-permute-start.11
  51.3 9.8 %context_anchor.8.rest_0_.refs_9_ = bf16[768,256]{1,0:T(8,128)(2,1)S(1)} custom-call(s32[8]{0:T(128)S(1)} %copy-done.4, bf16[768,2048]{1,0:T(8,128)(2,1)S(1)} %copy-done, f32[768,1536]{1,0:T(8,128)S(1)} %context_own.5.rest_0_.refs_2_, bf16[768,256]{1,0:T(8,128)(2,1)S(1)} %get-tuple-element.8.k_ref.one_ref.refs_3_, ...), custom_call_target="tpu_custom_call" | custom-call | flops 1207959552 | bytes 1572864 | tf_op jit(solution)/shard_map/context_anchor/pallas_call | solution.py:349
  61.1 1.1 query_project.1.refs_7_.refs_8_.one_ref
  62.2 1.6 %collective-permute-start.13 = (bf16[64,1024]{1,0:T(8,128)(2,1)S(1)}, bf16[64,1024]{1,0:T(8,128)(2,1)S(1)}, u32[]{:S(2)}, u32[]{:S(2)}) collective-permute-start(bf16[64,1024]{1,0:T(8,128)(2,1)S(1)} %query_project.1.refs_7_.refs_8_.one_ref), channel_id=1, source_target_pairs={{0,1},{1,0},{2,3},{3,2},{4,5},{5,4},{6,7},{7,6},{8,9},{9,8},{10,11... | collective-permute-start | bytes 393224 | tf_op jit(solution)/shard_map/ppermute | solution.py:43
  63.9 9.8 %context_anchor.9.refs_8_.refs_10_ = bf16[768,256]{1,0:T(8,128)(2,1)S(1)} custom-call(s32[8]{0:T(128)S(1)} %copy-done.4, bf16[768,2048]{1,0:T(8,128)(2,1)S(1)} %copy-done, f32[768,1536]{1,0:T(8,128)S(1)} %context_own.5.rest_0_.refs_2_, bf16[768,256]{1,0:T(8,128)(2,1)S(1)} %get-tuple-element.8.k_ref.one_ref.refs_3_, ...), custom_call_target="tpu_custom_call" | custom-call | flops 1207959552 | bytes 1572864 | tf_op jit(solution)/shard_map/context_anchor/pallas_call | solution.py:349
  73.7 18.7 %context_anchor.10.rest_0_.refs_11_ = bf16[768,512]{1,0:T(8,128)(2,1)S(1)} custom-call(s32[8]{0:T(128)S(1)} %copy-done.4, bf16[768,2048]{1,0:T(8,128)(2,1)S(1)} %copy-done, f32[768,1024]{1,0:T(8,128)S(1)} %context_own.6.rest_0_.refs_2_, bf16[768,256]{1,0:T(8,128)(2,1)S(1)} %get-tuple-element.8.k_ref.one_ref.refs_3_, ...), custom_call_target="tpu_custom_call" | custom-call | flops 2415919104 | bytes 3145728 | tf_op jit(solution)/shard_map/context_anchor/pallas_call | solution.py:349
  92.4 2.7 %collective-permute-start.14 = (bf16[64,1024]{1,0:T(8,128)(2,1)S(1)}, bf16[64,1024]{1,0:T(8,128)(2,1)S(1)}, u32[]{:S(2)}, u32[]{:S(2)}) collective-permute-start(bf16[64,1024]{1,0:T(8,128)(2,1)S(1)} %query_sum.2.refs_12_.refs_13_.one_ref), channel_id=1, source_target_pairs={{0,2},{1,3},{2,0},{3,1},{4,6},{5,7},{6,4},{7,5},{8,10},{9,11},{10,... | collective-permute-start | bytes 393224 | tf_op jit(solution)/shard_map/ppermute | solution.py:43
  95.1 19.8 %context_anchor.11 = bf16[768,2048]{1,0:T(8,128)(2,1)} custom-call(s32[8]{0:T(128)S(1)} %copy-done.4, bf16[768,2048]{1,0:T(8,128)(2,1)S(1)} %copy-done, f32[768,1024]{1,0:T(8,128)S(1)} %context_own.7.rest_0_.refs_2_, bf16[768,256]{1,0:T(8,128)(2,1)S(1)} %get-tuple-element.8.k_ref.one_ref.refs_3_, ...), custom_call_target="tpu_custom_call" | custom-call | flops 2415919104 | bytes 3145728 | tf_op jit(solution)/shard_map/context_anchor/pallas_call | solution.py:349
  114.9 0.7 query_sum.3
  (32 shorter events, 0.6 us)
Async XLA Ops:
  0.6 1.4 %copy-start.3 = (bf16[8,2048]{1,0:T(8,128)(2,1)S(1)}, bf16[8,2048]{1,0:T(8,128)(2,1)}, u32[]{:S(2)}) copy-start(bf16[8,2048]{1,0:T(8,128)(2,1)} %known_ref.1) | copy-start | bytes 98308
  0.6 3.7 %copy-start = (bf16[768,2048]{1,0:T(8,128)(2,1)S(1)}, bf16[768,2048]{1,0:T(8,128)(2,1)}, u32[]{:S(2)}) copy-start(bf16[768,2048]{1,0:T(8,128)(2,1)} %refs_1_.11) | copy-start | bytes 9437188
  2.0 3.5 %collective-permute-start.2 = (bf16[768,256]{1,0:T(8,128)(2,1)S(1)}, bf16[768,256]{1,0:T(8,128)(2,1)S(1)}, u32[]{:S(2)}, u32[]{:S(2)}) collective-permute-start(bf16[768,256]{1,0:T(8,128)(2,1)S(1)} %get-tuple-element.9.rest_0_.v_ref.refs_4_), channel_id=1, source_target_pairs={{0,4},{4,0},{8,12},{12,8},{16,20},{20,16},{24,28},{28,24},{1,5},{5... | collective-permute-start | bytes 1179656 | tf_op jit(solution)/shard_map/ppermute | solution.py:43
  2.0 1.7 %collective-permute-start = (bf16[8,2048]{1,0:T(8,128)(2,1)S(1)}, bf16[8,2048]{1,0:T(8,128)(2,1)S(1)}, u32[]{:S(2)}, u32[]{:S(2)}) collective-permute-start(bf16[8,2048]{1,0:T(8,128)(2,1)S(1)} %copy-done.3), channel_id=1, source_target_pairs={{0,4},{4,0},{8,12},{12,8},{16,20},{20,16},{24,28},{28,24},{1,5},{5... | collective-permute-start | bytes 98312 | tf_op jit(solution)/shard_map/ppermute | solution.py:43
  3.8 4.3 %collective-permute-start.1 = (bf16[16,2048]{1,0:T(8,128)(2,1)S(1)}, bf16[16,2048]{1,0:T(8,128)(2,1)S(1)}, u32[]{:S(2)}, u32[]{:S(2)}) collective-permute-start(bf16[16,2048]{1,0:T(8,128)(2,1)S(1)} %query_join.2.rest_0_.known_ref), channel_id=1, source_target_pairs={{0,8},{4,20},{8,0},{12,28},{16,24},{20,4},{24,16},{28,12},{1,9},{5... | collective-permute-start | bytes 196616 | tf_op jit(solution)/shard_map/ppermute | solution.py:43
  5.5 15.3 %collective-permute-start.5 = (bf16[768,256]{1,0:T(8,128)(2,1)S(1)}, bf16[768,256]{1,0:T(8,128)(2,1)S(1)}, u32[]{:S(2)}, u32[]{:S(2)}) collective-permute-start(bf16[768,256]{1,0:T(8,128)(2,1)S(1)} %anchor_relay.4.rest_0_.one_ref), channel_id=1, source_target_pairs={{0,8},{4,20},{8,0},{12,28},{16,24},{20,4},{24,16},{28,12},{1,9},{5... | collective-permute-start | bytes 1179656 | tf_op jit(solution)/shard_map/ppermute | solution.py:43
  8.1 5.5 %copy-start.2 = (bf16[2,8,1024]{2,1,0:T(8,128)(2,1)S(1)}, bf16[2,8,1024]{2,1,0:T(8,128)(2,1)}, u32[]{:S(2)}) copy-start(bf16[2,8,1024]{2,1,0:T(8,128)(2,1)} %self_ref.1) | copy-start | bytes 98308
  8.1 5.5 %copy-start.4 = (s32[8]{0:T(128)S(1)}, s32[8]{0:T(128)}, u32[]{:S(2)}) copy-start(s32[8]{0:T(128)} %refs_0_.11) | copy-start | bytes 100
  8.1 5.5 %collective-permute-start.3 = (bf16[32,2048]{1,0:T(8,128)(2,1)S(1)}, bf16[32,2048]{1,0:T(8,128)(2,1)S(1)}, u32[]{:S(2)}, u32[]{:S(2)}) collective-permute-start(bf16[32,2048]{1,0:T(8,128)(2,1)S(1)} %query_join.3.rest_0_.known_ref), channel_id=1, source_target_pairs={{0,16},{4,12},{8,24},{12,4},{16,0},{20,28},{24,8},{28,20},{1,17},{... | collective-permute-start | bytes 393224 | tf_op jit(solution)/shard_map/ppermute | solution.py:43
  18.8 3.9 %collective-permute-start.4 = (bf16[64,1152]{1,0:T(8,128)(2,1)S(1)}, bf16[64,1152]{1,0:T(8,128)(2,1)S(1)}, u32[]{:S(2)}, u32[]{:S(2)}) collective-permute-start(bf16[64,1152]{1,0:T(8,128)(2,1)S(1)} %get-tuple-element.11), channel_id=1, source_target_pairs={{0,4},{4,0},{8,12},{12,8},{16,20},{20,16},{24,28},{28,24},{1,5},{5... | collective-permute-start | bytes 442376 | tf_op jit(solution)/shard_map/ppermute | solution.py:43
  21.1 7.4 %collective-permute-start.9 = (bf16[768,128]{1,0:T(8,128)(2,1)S(1)}, bf16[768,128]{1,0:T(8,128)(2,1)S(1)}, u32[]{:S(2)}, u32[]{:S(2)}) collective-permute-start(bf16[768,128]{1,0:T(8,128)(2,1)S(1)} %get-tuple-element.13.one_ref), channel_id=1, source_target_pairs={{0,16},{4,12},{8,24},{12,4},{16,0},{20,28},{24,8},{28,20},{1,17},{... | collective-permute-start | bytes 589832 | tf_op jit(solution)/shard_map/ppermute | solution.py:43
  23.0 5.2 %collective-permute-start.7 = (bf16[64,1152]{1,0:T(8,128)(2,1)S(1)}, bf16[64,1152]{1,0:T(8,128)(2,1)S(1)}, u32[]{:S(2)}, u32[]{:S(2)}) collective-permute-start(bf16[64,1152]{1,0:T(8,128)(2,1)S(1)} %query_merge.3.rest_0_.one_ref), channel_id=1, source_target_pairs={{0,8},{4,20},{8,0},{12,28},{16,24},{20,4},{24,16},{28,12},{1,9},{5... | collective-permute-start | bytes 442376 | tf_op jit(solution)/shard_map/ppermute | solution.py:43
  28.6 2.2 %collective-permute-start.10 = (bf16[768,128]{1,0:T(8,128)(2,1)S(1)}, bf16[768,128]{1,0:T(8,128)(2,1)S(1)}, u32[]{:S(2)}, u32[]{:S(2)}) collective-permute-start(bf16[768,128]{1,0:T(8,128)(2,1)S(1)} %anchor_relay.6.refs_5_.refs_7_), channel_id=1, source_target_pairs={{0,4},{4,0},{8,12},{12,8},{16,20},{20,16},{24,28},{28,24},{1,5},{5... | collective-permute-start | bytes 589832 | tf_op jit(solution)/shard_map/ppermute | solution.py:43
  28.7 22.1 %collective-permute-start.6 = (bf16[768,128]{1,0:T(8,128)(2,1)S(1)}, bf16[768,128]{1,0:T(8,128)(2,1)S(1)}, u32[]{:S(2)}, u32[]{:S(2)}) collective-permute-start(bf16[768,128]{1,0:T(8,128)(2,1)S(1)} %get-tuple-element.12.rest_0_.one_ref), channel_id=1, source_target_pairs={{0,16},{4,12},{8,24},{12,4},{16,0},{20,28},{24,8},{28,20},{1,17},{... | collective-permute-start | bytes 589832 | tf_op jit(solution)/shard_map/ppermute | solution.py:43
  30.0 20.3 %collective-permute-start.8 = (bf16[64,1152]{1,0:T(8,128)(2,1)S(1)}, bf16[64,1152]{1,0:T(8,128)(2,1)S(1)}, u32[]{:S(2)}, u32[]{:S(2)}) collective-permute-start(bf16[64,1152]{1,0:T(8,128)(2,1)S(1)} %query_merge.4.rest_0_.one_ref), channel_id=1, source_target_pairs={{0,16},{4,12},{8,24},{12,4},{16,0},{20,28},{24,8},{28,20},{1,17},{... | collective-permute-start | bytes 442376 | tf_op jit(solution)/shard_map/ppermute | solution.py:43
  50.6 10.5 %collective-permute-start.12 = (bf16[64,1024]{1,0:T(8,128)(2,1)S(1)}, bf16[64,1024]{1,0:T(8,128)(2,1)S(1)}, u32[]{:S(2)}, u32[]{:S(2)}) collective-permute-start(bf16[64,1024]{1,0:T(8,128)(2,1)S(1)} %query_merge.5.rest_0_.own_ref), channel_id=1, source_target_pairs={{0,4},{4,0},{8,12},{12,8},{16,20},{20,16},{24,28},{28,24},{1,5},{5... | collective-permute-start | bytes 393224 | tf_op jit(solution)/shard_map/ppermute | solution.py:43
  50.8 10.4 %copy-start.1 = (bf16[2048,1024]{1,0:T(8,128)(2,1)S(1)}, bf16[2048,1024]{1,0:T(8,128)(2,1)}, u32[]{:S(2)}) copy-start(bf16[2048,1024]{1,0:T(8,128)(2,1)} %w_ref.1) | copy-start | bytes 12582916
  50.8 22.9 %collective-permute-start.11 = (bf16[768,128]{1,0:T(8,128)(2,1)S(1)}, bf16[768,128]{1,0:T(8,128)(2,1)S(1)}, u32[]{:S(2)}, u32[]{:S(2)}) collective-permute-start(bf16[768,128]{1,0:T(8,128)(2,1)S(1)} %anchor_relay.7.refs_7_.refs_5_), channel_id=1, source_target_pairs={{0,4},{4,0},{8,12},{12,8},{16,20},{20,16},{24,28},{28,24},{1,5},{5... | collective-permute-start | bytes 589832 | tf_op jit(solution)/shard_map/ppermute | solution.py:43
  62.2 30.1 %collective-permute-start.13 = (bf16[64,1024]{1,0:T(8,128)(2,1)S(1)}, bf16[64,1024]{1,0:T(8,128)(2,1)S(1)}, u32[]{:S(2)}, u32[]{:S(2)}) collective-permute-start(bf16[64,1024]{1,0:T(8,128)(2,1)S(1)} %query_project.1.refs_7_.refs_8_.one_ref), channel_id=1, source_target_pairs={{0,1},{1,0},{2,3},{3,2},{4,5},{5,4},{6,7},{7,6},{8,9},{9,8},{10,11... | collective-permute-start | bytes 393224 | tf_op jit(solution)/shard_map/ppermute | solution.py:43
  92.4 22.5 %collective-permute-start.14 = (bf16[64,1024]{1,0:T(8,128)(2,1)S(1)}, bf16[64,1024]{1,0:T(8,128)(2,1)S(1)}, u32[]{:S(2)}, u32[]{:S(2)}) collective-permute-start(bf16[64,1024]{1,0:T(8,128)(2,1)S(1)} %query_sum.2.refs_12_.refs_13_.one_ref), channel_id=1, source_target_pairs={{0,2},{1,3},{2,0},{3,1},{4,6},{5,7},{6,4},{7,5},{8,10},{9,11},{10,... | collective-permute-start | bytes 393224 | tf_op jit(solution)/shard_map/ppermute | solution.py:43

commit v6 on v5

--- a/solution.py
+++ b/solution.py
@@ -64,6 +64,7 @@
         out_specs=[VMEM] * 2,
         scratch_shapes=[pltpu.SemaphoreType.DMA((2,))],
         compiler_params=params(52),
+        cost_estimate=pl.CostEstimate(flops=0, bytes_accessed=2**22, transcendentals=0),
         name="pick_columns",
     )(ctx_kv)
 
@@ -79,6 +80,7 @@
         in_specs=[VMEM] * len(inputs) + [ANY] * len(after),
         out_specs=[VMEM] * len(shapes),
         compiler_params=params(),
+        cost_estimate=pl.CostEstimate(flops=0, bytes_accessed=2**20, transcendentals=0),
         name=name,
     )(*inputs, *after)
 
@@ -133,10 +135,38 @@
     return small_call(kernel, "query_sum", [one.shape], (one, two), after)[0]
 
 
-def fill_values(vaug, values):
-    for j in range(values.shape[1] // HD):
-        vaug[:, 2 * j * HD : (2 * j + 1) * HD] = values[:, j * HD : (j + 1) * HD]
-        vaug[:, (2 * j + 1) * HD : (2 * j + 2) * HD] = jnp.ones((values.shape[0], HD), BF)
+def prepare(first, second, swapped, after=()):
+    slab, columns = first.shape
+
+    def kernel(first_ref, second_ref, *rest):
+        keys_ref, values_ref = rest[-2:]
+
+        def fill(k_ref, v_ref):
+            def run():
+                for j in range(columns // HD):
+                    cols = slice(j * HD, (j + 1) * HD)
+                    at = 2 * j * HD
+                    scaled = k_ref[:, cols].astype(F32) * SCALE2
+                    high = scaled.astype(BF)
+                    keys_ref[:, at : at + HD] = high
+                    keys_ref[:, at + HD : at + 2 * HD] = (scaled - high.astype(F32)).astype(BF)
+                    values_ref[:, at : at + HD] = v_ref[:, cols]
+                    values_ref[:, at + HD : at + 2 * HD] = jnp.ones((slab, HD), BF)
+
+            return run
+
+        if swapped:
+            even = bit(lax.axis_index("hst"), 0) == 0
+            choose(even, fill(first_ref, second_ref), fill(second_ref, first_ref))
+        else:
+            fill(first_ref, second_ref)()
+
+    shapes = [(slab, 2 * columns)] * 2
+    return small_call(kernel, "operands", shapes, (first, second), after)
+
+
+def twice(query):
+    return jnp.concatenate([query, query], 1)
 
 
 def lanes(index, width):
@@ -152,12 +182,11 @@
 
 
 def own_kernel(first, count, per_kv, q_ref, k_ref, v_ref, *rest):
-    state_ref, vaug = rest[-2], rest[-1]
+    state_ref = rest[-1]
     slab = q_ref.shape[0]
     tile = row_tile(slab)
     half = tile // 2
     heads = body_size(count, 4)
-    fill_values(vaug, v_ref)
     rows = lax.broadcasted_iota(jnp.int32, (half, half), 0)
     cols = lax.broadcasted_iota(jnp.int32, (half, half), 1)
     causal = cols <= rows
@@ -170,13 +199,13 @@
         def scores(at):
             h, j = units[at]
             query = q_ref[j * tile :, lanes(first + i * heads + h, HD)]
-            return dot_t(query, k_ref[j * tile : (j + 1) * tile, lanes(kv, HD)])
+            return dot_t(twice(query), k_ref[j * tile : (j + 1) * tile, lanes(kv, 2 * HD)])
 
         def power(x):
-            return jnp.exp2(x * SCALE2).astype(BF)
+            return jnp.exp2(x).astype(BF)
 
         def corner(x):
-            return jnp.where(causal, jnp.exp2(x * SCALE2), 0.0).astype(BF)
+            return jnp.where(causal, jnp.exp2(x), 0.0).astype(BF)
 
         current = scores(0)
         totals = [None] * chunks
@@ -185,7 +214,7 @@
             top = jnp.concatenate([corner(current[:half, :half]), jnp.zeros((half, half), BF)], 1)
             low = jnp.concatenate([power(current[half:tile, :half]), corner(current[half:tile, half:])], 1)
             expo = [top, low] if j == chunks - 1 else [top, low, power(current[tile:])]
-            part = dot(jnp.concatenate(expo, 0), vaug[j * tile : (j + 1) * tile, lanes(kv, 2 * HD)])
+            part = dot(jnp.concatenate(expo, 0), v_ref[j * tile : (j + 1) * tile, lanes(kv, 2 * HD)])
             for r in range(j, chunks):
                 piece = part[(r - j) * tile : (r - j + 1) * tile]
                 totals[r] = piece if j == 0 else totals[r] + piece
@@ -204,7 +233,6 @@
         out_shape=jax.ShapeDtypeStruct((slab, count * 2 * HD), F32),
         in_specs=[VMEM] * 3 + [ANY] * len(after),
         out_specs=VMEM,
-        scratch_shapes=[pltpu.VMEM((slab, 2 * own_v.shape[1]), BF)],
         compiler_params=params(),
         cost_estimate=pl.CostEstimate(
             flops=work * HD * 8, bytes_accessed=count * slab * HD * 6, transcendentals=work
@@ -214,12 +242,12 @@
 
 
 def anchor_kernel(first, count, base, per_kv, last, befores, *refs):
-    lengths_ref, q_ref, state_ref, k_ref, v_ref, even_ref, odd_ref = refs[:7]
+    lengths_ref, q_ref, state_ref, k_ref, v_ref, keys, vaug = refs[:7]
     earlier = refs[7 : 7 + len(befores)]
     if last:
-        full_ref, out_ref, keys, vaug, sems = refs[-5:]
+        full_ref, out_ref, sems = refs[-3:]
     else:
-        out_ref, keys, vaug = refs[-3:]
+        out_ref = refs[-1]
     slab = q_ref.shape[0]
     heads = body_size(count, 2 if last else 4)
     kv = first // per_kv
@@ -234,23 +262,13 @@
     for move in moves:
         move.start()
 
-    @pl.when(host % 2 == 0)
-    def _():
-        keys[...] = even_ref[...]
-        fill_values(vaug, odd_ref)
-
-    @pl.when(host % 2 == 1)
-    def _():
-        keys[...] = odd_ref[...]
-        fill_values(vaug, even_ref)
-
     def part(start):
         def query_of(h):
             at = (first + start + h) * HD
             return q_ref[:, at : at + HD]
 
         def scores(h):
-            return dot_t(query_of(h), keys[...])
+            return dot_t(twice(query_of(h)), keys[...])
 
         def state_of(h):
             at = (first - base + start + h) * 2 * HD
@@ -280,7 +298,7 @@
             current = scores(0)
             for h in range(heads):
                 following = scores(h + 1) if h + 1 < heads else None
-                expo = jnp.exp2(current * SCALE2).astype(BF)
+                expo = jnp.exp2(current).astype(BF)
                 total = dot(expo, vaug[...]) + state_of(h)
                 worst = finish(h, total, worst)
                 current = following
@@ -317,16 +335,16 @@
         query = q_ref[at, lanes(q_head + h, HD)]
         row_ids = lax.broadcasted_iota(jnp.int32, (tile, slab), 0) + r * tile
         key_ids = lax.broadcasted_iota(jnp.int32, (tile, slab), 1)
-        own = dot_t(query, k_ref[:, kv * HD : (kv + 1) * HD]) * SCALE2
+        own = dot_t(twice(query), k_ref[:, 2 * kv * HD : 2 * (kv + 1) * HD])
         own = jnp.where((key_ids <= row_ids) & (key_ids < own_len), own, MASKED)
-        far = dot_t(query, keys[...]) * SCALE2
+        far = dot_t(twice(query), keys[...])
         far = jnp.where(host > 0, far, MASKED)
         peak = jnp.maximum(jnp.max(own, 1, keepdims=True), jnp.max(far, 1, keepdims=True))
         own = jnp.exp2(own - peak)
         far = jnp.where(host > 0, jnp.exp2(far - peak), 0.0)
         sums = jnp.sum(own, 1, keepdims=True) + jnp.sum(far, 1, keepdims=True)
         values = jnp.where(host > 0, vaug[:, :HD].astype(F32), 0.0).astype(BF)
-        total = dot(own.astype(BF), v_ref[:, kv * HD : (kv + 1) * HD]) + dot(far.astype(BF), values)
+        total = dot(own.astype(BF), v_ref[:, 2 * kv * HD : (2 * kv + 1) * HD]) + dot(far.astype(BF), values)
         live = row_ids[:, :1] < own_len
         out_ref[at, lanes(out_head + h, HD)] = jnp.where(live, total / sums, 0.0).astype(BF)
         return carry
@@ -341,10 +359,9 @@
     earlier = list(befores.values()) if last else []
     places = tuple((at, x.shape[1] // HD) for at, x in befores.items()) if last else ()
     results = jax.ShapeDtypeStruct((slab, count * HD), BF)
-    scratch = [pltpu.VMEM((slab, HD), BF), pltpu.VMEM((slab, 2 * HD), BF)]
+    scratch = []
     if last:
-        scratch = [pltpu.VMEM(results.shape, BF)] + scratch
-        scratch += [pltpu.SemaphoreType.DMA((len(earlier) + count,))]
+        scratch = [pltpu.VMEM(results.shape, BF), pltpu.SemaphoreType.DMA((len(earlier) + count,))]
         results = jax.ShapeDtypeStruct((slab, width), BF)
     return pl.pallas_call(
         functools.partial(anchor_kernel, first, count, base, per_kv, last, places),
@@ -381,7 +398,7 @@
 
 def source_kernel(per_kv, q_rows, group_size, lengths_ref, k_ref, v_ref, self_ref, known_ref, landed_ref, *rest):
     keep_ref, send_ref, q_all, vaug = rest[-4:]
-    slab, columns = k_ref.shape
+    slab, columns = v_ref.shape
     width = per_kv * columns
     query_count = 8 * q_rows
     block = 2 * q_rows
@@ -425,7 +442,7 @@
         queries = q_all[j * rows : (j + 1) * rows, :]
         self_keys = jnp.concatenate([selves_kv[0][:, cols], pad], 0).astype(BF)
         self_values = jnp.concatenate([selves_kv[1][:, cols], pad], 0).astype(BF)
-        near = dot_t(queries, k_ref[:, cols]) * SCALE2
+        near = dot_t(twice(queries), k_ref[:, 2 * j * HD : 2 * (j + 1) * HD])
         selves = jnp.where(self_ok, dot_t(queries, self_keys) * SCALE2, MASKED)
         return near, selves, jnp.concatenate([self_values, jnp.ones((HD, HD), BF)], 1)
 
@@ -474,7 +491,7 @@
 
 
 def source_part(lengths, own_k, own_v, query_kv, known, landed, q_rows, per_kv, after=()):
-    slab, columns = own_k.shape
+    slab, columns = own_v.shape
     width = per_kv * columns
     count = 8 * q_rows
     work = count * (width // HD) * slab
@@ -603,11 +620,12 @@
         own_k, own_v = pick(ctx_kv, kv_local, local_heads)
         query_out = general_queries(lengths, own_k, own_v, self_kv, query_q, out_weight, per_kv)
         k, v = spread(jnp.stack([own_k, own_v]), "hst", 0)
-        anchor = jnp.where(host % 2 == 0, k, v), jnp.where(host % 2 == 0, v, k)
+        own_k, own_v = prepare(own_k, own_v, False)
+        anchor = prepare(k, v, False)
         state = own_part(ctx_q, own_k, own_v, 0, local_heads, per_kv)
         results = {}
         for first in range(0, local_heads, per_kv):
-            cols = slice(first // per_kv * HD, (first // per_kv + 1) * HD)
+            cols = slice(2 * first // per_kv * HD, 2 * (first // per_kv + 1) * HD)
             last = first + per_kv == local_heads
             results[first] = anchor_part(
                 lengths, ctx_q, state, 0, own_k, own_v, [x[:, cols] for x in anchor],
@@ -618,7 +636,7 @@
     states = {}
 
     def own(first, count, after=()):
-        states[first] = own_part(ctx_q, own_k, own_v, first, count, per_kv, after)
+        states[first] = own_part(ctx_q, own_keys, own_values, first, count, per_kv, after)
         return states[first]
 
     along = ((2, 4), (4, 2))
@@ -638,49 +656,57 @@
     landed = swap(query_q, "hst", hosts, 1, 1)
     own_k, own_v = pick(ctx_kv, kv_local, local_heads)
     value_landed = swap(own_v, "hst", hosts, 1, 1)
-    queries = join(is_even, query_q, landed, (own_v,))
+    own_keys, own_values = prepare(own_k, own_v, False)
+    queries = join(is_even, query_q, landed, (own_keys,))
     landed = swap(queries, "hst", hosts, *along[0])
     done = own(0, 2, (queries,))
-    (held,) = relay(is_even, own_k, value_landed, (done,))
-    held_landed = swap(held, "hst", hosts, *along[0])
-    queries = join(near_low, queries, landed, (held,))
+    parts = list(relay(is_even, own_k, value_landed, (done,), kv_local))
+    parts_landed = [swap(x, "hst", hosts, *along[0]) for x in parts]
+    queries = join(near_low, queries, landed, (parts[0],))
     landed = swap(queries, "hst", hosts, *along[1])
     done = own(2, 6, (queries,))
-    keep, send = source_part(lengths, own_k, own_v, query_kv, queries, landed, q_rows, per_kv, (done,))
-    landed = swap(send, "hst", hosts, 1, 1)
-    done = own(8, 4, (keep,))
-    parts = relay(source_first, held, held_landed, (done,), kv_local)
-    parts_landed = [swap(x, "hst", hosts, *along[1]) for x in parts]
-    source = merge_part(keep, landed, False, (parts[-1],))
-    landed = swap(source, "hst", hosts, *along[0])
-    done = own(12, 4, (source,))
     anchor = {}
+
+    def pass_on(kv, after):
+        (parts[kv],) = relay(source_first, parts[kv], parts_landed[kv], after)
+        parts_landed[kv] = swap(parts[kv], "hst", hosts, *along[1])
+        return parts[kv]
 
     def complete(kv, after):
         (held,) = relay(done_early, parts[kv], parts_landed[kv], after)
         anchor[kv] = held, swap(held, "hst", hosts, 1, 1)
         return held
 
+    done = pass_on(0, (done,))
+    keep, send = source_part(lengths, own_keys, own_v, query_kv, queries, landed, q_rows, per_kv, (done,))
+    landed = swap(send, "hst", hosts, 1, 1)
+    done = own(8, 4, (keep,))
+    source = merge_part(keep, landed, False, (done,))
+    landed = swap(source, "hst", hosts, *along[0])
+    done = complete(0, (source,))
+    done = own(12, 4, (done,))
     source = merge_part(source, landed, False, (done,))
     landed = swap(source, "hst", hosts, *along[1])
-    done = complete(0, (source,))
+    done = pass_on(1, (source,))
+    anchor[0] = prepare(*anchor[0], True, (done,))
     results = {}
 
     def anchors(first, count, after, last=False):
         base = max(x for x in states if x <= first)
         results[first] = anchor_part(
-            lengths, ctx_q, states[base], base, own_k, own_v, anchor[first // per_kv],
+            lengths, ctx_q, states[base], base, own_keys, own_values, anchor[first // per_kv],
             first, count, per_kv, dict(results) if last else None, after,
         )
         return results[first]
 
-    done = anchors(0, 2, (done,))
+    done = anchors(0, 2, ())
     done = anchors(2, 2, (done,))
     source = merge_part(source, landed, True, (done,))
     landed = swap(source, "hst", hosts, 1, 1)
     done = complete(1, (source,))
     done = anchors(4, 2, (done,))
     terms = project_part(source, landed, out_weight, (done,))
+    anchor[1] = prepare(*anchor[1], True, (terms,))
     shares = [[(12, 4, True)], [(6, 2, False), (8, 4, False)]]
     step = 1
     while step < groups:

time: 116 us -> 139 us (1.20); the launches traced: 116 us -> 137 us
  Pallas kernels: 95.3 us -> 117 us
  waiting for transfers between devices: 7.26 us -> 4.45 us
  starting transfers between devices: 12 us -> 13.7 us
    pallas_call x6, Pallas kernels: 77.6 us -> 88.6 us  [anchor_part(): pl.pallas_call(functools.partial(anchor_kernel, first, count, base, per_k...]
    pallas_call x1, Pallas kernels: 1.09 us -> 11.1 us  [project_part(): pl.pallas_call(kernel, out_shape=jax.ShapeDtypeStruct((rows, columns), BF...]
    ppermute x15 -> x16, waiting for transfers between devices: 7.26 us -> 4.45 us  [swap(): lax.ppermute(value, axis, [(i, i ^ (odd if i & 1 else even)) for i in ran...]
    ppermute x15 -> x16, starting transfers between devices: 12 us -> 13.7 us  [swap(): lax.ppermute(value, axis, [(i, i ^ (odd if i & 1 else even)) for i in ran...]
  transfers between devices with their start and end apart: 15 -> 16, of which waited for: 4 -> 4; matrix products, arithmetic and copies ran while one was open for 0% -> 0% of each run, Pallas kernels for 81% -> 84%
where the time goes in v6:
time: 139 us; the launch traced here: 137 us
  Pallas kernels  117 us (84%)
  starting transfers between devices  13.7 us (10%)
  waiting for transfers between devices  4.45 us (3%)
    pallas_call x6, Pallas kernels, anchor_part(): pl.pallas_call(functools.partial(anchor_kernel, first, count, base, per_k...  88.6 us
    ppermute x16, starting transfers between devices, swap(): lax.ppermute(value, axis, [(i, i ^ (odd if i & 1 else even)) for i in ran...  13.7 us
    pallas_call x1, Pallas kernels, project_part(): pl.pallas_call(kernel, out_shape=jax.ShapeDtypeStruct((rows, columns), BF...  11.1 us
    pallas_call x4, Pallas kernels, own_part(): pl.pallas_call(functools.partial(own_kernel, first, count, per_kv), out_s...  8.13 us
    pallas_call x1, Pallas kernels, source_part(): pl.pallas_call(functools.partial(source_kernel, per_kv, q_rows, H // KVH)...  5.24 us
    ppermute x16, waiting for transfers between devices, swap(): lax.ppermute(value, axis, [(i, i ^ (odd if i & 1 else even)) for i in ran...  4.45 us
  transfers between devices with their start and end apart: 16, of which 4 were waited for; matrix products, arithmetic and copies ran while one was open for 0% of the time, Pallas kernels for 84%

profile of v6, /device:TPU:6, one launch (start us, length us, event | category | flops | bytes accessed | tf_op | source)
XLA Modules:
  0.0 136.5 jit_solution(4909356841420254335)
XLA Ops:
  0.6 1.3 pick_columns.1
  2.0 0.5 collective-permute-start.1
  2.8 1.0 collective-permute-done.1.landed_ref
  3.8 0.5 collective-permute-start.3
  4.3 1.1 context_own.4.rest_0_.refs_2_
  5.6 1.6 %collective-permute-start.2 = (bf16[768,128]{1,0:T(8,128)(2,1)S(1)}, bf16[768,128]{1,0:T(8,128)(2,1)S(1)}, u32[]{:S(2)}, u32[]{:S(2)}) collective-permute-start(bf16[768,128]{1,0:T(8,128)(2,1)S(1)} %get-tuple-element.18.rest_0_.one_ref), channel_id=1, source_target_pairs={{0,8},{4,20},{8,0},{12,28},{16,24},{20,4},{24,16},{28,12},{1,9},{5... | collective-permute-start | bytes 589832 | tf_op jit(solution)/shard_map/ppermute | solution.py:43
  7.1 0.9 collective-permute-done.3.landed_ref
  8.1 0.6 collective-permute-start.5
  8.8 3.1 %context_own.5.rest_0_.refs_2_ = f32[768,1536]{1,0:T(8,128)S(1)} custom-call(bf16[768,2048]{1,0:T(8,128)(2,1)S(1)} %copy-done, bf16[768,512]{1,0:T(8,128)(2,1)S(1)} %get-tuple-element.16.rest_0_.k_ref.refs_3_, bf16[768,512]{1,0:T(8,128)(2,1)S(1)} %get-tuple-element.17.v_ref.refs_4_, bf16[32,2048]{1,0:T(8,128)(2,1)S(1)} %query_join.3.rest_0_.known_ref), custom_call_target="tpu_custom_call" | custom-call | flops 2415919104 | bytes 3538944 | tf_op jit(solution)/shard_map/context_own/pallas_call | solution.py:231
  11.9 0.8 collective-permute-done.2.two_ref
  12.7 1.2 collective-permute-start.4
  14.0 5.2 %query_source.1 = (bf16[64,1152]{1,0:T(8,128)(2,1)S(1)}, bf16[64,1152]{1,0:T(8,128)(2,1)S(1)}) custom-call(s32[8]{0:T(128)S(1)} %copy-done.3, bf16[768,512]{1,0:T(8,128)(2,1)S(1)} %get-tuple-element.16.rest_0_.k_ref.refs_3_, bf16[768,256]{1,0:T(8,128)(2,1)S(1)} %get-tuple-element.15.second_ref.v_ref, bf16[2,8,1024]{2,1,0:T(8,128)(2,1)S(1)} %copy-done.4, ...), custom_call_target="tpu_custom_call" | custom-call | flops 805306368 | bytes 2097152 | tf_op jit(solution)/shard_map/query_source/pallas_call | solution.py:498
  19.3 2.0 %context_own.6.rest_0_.refs_2_ = f32[768,1024]{1,0:T(8,128)S(1)} custom-call(bf16[768,2048]{1,0:T(8,128)(2,1)S(1)} %copy-done, bf16[768,512]{1,0:T(8,128)(2,1)S(1)} %get-tuple-element.16.rest_0_.k_ref.refs_3_, bf16[768,512]{1,0:T(8,128)(2,1)S(1)} %get-tuple-element.17.v_ref.refs_4_, bf16[64,1152]{1,0:T(8,128)(2,1)S(1)} %get-tuple-element.19.rest_0_.one_ref), custom_call_target="tpu_custom_call" | custom-call | flops 1610612736 | bytes 2359296 | tf_op jit(solution)/shard_map/context_own/pallas_call | solution.py:231
  21.3 0.3 query_merge.3.rest_0_.one_ref
  21.9 0.6 collective-permute-start.11
  22.5 1.5 %collective-permute-start.8 = (bf16[64,1152]{1,0:T(8,128)(2,1)S(1)}, bf16[64,1152]{1,0:T(8,128)(2,1)S(1)}, u32[]{:S(2)}, u32[]{:S(2)}) collective-permute-start(bf16[64,1152]{1,0:T(8,128)(2,1)S(1)} %query_merge.3.rest_0_.one_ref), channel_id=1, source_target_pairs={{0,8},{4,20},{8,0},{12,28},{16,24},{20,4},{24,16},{28,12},{1,9},{5... | collective-permute-start | bytes 442376 | tf_op jit(solution)/shard_map/ppermute | solution.py:43
  23.9 2.0 %context_own.7.rest_0_.refs_2_ = f32[768,1024]{1,0:T(8,128)S(1)} custom-call(bf16[768,2048]{1,0:T(8,128)(2,1)S(1)} %copy-done, bf16[768,512]{1,0:T(8,128)(2,1)S(1)} %get-tuple-element.16.rest_0_.k_ref.refs_3_, bf16[768,512]{1,0:T(8,128)(2,1)S(1)} %get-tuple-element.17.v_ref.refs_4_, bf16[768,128]{1,0:T(8,128)(2,1)S(1)} %anchor_relay.7.rest_0_.first_ref), custom_call_target="tpu_custom_call" | custom-call | flops 1610612736 | bytes 2359296 | tf_op jit(solution)/shard_map/context_own/pallas_call | solution.py:231
  25.9 1.7 %collective-permute-done.8.two_ref = bf16[64,1152]{1,0:T(8,128)(2,1)S(1)} collective-permute-done((bf16[64,1152]{1,0:T(8,128)(2,1)S(1)}, bf16[64,1152]{1,0:T(8,128)(2,1)S(1)}, u32[]{:S(2)}, u32[]{:S(2)}) %collective-permute-start.8) | collective-permute-done | bytes 147488 | tf_op jit(solution)/shard_map/ppermute | solution.py:43
  27.6 0.3 query_merge.4.rest_0_.one_ref
  27.9 1.2 collective-permute-start.10
  29.2 1.0 collective-permute-start.9
  30.3 11.2 %context_anchor.6.refs_7_ = bf16[768,256]{1,0:T(8,128)(2,1)S(1)} custom-call(s32[8]{0:T(128)S(1)} %copy-done.3, bf16[768,2048]{1,0:T(8,128)(2,1)S(1)} %copy-done, f32[768,512]{1,0:T(8,128)S(1)} %context_own.4.rest_0_.refs_2_, bf16[768,512]{1,0:T(8,128)(2,1)S(1)} %get-tuple-element.16.rest_0_.k_ref.refs_3_, ...), custom_call_target="tpu_custom_call" | custom-call | flops 1207959552 | bytes 1572864 | tf_op jit(solution)/shard_map/context_anchor/pallas_call | solution.py:366
  41.4 11.2 %context_anchor.7.rest_0_.refs_8_ = bf16[768,256]{1,0:T(8,128)(2,1)S(1)} custom-call(s32[8]{0:T(128)S(1)} %copy-done.3, bf16[768,2048]{1,0:T(8,128)(2,1)S(1)} %copy-done, f32[768,1536]{1,0:T(8,128)S(1)} %context_own.5.rest_0_.refs_2_, bf16[768,512]{1,0:T(8,128)(2,1)S(1)} %get-tuple-element.16.rest_0_.k_ref.refs_3_, ...), custom_call_target="tpu_custom_call" | custom-call | flops 1207959552 | bytes 1572864 | tf_op jit(solution)/shard_map/context_anchor/pallas_call | solution.py:366
  53.1 0.5 collective-permute-start.12
  53.6 11.2 %context_anchor.8.rest_0_.refs_9_ = bf16[768,256]{1,0:T(8,128)(2,1)S(1)} custom-call(s32[8]{0:T(128)S(1)} %copy-done.3, bf16[768,2048]{1,0:T(8,128)(2,1)S(1)} %copy-done, f32[768,1536]{1,0:T(8,128)S(1)} %context_own.5.rest_0_.refs_2_, bf16[768,512]{1,0:T(8,128)(2,1)S(1)} %get-tuple-element.16.rest_0_.k_ref.refs_3_, ...), custom_call_target="tpu_custom_call" | custom-call | flops 1207959552 | bytes 1572864 | tf_op jit(solution)/shard_map/context_anchor/pallas_call | solution.py:366
  64.8 11.1 %query_project.1.rest_0_.refs_7_.refs_8_.one_ref = bf16[64,1024]{1,0:T(8,128)(2,1)S(1)} custom-call(bf16[2048,1024]{1,0:T(8,128)(2,1)S(1)} %copy-done.1, bf16[64,1024]{1,0:T(8,128)(2,1)S(1)} %query_merge.5.rest_0_.own_ref, bf16[64,1024]{1,0:T(8,128)(2,1)S(1)} %collective-permute-done.13.other_ref, bf16[768,256]{1,0:T(8,128)(2,1)S(1)} %context_anchor.8.rest_0_.refs_9_), custom_call_target="tpu_custom_call" | custom-call | flops 268435456 | bytes 4194304 | tf_op jit(solution)/shard_map/query_project/pallas_call | solution.py:556
  75.9 1.6 %collective-permute-start.14 = (bf16[64,1024]{1,0:T(8,128)(2,1)S(1)}, bf16[64,1024]{1,0:T(8,128)(2,1)S(1)}, u32[]{:S(2)}, u32[]{:S(2)}) collective-permute-start(bf16[64,1024]{1,0:T(8,128)(2,1)S(1)} %query_project.1.rest_0_.refs_7_.refs_8_.one_ref), channel_id=1, source_target_pairs={{0,1},{1,0},{2,3},{3,2},{4,5},{5,4},{6,7},{7,6},{8,9},{9,8},{10,11... | collective-permute-start | bytes 393224 | tf_op jit(solution)/shard_map/ppermute | solution.py:43
  77.6 11.2 %context_anchor.9.refs_8_.refs_10_ = bf16[768,256]{1,0:T(8,128)(2,1)S(1)} custom-call(s32[8]{0:T(128)S(1)} %copy-done.3, bf16[768,2048]{1,0:T(8,128)(2,1)S(1)} %copy-done, f32[768,1536]{1,0:T(8,128)S(1)} %context_own.5.rest_0_.refs_2_, bf16[768,512]{1,0:T(8,128)(2,1)S(1)} %get-tuple-element.16.rest_0_.k_ref.refs_3_, ...), custom_call_target="tpu_custom_call" | custom-call | flops 1207959552 | bytes 1572864 | tf_op jit(solution)/shard_map/context_anchor/pallas_call | solution.py:366
  88.9 21.4 %context_anchor.10.rest_0_.refs_11_ = bf16[768,512]{1,0:T(8,128)(2,1)S(1)} custom-call(s32[8]{0:T(128)S(1)} %copy-done.3, bf16[768,2048]{1,0:T(8,128)(2,1)S(1)} %copy-done, f32[768,1024]{1,0:T(8,128)S(1)} %context_own.6.rest_0_.refs_2_, bf16[768,512]{1,0:T(8,128)(2,1)S(1)} %get-tuple-element.16.rest_0_.k_ref.refs_3_, ...), custom_call_target="tpu_custom_call" | custom-call | flops 2415919104 | bytes 3145728 | tf_op jit(solution)/shard_map/context_anchor/pallas_call | solution.py:366
  110.4 2.6 %collective-permute-start.15 = (bf16[64,1024]{1,0:T(8,128)(2,1)S(1)}, bf16[64,1024]{1,0:T(8,128)(2,1)S(1)}, u32[]{:S(2)}, u32[]{:S(2)}) collective-permute-start(bf16[64,1024]{1,0:T(8,128)(2,1)S(1)} %query_sum.2.refs_12_.refs_13_.one_ref), channel_id=1, source_target_pairs={{0,2},{1,3},{2,0},{3,1},{4,6},{5,7},{6,4},{7,5},{8,10},{9,11},{10,... | collective-permute-start | bytes 393224 | tf_op jit(solution)/shard_map/ppermute | solution.py:43
  113.0 22.6 %context_anchor.11 = bf16[768,2048]{1,0:T(8,128)(2,1)} custom-call(s32[8]{0:T(128)S(1)} %copy-done.3, bf16[768,2048]{1,0:T(8,128)(2,1)S(1)} %copy-done, f32[768,1024]{1,0:T(8,128)S(1)} %context_own.7.rest_0_.refs_2_, bf16[768,512]{1,0:T(8,128)(2,1)S(1)} %get-tuple-element.16.rest_0_.k_ref.refs_3_, bf16[768,512]{1,0:T(8,128)(2,1)S(1)} %get-tuple-element.17.v_ref.refs_4_, ...), custom_call_target="tpu_custom_call" | custom-call | flops 2415919104 | bytes 3145728 | tf_op jit(solution)/shard_map/context_anchor/pallas_call | solution.py:366
  135.6 0.7 query_sum.3
  (38 shorter events, 1.8 us)
Async XLA Ops:
  0.6 1.4 %copy-start.2 = (bf16[8,2048]{1,0:T(8,128)(2,1)S(1)}, bf16[8,2048]{1,0:T(8,128)(2,1)}, u32[]{:S(2)}) copy-start(bf16[8,2048]{1,0:T(8,128)(2,1)} %known_ref.1) | copy-start | bytes 98308
  0.6 3.7 %copy-start = (bf16[768,2048]{1,0:T(8,128)(2,1)S(1)}, bf16[768,2048]{1,0:T(8,128)(2,1)}, u32[]{:S(2)}) copy-start(bf16[768,2048]{1,0:T(8,128)(2,1)} %refs_1_.11) | copy-start | bytes 9437188
  2.0 3.5 %collective-permute-start = (bf16[768,256]{1,0:T(8,128)(2,1)S(1)}, bf16[768,256]{1,0:T(8,128)(2,1)S(1)}, u32[]{:S(2)}, u32[]{:S(2)}) collective-permute-start(bf16[768,256]{1,0:T(8,128)(2,1)S(1)} %get-tuple-element.15.second_ref.v_ref), channel_id=1, source_target_pairs={{0,4},{4,0},{8,12},{12,8},{16,20},{20,16},{24,28},{28,24},{1,5},{5... | collective-permute-start | bytes 1179656 | tf_op jit(solution)/shard_map/ppermute | solution.py:43
  2.0 1.7 %collective-permute-start.1 = (bf16[8,2048]{1,0:T(8,128)(2,1)S(1)}, bf16[8,2048]{1,0:T(8,128)(2,1)S(1)}, u32[]{:S(2)}, u32[]{:S(2)}) collective-permute-start(bf16[8,2048]{1,0:T(8,128)(2,1)S(1)} %copy-done.2), channel_id=1, source_target_pairs={{0,4},{4,0},{8,12},{12,8},{16,20},{20,16},{24,28},{28,24},{1,5},{5... | collective-permute-start | bytes 98312 | tf_op jit(solution)/shard_map/ppermute | solution.py:43
  3.8 4.3 %collective-permute-start.3 = (bf16[16,2048]{1,0:T(8,128)(2,1)S(1)}, bf16[16,2048]{1,0:T(8,128)(2,1)S(1)}, u32[]{:S(2)}, u32[]{:S(2)}) collective-permute-start(bf16[16,2048]{1,0:T(8,128)(2,1)S(1)} %query_join.2.rest_0_.known_ref), channel_id=1, source_target_pairs={{0,8},{4,20},{8,0},{12,28},{16,24},{20,4},{24,16},{28,12},{1,9},{5... | collective-permute-start | bytes 196616 | tf_op jit(solution)/shard_map/ppermute | solution.py:43
  5.6 7.1 %collective-permute-start.2 = (bf16[768,128]{1,0:T(8,128)(2,1)S(1)}, bf16[768,128]{1,0:T(8,128)(2,1)S(1)}, u32[]{:S(2)}, u32[]{:S(2)}) collective-permute-start(bf16[768,128]{1,0:T(8,128)(2,1)S(1)} %get-tuple-element.18.rest_0_.one_ref), channel_id=1, source_target_pairs={{0,8},{4,20},{8,0},{12,28},{16,24},{20,4},{24,16},{28,12},{1,9},{5... | collective-permute-start | bytes 589832 | tf_op jit(solution)/shard_map/ppermute | solution.py:43
  8.1 5.9 %collective-permute-start.5 = (bf16[32,2048]{1,0:T(8,128)(2,1)S(1)}, bf16[32,2048]{1,0:T(8,128)(2,1)S(1)}, u32[]{:S(2)}, u32[]{:S(2)}) collective-permute-start(bf16[32,2048]{1,0:T(8,128)(2,1)S(1)} %query_join.3.rest_0_.known_ref), channel_id=1, source_target_pairs={{0,16},{4,12},{8,24},{12,4},{16,0},{20,28},{24,8},{28,20},{1,17},{... | collective-permute-start | bytes 393224 | tf_op jit(solution)/shard_map/ppermute | solution.py:43
  8.7 20.5 %collective-permute-start.7 = (bf16[768,128]{1,0:T(8,128)(2,1)S(1)}, bf16[768,128]{1,0:T(8,128)(2,1)S(1)}, u32[]{:S(2)}, u32[]{:S(2)}) collective-permute-start(bf16[768,128]{1,0:T(8,128)(2,1)S(1)} %get-tuple-element.21.one_ref), channel_id=1, source_target_pairs={{0,8},{4,20},{8,0},{12,28},{16,24},{20,4},{24,16},{28,12},{1,9},{5... | collective-permute-start | bytes 589832 | tf_op jit(solution)/shard_map/ppermute | solution.py:43
  11.9 2.1 %copy-start.3 = (s32[8]{0:T(128)S(1)}, s32[8]{0:T(128)}, u32[]{:S(2)}) copy-start(s32[8]{0:T(128)} %refs_0_.11) | copy-start | bytes 100
  11.9 2.1 %copy-start.4 = (bf16[2,8,1024]{2,1,0:T(8,128)(2,1)S(1)}, bf16[2,8,1024]{2,1,0:T(8,128)(2,1)}, u32[]{:S(2)}) copy-start(bf16[2,8,1024]{2,1,0:T(8,128)(2,1)} %self_ref.1) | copy-start | bytes 98308
  12.7 8.9 %collective-permute-start.4 = (bf16[768,128]{1,0:T(8,128)(2,1)S(1)}, bf16[768,128]{1,0:T(8,128)(2,1)S(1)}, u32[]{:S(2)}, u32[]{:S(2)}) collective-permute-start(bf16[768,128]{1,0:T(8,128)(2,1)S(1)} %anchor_relay.6.rest_0_.one_ref), channel_id=1, source_target_pairs={{0,16},{4,12},{8,24},{12,4},{16,0},{20,28},{24,8},{28,20},{1,17},{... | collective-permute-start | bytes 589832 | tf_op jit(solution)/shard_map/ppermute | solution.py:43
  19.2 2.0 %collective-permute-start.6 = (bf16[64,1152]{1,0:T(8,128)(2,1)S(1)}, bf16[64,1152]{1,0:T(8,128)(2,1)S(1)}, u32[]{:S(2)}, u32[]{:S(2)}) collective-permute-start(bf16[64,1152]{1,0:T(8,128)(2,1)S(1)} %get-tuple-element.20), channel_id=1, source_target_pairs={{0,4},{4,0},{8,12},{12,8},{16,20},{20,16},{24,28},{28,24},{1,5},{5... | collective-permute-start | bytes 442376 | tf_op jit(solution)/shard_map/ppermute | solution.py:43
  21.9 8.2 %collective-permute-start.11 = (bf16[768,128]{1,0:T(8,128)(2,1)S(1)}, bf16[768,128]{1,0:T(8,128)(2,1)S(1)}, u32[]{:S(2)}, u32[]{:S(2)}) collective-permute-start(bf16[768,128]{1,0:T(8,128)(2,1)S(1)} %anchor_relay.7.rest_0_.first_ref), channel_id=1, source_target_pairs={{0,4},{4,0},{8,12},{12,8},{16,20},{20,16},{24,28},{28,24},{1,5},{5... | collective-permute-start | bytes 589832 | tf_op jit(solution)/shard_map/ppermute | solution.py:43
  22.5 5.1 %collective-permute-start.8 = (bf16[64,1152]{1,0:T(8,128)(2,1)S(1)}, bf16[64,1152]{1,0:T(8,128)(2,1)S(1)}, u32[]{:S(2)}, u32[]{:S(2)}) collective-permute-start(bf16[64,1152]{1,0:T(8,128)(2,1)S(1)} %query_merge.3.rest_0_.one_ref), channel_id=1, source_target_pairs={{0,8},{4,20},{8,0},{12,28},{16,24},{20,4},{24,16},{28,12},{1,9},{5... | collective-permute-start | bytes 442376 | tf_op jit(solution)/shard_map/ppermute | solution.py:43
  27.9 24.7 %collective-permute-start.10 = (bf16[64,1152]{1,0:T(8,128)(2,1)S(1)}, bf16[64,1152]{1,0:T(8,128)(2,1)S(1)}, u32[]{:S(2)}, u32[]{:S(2)}) collective-permute-start(bf16[64,1152]{1,0:T(8,128)(2,1)S(1)} %query_merge.4.rest_0_.one_ref), channel_id=1, source_target_pairs={{0,16},{4,12},{8,24},{12,4},{16,0},{20,28},{24,8},{28,20},{1,17},{... | collective-permute-start | bytes 442376 | tf_op jit(solution)/shard_map/ppermute | solution.py:43
  29.2 23.9 %collective-permute-start.9 = (bf16[768,128]{1,0:T(8,128)(2,1)S(1)}, bf16[768,128]{1,0:T(8,128)(2,1)S(1)}, u32[]{:S(2)}, u32[]{:S(2)}) collective-permute-start(bf16[768,128]{1,0:T(8,128)(2,1)S(1)} %anchor_relay.8.rest_0_.one_ref), channel_id=1, source_target_pairs={{0,16},{4,12},{8,24},{12,4},{16,0},{20,28},{24,8},{28,20},{1,17},{... | collective-permute-start | bytes 589832 | tf_op jit(solution)/shard_map/ppermute | solution.py:43
  52.9 11.8 %collective-permute-start.13 = (bf16[64,1024]{1,0:T(8,128)(2,1)S(1)}, bf16[64,1024]{1,0:T(8,128)(2,1)S(1)}, u32[]{:S(2)}, u32[]{:S(2)}) collective-permute-start(bf16[64,1024]{1,0:T(8,128)(2,1)S(1)} %query_merge.5.rest_0_.own_ref), channel_id=1, source_target_pairs={{0,4},{4,0},{8,12},{12,8},{16,20},{20,16},{24,28},{28,24},{1,5},{5... | collective-permute-start | bytes 393224 | tf_op jit(solution)/shard_map/ppermute | solution.py:43
  53.1 11.7 %copy-start.1 = (bf16[2048,1024]{1,0:T(8,128)(2,1)S(1)}, bf16[2048,1024]{1,0:T(8,128)(2,1)}, u32[]{:S(2)}) copy-start(bf16[2048,1024]{1,0:T(8,128)(2,1)} %w_ref.1) | copy-start | bytes 12582916
  53.1 35.7 %collective-permute-start.12 = (bf16[768,128]{1,0:T(8,128)(2,1)S(1)}, bf16[768,128]{1,0:T(8,128)(2,1)S(1)}, u32[]{:S(2)}, u32[]{:S(2)}) collective-permute-start(bf16[768,128]{1,0:T(8,128)(2,1)S(1)} %anchor_relay.9.refs_7_.first_ref), channel_id=1, source_target_pairs={{0,4},{4,0},{8,12},{12,8},{16,20},{20,16},{24,28},{28,24},{1,5},{5... | collective-permute-start | bytes 589832 | tf_op jit(solution)/shard_map/ppermute | solution.py:43
  75.9 34.4 %collective-permute-start.14 = (bf16[64,1024]{1,0:T(8,128)(2,1)S(1)}, bf16[64,1024]{1,0:T(8,128)(2,1)S(1)}, u32[]{:S(2)}, u32[]{:S(2)}) collective-permute-start(bf16[64,1024]{1,0:T(8,128)(2,1)S(1)} %query_project.1.rest_0_.refs_7_.refs_8_.one_ref), channel_id=1, source_target_pairs={{0,1},{1,0},{2,3},{3,2},{4,5},{5,4},{6,7},{7,6},{8,9},{9,8},{10,11... | collective-permute-start | bytes 393224 | tf_op jit(solution)/shard_map/ppermute | solution.py:43
  110.4 25.2 %collective-permute-start.15 = (bf16[64,1024]{1,0:T(8,128)(2,1)S(1)}, bf16[64,1024]{1,0:T(8,128)(2,1)S(1)}, u32[]{:S(2)}, u32[]{:S(2)}) collective-permute-start(bf16[64,1024]{1,0:T(8,128)(2,1)S(1)} %query_sum.2.refs_12_.refs_13_.one_ref), channel_id=1, source_target_pairs={{0,2},{1,3},{2,0},{3,1},{4,6},{5,7},{6,4},{7,5},{8,10},{9,11},{10,... | collective-permute-start | bytes 393224 | tf_op jit(solution)/shard_map/ppermute | solution.py:43

commit v7 on v6

--- a/solution.py
+++ b/solution.py
@@ -39,6 +39,10 @@
     return lax.psum(kept, axis)
 
 
+def send(value, axis, pairs):
+    return lax.ppermute(value, axis, pairs)
+
+
 def swap(value, axis, size, even, odd):
     return lax.ppermute(value, axis, [(i, i ^ (odd if i & 1 else even)) for i in range(size)])
 
@@ -177,8 +181,12 @@
     return 256 if slab % 256 == 0 else slab
 
 
-def body_size(count, most):
-    return max(x for x in range(1, most + 1) if count % x == 0)
+def body_size(first, count, per_kv, most):
+    def fits(size):
+        bodies = range(first, first + count, size)
+        return count % size == 0 and all(x // per_kv == (x + size - 1) // per_kv for x in bodies)
+
+    return max(x for x in range(1, most + 1) if fits(x))
 
 
 def own_kernel(first, count, per_kv, q_ref, k_ref, v_ref, *rest):
@@ -186,7 +194,7 @@
     slab = q_ref.shape[0]
     tile = row_tile(slab)
     half = tile // 2
-    heads = body_size(count, 4)
+    heads = body_size(first, count, per_kv, 4)
     rows = lax.broadcasted_iota(jnp.int32, (half, half), 0)
     cols = lax.broadcasted_iota(jnp.int32, (half, half), 1)
     causal = cols <= rows
@@ -241,15 +249,19 @@
     )(ctx_q, own_k, own_v, *after)
 
 
-def anchor_kernel(first, count, base, per_kv, last, befores, *refs):
-    lengths_ref, q_ref, state_ref, k_ref, v_ref, keys, vaug = refs[:7]
-    earlier = refs[7 : 7 + len(befores)]
+def anchor_kernel(first, count, bases, per_kv, last, befores, *refs):
+    lengths_ref, q_ref, k_ref, v_ref, keys, vaug = refs[:6]
+    state_refs = refs[6 : 6 + len(bases)]
+    earlier = refs[6 + len(bases) : 6 + len(bases) + len(befores)]
     if last:
         full_ref, out_ref, sems = refs[-3:]
     else:
         out_ref = refs[-1]
     slab = q_ref.shape[0]
-    heads = body_size(count, 2 if last else 4)
+    heads = body_size(first, count, per_kv, 2 if last else 4)
+    tile = row_tile(slab)
+    chunks = slab // tile
+    units = [(h, j) for h in range(heads) for j in range(chunks)]
     kv = first // per_kv
     host = lax.axis_index("hst")
     own_len = lengths_ref[host]
@@ -267,12 +279,14 @@
             at = (first + start + h) * HD
             return q_ref[:, at : at + HD]
 
-        def scores(h):
-            return dot_t(twice(query_of(h)), keys[...])
+        def scores(h, j):
+            return dot_t(twice(query_of(h)), keys[j * tile : (j + 1) * tile, :])
 
         def state_of(h):
-            at = (first - base + start + h) * 2 * HD
-            return state_ref[:, at : at + 2 * HD]
+            head = first + start + h
+            n = max(n for n, base in enumerate(bases) if base <= head)
+            at = (head - bases[n]) * 2 * HD
+            return state_refs[n][:, at : at + 2 * HD]
 
         def finish(h, total, worst):
             sums = total[:, HD:]
@@ -295,12 +309,13 @@
         @pl.when(host > 0)
         def _():
             worst = jnp.ones((slab, HD), F32)
-            current = scores(0)
-            for h in range(heads):
-                following = scores(h + 1) if h + 1 < heads else None
-                expo = jnp.exp2(current).astype(BF)
-                total = dot(expo, vaug[...]) + state_of(h)
-                worst = finish(h, total, worst)
+            current = scores(*units[0])
+            for at, (h, j) in enumerate(units):
+                following = scores(*units[at + 1]) if at + 1 < len(units) else None
+                part = dot(jnp.exp2(current).astype(BF), vaug[j * tile : (j + 1) * tile, :])
+                total = (state_of(h) if j == 0 else total) + part
+                if j == chunks - 1:
+                    worst = finish(h, total, worst)
                 current = following
             check(worst)
 
@@ -326,7 +341,7 @@
 
 def exact_block(q_head, out_head, heads, host, own_len, kv, q_ref, k_ref, v_ref, keys, vaug, out_ref):
     slab = q_ref.shape[0]
-    tile = 128
+    tile = 64
 
     def body(i, carry):
         h = lax.div(i, slab // tile)
@@ -352,10 +367,12 @@
     lax.fori_loop(0, heads * (slab // tile), body, 0)
 
 
-def anchor_part(lengths, ctx_q, state, base, own_k, own_v, anchor, first, count, per_kv, befores=None, after=()):
+def anchor_part(lengths, ctx_q, states, own_k, own_v, anchor, first, count, per_kv, befores=None, after=()):
     slab, width = ctx_q.shape
     work = count * slab * slab
     last = befores is not None
+    ends = {x: x + y.shape[1] // (2 * HD) for x, y in states.items()}
+    bases = tuple(x for x in sorted(states) if x < first + count and ends[x] > first)
     earlier = list(befores.values()) if last else []
     places = tuple((at, x.shape[1] // HD) for at, x in befores.items()) if last else ()
     results = jax.ShapeDtypeStruct((slab, count * HD), BF)
@@ -364,9 +381,9 @@
         scratch = [pltpu.VMEM(results.shape, BF), pltpu.SemaphoreType.DMA((len(earlier) + count,))]
         results = jax.ShapeDtypeStruct((slab, width), BF)
     return pl.pallas_call(
-        functools.partial(anchor_kernel, first, count, base, per_kv, last, places),
+        functools.partial(anchor_kernel, first, count, bases, per_kv, last, places),
         out_shape=results,
-        in_specs=[SMEM] + [VMEM] * (6 + len(earlier)) + [ANY] * len(after),
+        in_specs=[SMEM] + [VMEM] * (5 + len(bases) + len(earlier)) + [ANY] * len(after),
         out_specs=ANY if last else VMEM,
         scratch_shapes=scratch,
         compiler_params=params(),
@@ -374,7 +391,7 @@
             flops=work * HD * 8, bytes_accessed=count * slab * HD * 8, transcendentals=work
         ),
         name="context_anchor",
-    )(lengths, ctx_q, state, own_k, own_v, *anchor, *earlier, *after)
+    )(lengths, ctx_q, own_k, own_v, *anchor, *[states[x] for x in bases], *earlier, *after)
 
 
 PART = 16
@@ -478,16 +495,45 @@
 
     @pl.when(jnp.logical_not(jnp.min(worst) > TINY))
     def _():
-        key_ids = lax.broadcasted_iota(jnp.int32, (rows, slab), 1)
+        key_ids = lax.broadcasted_iota(jnp.int32, (query_count, slab), 1)
+        heads_ok = (host * q_rows + lane <= query_ids) & (lane < q_rows)
         for j in range(columns // HD):
-            near, selves, self_values = operands(j)
-            near = jnp.where(key_ids < own_len, near, MASKED)
-            peak = jnp.maximum(jnp.max(near, 1, keepdims=True), jnp.max(selves, 1, keepdims=True))
-            near = jnp.exp2(near - peak).astype(BF)
-            selves = jnp.exp2(selves - peak).astype(BF)
-            total = dot(near, vaug[:, 2 * j * HD : (2 * j + 2) * HD]) + dot(selves, self_values)
-            sums = total[:, HD:]
-            store(j, total[:, :HD] / sums, peak + jnp.log2(sums))
+            cols = slice(j * HD, (j + 1) * HD)
+            self_keys = jnp.concatenate([selves_kv[0][:, cols], pad], 0).astype(BF)
+            self_values = jnp.concatenate([selves_kv[1][:, cols], pad], 0).astype(BF)
+            self_values = jnp.concatenate([self_values, jnp.ones((HD, HD), BF)], 1)
+            mine = odd if j else jnp.logical_not(odd)
+
+            def body(h, stats):
+                at = pl.ds(pl.multiple_of((j * per_kv + h) * query_count, query_count), query_count)
+                queries = q_all[at, :]
+                near = dot_t(twice(queries), k_ref[:, 2 * j * HD : 2 * (j + 1) * HD])
+                near = jnp.where(key_ids < own_len, near, MASKED)
+                selves = jnp.where(heads_ok, dot_t(queries, self_keys) * SCALE2, MASKED)
+                peak = jnp.maximum(jnp.max(near, 1, keepdims=True), jnp.max(selves, 1, keepdims=True))
+                near = jnp.exp2(near - peak).astype(BF)
+                selves = jnp.exp2(selves - peak).astype(BF)
+                total = dot(near, vaug[:, 2 * j * HD : (2 * j + 2) * HD]) + dot(selves, self_values)
+                result = (total[:, :HD] / total[:, HD:]).astype(BF)
+
+                def put(out_ref):
+                    def run():
+                        out_ref[:, lanes(h, HD)] = result
+
+                    return run
+
+                choose(mine, put(keep_ref), put(send_ref))
+                return jnp.where(lane == h, peak + jnp.log2(total[:, HD:]), stats)
+
+            stats = lax.fori_loop(0, per_kv, body, jnp.zeros((query_count, HD), F32))
+
+            def put_level(out_ref):
+                def run():
+                    write_level(out_ref, per_kv * HD, stats)
+
+                return run
+
+            choose(mine, put_level(keep_ref), put_level(send_ref))
 
 
 def source_part(lengths, own_k, own_v, query_kv, known, landed, q_rows, per_kv, after=()):
@@ -628,7 +674,7 @@
             cols = slice(2 * first // per_kv * HD, 2 * (first // per_kv + 1) * HD)
             last = first + per_kv == local_heads
             results[first] = anchor_part(
-                lengths, ctx_q, state, 0, own_k, own_v, [x[:, cols] for x in anchor],
+                lengths, ctx_q, {0: state}, own_k, own_v, [x[:, cols] for x in anchor],
                 first, per_kv, per_kv, dict(results) if last else None,
             )
         return results[first], query_out
@@ -661,7 +707,7 @@
     landed = swap(queries, "hst", hosts, *along[0])
     done = own(0, 2, (queries,))
     parts = list(relay(is_even, own_k, value_landed, (done,), kv_local))
-    parts_landed = [swap(x, "hst", hosts, *along[0]) for x in parts]
+    parts_landed = [send(x, "hst", [(0, 2), (1, 5)]) for x in parts]
     queries = join(near_low, queries, landed, (parts[0],))
     landed = swap(queries, "hst", hosts, *along[1])
     done = own(2, 6, (queries,))
@@ -669,7 +715,7 @@
 
     def pass_on(kv, after):
         (parts[kv],) = relay(source_first, parts[kv], parts_landed[kv], after)
-        parts_landed[kv] = swap(parts[kv], "hst", hosts, *along[1])
+        parts_landed[kv] = send(parts[kv], "hst", [(0, 4), (2, 6), (1, 3), (5, 7)])
         return parts[kv]
 
     def complete(kv, after):
@@ -678,36 +724,35 @@
         return held
 
     done = pass_on(0, (done,))
-    keep, send = source_part(lengths, own_keys, own_v, query_kv, queries, landed, q_rows, per_kv, (done,))
-    landed = swap(send, "hst", hosts, 1, 1)
+    keep, give = source_part(lengths, own_keys, own_v, query_kv, queries, landed, q_rows, per_kv, (done,))
+    landed = swap(give, "hst", hosts, 1, 1)
     done = own(8, 4, (keep,))
+    done = pass_on(1, (done,))
+    done = complete(0, (done,))
     source = merge_part(keep, landed, False, (done,))
     landed = swap(source, "hst", hosts, *along[0])
-    done = complete(0, (source,))
-    done = own(12, 4, (done,))
-    source = merge_part(source, landed, False, (done,))
-    landed = swap(source, "hst", hosts, *along[1])
-    done = pass_on(1, (source,))
+    done = own(12, 4, (source,))
     anchor[0] = prepare(*anchor[0], True, (done,))
     results = {}
 
     def anchors(first, count, after, last=False):
-        base = max(x for x in states if x <= first)
         results[first] = anchor_part(
-            lengths, ctx_q, states[base], base, own_keys, own_values, anchor[first // per_kv],
+            lengths, ctx_q, states, own_keys, own_values, anchor[first // per_kv],
             first, count, per_kv, dict(results) if last else None, after,
         )
         return results[first]
 
     done = anchors(0, 2, ())
-    done = anchors(2, 2, (done,))
+    source = merge_part(source, landed, False, (done,))
+    landed = swap(source, "hst", hosts, *along[1])
+    done = anchors(2, 4, (source,))
     source = merge_part(source, landed, True, (done,))
     landed = swap(source, "hst", hosts, 1, 1)
     done = complete(1, (source,))
-    done = anchors(4, 2, (done,))
+    done = anchors(6, 2, (done,))
     terms = project_part(source, landed, out_weight, (done,))
     anchor[1] = prepare(*anchor[1], True, (terms,))
-    shares = [[(12, 4, True)], [(6, 2, False), (8, 4, False)]]
+    shares = [[(12, 4, True)], [(8, 4, False)]]
     step = 1
     while step < groups:
         landed = swap(terms, "tp", groups, step, step)

time: 139 us -> 185 us (1.33); the launches traced: 137 us -> 184 us
  Pallas kernels: 117 us -> 165 us
  starting transfers between devices: 13.7 us -> 15.9 us
    pallas_call x6 -> x5, Pallas kernels: 88.6 us -> 140 us  [anchor_part(): pl.pallas_call(functools.partial(anchor_kernel, first, count, bases, per_...]
    pallas_call x1, Pallas kernels: 11.1 us -> 0.87 us  [project_part(): pl.pallas_call(kernel, out_shape=jax.ShapeDtypeStruct((rows, columns), BF...]
    pallas_call x1, Pallas kernels: 5.24 us -> 11.7 us  [source_part(): pl.pallas_call(functools.partial(source_kernel, per_kv, q_rows, H // KVH)...]
    ppermute x0 -> x4, starting transfers between devices: none -> 3.91 us  [send(): return lax.ppermute(value, axis, pairs)]
    ppermute x16 -> x12, starting transfers between devices: 13.7 us -> 12 us  [swap(): lax.ppermute(value, axis, [(i, i ^ (odd if i & 1 else even)) for i in ran...]
    ppermute x16 -> x12, waiting for transfers between devices: 4.45 us -> 2.8 us  [swap(): lax.ppermute(value, axis, [(i, i ^ (odd if i & 1 else even)) for i in ran...]
  transfers between devices with their start and end apart: 16 -> 16, of which waited for: 4 -> 2; matrix products, arithmetic and copies ran while one was open for 0% -> 0% of each run, Pallas kernels for 84% -> 88%
where the time goes in v7:
time: 185 us; the launch traced here: 184 us
  Pallas kernels  165 us (89%)
  starting transfers between devices  15.9 us (9%)
  waiting for transfers between devices  2.81 us (2%)
    pallas_call x5, Pallas kernels, anchor_part(): pl.pallas_call(functools.partial(anchor_kernel, first, count, bases, per_...  140 us
    ppermute x12, starting transfers between devices, swap(): lax.ppermute(value, axis, [(i, i ^ (odd if i & 1 else even)) for i in ran...  12 us
    pallas_call x1, Pallas kernels, source_part(): pl.pallas_call(functools.partial(source_kernel, per_kv, q_rows, H // KVH)...  11.7 us
    pallas_call x4, Pallas kernels, own_part(): pl.pallas_call(functools.partial(own_kernel, first, count, per_kv), out_s...  8.14 us
    ppermute x4, starting transfers between devices, send(): return lax.ppermute(value, axis, pairs)  3.91 us
  transfers between devices with their start and end apart: 16, of which 2 were waited for; matrix products, arithmetic and copies ran while one was open for 0% of the time, Pallas kernels for 88%

profile of v7, /device:TPU:6, one launch (start us, length us, event | category | flops | bytes accessed | tf_op | source)
XLA Modules:
  0.0 184.5 jit_solution(16072475989711231294)
XLA Ops:
  0.6 1.3 pick_columns.1
  2.0 0.5 collective-permute-start.1
  2.5 0.3 operands.3
  2.8 1.0 collective-permute-done.1.landed_ref
  3.8 0.5 collective-permute-start.3
  4.3 1.1 context_own.4.rest_0_.refs_6_
  5.6 0.7 collective-permute-start.5
  6.3 1.8 collective-permute-done.3.landed_ref
  8.1 0.6 collective-permute-start.4
  8.7 0.7 collective-permute-start.2
  9.3 3.1 %context_own.5.rest_0_.refs_6_ = f32[768,1536]{1,0:T(8,128)S(1)} custom-call(bf16[768,2048]{1,0:T(8,128)(2,1)S(1)} %copy-done, bf16[768,512]{1,0:T(8,128)(2,1)S(1)} %get-tuple-element.16.rest_0_.k_ref.refs_2_, bf16[768,512]{1,0:T(8,128)(2,1)S(1)} %get-tuple-element.17.v_ref.refs_3_, bf16[32,2048]{1,0:T(8,128)(2,1)S(1)} %query_join.3.rest_0_.known_ref), custom_call_target="tpu_custom_call" | custom-call | flops 2415919104 | bytes 3538944 | tf_op jit(solution)/shard_map/context_own/pallas_call | solution.py:239
  12.5 1.3 collective-permute-start.8
  13.8 11.7 %query_source.1 = (bf16[64,1152]{1,0:T(8,128)(2,1)S(1)}, bf16[64,1152]{1,0:T(8,128)(2,1)S(1)}) custom-call(s32[8]{0:T(128)S(1)} %copy-done.3, bf16[768,512]{1,0:T(8,128)(2,1)S(1)} %get-tuple-element.16.rest_0_.k_ref.refs_2_, bf16[768,256]{1,0:T(8,128)(2,1)S(1)} %get-tuple-element.15.second_ref.v_ref, bf16[2,8,1024]{2,1,0:T(8,128)(2,1)S(1)} %copy-done.4, ...), custom_call_target="tpu_custom_call" | custom-call | flops 805306368 | bytes 2097152 | tf_op jit(solution)/shard_map/query_source/pallas_call | solution.py:544
  25.6 2.0 %context_own.6.rest_0_.refs_6_ = f32[768,1024]{1,0:T(8,128)S(1)} custom-call(bf16[768,2048]{1,0:T(8,128)(2,1)S(1)} %copy-done, bf16[768,512]{1,0:T(8,128)(2,1)S(1)} %get-tuple-element.16.rest_0_.k_ref.refs_2_, bf16[768,512]{1,0:T(8,128)(2,1)S(1)} %get-tuple-element.17.v_ref.refs_3_, bf16[64,1152]{1,0:T(8,128)(2,1)S(1)} %get-tuple-element.20.rest_0_.one_ref), custom_call_target="tpu_custom_call" | custom-call | flops 1610612736 | bytes 2359296 | tf_op jit(solution)/shard_map/context_own/pallas_call | solution.py:239
  27.7 0.6 collective-permute-start.10
  28.2 1.3 collective-permute-start.6
  29.5 0.3 query_merge.3.rest_0_.one_ref
  29.9 1.0 collective-permute-start.9
  30.9 2.0 %context_own.7.rest_0_.refs_6_ = f32[768,1024]{1,0:T(8,128)S(1)} custom-call(bf16[768,2048]{1,0:T(8,128)(2,1)S(1)} %copy-done, bf16[768,512]{1,0:T(8,128)(2,1)S(1)} %get-tuple-element.16.rest_0_.k_ref.refs_2_, bf16[768,512]{1,0:T(8,128)(2,1)S(1)} %get-tuple-element.17.v_ref.refs_3_, bf16[64,1152]{1,0:T(8,128)(2,1)S(1)} %query_merge.3.rest_0_.one_ref), custom_call_target="tpu_custom_call" | custom-call | flops 1610612736 | bytes 2359296 | tf_op jit(solution)/shard_map/context_own/pallas_call | solution.py:239
  33.0 17.9 %context_anchor.5.rest_0_.refs_7_ = bf16[768,256]{1,0:T(8,128)(2,1)S(1)} custom-call(s32[8]{0:T(128)S(1)} %copy-done.3, bf16[768,2048]{1,0:T(8,128)(2,1)S(1)} %copy-done, bf16[768,512]{1,0:T(8,128)(2,1)S(1)} %get-tuple-element.16.rest_0_.k_ref.refs_2_, bf16[768,512]{1,0:T(8,128)(2,1)S(1)} %get-tuple-element.17.v_ref.refs_3_, ...), custom_call_target="tpu_custom_call" | custom-call | flops 1207959552 | bytes 1572864 | tf_op jit(solution)/shard_map/context_anchor/pallas_call | solution.py:383
  50.9 0.3 query_merge.4.refs_7_.one_ref
  51.2 3.8 %collective-permute-start.11 = (bf16[64,1152]{1,0:T(8,128)(2,1)S(1)}, bf16[64,1152]{1,0:T(8,128)(2,1)S(1)}, u32[]{:S(2)}, u32[]{:S(2)}) collective-permute-start(bf16[64,1152]{1,0:T(8,128)(2,1)S(1)} %query_merge.4.refs_7_.one_ref), channel_id=1, source_target_pairs={{0,16},{4,12},{8,24},{12,4},{16,0},{20,28},{24,8},{28,20},{1,17},{... | collective-permute-start | bytes 442376 | tf_op jit(solution)/shard_map/ppermute | solution.py:47
  55.0 34.3 %context_anchor.6.rest_0_.refs_8_ = bf16[768,512]{1,0:T(8,128)(2,1)S(1)} custom-call(s32[8]{0:T(128)S(1)} %copy-done.3, bf16[768,2048]{1,0:T(8,128)(2,1)S(1)} %copy-done, bf16[768,512]{1,0:T(8,128)(2,1)S(1)} %get-tuple-element.16.rest_0_.k_ref.refs_2_, bf16[768,512]{1,0:T(8,128)(2,1)S(1)} %get-tuple-element.17.v_ref.refs_3_, ...), custom_call_target="tpu_custom_call" | custom-call | flops 2415919104 | bytes 3145728 | tf_op jit(solution)/shard_map/context_anchor/pallas_call | solution.py:383
  89.3 0.3 query_merge.5.rest_0_.own_ref
  89.8 0.5 collective-permute-start.13
  90.3 17.7 %context_anchor.7.rest_0_.refs_9_ = bf16[768,256]{1,0:T(8,128)(2,1)S(1)} custom-call(s32[8]{0:T(128)S(1)} %copy-done.3, bf16[768,2048]{1,0:T(8,128)(2,1)S(1)} %copy-done, bf16[768,512]{1,0:T(8,128)(2,1)S(1)} %get-tuple-element.16.rest_0_.k_ref.refs_2_, bf16[768,512]{1,0:T(8,128)(2,1)S(1)} %get-tuple-element.17.v_ref.refs_3_, ...), custom_call_target="tpu_custom_call" | custom-call | flops 1207959552 | bytes 1572864 | tf_op jit(solution)/shard_map/context_anchor/pallas_call | solution.py:383
  108.0 0.9 query_project.1.rest_0_.refs_7_.refs_8_.one_ref
  108.9 1.6 collective-permute-start.14
  110.7 34.8 %context_anchor.8.rest_0_.refs_10_ = bf16[768,512]{1,0:T(8,128)(2,1)S(1)} custom-call(s32[8]{0:T(128)S(1)} %copy-done.3, bf16[768,2048]{1,0:T(8,128)(2,1)S(1)} %copy-done, bf16[768,512]{1,0:T(8,128)(2,1)S(1)} %get-tuple-element.16.rest_0_.k_ref.refs_2_, bf16[768,512]{1,0:T(8,128)(2,1)S(1)} %get-tuple-element.17.v_ref.refs_3_, ...), custom_call_target="tpu_custom_call" | custom-call | flops 2415919104 | bytes 3145728 | tf_op jit(solution)/shard_map/context_anchor/pallas_call | solution.py:383
  145.5 2.7 %collective-permute-start.15 = (bf16[64,1024]{1,0:T(8,128)(2,1)S(1)}, bf16[64,1024]{1,0:T(8,128)(2,1)S(1)}, u32[]{:S(2)}, u32[]{:S(2)}) collective-permute-start(bf16[64,1024]{1,0:T(8,128)(2,1)S(1)} %query_sum.2.refs_11_.refs_12_.one_ref), channel_id=1, source_target_pairs={{0,2},{1,3},{2,0},{3,1},{4,6},{5,7},{6,4},{7,5},{8,10},{9,11},{10,... | collective-permute-start | bytes 393224 | tf_op jit(solution)/shard_map/ppermute | solution.py:47
  148.2 35.6 %context_anchor.9 = bf16[768,2048]{1,0:T(8,128)(2,1)} custom-call(s32[8]{0:T(128)S(1)} %copy-done.3, bf16[768,2048]{1,0:T(8,128)(2,1)S(1)} %copy-done, bf16[768,512]{1,0:T(8,128)(2,1)S(1)} %get-tuple-element.16.rest_0_.k_ref.refs_2_, bf16[768,512]{1,0:T(8,128)(2,1)S(1)} %get-tuple-element.17.v_ref.refs_3_, bf16[768,256]{1,0:T(8,128)(2,1)S(1)} %get-tuple-element.24.refs_4_, ...), custom_call_target="tpu_custom_call" | custom-call | flops 2415919104 | bytes 3145728 | tf_op jit(solution)/shard_map/context_anchor/pallas_call | solution.py:383
  183.8 0.7 query_sum.3
  (37 shorter events, 0.9 us)
Async XLA Ops:
  0.6 1.4 copy-start.2
  0.6 3.7 %copy-start = (bf16[768,2048]{1,0:T(8,128)(2,1)S(1)}, bf16[768,2048]{1,0:T(8,128)(2,1)}, u32[]{:S(2)}) copy-start(bf16[768,2048]{1,0:T(8,128)(2,1)} %refs_1_.9) | copy-start | bytes 9437188
  2.0 3.5 %collective-permute-start = (bf16[768,256]{1,0:T(8,128)(2,1)S(1)}, bf16[768,256]{1,0:T(8,128)(2,1)S(1)}, u32[]{:S(2)}, u32[]{:S(2)}) collective-permute-start(bf16[768,256]{1,0:T(8,128)(2,1)S(1)} %get-tuple-element.15.second_ref.v_ref), channel_id=1, source_target_pairs={{0,4},{4,0},{8,12},{12,8},{16,20},{20,16},{24,28},{28,24},{1,5},{5... | collective-permute-start | bytes 1179656 | tf_op jit(solution)/shard_map/ppermute | solution.py:47
  2.0 1.7 collective-permute-start.1
  3.8 4.3 %collective-permute-start.3 = (bf16[16,2048]{1,0:T(8,128)(2,1)S(1)}, bf16[16,2048]{1,0:T(8,128)(2,1)S(1)}, u32[]{:S(2)}, u32[]{:S(2)}) collective-permute-start(bf16[16,2048]{1,0:T(8,128)(2,1)S(1)} %query_join.2.rest_0_.known_ref), channel_id=1, source_target_pairs={{0,8},{4,20},{8,0},{12,28},{16,24},{20,4},{24,16},{28,12},{1,9},{5... | collective-permute-start | bytes 196616 | tf_op jit(solution)/shard_map/ppermute | solution.py:47
  5.6 6.9 %collective-permute-start.5 = (bf16[768,128]{1,0:T(8,128)(2,1)S(1)}, bf16[768,128]{1,0:T(8,128)(2,1)S(1)}, u32[]{:S(2)}, u32[]{:S(2)}) collective-permute-start(bf16[768,128]{1,0:T(8,128)(2,1)S(1)} %get-tuple-element.19.rest_0_.one_ref), channel_id=1, source_target_pairs={{0,8},{4,20},{1,9},{5,21},{2,10},{6,22},{3,11},{7,23}} | collective-permute-start | bytes 589832 | tf_op jit(solution)/shard_map/ppermute | solution.py:43
  8.1 5.7 %collective-permute-start.4 = (bf16[32,2048]{1,0:T(8,128)(2,1)S(1)}, bf16[32,2048]{1,0:T(8,128)(2,1)S(1)}, u32[]{:S(2)}, u32[]{:S(2)}) collective-permute-start(bf16[32,2048]{1,0:T(8,128)(2,1)S(1)} %query_join.3.rest_0_.known_ref), channel_id=1, source_target_pairs={{0,16},{4,12},{8,24},{12,4},{16,0},{20,28},{24,8},{28,20},{1,17},{... | collective-permute-start | bytes 393224 | tf_op jit(solution)/shard_map/ppermute | solution.py:47
  8.7 18.9 %collective-permute-start.2 = (bf16[768,128]{1,0:T(8,128)(2,1)S(1)}, bf16[768,128]{1,0:T(8,128)(2,1)S(1)}, u32[]{:S(2)}, u32[]{:S(2)}) collective-permute-start(bf16[768,128]{1,0:T(8,128)(2,1)S(1)} %get-tuple-element.18.one_ref), channel_id=1, source_target_pairs={{0,8},{4,20},{1,9},{5,21},{2,10},{6,22},{3,11},{7,23}} | collective-permute-start | bytes 589832 | tf_op jit(solution)/shard_map/ppermute | solution.py:43
  12.4 1.4 copy-start.3
  12.4 1.4 copy-start.4
  12.5 15.1 %collective-permute-start.8 = (bf16[768,128]{1,0:T(8,128)(2,1)S(1)}, bf16[768,128]{1,0:T(8,128)(2,1)S(1)}, u32[]{:S(2)}, u32[]{:S(2)}) collective-permute-start(bf16[768,128]{1,0:T(8,128)(2,1)S(1)} %anchor_relay.6.rest_0_.one_ref), channel_id=1, source_target_pairs={{0,16},{8,24},{4,12},{20,28},{1,17},{9,25},{5,13},{21,29},{2,18},{... | collective-permute-start | bytes 589832 | tf_op jit(solution)/shard_map/ppermute | solution.py:43
  25.5 4.0 %collective-permute-start.7 = (bf16[64,1152]{1,0:T(8,128)(2,1)S(1)}, bf16[64,1152]{1,0:T(8,128)(2,1)S(1)}, u32[]{:S(2)}, u32[]{:S(2)}) collective-permute-start(bf16[64,1152]{1,0:T(8,128)(2,1)S(1)} %get-tuple-element.21), channel_id=1, source_target_pairs={{0,4},{4,0},{8,12},{12,8},{16,20},{20,16},{24,28},{28,24},{1,5},{5... | collective-permute-start | bytes 442376 | tf_op jit(solution)/shard_map/ppermute | solution.py:47
  27.7 5.2 %collective-permute-start.10 = (bf16[768,128]{1,0:T(8,128)(2,1)S(1)}, bf16[768,128]{1,0:T(8,128)(2,1)S(1)}, u32[]{:S(2)}, u32[]{:S(2)}) collective-permute-start(bf16[768,128]{1,0:T(8,128)(2,1)S(1)} %anchor_relay.8.rest_0_.first_ref), channel_id=1, source_target_pairs={{0,4},{4,0},{8,12},{12,8},{16,20},{20,16},{24,28},{28,24},{1,5},{5... | collective-permute-start | bytes 589832 | tf_op jit(solution)/shard_map/ppermute | solution.py:47
  28.2 61.4 %collective-permute-start.6 = (bf16[768,128]{1,0:T(8,128)(2,1)S(1)}, bf16[768,128]{1,0:T(8,128)(2,1)S(1)}, u32[]{:S(2)}, u32[]{:S(2)}) collective-permute-start(bf16[768,128]{1,0:T(8,128)(2,1)S(1)} %anchor_relay.7.rest_0_.one_ref), channel_id=1, source_target_pairs={{0,16},{8,24},{4,12},{20,28},{1,17},{9,25},{5,13},{21,29},{2,18},{... | collective-permute-start | bytes 589832 | tf_op jit(solution)/shard_map/ppermute | solution.py:43
  29.9 21.0 %collective-permute-start.9 = (bf16[64,1152]{1,0:T(8,128)(2,1)S(1)}, bf16[64,1152]{1,0:T(8,128)(2,1)S(1)}, u32[]{:S(2)}, u32[]{:S(2)}) collective-permute-start(bf16[64,1152]{1,0:T(8,128)(2,1)S(1)} %query_merge.3.rest_0_.one_ref), channel_id=1, source_target_pairs={{0,8},{4,20},{8,0},{12,28},{16,24},{20,4},{24,16},{28,12},{1,9},{5... | collective-permute-start | bytes 442376 | tf_op jit(solution)/shard_map/ppermute | solution.py:47
  51.2 38.1 %collective-permute-start.11 = (bf16[64,1152]{1,0:T(8,128)(2,1)S(1)}, bf16[64,1152]{1,0:T(8,128)(2,1)S(1)}, u32[]{:S(2)}, u32[]{:S(2)}) collective-permute-start(bf16[64,1152]{1,0:T(8,128)(2,1)S(1)} %query_merge.4.refs_7_.one_ref), channel_id=1, source_target_pairs={{0,16},{4,12},{8,24},{12,4},{16,0},{20,28},{24,8},{28,20},{1,17},{... | collective-permute-start | bytes 442376 | tf_op jit(solution)/shard_map/ppermute | solution.py:47
  89.7 18.3 %copy-start.1 = (bf16[2048,1024]{1,0:T(8,128)(2,1)S(1)}, bf16[2048,1024]{1,0:T(8,128)(2,1)}, u32[]{:S(2)}) copy-start(bf16[2048,1024]{1,0:T(8,128)(2,1)} %w_ref.1) | copy-start | bytes 12582916
  89.7 20.8 %collective-permute-start.12 = (bf16[768,128]{1,0:T(8,128)(2,1)S(1)}, bf16[768,128]{1,0:T(8,128)(2,1)S(1)}, u32[]{:S(2)}, u32[]{:S(2)}) collective-permute-start(bf16[768,128]{1,0:T(8,128)(2,1)S(1)} %anchor_relay.9.refs_7_.first_ref), channel_id=1, source_target_pairs={{0,4},{4,0},{8,12},{12,8},{16,20},{20,16},{24,28},{28,24},{1,5},{5... | collective-permute-start | bytes 589832 | tf_op jit(solution)/shard_map/ppermute | solution.py:47
  89.8 18.2 %collective-permute-start.13 = (bf16[64,1024]{1,0:T(8,128)(2,1)S(1)}, bf16[64,1024]{1,0:T(8,128)(2,1)S(1)}, u32[]{:S(2)}, u32[]{:S(2)}) collective-permute-start(bf16[64,1024]{1,0:T(8,128)(2,1)S(1)} %query_merge.5.rest_0_.own_ref), channel_id=1, source_target_pairs={{0,4},{4,0},{8,12},{12,8},{16,20},{20,16},{24,28},{28,24},{1,5},{5... | collective-permute-start | bytes 393224 | tf_op jit(solution)/shard_map/ppermute | solution.py:47
  108.9 36.6 %collective-permute-start.14 = (bf16[64,1024]{1,0:T(8,128)(2,1)S(1)}, bf16[64,1024]{1,0:T(8,128)(2,1)S(1)}, u32[]{:S(2)}, u32[]{:S(2)}) collective-permute-start(bf16[64,1024]{1,0:T(8,128)(2,1)S(1)} %query_project.1.rest_0_.refs_7_.refs_8_.one_ref), channel_id=1, source_target_pairs={{0,1},{1,0},{2,3},{3,2},{4,5},{5,4},{6,7},{7,6},{8,9},{9,8},{10,11... | collective-permute-start | bytes 393224 | tf_op jit(solution)/shard_map/ppermute | solution.py:47
  145.5 38.3 %collective-permute-start.15 = (bf16[64,1024]{1,0:T(8,128)(2,1)S(1)}, bf16[64,1024]{1,0:T(8,128)(2,1)S(1)}, u32[]{:S(2)}, u32[]{:S(2)}) collective-permute-start(bf16[64,1024]{1,0:T(8,128)(2,1)S(1)} %query_sum.2.refs_11_.refs_12_.one_ref), channel_id=1, source_target_pairs={{0,2},{1,3},{2,0},{3,1},{4,6},{5,7},{6,4},{7,5},{8,10},{9,11},{10,... | collective-permute-start | bytes 393224 | tf_op jit(solution)/shard_map/ppermute | solution.py:47

commit v8 on v7

--- a/solution.py
+++ b/solution.py
@@ -39,10 +39,6 @@
     return lax.psum(kept, axis)
 
 
-def send(value, axis, pairs):
-    return lax.ppermute(value, axis, pairs)
-
-
 def swap(value, axis, size, even, odd):
     return lax.ppermute(value, axis, [(i, i ^ (odd if i & 1 else even)) for i in range(size)])
 
@@ -152,8 +148,9 @@
                     at = 2 * j * HD
                     scaled = k_ref[:, cols].astype(F32) * SCALE2
                     high = scaled.astype(BF)
-                    keys_ref[:, at : at + HD] = high
-                    keys_ref[:, at + HD : at + 2 * HD] = (scaled - high.astype(F32)).astype(BF)
+                    low = scaled - high.astype(F32)
+                    keys_ref[at : at + HD, :] = high.astype(F32).T.astype(BF)
+                    keys_ref[at + HD : at + 2 * HD, :] = low.T.astype(BF)
                     values_ref[:, at : at + HD] = v_ref[:, cols]
                     values_ref[:, at + HD : at + 2 * HD] = jnp.ones((slab, HD), BF)
 
@@ -165,7 +162,7 @@
         else:
             fill(first_ref, second_ref)()
 
-    shapes = [(slab, 2 * columns)] * 2
+    shapes = [(2 * columns, slab), (slab, 2 * columns)]
     return small_call(kernel, "operands", shapes, (first, second), after)
 
 
@@ -207,7 +204,7 @@
         def scores(at):
             h, j = units[at]
             query = q_ref[j * tile :, lanes(first + i * heads + h, HD)]
-            return dot_t(twice(query), k_ref[j * tile : (j + 1) * tile, lanes(kv, 2 * HD)])
+            return dot(twice(query), k_ref[lanes(kv, 2 * HD), j * tile : (j + 1) * tile])
 
         def power(x):
             return jnp.exp2(x).astype(BF)
@@ -259,9 +256,6 @@
         out_ref = refs[-1]
     slab = q_ref.shape[0]
     heads = body_size(first, count, per_kv, 2 if last else 4)
-    tile = row_tile(slab)
-    chunks = slab // tile
-    units = [(h, j) for h in range(heads) for j in range(chunks)]
     kv = first // per_kv
     host = lax.axis_index("hst")
     own_len = lengths_ref[host]
@@ -279,8 +273,8 @@
             at = (first + start + h) * HD
             return q_ref[:, at : at + HD]
 
-        def scores(h, j):
-            return dot_t(twice(query_of(h)), keys[j * tile : (j + 1) * tile, :])
+        def scores(h):
+            return dot(twice(query_of(h)), keys[...])
 
         def state_of(h):
             head = first + start + h
@@ -288,10 +282,9 @@
             at = (head - bases[n]) * 2 * HD
             return state_refs[n][:, at : at + 2 * HD]
 
-        def finish(h, total, worst):
-            sums = total[:, HD:]
+        def finish(h, total, sums, worst):
             inverse = pl.reciprocal(sums, approx=True)
-            out_ref[:, (start + h) * HD : (start + h + 1) * HD] = (total[:, :HD] * inverse).astype(BF)
+            out_ref[:, (start + h) * HD : (start + h + 1) * HD] = (total * inverse).astype(BF)
             return jnp.minimum(worst, jnp.minimum(sums, inverse))
 
         def check(worst):
@@ -303,19 +296,21 @@
         def _():
             worst = jnp.ones((slab, HD), F32)
             for h in range(heads):
-                worst = finish(h, state_of(h), worst)
+                state = state_of(h)
+                worst = finish(h, state[:, :HD], state[:, HD:], worst)
             check(worst)
 
         @pl.when(host > 0)
         def _():
             worst = jnp.ones((slab, HD), F32)
-            current = scores(*units[0])
-            for at, (h, j) in enumerate(units):
-                following = scores(*units[at + 1]) if at + 1 < len(units) else None
-                part = dot(jnp.exp2(current).astype(BF), vaug[j * tile : (j + 1) * tile, :])
-                total = (state_of(h) if j == 0 else total) + part
-                if j == chunks - 1:
-                    worst = finish(h, total, worst)
+            current = scores(0)
+            for h in range(heads):
+                following = scores(h + 1) if h + 1 < heads else None
+                expo = jnp.exp2(current)
+                state = state_of(h)
+                total = dot(expo.astype(BF), vaug[:, :HD]) + state[:, :HD]
+                sums = jnp.sum(expo, axis=1, keepdims=True) + state[:, HD:]
+                worst = finish(h, total, sums, worst)
                 current = following
             check(worst)
 
@@ -350,9 +345,9 @@
         query = q_ref[at, lanes(q_head + h, HD)]
         row_ids = lax.broadcasted_iota(jnp.int32, (tile, slab), 0) + r * tile
         key_ids = lax.broadcasted_iota(jnp.int32, (tile, slab), 1)
-        own = dot_t(twice(query), k_ref[:, 2 * kv * HD : 2 * (kv + 1) * HD])
+        own = dot(twice(query), k_ref[2 * kv * HD : 2 * (kv + 1) * HD, :])
         own = jnp.where((key_ids <= row_ids) & (key_ids < own_len), own, MASKED)
-        far = dot_t(twice(query), keys[...])
+        far = dot(twice(query), keys[...])
         far = jnp.where(host > 0, far, MASKED)
         peak = jnp.maximum(jnp.max(own, 1, keepdims=True), jnp.max(far, 1, keepdims=True))
         own = jnp.exp2(own - peak)
@@ -459,7 +454,7 @@
         queries = q_all[j * rows : (j + 1) * rows, :]
         self_keys = jnp.concatenate([selves_kv[0][:, cols], pad], 0).astype(BF)
         self_values = jnp.concatenate([selves_kv[1][:, cols], pad], 0).astype(BF)
-        near = dot_t(twice(queries), k_ref[:, 2 * j * HD : 2 * (j + 1) * HD])
+        near = dot(twice(queries), k_ref[2 * j * HD : 2 * (j + 1) * HD, :])
         selves = jnp.where(self_ok, dot_t(queries, self_keys) * SCALE2, MASKED)
         return near, selves, jnp.concatenate([self_values, jnp.ones((HD, HD), BF)], 1)
 
@@ -507,7 +502,7 @@
             def body(h, stats):
                 at = pl.ds(pl.multiple_of((j * per_kv + h) * query_count, query_count), query_count)
                 queries = q_all[at, :]
-                near = dot_t(twice(queries), k_ref[:, 2 * j * HD : 2 * (j + 1) * HD])
+                near = dot(twice(queries), k_ref[2 * j * HD : 2 * (j + 1) * HD, :])
                 near = jnp.where(key_ids < own_len, near, MASKED)
                 selves = jnp.where(heads_ok, dot_t(queries, self_keys) * SCALE2, MASKED)
                 peak = jnp.maximum(jnp.max(near, 1, keepdims=True), jnp.max(selves, 1, keepdims=True))
@@ -674,7 +669,7 @@
             cols = slice(2 * first // per_kv * HD, 2 * (first // per_kv + 1) * HD)
             last = first + per_kv == local_heads
             results[first] = anchor_part(
-                lengths, ctx_q, {0: state}, own_k, own_v, [x[:, cols] for x in anchor],
+                lengths, ctx_q, {0: state}, own_k, own_v, (anchor[0][cols, :], anchor[1][:, cols]),
                 first, per_kv, per_kv, dict(results) if last else None,
             )
         return results[first], query_out
@@ -707,7 +702,7 @@
     landed = swap(queries, "hst", hosts, *along[0])
     done = own(0, 2, (queries,))
     parts = list(relay(is_even, own_k, value_landed, (done,), kv_local))
-    parts_landed = [send(x, "hst", [(0, 2), (1, 5)]) for x in parts]
+    parts_landed = [swap(x, "hst", hosts, *along[0]) for x in parts]
     queries = join(near_low, queries, landed, (parts[0],))
     landed = swap(queries, "hst", hosts, *along[1])
     done = own(2, 6, (queries,))
@@ -715,7 +710,7 @@
 
     def pass_on(kv, after):
         (parts[kv],) = relay(source_first, parts[kv], parts_landed[kv], after)
-        parts_landed[kv] = send(parts[kv], "hst", [(0, 4), (2, 6), (1, 3), (5, 7)])
+        parts_landed[kv] = swap(parts[kv], "hst", hosts, *along[1])
         return parts[kv]
 
     def complete(kv, after):

time: 185 us -> 162 us (0.88)
  Pallas kernels: 165 us -> 145 us
  starting transfers between devices: 15.9 us -> 13.5 us
    pallas_call x5, Pallas kernels: 140 us -> 120 us  [anchor_part(): pl.pallas_call(functools.partial(anchor_kernel, first, count, bases, per_...]
    ppermute x4 -> x0, starting transfers between devices: 3.91 us -> none  [send(): return lax.ppermute(value, axis, pairs)]
    ppermute x12 -> x16, starting transfers between devices: 12 us -> 13.5 us  [swap(): lax.ppermute(value, axis, [(i, i ^ (odd if i & 1 else even)) for i in ran...]
  transfers between devices with their start and end apart: 16 -> 16, of which waited for: 2 -> 3; matrix products, arithmetic and copies ran while one was open for 0% -> 0% of each run, Pallas kernels for 88% -> 88%
where the time goes in v8:
time: 162 us
  Pallas kernels  145 us (90%)
  starting transfers between devices  13.5 us (8%)
  waiting for transfers between devices  2.76 us (2%)
    pallas_call x5, Pallas kernels, anchor_part(): pl.pallas_call(functools.partial(anchor_kernel, first, count, bases, per_...  120 us
    ppermute x16, starting transfers between devices, swap(): lax.ppermute(value, axis, [(i, i ^ (odd if i & 1 else even)) for i in ran...  13.5 us
    pallas_call x1, Pallas kernels, source_part(): pl.pallas_call(functools.partial(source_kernel, per_kv, q_rows, H // KVH)...  11.9 us
    pallas_call x4, Pallas kernels, own_part(): pl.pallas_call(functools.partial(own_kernel, first, count, per_kv), out_s...  7.96 us
  transfers between devices with their start and end apart: 16, of which 3 were waited for; matrix products, arithmetic and copies ran while one was open for 0% of the time, Pallas kernels for 88%

profile of v8, /device:TPU:6, one launch (start us, length us, event | category | flops | bytes accessed | tf_op | source)
XLA Modules:
  0.0 162.1 jit_solution(6406393240819434743)
XLA Ops:
  0.6 1.3 pick_columns.1
  2.0 0.5 collective-permute-start.1
  2.5 0.4 operands.3
  2.9 0.9 collective-permute-done.1.landed_ref
  3.8 0.5 collective-permute-start.3
  4.3 1.1 context_own.4.rest_0_.refs_6_
  5.5 1.6 collective-permute-start.5
  7.1 1.0 collective-permute-done.3.landed_ref
  8.1 0.6 collective-permute-start.4
  8.8 3.0 %context_own.5.rest_0_.refs_6_ = f32[768,1536]{1,0:T(8,128)S(1)} custom-call(bf16[768,2048]{1,0:T(8,128)(2,1)S(1)} %copy-done, bf16[512,768]{1,0:T(8,128)(2,1)S(1)} %get-tuple-element.16.rest_0_.k_ref.refs_2_, bf16[768,512]{1,0:T(8,128)(2,1)S(1)} %get-tuple-element.17.v_ref.refs_3_, bf16[32,2048]{1,0:T(8,128)(2,1)S(1)} %query_join.3.rest_0_.known_ref), custom_call_target="tpu_custom_call" | custom-call | flops 2415919104 | bytes 3538944 | tf_op jit(solution)/shard_map/context_own/pallas_call | solution.py:236
  11.8 0.9 collective-permute-done.5.two_ref
  12.7 1.2 collective-permute-start.8
  13.9 11.9 %query_source.1 = (bf16[64,1152]{1,0:T(8,128)(2,1)S(1)}, bf16[64,1152]{1,0:T(8,128)(2,1)S(1)}) custom-call(s32[8]{0:T(128)S(1)} %copy-done.3, bf16[512,768]{1,0:T(8,128)(2,1)S(1)} %get-tuple-element.16.rest_0_.k_ref.refs_2_, bf16[768,256]{1,0:T(8,128)(2,1)S(1)} %get-tuple-element.15.second_ref.v_ref, bf16[2,8,1024]{2,1,0:T(8,128)(2,1)S(1)} %copy-done.4, ...), custom_call_target="tpu_custom_call" | custom-call | flops 805306368 | bytes 2097152 | tf_op jit(solution)/shard_map/query_source/pallas_call | solution.py:539
  25.9 1.9 %context_own.6.rest_0_.refs_6_ = f32[768,1024]{1,0:T(8,128)S(1)} custom-call(bf16[768,2048]{1,0:T(8,128)(2,1)S(1)} %copy-done, bf16[512,768]{1,0:T(8,128)(2,1)S(1)} %get-tuple-element.16.rest_0_.k_ref.refs_2_, bf16[768,512]{1,0:T(8,128)(2,1)S(1)} %get-tuple-element.17.v_ref.refs_3_, bf16[64,1152]{1,0:T(8,128)(2,1)S(1)} %get-tuple-element.20.rest_0_.one_ref), custom_call_target="tpu_custom_call" | custom-call | flops 1610612736 | bytes 2359296 | tf_op jit(solution)/shard_map/context_own/pallas_call | solution.py:236
  27.9 0.6 collective-permute-start.10
  28.4 1.2 collective-permute-start.6
  29.6 0.3 query_merge.3.rest_0_.one_ref
  30.0 1.0 collective-permute-start.9
  30.9 1.9 %context_own.7.rest_0_.refs_6_ = f32[768,1024]{1,0:T(8,128)S(1)} custom-call(bf16[768,2048]{1,0:T(8,128)(2,1)S(1)} %copy-done, bf16[512,768]{1,0:T(8,128)(2,1)S(1)} %get-tuple-element.16.rest_0_.k_ref.refs_2_, bf16[768,512]{1,0:T(8,128)(2,1)S(1)} %get-tuple-element.17.v_ref.refs_3_, bf16[64,1152]{1,0:T(8,128)(2,1)S(1)} %query_merge.3.rest_0_.one_ref), custom_call_target="tpu_custom_call" | custom-call | flops 1610612736 | bytes 2359296 | tf_op jit(solution)/shard_map/context_own/pallas_call | solution.py:236
  33.1 15.3 %context_anchor.5.rest_0_.refs_7_ = bf16[768,256]{1,0:T(8,128)(2,1)S(1)} custom-call(s32[8]{0:T(128)S(1)} %copy-done.3, bf16[768,2048]{1,0:T(8,128)(2,1)S(1)} %copy-done, bf16[512,768]{1,0:T(8,128)(2,1)S(1)} %get-tuple-element.16.rest_0_.k_ref.refs_2_, bf16[768,512]{1,0:T(8,128)(2,1)S(1)} %get-tuple-element.17.v_ref.refs_3_, ...), custom_call_target="tpu_custom_call" | custom-call | flops 1207959552 | bytes 1572864 | tf_op jit(solution)/shard_map/context_anchor/pallas_call | solution.py:378
  48.4 0.3 query_merge.4.refs_7_.one_ref
  48.7 1.3 collective-permute-start.11
  50.1 29.4 %context_anchor.6.rest_0_.refs_8_ = bf16[768,512]{1,0:T(8,128)(2,1)S(1)} custom-call(s32[8]{0:T(128)S(1)} %copy-done.3, bf16[768,2048]{1,0:T(8,128)(2,1)S(1)} %copy-done, bf16[512,768]{1,0:T(8,128)(2,1)S(1)} %get-tuple-element.16.rest_0_.k_ref.refs_2_, bf16[768,512]{1,0:T(8,128)(2,1)S(1)} %get-tuple-element.17.v_ref.refs_3_, ...), custom_call_target="tpu_custom_call" | custom-call | flops 2415919104 | bytes 3145728 | tf_op jit(solution)/shard_map/context_anchor/pallas_call | solution.py:378
  79.5 0.3 query_merge.5.rest_0_.own_ref
  79.9 0.5 collective-permute-start.13
  80.4 15.1 %context_anchor.7.rest_0_.refs_9_ = bf16[768,256]{1,0:T(8,128)(2,1)S(1)} custom-call(s32[8]{0:T(128)S(1)} %copy-done.3, bf16[768,2048]{1,0:T(8,128)(2,1)S(1)} %copy-done, bf16[512,768]{1,0:T(8,128)(2,1)S(1)} %get-tuple-element.16.rest_0_.k_ref.refs_2_, bf16[768,512]{1,0:T(8,128)(2,1)S(1)} %get-tuple-element.17.v_ref.refs_3_, ...), custom_call_target="tpu_custom_call" | custom-call | flops 1207959552 | bytes 1572864 | tf_op jit(solution)/shard_map/context_anchor/pallas_call | solution.py:378
  95.6 0.9 query_project.1.rest_0_.refs_7_.refs_8_.one_ref
  96.5 1.6 %collective-permute-start.14 = (bf16[64,1024]{1,0:T(8,128)(2,1)S(1)}, bf16[64,1024]{1,0:T(8,128)(2,1)S(1)}, u32[]{:S(2)}, u32[]{:S(2)}) collective-permute-start(bf16[64,1024]{1,0:T(8,128)(2,1)S(1)} %query_project.1.rest_0_.refs_7_.refs_8_.one_ref), channel_id=1, source_target_pairs={{0,1},{1,0},{2,3},{3,2},{4,5},{5,4},{6,7},{7,6},{8,9},{9,8},{10,11... | collective-permute-start | bytes 393224 | tf_op jit(solution)/shard_map/ppermute | solution.py:43
  98.3 29.9 %context_anchor.8.rest_0_.refs_10_ = bf16[768,512]{1,0:T(8,128)(2,1)S(1)} custom-call(s32[8]{0:T(128)S(1)} %copy-done.3, bf16[768,2048]{1,0:T(8,128)(2,1)S(1)} %copy-done, bf16[512,768]{1,0:T(8,128)(2,1)S(1)} %get-tuple-element.16.rest_0_.k_ref.refs_2_, bf16[768,512]{1,0:T(8,128)(2,1)S(1)} %get-tuple-element.17.v_ref.refs_3_, ...), custom_call_target="tpu_custom_call" | custom-call | flops 2415919104 | bytes 3145728 | tf_op jit(solution)/shard_map/context_anchor/pallas_call | solution.py:378
  128.2 2.7 %collective-permute-start.15 = (bf16[64,1024]{1,0:T(8,128)(2,1)S(1)}, bf16[64,1024]{1,0:T(8,128)(2,1)S(1)}, u32[]{:S(2)}, u32[]{:S(2)}) collective-permute-start(bf16[64,1024]{1,0:T(8,128)(2,1)S(1)} %query_sum.2.refs_11_.refs_12_.one_ref), channel_id=1, source_target_pairs={{0,2},{1,3},{2,0},{3,1},{4,6},{5,7},{6,4},{7,5},{8,10},{9,11},{10,... | collective-permute-start | bytes 393224 | tf_op jit(solution)/shard_map/ppermute | solution.py:43
  130.9 30.5 %context_anchor.9 = bf16[768,2048]{1,0:T(8,128)(2,1)} custom-call(s32[8]{0:T(128)S(1)} %copy-done.3, bf16[768,2048]{1,0:T(8,128)(2,1)S(1)} %copy-done, bf16[512,768]{1,0:T(8,128)(2,1)S(1)} %get-tuple-element.16.rest_0_.k_ref.refs_2_, bf16[768,512]{1,0:T(8,128)(2,1)S(1)} %get-tuple-element.17.v_ref.refs_3_, bf16[256,768]{1,0:T(8,128)(2,1)S(1)} %get-tuple-element.24.refs_4_, ...), custom_call_target="tpu_custom_call" | custom-call | flops 2415919104 | bytes 3145728 | tf_op jit(solution)/shard_map/context_anchor/pallas_call | solution.py:378
  161.4 0.7 query_sum.3
  (37 shorter events, 1.0 us)
Async XLA Ops:
  0.6 1.4 copy-start.2
  0.6 3.7 %copy-start = (bf16[768,2048]{1,0:T(8,128)(2,1)S(1)}, bf16[768,2048]{1,0:T(8,128)(2,1)}, u32[]{:S(2)}) copy-start(bf16[768,2048]{1,0:T(8,128)(2,1)} %refs_1_.9) | copy-start | bytes 9437188
  2.0 3.5 %collective-permute-start = (bf16[768,256]{1,0:T(8,128)(2,1)S(1)}, bf16[768,256]{1,0:T(8,128)(2,1)S(1)}, u32[]{:S(2)}, u32[]{:S(2)}) collective-permute-start(bf16[768,256]{1,0:T(8,128)(2,1)S(1)} %get-tuple-element.15.second_ref.v_ref), channel_id=1, source_target_pairs={{0,4},{4,0},{8,12},{12,8},{16,20},{20,16},{24,28},{28,24},{1,5},{5... | collective-permute-start | bytes 1179656 | tf_op jit(solution)/shard_map/ppermute | solution.py:43
  2.0 1.7 %collective-permute-start.1 = (bf16[8,2048]{1,0:T(8,128)(2,1)S(1)}, bf16[8,2048]{1,0:T(8,128)(2,1)S(1)}, u32[]{:S(2)}, u32[]{:S(2)}) collective-permute-start(bf16[8,2048]{1,0:T(8,128)(2,1)S(1)} %copy-done.2), channel_id=1, source_target_pairs={{0,4},{4,0},{8,12},{12,8},{16,20},{20,16},{24,28},{28,24},{1,5},{5... | collective-permute-start | bytes 98312 | tf_op jit(solution)/shard_map/ppermute | solution.py:43
  3.8 4.3 %collective-permute-start.3 = (bf16[16,2048]{1,0:T(8,128)(2,1)S(1)}, bf16[16,2048]{1,0:T(8,128)(2,1)S(1)}, u32[]{:S(2)}, u32[]{:S(2)}) collective-permute-start(bf16[16,2048]{1,0:T(8,128)(2,1)S(1)} %query_join.2.rest_0_.known_ref), channel_id=1, source_target_pairs={{0,8},{4,20},{8,0},{12,28},{16,24},{20,4},{24,16},{28,12},{1,9},{5... | collective-permute-start | bytes 196616 | tf_op jit(solution)/shard_map/ppermute | solution.py:43
  5.5 7.1 %collective-permute-start.5 = (bf16[768,128]{1,0:T(8,128)(2,1)S(1)}, bf16[768,128]{1,0:T(8,128)(2,1)S(1)}, u32[]{:S(2)}, u32[]{:S(2)}) collective-permute-start(bf16[768,128]{1,0:T(8,128)(2,1)S(1)} %get-tuple-element.19.rest_0_.one_ref), channel_id=1, source_target_pairs={{0,8},{4,20},{8,0},{12,28},{16,24},{20,4},{24,16},{28,12},{1,9},{5... | collective-permute-start | bytes 589832 | tf_op jit(solution)/shard_map/ppermute | solution.py:43
  8.1 5.8 %collective-permute-start.4 = (bf16[32,2048]{1,0:T(8,128)(2,1)S(1)}, bf16[32,2048]{1,0:T(8,128)(2,1)S(1)}, u32[]{:S(2)}, u32[]{:S(2)}) collective-permute-start(bf16[32,2048]{1,0:T(8,128)(2,1)S(1)} %query_join.3.rest_0_.known_ref), channel_id=1, source_target_pairs={{0,16},{4,12},{8,24},{12,4},{16,0},{20,28},{24,8},{28,20},{1,17},{... | collective-permute-start | bytes 393224 | tf_op jit(solution)/shard_map/ppermute | solution.py:43
  8.7 19.1 %collective-permute-start.2 = (bf16[768,128]{1,0:T(8,128)(2,1)S(1)}, bf16[768,128]{1,0:T(8,128)(2,1)S(1)}, u32[]{:S(2)}, u32[]{:S(2)}) collective-permute-start(bf16[768,128]{1,0:T(8,128)(2,1)S(1)} %get-tuple-element.18.one_ref), channel_id=1, source_target_pairs={{0,8},{4,20},{8,0},{12,28},{16,24},{20,4},{24,16},{28,12},{1,9},{5... | collective-permute-start | bytes 589832 | tf_op jit(solution)/shard_map/ppermute | solution.py:43
  11.8 2.1 %copy-start.3 = (s32[8]{0:T(128)S(1)}, s32[8]{0:T(128)}, u32[]{:S(2)}) copy-start(s32[8]{0:T(128)} %refs_0_.9) | copy-start | bytes 100
  11.8 2.1 %copy-start.4 = (bf16[2,8,1024]{2,1,0:T(8,128)(2,1)S(1)}, bf16[2,8,1024]{2,1,0:T(8,128)(2,1)}, u32[]{:S(2)}) copy-start(bf16[2,8,1024]{2,1,0:T(8,128)(2,1)} %self_ref.1) | copy-start | bytes 98308
  12.7 15.1 %collective-permute-start.8 = (bf16[768,128]{1,0:T(8,128)(2,1)S(1)}, bf16[768,128]{1,0:T(8,128)(2,1)S(1)}, u32[]{:S(2)}, u32[]{:S(2)}) collective-permute-start(bf16[768,128]{1,0:T(8,128)(2,1)S(1)} %anchor_relay.6.rest_0_.one_ref), channel_id=1, source_target_pairs={{0,16},{4,12},{8,24},{12,4},{16,0},{20,28},{24,8},{28,20},{1,17},{... | collective-permute-start | bytes 589832 | tf_op jit(solution)/shard_map/ppermute | solution.py:43
  25.8 3.9 %collective-permute-start.7 = (bf16[64,1152]{1,0:T(8,128)(2,1)S(1)}, bf16[64,1152]{1,0:T(8,128)(2,1)S(1)}, u32[]{:S(2)}, u32[]{:S(2)}) collective-permute-start(bf16[64,1152]{1,0:T(8,128)(2,1)S(1)} %get-tuple-element.21), channel_id=1, source_target_pairs={{0,4},{4,0},{8,12},{12,8},{16,20},{20,16},{24,28},{28,24},{1,5},{5... | collective-permute-start | bytes 442376 | tf_op jit(solution)/shard_map/ppermute | solution.py:43
  27.9 5.0 %collective-permute-start.10 = (bf16[768,128]{1,0:T(8,128)(2,1)S(1)}, bf16[768,128]{1,0:T(8,128)(2,1)S(1)}, u32[]{:S(2)}, u32[]{:S(2)}) collective-permute-start(bf16[768,128]{1,0:T(8,128)(2,1)S(1)} %anchor_relay.8.rest_0_.first_ref), channel_id=1, source_target_pairs={{0,4},{4,0},{8,12},{12,8},{16,20},{20,16},{24,28},{28,24},{1,5},{5... | collective-permute-start | bytes 589832 | tf_op jit(solution)/shard_map/ppermute | solution.py:43
  28.4 51.4 %collective-permute-start.6 = (bf16[768,128]{1,0:T(8,128)(2,1)S(1)}, bf16[768,128]{1,0:T(8,128)(2,1)S(1)}, u32[]{:S(2)}, u32[]{:S(2)}) collective-permute-start(bf16[768,128]{1,0:T(8,128)(2,1)S(1)} %anchor_relay.7.rest_0_.one_ref), channel_id=1, source_target_pairs={{0,16},{4,12},{8,24},{12,4},{16,0},{20,28},{24,8},{28,20},{1,17},{... | collective-permute-start | bytes 589832 | tf_op jit(solution)/shard_map/ppermute | solution.py:43
  30.0 18.4 %collective-permute-start.9 = (bf16[64,1152]{1,0:T(8,128)(2,1)S(1)}, bf16[64,1152]{1,0:T(8,128)(2,1)S(1)}, u32[]{:S(2)}, u32[]{:S(2)}) collective-permute-start(bf16[64,1152]{1,0:T(8,128)(2,1)S(1)} %query_merge.3.rest_0_.one_ref), channel_id=1, source_target_pairs={{0,8},{4,20},{8,0},{12,28},{16,24},{20,4},{24,16},{28,12},{1,9},{5... | collective-permute-start | bytes 442376 | tf_op jit(solution)/shard_map/ppermute | solution.py:43
  48.7 30.7 %collective-permute-start.11 = (bf16[64,1152]{1,0:T(8,128)(2,1)S(1)}, bf16[64,1152]{1,0:T(8,128)(2,1)S(1)}, u32[]{:S(2)}, u32[]{:S(2)}) collective-permute-start(bf16[64,1152]{1,0:T(8,128)(2,1)S(1)} %query_merge.4.refs_7_.one_ref), channel_id=1, source_target_pairs={{0,16},{4,12},{8,24},{12,4},{16,0},{20,28},{24,8},{28,20},{1,17},{... | collective-permute-start | bytes 442376 | tf_op jit(solution)/shard_map/ppermute | solution.py:43
  79.8 15.7 %copy-start.1 = (bf16[2048,1024]{1,0:T(8,128)(2,1)S(1)}, bf16[2048,1024]{1,0:T(8,128)(2,1)}, u32[]{:S(2)}) copy-start(bf16[2048,1024]{1,0:T(8,128)(2,1)} %w_ref.1) | copy-start | bytes 12582916
  79.9 18.3 %collective-permute-start.12 = (bf16[768,128]{1,0:T(8,128)(2,1)S(1)}, bf16[768,128]{1,0:T(8,128)(2,1)S(1)}, u32[]{:S(2)}, u32[]{:S(2)}) collective-permute-start(bf16[768,128]{1,0:T(8,128)(2,1)S(1)} %anchor_relay.9.refs_7_.first_ref), channel_id=1, source_target_pairs={{0,4},{4,0},{8,12},{12,8},{16,20},{20,16},{24,28},{28,24},{1,5},{5... | collective-permute-start | bytes 589832 | tf_op jit(solution)/shard_map/ppermute | solution.py:43
  79.9 15.6 %collective-permute-start.13 = (bf16[64,1024]{1,0:T(8,128)(2,1)S(1)}, bf16[64,1024]{1,0:T(8,128)(2,1)S(1)}, u32[]{:S(2)}, u32[]{:S(2)}) collective-permute-start(bf16[64,1024]{1,0:T(8,128)(2,1)S(1)} %query_merge.5.rest_0_.own_ref), channel_id=1, source_target_pairs={{0,4},{4,0},{8,12},{12,8},{16,20},{20,16},{24,28},{28,24},{1,5},{5... | collective-permute-start | bytes 393224 | tf_op jit(solution)/shard_map/ppermute | solution.py:43
  96.5 31.7 %collective-permute-start.14 = (bf16[64,1024]{1,0:T(8,128)(2,1)S(1)}, bf16[64,1024]{1,0:T(8,128)(2,1)S(1)}, u32[]{:S(2)}, u32[]{:S(2)}) collective-permute-start(bf16[64,1024]{1,0:T(8,128)(2,1)S(1)} %query_project.1.rest_0_.refs_7_.refs_8_.one_ref), channel_id=1, source_target_pairs={{0,1},{1,0},{2,3},{3,2},{4,5},{5,4},{6,7},{7,6},{8,9},{9,8},{10,11... | collective-permute-start | bytes 393224 | tf_op jit(solution)/shard_map/ppermute | solution.py:43
  128.2 33.1 %collective-permute-start.15 = (bf16[64,1024]{1,0:T(8,128)(2,1)S(1)}, bf16[64,1024]{1,0:T(8,128)(2,1)S(1)}, u32[]{:S(2)}, u32[]{:S(2)}) collective-permute-start(bf16[64,1024]{1,0:T(8,128)(2,1)S(1)} %query_sum.2.refs_11_.refs_12_.one_ref), channel_id=1, source_target_pairs={{0,2},{1,3},{2,0},{3,1},{4,6},{5,7},{6,4},{7,5},{8,10},{9,11},{10,... | collective-permute-start | bytes 393224 | tf_op jit(solution)/shard_map/ppermute | solution.py:43

commit v9 on v8

--- a/solution.py
+++ b/solution.py
@@ -17,7 +17,6 @@
 BF = jnp.bfloat16
 F32 = jnp.float32
 VMEM = pl.BlockSpec(memory_space=pltpu.VMEM)
-SMEM = pl.BlockSpec(memory_space=pltpu.SMEM)
 ANY = pl.BlockSpec(memory_space=pl.ANY)
 HBM = pl.BlockSpec(memory_space=pltpu.HBM)
 
@@ -246,8 +245,15 @@
     )(ctx_q, own_k, own_v, *after)
 
 
+def length_of(lengths_ref, host):
+    lengths = lengths_ref[...]
+    index = lax.broadcasted_iota(jnp.int32, lengths.shape, 1)
+    return jnp.sum(jnp.where(index == host, lengths, 0), axis=1, keepdims=True)
+
+
 def anchor_kernel(first, count, bases, per_kv, last, befores, *refs):
     lengths_ref, q_ref, k_ref, v_ref, keys, vaug = refs[:6]
+    hosts = lengths_ref.shape[1]
     state_refs = refs[6 : 6 + len(bases)]
     earlier = refs[6 + len(bases) : 6 + len(bases) + len(befores)]
     if last:
@@ -258,7 +264,6 @@
     heads = body_size(first, count, per_kv, 2 if last else 4)
     kv = first // per_kv
     host = lax.axis_index("hst")
-    own_len = lengths_ref[host]
 
     def hand_over(source, start, width, sem):
         target = full_ref.at[:, pl.ds(start * HD, width * HD)]
@@ -290,7 +295,7 @@
         def check(worst):
             @pl.when(jnp.logical_not(jnp.min(worst) > TINY))
             def _():
-                exact_block(first + start, start, heads, host, own_len, kv, q_ref, k_ref, v_ref, keys, vaug, out_ref)
+                exact_block(first + start, start, heads, host, kv, q_ref, k_ref, v_ref, keys, vaug, out_ref)
 
         @pl.when(host == 0)
         def _():
@@ -314,8 +319,9 @@
                 current = following
             check(worst)
 
-        @pl.when(own_len < slab)
+        @pl.when(host * 4 >= hosts * 3)
         def _():
+            own_len = length_of(lengths_ref, host)
             row_ids = lax.broadcasted_iota(jnp.int32, (slab, HD), 0)
             for h in range(start, start + heads):
                 cols = slice(h * HD, (h + 1) * HD)
@@ -334,7 +340,7 @@
         move.wait()
 
 
-def exact_block(q_head, out_head, heads, host, own_len, kv, q_ref, k_ref, v_ref, keys, vaug, out_ref):
+def exact_block(q_head, out_head, heads, host, kv, q_ref, k_ref, v_ref, keys, vaug, out_ref):
     slab = q_ref.shape[0]
     tile = 64
 
@@ -346,7 +352,7 @@
         row_ids = lax.broadcasted_iota(jnp.int32, (tile, slab), 0) + r * tile
         key_ids = lax.broadcasted_iota(jnp.int32, (tile, slab), 1)
         own = dot(twice(query), k_ref[2 * kv * HD : 2 * (kv + 1) * HD, :])
-        own = jnp.where((key_ids <= row_ids) & (key_ids < own_len), own, MASKED)
+        own = jnp.where(key_ids <= row_ids, own, MASKED)
         far = dot(twice(query), keys[...])
         far = jnp.where(host > 0, far, MASKED)
         peak = jnp.maximum(jnp.max(own, 1, keepdims=True), jnp.max(far, 1, keepdims=True))
@@ -355,8 +361,7 @@
         sums = jnp.sum(own, 1, keepdims=True) + jnp.sum(far, 1, keepdims=True)
         values = jnp.where(host > 0, vaug[:, :HD].astype(F32), 0.0).astype(BF)
         total = dot(own.astype(BF), v_ref[:, 2 * kv * HD : (2 * kv + 1) * HD]) + dot(far.astype(BF), values)
-        live = row_ids[:, :1] < own_len
-        out_ref[at, lanes(out_head + h, HD)] = jnp.where(live, total / sums, 0.0).astype(BF)
+        out_ref[at, lanes(out_head + h, HD)] = (total / sums).astype(BF)
         return carry
 
     lax.fori_loop(0, heads * (slab // tile), body, 0)
@@ -378,7 +383,7 @@
     return pl.pallas_call(
         functools.partial(anchor_kernel, first, count, bases, per_kv, last, places),
         out_shape=results,
-        in_specs=[SMEM] + [VMEM] * (5 + len(bases) + len(earlier)) + [ANY] * len(after),
+        in_specs=[VMEM] * (6 + len(bases) + len(earlier)) + [ANY] * len(after),
         out_specs=ANY if last else VMEM,
         scratch_shapes=scratch,
         compiler_params=params(),
@@ -415,7 +420,7 @@
     query_count = 8 * q_rows
     block = 2 * q_rows
     host = lax.axis_index("hst")
-    own_len = lengths_ref[host]
+    own_len = length_of(lengths_ref, host)
     rows = per_kv * query_count
     odd = bit(host, 0) == 1
     low = jnp.where(odd, bit(host, 1), bit(host, 2)) == 0
@@ -539,7 +544,7 @@
     return pl.pallas_call(
         functools.partial(source_kernel, per_kv, q_rows, H // KVH),
         out_shape=[jax.ShapeDtypeStruct((count, (per_kv + 1) * HD), BF)] * 2,
-        in_specs=[SMEM] + [VMEM] * 5 + [ANY] * len(after),
+        in_specs=[VMEM] * 6 + [ANY] * len(after),
         out_specs=[VMEM] * 2,
         scratch_shapes=[pltpu.VMEM((count * width // HD, HD), BF), pltpu.VMEM((slab, 2 * columns), BF)],
         compiler_params=params(),
@@ -548,32 +553,25 @@
     )(lengths, own_k, own_v, query_kv, known, landed, *after)
 
 
-def merged(refs, width):
-    levels = [read_level(ref, width) for ref in refs]
-    peak = jnp.maximum(*levels)
-    weights = [jnp.exp2(x - peak) for x in levels]
-    whole = weights[0] + weights[1]
-    return [w / whole for w in weights], peak + jnp.log2(whole)
-
-
-def blend(shares, refs, h):
-    cols = slice(h * HD, (h + 1) * HD)
-    return sum(w[:, h : h + 1] * ref[:, cols].astype(F32) for w, ref in zip(shares, refs))
-
-
-def merge_part(one, two, last, after=()):
-    rows, wide = one.shape
+def merge_part(groups, last, after=()):
+    rows, wide = groups[0].shape
     width = wide - HD
 
-    def kernel(one_ref, two_ref, *rest):
-        out_ref = rest[-1]
-        shares, level = merged((one_ref, two_ref), width)
+    def kernel(*refs):
+        in_refs, out_ref = refs[: len(groups)], refs[-1]
+        levels = [read_level(ref, width) for ref in in_refs]
+        peak = functools.reduce(jnp.maximum, levels)
+        weights = [jnp.exp2(x - peak) for x in levels]
+        whole = functools.reduce(jnp.add, weights)
+        shares = [w / whole for w in weights]
         if not last:
-            write_level(out_ref, width, level)
+            write_level(out_ref, width, peak + jnp.log2(whole))
         for h in range(width // HD):
-            out_ref[:, h * HD : (h + 1) * HD] = blend(shares, (one_ref, two_ref), h).astype(BF)
-
-    return small_call(kernel, "query_merge", [(rows, width if last else wide)], (one, two), after)[0]
+            cols = slice(h * HD, (h + 1) * HD)
+            total = sum(w[:, h : h + 1] * ref[:, cols].astype(F32) for w, ref in zip(shares, in_refs))
+            out_ref[:, cols] = total.astype(BF)
+
+    return small_call(kernel, "query_merge", [(rows, width if last else wide)], groups, after)[0]
 
 
 def project_part(own, other, out_weight, after=()):
@@ -661,6 +659,7 @@
         own_k, own_v = pick(ctx_kv, kv_local, local_heads)
         query_out = general_queries(lengths, own_k, own_v, self_kv, query_q, out_weight, per_kv)
         k, v = spread(jnp.stack([own_k, own_v]), "hst", 0)
+        lengths = lengths.reshape(1, hosts)
         own_k, own_v = prepare(own_k, own_v, False)
         anchor = prepare(k, v, False)
         state = own_part(ctx_q, own_k, own_v, 0, local_heads, per_kv)
@@ -674,6 +673,7 @@
             )
         return results[first], query_out
 
+    lengths = lengths.reshape(1, hosts)
     states = {}
 
     def own(first, count, after=()):
@@ -724,8 +724,8 @@
     done = own(8, 4, (keep,))
     done = pass_on(1, (done,))
     done = complete(0, (done,))
-    source = merge_part(keep, landed, False, (done,))
-    landed = swap(source, "hst", hosts, *along[0])
+    source = merge_part([keep, landed], False, (done,))
+    landed = [swap(source, "hst", hosts, x, x) for x in (6, 2, 4)]
     done = own(12, 4, (source,))
     anchor[0] = prepare(*anchor[0], True, (done,))
     results = {}
@@ -738,16 +738,13 @@
         return results[first]
 
     done = anchors(0, 2, ())
-    source = merge_part(source, landed, False, (done,))
-    landed = swap(source, "hst", hosts, *along[1])
-    done = anchors(2, 4, (source,))
-    source = merge_part(source, landed, True, (done,))
-    landed = swap(source, "hst", hosts, 1, 1)
-    done = complete(1, (source,))
-    done = anchors(6, 2, (done,))
-    terms = project_part(source, landed, out_weight, (done,))
+    attended = merge_part([source, *landed], True, (done,))
+    landed = swap(attended, "hst", hosts, 1, 1)
+    done = complete(1, (attended,))
+    done = anchors(2, 2, (done,))
+    terms = project_part(attended, landed, out_weight, (done,))
     anchor[1] = prepare(*anchor[1], True, (terms,))
-    shares = [[(12, 4, True)], [(8, 4, False)]]
+    shares = [[(10, 6, True)], [(4, 4, False), (8, 2, False)]]
     step = 1
     while step < groups:
         landed = swap(terms, "tp", groups, step, step)

time: 162 us -> 161 us (level)
  Pallas kernels: 145 us -> 142 us
    pallas_call x5, Pallas kernels: 120 us -> 118 us  [anchor_part(): pl.pallas_call(functools.partial(anchor_kernel, first, count, bases, per_...]
    ppermute x16 -> x17, starting transfers between devices: 13.5 us -> 14.8 us  [swap(): lax.ppermute(value, axis, [(i, i ^ (odd if i & 1 else even)) for i in ran...]
  transfers between devices with their start and end apart: 16 -> 17, of which waited for: 3 -> 3; matrix products, arithmetic and copies ran while one was open for 0% -> 0% of each run, Pallas kernels for 88% -> 87%
where the time goes in v9:
time: 161 us; the launch traced here: 160 us
  Pallas kernels  142 us (88%)
  starting transfers between devices  14.8 us (9%)
  waiting for transfers between devices  2.76 us (2%)
    pallas_call x5, Pallas kernels, anchor_part(): pl.pallas_call(functools.partial(anchor_kernel, first, count, bases, per_...  118 us
    ppermute x17, starting transfers between devices, swap(): lax.ppermute(value, axis, [(i, i ^ (odd if i & 1 else even)) for i in ran...  14.8 us
    pallas_call x1, Pallas kernels, source_part(): pl.pallas_call(functools.partial(source_kernel, per_kv, q_rows, H // KVH)...  11.3 us
    pallas_call x4, Pallas kernels, own_part(): pl.pallas_call(functools.partial(own_kernel, first, count, per_kv), out_s...  7.96 us
  transfers between devices with their start and end apart: 17, of which 3 were waited for; matrix products, arithmetic and copies ran while one was open for 0% of the time, Pallas kernels for 87%

profile of v9, /device:TPU:6, one launch (start us, length us, event | category | flops | bytes accessed | tf_op | source)
XLA Modules:
  0.0 160.4 jit_solution(13081914350493783279)
XLA Ops:
  0.6 1.3 pick_columns.1
  2.0 0.5 collective-permute-start.1
  2.5 0.4 operands.3
  2.9 0.9 collective-permute-done.1.landed_ref
  3.8 0.5 collective-permute-start.3
  4.3 1.1 context_own.4.rest_0_.refs_6_
  5.5 1.6 collective-permute-start.5
  7.1 1.0 collective-permute-done.3.landed_ref
  8.1 0.6 collective-permute-start.4
  8.8 3.0 %context_own.5.rest_0_.refs_6_ = f32[768,1536]{1,0:T(8,128)S(1)} custom-call(bf16[768,2048]{1,0:T(8,128)(2,1)S(1)} %copy-done, bf16[512,768]{1,0:T(8,128)(2,1)S(1)} %get-tuple-element.16.rest_0_.k_ref.refs_2_, bf16[768,512]{1,0:T(8,128)(2,1)S(1)} %get-tuple-element.17.v_ref.refs_3_, bf16[32,2048]{1,0:T(8,128)(2,1)S(1)} %query_join.3.rest_0_.known_ref), custom_call_target="tpu_custom_call" | custom-call | flops 2415919104 | bytes 3538944 | tf_op jit(solution)/shard_map/context_own/pallas_call | solution.py:235
  11.8 0.9 collective-permute-done.5.two_ref
  12.7 1.2 collective-permute-start.8
  13.9 11.3 %query_source.1 = (bf16[64,1152]{1,0:T(8,128)(2,1)S(1)}, bf16[64,1152]{1,0:T(8,128)(2,1)S(1)}) custom-call(s32[1,8]{1,0:T(1,128)S(1)} %bitcast.1, bf16[512,768]{1,0:T(8,128)(2,1)S(1)} %get-tuple-element.16.rest_0_.k_ref.refs_2_, bf16[768,256]{1,0:T(8,128)(2,1)S(1)} %get-tuple-element.15.second_ref.v_ref, bf16[2,8,1024]{2,1,0:T(8,128)(2,1)S(1)} %copy-done.4, ...), custom_call_target="tpu_custom_call" | custom-call | flops 805306368 | bytes 2097152 | tf_op jit(solution)/shard_map/query_source/pallas_call | solution.py:544
  25.3 1.9 %context_own.6.rest_0_.refs_6_ = f32[768,1024]{1,0:T(8,128)S(1)} custom-call(bf16[768,2048]{1,0:T(8,128)(2,1)S(1)} %copy-done, bf16[512,768]{1,0:T(8,128)(2,1)S(1)} %get-tuple-element.16.rest_0_.k_ref.refs_2_, bf16[768,512]{1,0:T(8,128)(2,1)S(1)} %get-tuple-element.17.v_ref.refs_3_, bf16[64,1152]{1,0:T(8,128)(2,1)S(1)} %get-tuple-element.20.rest_0_.refs_0_), custom_call_target="tpu_custom_call" | custom-call | flops 1610612736 | bytes 2359296 | tf_op jit(solution)/shard_map/context_own/pallas_call | solution.py:235
  27.3 0.6 collective-permute-start.12
  27.9 1.2 collective-permute-start.6
  29.2 0.3 query_merge.2.rest_0_.refs_0_
  29.5 1.0 collective-permute-start.10
  30.5 1.4 collective-permute-start.11
  31.8 1.2 collective-permute-start.9
  33.0 1.9 %context_own.7.rest_0_.refs_7_ = f32[768,1024]{1,0:T(8,128)S(1)} custom-call(bf16[768,2048]{1,0:T(8,128)(2,1)S(1)} %copy-done, bf16[512,768]{1,0:T(8,128)(2,1)S(1)} %get-tuple-element.16.rest_0_.k_ref.refs_2_, bf16[768,512]{1,0:T(8,128)(2,1)S(1)} %get-tuple-element.17.v_ref.refs_3_, bf16[64,1152]{1,0:T(8,128)(2,1)S(1)} %query_merge.2.rest_0_.refs_0_), custom_call_target="tpu_custom_call" | custom-call | flops 1610612736 | bytes 2359296 | tf_op jit(solution)/shard_map/context_own/pallas_call | solution.py:235
  35.2 14.8 %context_anchor.5.refs_4_.refs_8_ = bf16[768,256]{1,0:T(8,128)(2,1)S(1)} custom-call(s32[1,8]{1,0:T(1,128)S(1)} %bitcast.2, bf16[768,2048]{1,0:T(8,128)(2,1)S(1)} %copy-done, bf16[512,768]{1,0:T(8,128)(2,1)S(1)} %get-tuple-element.16.rest_0_.k_ref.refs_2_, bf16[768,512]{1,0:T(8,128)(2,1)S(1)} %get-tuple-element.17.v_ref.refs_3_, ...), custom_call_target="tpu_custom_call" | custom-call | flops 1207959552 | bytes 1572864 | tf_op jit(solution)/shard_map/context_anchor/pallas_call | solution.py:383
  50.1 0.5 query_merge.3.rest_0_.own_ref
  50.7 0.5 collective-permute-start.13
  51.2 14.6 %context_anchor.6.rest_0_.refs_9_ = bf16[768,256]{1,0:T(8,128)(2,1)S(1)} custom-call(s32[1,8]{1,0:T(1,128)S(1)} %bitcast.3, bf16[768,2048]{1,0:T(8,128)(2,1)S(1)} %copy-done, bf16[512,768]{1,0:T(8,128)(2,1)S(1)} %get-tuple-element.16.rest_0_.k_ref.refs_2_, bf16[768,512]{1,0:T(8,128)(2,1)S(1)} %get-tuple-element.17.v_ref.refs_3_, ...), custom_call_target="tpu_custom_call" | custom-call | flops 1207959552 | bytes 1572864 | tf_op jit(solution)/shard_map/context_anchor/pallas_call | solution.py:383
  65.9 0.9 query_project.1.rest_0_.refs_7_.refs_8_.one_ref
  66.8 1.6 %collective-permute-start.15 = (bf16[64,1024]{1,0:T(8,128)(2,1)S(1)}, bf16[64,1024]{1,0:T(8,128)(2,1)S(1)}, u32[]{:S(2)}, u32[]{:S(2)}) collective-permute-start(bf16[64,1024]{1,0:T(8,128)(2,1)S(1)} %query_project.1.rest_0_.refs_7_.refs_8_.one_ref), channel_id=1, source_target_pairs={{0,1},{1,0},{2,3},{3,2},{4,5},{5,4},{6,7},{7,6},{8,9},{9,8},{10,11... | collective-permute-start | bytes 393224 | tf_op jit(solution)/shard_map/ppermute | solution.py:42
  68.4 28.9 %context_anchor.7.refs_8_.refs_10_ = bf16[768,512]{1,0:T(8,128)(2,1)S(1)} custom-call(s32[1,8]{1,0:T(1,128)S(1)} %bitcast.4, bf16[768,2048]{1,0:T(8,128)(2,1)S(1)} %copy-done, bf16[512,768]{1,0:T(8,128)(2,1)S(1)} %get-tuple-element.16.rest_0_.k_ref.refs_2_, bf16[768,512]{1,0:T(8,128)(2,1)S(1)} %get-tuple-element.17.v_ref.refs_3_, ...), custom_call_target="tpu_custom_call" | custom-call | flops 2415919104 | bytes 3145728 | tf_op jit(solution)/shard_map/context_anchor/pallas_call | solution.py:383
  97.6 14.7 %context_anchor.8.rest_0_.refs_11_ = bf16[768,256]{1,0:T(8,128)(2,1)S(1)} custom-call(s32[1,8]{1,0:T(1,128)S(1)} %bitcast.5, bf16[768,2048]{1,0:T(8,128)(2,1)S(1)} %copy-done, bf16[512,768]{1,0:T(8,128)(2,1)S(1)} %get-tuple-element.16.rest_0_.k_ref.refs_2_, bf16[768,512]{1,0:T(8,128)(2,1)S(1)} %get-tuple-element.17.v_ref.refs_3_, ...), custom_call_target="tpu_custom_call" | custom-call | flops 1207959552 | bytes 1572864 | tf_op jit(solution)/shard_map/context_anchor/pallas_call | solution.py:383
  112.3 2.7 %collective-permute-start.16 = (bf16[64,1024]{1,0:T(8,128)(2,1)S(1)}, bf16[64,1024]{1,0:T(8,128)(2,1)S(1)}, u32[]{:S(2)}, u32[]{:S(2)}) collective-permute-start(bf16[64,1024]{1,0:T(8,128)(2,1)S(1)} %query_sum.2.refs_12_.refs_13_.one_ref), channel_id=1, source_target_pairs={{0,2},{1,3},{2,0},{3,1},{4,6},{5,7},{6,4},{7,5},{8,10},{9,11},{10,... | collective-permute-start | bytes 393224 | tf_op jit(solution)/shard_map/ppermute | solution.py:42
  114.9 44.7 %context_anchor.9 = bf16[768,2048]{1,0:T(8,128)(2,1)} custom-call(s32[1,8]{1,0:T(1,128)S(1)} %bitcast.6, bf16[768,2048]{1,0:T(8,128)(2,1)S(1)} %copy-done, bf16[512,768]{1,0:T(8,128)(2,1)S(1)} %get-tuple-element.16.rest_0_.k_ref.refs_2_, bf16[768,512]{1,0:T(8,128)(2,1)S(1)} %get-tuple-element.17.v_ref.refs_3_, ...), custom_call_target="tpu_custom_call" | custom-call | flops 3623878656 | bytes 4718592 | tf_op jit(solution)/shard_map/context_anchor/pallas_call | solution.py:383
  159.7 0.7 query_sum.3
  (38 shorter events, 1.0 us)
Async XLA Ops:
  0.6 1.4 copy-start.2
  0.6 3.7 %copy-start = (bf16[768,2048]{1,0:T(8,128)(2,1)S(1)}, bf16[768,2048]{1,0:T(8,128)(2,1)}, u32[]{:S(2)}) copy-start(bf16[768,2048]{1,0:T(8,128)(2,1)} %refs_1_.9) | copy-start | bytes 9437188
  2.0 3.5 %collective-permute-start = (bf16[768,256]{1,0:T(8,128)(2,1)S(1)}, bf16[768,256]{1,0:T(8,128)(2,1)S(1)}, u32[]{:S(2)}, u32[]{:S(2)}) collective-permute-start(bf16[768,256]{1,0:T(8,128)(2,1)S(1)} %get-tuple-element.15.second_ref.v_ref), channel_id=1, source_target_pairs={{0,4},{4,0},{8,12},{12,8},{16,20},{20,16},{24,28},{28,24},{1,5},{5... | collective-permute-start | bytes 1179656 | tf_op jit(solution)/shard_map/ppermute | solution.py:42
  2.0 1.7 %collective-permute-start.1 = (bf16[8,2048]{1,0:T(8,128)(2,1)S(1)}, bf16[8,2048]{1,0:T(8,128)(2,1)S(1)}, u32[]{:S(2)}, u32[]{:S(2)}) collective-permute-start(bf16[8,2048]{1,0:T(8,128)(2,1)S(1)} %copy-done.2), channel_id=1, source_target_pairs={{0,4},{4,0},{8,12},{12,8},{16,20},{20,16},{24,28},{28,24},{1,5},{5... | collective-permute-start | bytes 98312 | tf_op jit(solution)/shard_map/ppermute | solution.py:42
  3.8 4.3 %collective-permute-start.3 = (bf16[16,2048]{1,0:T(8,128)(2,1)S(1)}, bf16[16,2048]{1,0:T(8,128)(2,1)S(1)}, u32[]{:S(2)}, u32[]{:S(2)}) collective-permute-start(bf16[16,2048]{1,0:T(8,128)(2,1)S(1)} %query_join.2.rest_0_.known_ref), channel_id=1, source_target_pairs={{0,8},{4,20},{8,0},{12,28},{16,24},{20,4},{24,16},{28,12},{1,9},{5... | collective-permute-start | bytes 196616 | tf_op jit(solution)/shard_map/ppermute | solution.py:42
  5.5 7.1 %collective-permute-start.5 = (bf16[768,128]{1,0:T(8,128)(2,1)S(1)}, bf16[768,128]{1,0:T(8,128)(2,1)S(1)}, u32[]{:S(2)}, u32[]{:S(2)}) collective-permute-start(bf16[768,128]{1,0:T(8,128)(2,1)S(1)} %get-tuple-element.19.rest_0_.one_ref), channel_id=1, source_target_pairs={{0,8},{4,20},{8,0},{12,28},{16,24},{20,4},{24,16},{28,12},{1,9},{5... | collective-permute-start | bytes 589832 | tf_op jit(solution)/shard_map/ppermute | solution.py:42
  8.1 5.8 %collective-permute-start.4 = (bf16[32,2048]{1,0:T(8,128)(2,1)S(1)}, bf16[32,2048]{1,0:T(8,128)(2,1)S(1)}, u32[]{:S(2)}, u32[]{:S(2)}) collective-permute-start(bf16[32,2048]{1,0:T(8,128)(2,1)S(1)} %query_join.3.rest_0_.known_ref), channel_id=1, source_target_pairs={{0,16},{4,12},{8,24},{12,4},{16,0},{20,28},{24,8},{28,20},{1,17},{... | collective-permute-start | bytes 393224 | tf_op jit(solution)/shard_map/ppermute | solution.py:42
  8.7 18.6 %collective-permute-start.2 = (bf16[768,128]{1,0:T(8,128)(2,1)S(1)}, bf16[768,128]{1,0:T(8,128)(2,1)S(1)}, u32[]{:S(2)}, u32[]{:S(2)}) collective-permute-start(bf16[768,128]{1,0:T(8,128)(2,1)S(1)} %get-tuple-element.18.one_ref), channel_id=1, source_target_pairs={{0,8},{4,20},{8,0},{12,28},{16,24},{20,4},{24,16},{28,12},{1,9},{5... | collective-permute-start | bytes 589832 | tf_op jit(solution)/shard_map/ppermute | solution.py:42
  11.8 2.1 %copy-start.3 = (s32[8]{0:T(128)S(1)}, s32[8]{0:T(128)}, u32[]{:S(2)}) copy-start(s32[8]{0:T(128)} %param.8) | copy-start | bytes 100
  11.8 2.1 %copy-start.4 = (bf16[2,8,1024]{2,1,0:T(8,128)(2,1)S(1)}, bf16[2,8,1024]{2,1,0:T(8,128)(2,1)}, u32[]{:S(2)}) copy-start(bf16[2,8,1024]{2,1,0:T(8,128)(2,1)} %self_ref.1) | copy-start | bytes 98308
  12.7 14.6 %collective-permute-start.8 = (bf16[768,128]{1,0:T(8,128)(2,1)S(1)}, bf16[768,128]{1,0:T(8,128)(2,1)S(1)}, u32[]{:S(2)}, u32[]{:S(2)}) collective-permute-start(bf16[768,128]{1,0:T(8,128)(2,1)S(1)} %anchor_relay.6.rest_0_.one_ref), channel_id=1, source_target_pairs={{0,16},{4,12},{8,24},{12,4},{16,0},{20,28},{24,8},{28,20},{1,17},{... | collective-permute-start | bytes 589832 | tf_op jit(solution)/shard_map/ppermute | solution.py:42
  25.3 3.9 %collective-permute-start.7 = (bf16[64,1152]{1,0:T(8,128)(2,1)S(1)}, bf16[64,1152]{1,0:T(8,128)(2,1)S(1)}, u32[]{:S(2)}, u32[]{:S(2)}) collective-permute-start(bf16[64,1152]{1,0:T(8,128)(2,1)S(1)} %get-tuple-element.21), channel_id=1, source_target_pairs={{0,4},{4,0},{8,12},{12,8},{16,20},{20,16},{24,28},{28,24},{1,5},{5... | collective-permute-start | bytes 442376 | tf_op jit(solution)/shard_map/ppermute | solution.py:42
  27.3 7.6 %collective-permute-start.12 = (bf16[768,128]{1,0:T(8,128)(2,1)S(1)}, bf16[768,128]{1,0:T(8,128)(2,1)S(1)}, u32[]{:S(2)}, u32[]{:S(2)}) collective-permute-start(bf16[768,128]{1,0:T(8,128)(2,1)S(1)} %anchor_relay.8.refs_2_.first_ref), channel_id=1, source_target_pairs={{0,4},{4,0},{8,12},{12,8},{16,20},{20,16},{24,28},{28,24},{1,5},{5... | collective-permute-start | bytes 589832 | tf_op jit(solution)/shard_map/ppermute | solution.py:42
  27.9 22.7 %collective-permute-start.6 = (bf16[768,128]{1,0:T(8,128)(2,1)S(1)}, bf16[768,128]{1,0:T(8,128)(2,1)S(1)}, u32[]{:S(2)}, u32[]{:S(2)}) collective-permute-start(bf16[768,128]{1,0:T(8,128)(2,1)S(1)} %anchor_relay.7.rest_0_.one_ref), channel_id=1, source_target_pairs={{0,16},{4,12},{8,24},{12,4},{16,0},{20,28},{24,8},{28,20},{1,17},{... | collective-permute-start | bytes 589832 | tf_op jit(solution)/shard_map/ppermute | solution.py:42
  29.5 20.5 %collective-permute-start.10 = (bf16[64,1152]{1,0:T(8,128)(2,1)S(1)}, bf16[64,1152]{1,0:T(8,128)(2,1)S(1)}, u32[]{:S(2)}, u32[]{:S(2)}) collective-permute-start(bf16[64,1152]{1,0:T(8,128)(2,1)S(1)} %query_merge.2.rest_0_.refs_0_), channel_id=1, source_target_pairs={{0,8},{4,12},{8,0},{12,4},{16,24},{20,28},{24,16},{28,20},{1,9},{5... | collective-permute-start | bytes 442376 | tf_op jit(solution)/shard_map/ppermute | solution.py:42
  30.5 19.6 %collective-permute-start.11 = (bf16[64,1152]{1,0:T(8,128)(2,1)S(1)}, bf16[64,1152]{1,0:T(8,128)(2,1)S(1)}, u32[]{:S(2)}, u32[]{:S(2)}) collective-permute-start(bf16[64,1152]{1,0:T(8,128)(2,1)S(1)} %query_merge.2.rest_0_.refs_0_), channel_id=1, source_target_pairs={{0,16},{4,20},{8,24},{12,28},{16,0},{20,4},{24,8},{28,12},{1,17},{... | collective-permute-start | bytes 442376 | tf_op jit(solution)/shard_map/ppermute | solution.py:42
  31.8 18.2 %collective-permute-start.9 = (bf16[64,1152]{1,0:T(8,128)(2,1)S(1)}, bf16[64,1152]{1,0:T(8,128)(2,1)S(1)}, u32[]{:S(2)}, u32[]{:S(2)}) collective-permute-start(bf16[64,1152]{1,0:T(8,128)(2,1)S(1)} %query_merge.2.rest_0_.refs_0_), channel_id=1, source_target_pairs={{0,24},{4,28},{8,16},{12,20},{16,8},{20,12},{24,0},{28,4},{1,25},{... | collective-permute-start | bytes 442376 | tf_op jit(solution)/shard_map/ppermute | solution.py:42
  50.5 15.3 %collective-permute-start.14 = (bf16[64,1024]{1,0:T(8,128)(2,1)S(1)}, bf16[64,1024]{1,0:T(8,128)(2,1)S(1)}, u32[]{:S(2)}, u32[]{:S(2)}) collective-permute-start(bf16[64,1024]{1,0:T(8,128)(2,1)S(1)} %query_merge.3.rest_0_.own_ref), channel_id=1, source_target_pairs={{0,4},{4,0},{8,12},{12,8},{16,20},{20,16},{24,28},{28,24},{1,5},{5... | collective-permute-start | bytes 393224 | tf_op jit(solution)/shard_map/ppermute | solution.py:42
  50.7 15.2 %copy-start.1 = (bf16[2048,1024]{1,0:T(8,128)(2,1)S(1)}, bf16[2048,1024]{1,0:T(8,128)(2,1)}, u32[]{:S(2)}) copy-start(bf16[2048,1024]{1,0:T(8,128)(2,1)} %w_ref.1) | copy-start | bytes 12582916
  50.7 46.7 %collective-permute-start.13 = (bf16[768,128]{1,0:T(8,128)(2,1)S(1)}, bf16[768,128]{1,0:T(8,128)(2,1)S(1)}, u32[]{:S(2)}, u32[]{:S(2)}) collective-permute-start(bf16[768,128]{1,0:T(8,128)(2,1)S(1)} %anchor_relay.9.refs_7_.first_ref), channel_id=1, source_target_pairs={{0,4},{4,0},{8,12},{12,8},{16,20},{20,16},{24,28},{28,24},{1,5},{5... | collective-permute-start | bytes 589832 | tf_op jit(solution)/shard_map/ppermute | solution.py:42
  66.8 45.5 %collective-permute-start.15 = (bf16[64,1024]{1,0:T(8,128)(2,1)S(1)}, bf16[64,1024]{1,0:T(8,128)(2,1)S(1)}, u32[]{:S(2)}, u32[]{:S(2)}) collective-permute-start(bf16[64,1024]{1,0:T(8,128)(2,1)S(1)} %query_project.1.rest_0_.refs_7_.refs_8_.one_ref), channel_id=1, source_target_pairs={{0,1},{1,0},{2,3},{3,2},{4,5},{5,4},{6,7},{7,6},{8,9},{9,8},{10,11... | collective-permute-start | bytes 393224 | tf_op jit(solution)/shard_map/ppermute | solution.py:42
  112.3 47.4 %collective-permute-start.16 = (bf16[64,1024]{1,0:T(8,128)(2,1)S(1)}, bf16[64,1024]{1,0:T(8,128)(2,1)S(1)}, u32[]{:S(2)}, u32[]{:S(2)}) collective-permute-start(bf16[64,1024]{1,0:T(8,128)(2,1)S(1)} %query_sum.2.refs_12_.refs_13_.one_ref), channel_id=1, source_target_pairs={{0,2},{1,3},{2,0},{3,1},{4,6},{5,7},{6,4},{7,5},{8,10},{9,11},{10,... | collective-permute-start | bytes 393224 | tf_op jit(solution)/shard_map/ppermute | solution.py:42

commit v10 on v9

--- a/solution.py
+++ b/solution.py
@@ -96,22 +96,28 @@
     return run
 
 
-def join(low_of, known, landed, after=()):
-    rows, width = known.shape
-
-    def kernel(known_ref, landed_ref, *rest):
-        out_ref = rest[-1]
-
-        def put(first, second):
-            def run():
-                both = jnp.concatenate([first[...].astype(F32), second[...].astype(F32)], 0)
-                out_ref[...] = both.astype(BF)
-
-            return run
-
-        choose(low_of(lax.axis_index("hst")), put(known_ref, landed_ref), put(landed_ref, known_ref))
-
-    return small_call(kernel, "query_join", [(2 * rows, width)], (known, landed), after)[0]
+def by_chip(own, others, bits, after=()):
+    rows, width = own.shape
+
+    def kernel(*refs):
+        out_ref, all_ref = refs[-2:]
+        host = lax.axis_index("hst")
+        for ref, flip in zip(refs, (0,) + tuple(bits)):
+            start = pl.multiple_of((jnp.bitwise_xor(host, flip) >> 1) * rows, rows)
+            all_ref[pl.ds(start, rows), :] = ref[...].astype(F32)
+        out_ref[...] = all_ref[...].astype(BF)
+
+    total = rows * (1 + len(bits))
+    return pl.pallas_call(
+        kernel,
+        out_shape=jax.ShapeDtypeStruct((total, width), BF),
+        in_specs=[VMEM] * (1 + len(bits)) + [ANY] * len(after),
+        out_specs=VMEM,
+        scratch_shapes=[pltpu.VMEM((total, width), F32)],
+        compiler_params=params(),
+        cost_estimate=pl.CostEstimate(flops=0, bytes_accessed=2**20, transcendentals=0),
+        name="query_chips",
+    )(own, *others, *after)
 
 
 def relay(keep_of, one, two, after=(), split=1):
@@ -418,26 +424,24 @@
     slab, columns = v_ref.shape
     width = per_kv * columns
     query_count = 8 * q_rows
-    block = 2 * q_rows
     host = lax.axis_index("hst")
     own_len = length_of(lengths_ref, host)
     rows = per_kv * query_count
     odd = bit(host, 0) == 1
-    low = jnp.where(odd, bit(host, 1), bit(host, 2)) == 0
-
-    def place(lower, upper, spread_out):
-        middle = (2, 1) if spread_out else (1, 2)
-        for ref, chips in ((lower, (0, middle[0])), (upper, (middle[1], 3))):
-            for n, chip in enumerate(chips):
-                for h in range(width // HD):
-                    to = h * query_count + chip * block
-                    q_all[to : to + block, :] = ref[n * block : (n + 1) * block, h * HD : (h + 1) * HD]
-
-    for is_low, is_odd in ((False, False), (False, True), (True, False), (True, True)):
-        @pl.when((low == is_low) & (odd == is_odd))
-        def _():
-            pair = (known_ref, landed_ref) if is_low else (landed_ref, known_ref)
-            place(*pair, is_odd)
+
+    def place(even_ref, odd_ref):
+        def run():
+            parts = []
+            for chip in range(4):
+                at = slice(chip * q_rows, (chip + 1) * q_rows)
+                parts += [even_ref[at, :].astype(F32), odd_ref[at, :].astype(F32)]
+            queries = jnp.concatenate(parts, 0).astype(BF)
+            for h in range(width // HD):
+                q_all[h * query_count : (h + 1) * query_count, :] = queries[:, h * HD : (h + 1) * HD]
+
+        return run
+
+    choose(odd, place(landed_ref, known_ref), place(known_ref, landed_ref))
 
     first = lax.axis_index("tp") * (width // HD) // group_size * HD
     own_cols = pl.ds(pl.multiple_of(first, HD), columns)
@@ -691,21 +695,17 @@
     def done_early(h):
         return (h <= 2) | (h == 5)
 
-    def near_low(h):
-        return jnp.where(bit(h, 0) == 1, bit(h, 2), bit(h, 1)) == 0
-
-    landed = swap(query_q, "hst", hosts, 1, 1)
+    bits = (6, 2, 4)
+    landed = [swap(query_q, "hst", hosts, x, x) for x in bits]
     own_k, own_v = pick(ctx_kv, kv_local, local_heads)
     value_landed = swap(own_v, "hst", hosts, 1, 1)
     own_keys, own_values = prepare(own_k, own_v, False)
-    queries = join(is_even, query_q, landed, (own_keys,))
-    landed = swap(queries, "hst", hosts, *along[0])
-    done = own(0, 2, (queries,))
+    done = own(0, 2)
     parts = list(relay(is_even, own_k, value_landed, (done,), kv_local))
     parts_landed = [swap(x, "hst", hosts, *along[0]) for x in parts]
-    queries = join(near_low, queries, landed, (parts[0],))
-    landed = swap(queries, "hst", hosts, *along[1])
-    done = own(2, 6, (queries,))
+    queries = by_chip(query_q, landed, bits, (parts[0],))
+    landed = swap(queries, "hst", hosts, 1, 1)
+    done = own(2, 2, (queries,))
     anchor = {}
 
     def pass_on(kv, after):
@@ -718,15 +718,17 @@
         anchor[kv] = held, swap(held, "hst", hosts, 1, 1)
         return held
 
-    done = pass_on(0, (done,))
     keep, give = source_part(lengths, own_keys, own_v, query_kv, queries, landed, q_rows, per_kv, (done,))
     landed = swap(give, "hst", hosts, 1, 1)
-    done = own(8, 4, (keep,))
+    done = own(4, 4, (keep,))
+    source = merge_part([keep, landed], False, (done,))
+    landed = swap(source, "hst", hosts, *along[0])
+    done = pass_on(0, (source,))
+    done = own(8, 8, (done,))
+    source = merge_part([source, landed], False, (done,))
+    landed = swap(source, "hst", hosts, *along[1])
+    done = complete(0, (source,))
     done = pass_on(1, (done,))
-    done = complete(0, (done,))
-    source = merge_part([keep, landed], False, (done,))
-    landed = [swap(source, "hst", hosts, x, x) for x in (6, 2, 4)]
-    done = own(12, 4, (source,))
     anchor[0] = prepare(*anchor[0], True, (done,))
     results = {}
 
@@ -737,14 +739,14 @@
         )
         return results[first]
 
-    done = anchors(0, 2, ())
-    attended = merge_part([source, *landed], True, (done,))
+    done = anchors(0, 4, ())
+    attended = merge_part([source, landed], True, (done,))
     landed = swap(attended, "hst", hosts, 1, 1)
     done = complete(1, (attended,))
-    done = anchors(2, 2, (done,))
+    done = anchors(4, 2, (done,))
     terms = project_part(attended, landed, out_weight, (done,))
     anchor[1] = prepare(*anchor[1], True, (terms,))
-    shares = [[(10, 6, True)], [(4, 4, False), (8, 2, False)]]
+    shares = [[(12, 4, True)], [(6, 2, False), (8, 4, False)]]
     step = 1
     while step < groups:
         landed = swap(terms, "tp", groups, step, step)

time: 161 us -> 160 us (level)
  transfers between devices with their start and end apart: 17 -> 17, of which waited for: 3 -> 2; matrix products, arithmetic and copies ran while one was open for 0% -> 0% of each run, Pallas kernels for 87% -> 88%
where the time goes in v10:
time: 160 us
  Pallas kernels  142 us (89%)
  starting transfers between devices  15.4 us (10%)
    pallas_call x5, Pallas kernels, anchor_part(): pl.pallas_call(functools.partial(anchor_kernel, first, count, bases, per_...  118 us
    ppermute x17, starting transfers between devices, swap(): lax.ppermute(value, axis, [(i, i ^ (odd if i & 1 else even)) for i in ran...  15.4 us
    pallas_call x1, Pallas kernels, source_part(): pl.pallas_call(functools.partial(source_kernel, per_kv, q_rows, H // KVH)...  11.4 us
    pallas_call x4, Pallas kernels, own_part(): pl.pallas_call(functools.partial(own_kernel, first, count, per_kv), out_s...  7.95 us
  transfers between devices with their start and end apart: 17, of which 2 were waited for; matrix products, arithmetic and copies ran while one was open for 0% of the time, Pallas kernels for 88%

profile of v10, /device:TPU:6, one launch (start us, length us, event | category | flops | bytes accessed | tf_op | source)
XLA Modules:
  0.0 159.5 jit_solution(3163358221677397374)
XLA Ops:
  0.6 1.3 pick_columns.1
  2.1 2.0 %collective-permute-start.4 = (bf16[8,2048]{1,0:T(8,128)(2,1)S(1)}, bf16[8,2048]{1,0:T(8,128)(2,1)S(1)}, u32[]{:S(2)}, u32[]{:S(2)}) collective-permute-start(bf16[8,2048]{1,0:T(8,128)(2,1)S(1)} %copy-done.3), channel_id=1, source_target_pairs={{0,8},{4,12},{8,0},{12,4},{16,24},{20,28},{24,16},{28,20},{1,9},{5... | collective-permute-start | bytes 98312 | tf_op jit(solution)/shard_map/ppermute | solution.py:42
  4.1 1.5 collective-permute-start.5
  5.6 0.4 operands.3
  6.0 1.1 context_own.4.rest_0_.refs_6_
  7.2 0.8 collective-permute-done.5.refs_3_
  8.1 0.2 collective-permute-start.2
  8.3 1.9 %collective-permute-start.1 = (bf16[768,128]{1,0:T(8,128)(2,1)S(1)}, bf16[768,128]{1,0:T(8,128)(2,1)S(1)}, u32[]{:S(2)}, u32[]{:S(2)}) collective-permute-start(bf16[768,128]{1,0:T(8,128)(2,1)S(1)} %get-tuple-element.18.one_ref), channel_id=1, source_target_pairs={{0,8},{4,20},{8,0},{12,28},{16,24},{20,4},{24,16},{28,12},{1,9},{5... | collective-permute-start | bytes 589832 | tf_op jit(solution)/shard_map/ppermute | solution.py:42
  10.2 1.1 context_own.5.rest_0_.refs_7_
  11.3 11.4 %query_source.1 = (bf16[64,1152]{1,0:T(8,128)(2,1)S(1)}, bf16[64,1152]{1,0:T(8,128)(2,1)S(1)}) custom-call(s32[1,8]{1,0:T(1,128)S(1)} %bitcast.1, bf16[512,768]{1,0:T(8,128)(2,1)S(1)} %get-tuple-element.16.k_ref.refs_2_, bf16[768,256]{1,0:T(8,128)(2,1)S(1)} %get-tuple-element.15.second_ref.v_ref, bf16[2,8,1024]{2,1,0:T(8,128)(2,1)S(1)} %copy-done.2, ...), custom_call_target="tpu_custom_call" | custom-call | flops 805306368 | bytes 2097152 | tf_op jit(solution)/shard_map/query_source/pallas_call | solution.py:548
  22.8 1.9 %context_own.6.refs_2_.refs_6_ = f32[768,1024]{1,0:T(8,128)S(1)} custom-call(bf16[768,2048]{1,0:T(8,128)(2,1)S(1)} %copy-done, bf16[512,768]{1,0:T(8,128)(2,1)S(1)} %get-tuple-element.16.k_ref.refs_2_, bf16[768,512]{1,0:T(8,128)(2,1)S(1)} %get-tuple-element.17.v_ref.refs_3_, bf16[64,1152]{1,0:T(8,128)(2,1)S(1)} %get-tuple-element.20.rest_0_.refs_0_), custom_call_target="tpu_custom_call" | custom-call | flops 1610612736 | bytes 2359296 | tf_op jit(solution)/shard_map/context_own/pallas_call | solution.py:241
  24.7 0.3 query_merge.3.rest_0_.refs_0_
  25.1 0.2 collective-permute-start.9
  25.3 1.9 %collective-permute-start.8 = (bf16[768,128]{1,0:T(8,128)(2,1)S(1)}, bf16[768,128]{1,0:T(8,128)(2,1)S(1)}, u32[]{:S(2)}, u32[]{:S(2)}) collective-permute-start(bf16[768,128]{1,0:T(8,128)(2,1)S(1)} %anchor_relay.6.rest_0_.one_ref), channel_id=1, source_target_pairs={{0,16},{4,12},{8,24},{12,4},{16,0},{20,28},{24,8},{28,20},{1,17},{... | collective-permute-start | bytes 589832 | tf_op jit(solution)/shard_map/ppermute | solution.py:42
  27.3 3.8 %context_own.7.refs_2_.refs_6_ = f32[768,2048]{1,0:T(8,128)S(1)} custom-call(bf16[768,2048]{1,0:T(8,128)(2,1)S(1)} %copy-done, bf16[512,768]{1,0:T(8,128)(2,1)S(1)} %get-tuple-element.16.k_ref.refs_2_, bf16[768,512]{1,0:T(8,128)(2,1)S(1)} %get-tuple-element.17.v_ref.refs_3_, bf16[768,128]{1,0:T(8,128)(2,1)S(1)} %anchor_relay.6.rest_0_.one_ref), custom_call_target="tpu_custom_call" | custom-call | flops 3221225472 | bytes 4718592 | tf_op jit(solution)/shard_map/context_own/pallas_call | solution.py:241
  31.1 0.3 query_merge.4.rest_0_.refs_0_
  31.5 0.4 collective-permute-done.8.two_ref
  31.9 0.4 collective-permute-start.12
  32.3 1.6 %collective-permute-start.11 = (bf16[64,1152]{1,0:T(8,128)(2,1)S(1)}, bf16[64,1152]{1,0:T(8,128)(2,1)S(1)}, u32[]{:S(2)}, u32[]{:S(2)}) collective-permute-start(bf16[64,1152]{1,0:T(8,128)(2,1)S(1)} %query_merge.4.rest_0_.refs_0_), channel_id=1, source_target_pairs={{0,16},{4,12},{8,24},{12,4},{16,0},{20,28},{24,8},{28,20},{1,17},{... | collective-permute-start | bytes 442376 | tf_op jit(solution)/shard_map/ppermute | solution.py:42
  33.9 0.5 collective-permute-start.10
  34.6 29.3 %context_anchor.5.refs_2_.refs_7_ = bf16[768,512]{1,0:T(8,128)(2,1)S(1)} custom-call(s32[1,8]{1,0:T(1,128)S(1)} %bitcast.2, bf16[768,2048]{1,0:T(8,128)(2,1)S(1)} %copy-done, bf16[512,768]{1,0:T(8,128)(2,1)S(1)} %get-tuple-element.16.k_ref.refs_2_, bf16[768,512]{1,0:T(8,128)(2,1)S(1)} %get-tuple-element.17.v_ref.refs_3_, ...), custom_call_target="tpu_custom_call" | custom-call | flops 2415919104 | bytes 3145728 | tf_op jit(solution)/shard_map/context_anchor/pallas_call | solution.py:389
  64.0 0.3 query_merge.5.rest_0_.own_ref
  64.4 0.5 collective-permute-start.13
  65.0 14.6 %context_anchor.6.rest_0_.refs_8_ = bf16[768,256]{1,0:T(8,128)(2,1)S(1)} custom-call(s32[1,8]{1,0:T(1,128)S(1)} %bitcast.3, bf16[768,2048]{1,0:T(8,128)(2,1)S(1)} %copy-done, bf16[512,768]{1,0:T(8,128)(2,1)S(1)} %get-tuple-element.16.k_ref.refs_2_, bf16[768,512]{1,0:T(8,128)(2,1)S(1)} %get-tuple-element.17.v_ref.refs_3_, ...), custom_call_target="tpu_custom_call" | custom-call | flops 1207959552 | bytes 1572864 | tf_op jit(solution)/shard_map/context_anchor/pallas_call | solution.py:389
  79.6 0.9 query_project.1.rest_0_.refs_7_.refs_8_.one_ref
  80.5 1.6 %collective-permute-start.15 = (bf16[64,1024]{1,0:T(8,128)(2,1)S(1)}, bf16[64,1024]{1,0:T(8,128)(2,1)S(1)}, u32[]{:S(2)}, u32[]{:S(2)}) collective-permute-start(bf16[64,1024]{1,0:T(8,128)(2,1)S(1)} %query_project.1.rest_0_.refs_7_.refs_8_.one_ref), channel_id=1, source_target_pairs={{0,1},{1,0},{2,3},{3,2},{4,5},{5,4},{6,7},{7,6},{8,9},{9,8},{10,11... | collective-permute-start | bytes 393224 | tf_op jit(solution)/shard_map/ppermute | solution.py:42
  82.1 14.6 %context_anchor.7.refs_8_.refs_9_ = bf16[768,256]{1,0:T(8,128)(2,1)S(1)} custom-call(s32[1,8]{1,0:T(1,128)S(1)} %bitcast.4, bf16[768,2048]{1,0:T(8,128)(2,1)S(1)} %copy-done, bf16[512,768]{1,0:T(8,128)(2,1)S(1)} %get-tuple-element.16.k_ref.refs_2_, bf16[768,512]{1,0:T(8,128)(2,1)S(1)} %get-tuple-element.17.v_ref.refs_3_, ...), custom_call_target="tpu_custom_call" | custom-call | flops 1207959552 | bytes 1572864 | tf_op jit(solution)/shard_map/context_anchor/pallas_call | solution.py:389
  96.8 0.2 operands.5
  97.0 29.0 %context_anchor.8.rest_0_.refs_10_ = bf16[768,512]{1,0:T(8,128)(2,1)S(1)} custom-call(s32[1,8]{1,0:T(1,128)S(1)} %bitcast.5, bf16[768,2048]{1,0:T(8,128)(2,1)S(1)} %copy-done, bf16[512,768]{1,0:T(8,128)(2,1)S(1)} %get-tuple-element.16.k_ref.refs_2_, bf16[768,512]{1,0:T(8,128)(2,1)S(1)} %get-tuple-element.17.v_ref.refs_3_, ...), custom_call_target="tpu_custom_call" | custom-call | flops 2415919104 | bytes 3145728 | tf_op jit(solution)/shard_map/context_anchor/pallas_call | solution.py:389
  126.0 2.7 %collective-permute-start.16 = (bf16[64,1024]{1,0:T(8,128)(2,1)S(1)}, bf16[64,1024]{1,0:T(8,128)(2,1)S(1)}, u32[]{:S(2)}, u32[]{:S(2)}) collective-permute-start(bf16[64,1024]{1,0:T(8,128)(2,1)S(1)} %query_sum.2.refs_11_.refs_12_.one_ref), channel_id=1, source_target_pairs={{0,2},{1,3},{2,0},{3,1},{4,6},{5,7},{6,4},{7,5},{8,10},{9,11},{10,... | collective-permute-start | bytes 393224 | tf_op jit(solution)/shard_map/ppermute | solution.py:42
  128.7 30.1 %context_anchor.9 = bf16[768,2048]{1,0:T(8,128)(2,1)} custom-call(s32[1,8]{1,0:T(1,128)S(1)} %bitcast.6, bf16[768,2048]{1,0:T(8,128)(2,1)S(1)} %copy-done, bf16[512,768]{1,0:T(8,128)(2,1)S(1)} %get-tuple-element.16.k_ref.refs_2_, bf16[768,512]{1,0:T(8,128)(2,1)S(1)} %get-tuple-element.17.v_ref.refs_3_, bf16[256,768]{1,0:T(8,128)(2,1)S(1)} %get-tuple-element.24.refs_4_, ...), custom_call_target="tpu_custom_call" | custom-call | flops 2415919104 | bytes 3145728 | tf_op jit(solution)/shard_map/context_anchor/pallas_call | solution.py:389
  158.8 0.7 query_sum.3
  (38 shorter events, 0.8 us)
Async XLA Ops:
  0.6 1.4 copy-start.3
  0.6 5.3 %copy-start = (bf16[768,2048]{1,0:T(8,128)(2,1)S(1)}, bf16[768,2048]{1,0:T(8,128)(2,1)}, u32[]{:S(2)}) copy-start(bf16[768,2048]{1,0:T(8,128)(2,1)} %refs_1_.9) | copy-start | bytes 9437188
  2.0 5.1 %collective-permute-start = (bf16[768,256]{1,0:T(8,128)(2,1)S(1)}, bf16[768,256]{1,0:T(8,128)(2,1)S(1)}, u32[]{:S(2)}, u32[]{:S(2)}) collective-permute-start(bf16[768,256]{1,0:T(8,128)(2,1)S(1)} %get-tuple-element.15.second_ref.v_ref), channel_id=1, source_target_pairs={{0,4},{4,0},{8,12},{12,8},{16,20},{20,16},{24,28},{28,24},{1,5},{5... | collective-permute-start | bytes 1179656 | tf_op jit(solution)/shard_map/ppermute | solution.py:42
  2.0 5.1 %collective-permute-start.3 = (bf16[8,2048]{1,0:T(8,128)(2,1)S(1)}, bf16[8,2048]{1,0:T(8,128)(2,1)S(1)}, u32[]{:S(2)}, u32[]{:S(2)}) collective-permute-start(bf16[8,2048]{1,0:T(8,128)(2,1)S(1)} %copy-done.3), channel_id=1, source_target_pairs={{0,24},{4,28},{8,16},{12,20},{16,8},{20,12},{24,0},{28,4},{1,25},{... | collective-permute-start | bytes 98312 | tf_op jit(solution)/shard_map/ppermute | solution.py:42
  2.1 5.1 %collective-permute-start.4 = (bf16[8,2048]{1,0:T(8,128)(2,1)S(1)}, bf16[8,2048]{1,0:T(8,128)(2,1)S(1)}, u32[]{:S(2)}, u32[]{:S(2)}) collective-permute-start(bf16[8,2048]{1,0:T(8,128)(2,1)S(1)} %copy-done.3), channel_id=1, source_target_pairs={{0,8},{4,12},{8,0},{12,4},{16,24},{20,28},{24,16},{28,20},{1,9},{5... | collective-permute-start | bytes 98312 | tf_op jit(solution)/shard_map/ppermute | solution.py:42
  4.1 3.9 %collective-permute-start.5 = (bf16[8,2048]{1,0:T(8,128)(2,1)S(1)}, bf16[8,2048]{1,0:T(8,128)(2,1)S(1)}, u32[]{:S(2)}, u32[]{:S(2)}) collective-permute-start(bf16[8,2048]{1,0:T(8,128)(2,1)S(1)} %copy-done.3), channel_id=1, source_target_pairs={{0,16},{4,20},{8,24},{12,28},{16,0},{20,4},{24,8},{28,12},{1,17},{... | collective-permute-start | bytes 98312 | tf_op jit(solution)/shard_map/ppermute | solution.py:42
  8.0 3.3 %collective-permute-start.6 = (bf16[32,2048]{1,0:T(8,128)(2,1)S(1)}, bf16[32,2048]{1,0:T(8,128)(2,1)S(1)}, u32[]{:S(2)}, u32[]{:S(2)}) collective-permute-start(bf16[32,2048]{1,0:T(8,128)(2,1)S(1)} %query_chips.1.rest_0_.known_ref), channel_id=1, source_target_pairs={{0,4},{4,0},{8,12},{12,8},{16,20},{20,16},{24,28},{28,24},{1,5},{5... | collective-permute-start | bytes 393224 | tf_op jit(solution)/shard_map/ppermute | solution.py:42
  8.1 17.2 %collective-permute-start.2 = (bf16[768,128]{1,0:T(8,128)(2,1)S(1)}, bf16[768,128]{1,0:T(8,128)(2,1)S(1)}, u32[]{:S(2)}, u32[]{:S(2)}) collective-permute-start(bf16[768,128]{1,0:T(8,128)(2,1)S(1)} %get-tuple-element.19.refs_4_.one_ref), channel_id=1, source_target_pairs={{0,8},{4,20},{8,0},{12,28},{16,24},{20,4},{24,16},{28,12},{1,9},{5... | collective-permute-start | bytes 589832 | tf_op jit(solution)/shard_map/ppermute | solution.py:42
  8.3 3.0 %copy-start.2 = (bf16[2,8,1024]{2,1,0:T(8,128)(2,1)S(1)}, bf16[2,8,1024]{2,1,0:T(8,128)(2,1)}, u32[]{:S(2)}) copy-start(bf16[2,8,1024]{2,1,0:T(8,128)(2,1)} %self_ref.1) | copy-start | bytes 98308
  8.3 3.0 %copy-start.4 = (s32[8]{0:T(128)S(1)}, s32[8]{0:T(128)}, u32[]{:S(2)}) copy-start(s32[8]{0:T(128)} %param.8) | copy-start | bytes 100
  8.3 25.6 %collective-permute-start.1 = (bf16[768,128]{1,0:T(8,128)(2,1)S(1)}, bf16[768,128]{1,0:T(8,128)(2,1)S(1)}, u32[]{:S(2)}, u32[]{:S(2)}) collective-permute-start(bf16[768,128]{1,0:T(8,128)(2,1)S(1)} %get-tuple-element.18.one_ref), channel_id=1, source_target_pairs={{0,8},{4,20},{8,0},{12,28},{16,24},{20,4},{24,16},{28,12},{1,9},{5... | collective-permute-start | bytes 589832 | tf_op jit(solution)/shard_map/ppermute | solution.py:42
  22.7 2.0 %collective-permute-start.7 = (bf16[64,1152]{1,0:T(8,128)(2,1)S(1)}, bf16[64,1152]{1,0:T(8,128)(2,1)S(1)}, u32[]{:S(2)}, u32[]{:S(2)}) collective-permute-start(bf16[64,1152]{1,0:T(8,128)(2,1)S(1)} %get-tuple-element.21), channel_id=1, source_target_pairs={{0,4},{4,0},{8,12},{12,8},{16,20},{20,16},{24,28},{28,24},{1,5},{5... | collective-permute-start | bytes 442376 | tf_op jit(solution)/shard_map/ppermute | solution.py:42
  25.1 6.1 %collective-permute-start.9 = (bf16[64,1152]{1,0:T(8,128)(2,1)S(1)}, bf16[64,1152]{1,0:T(8,128)(2,1)S(1)}, u32[]{:S(2)}, u32[]{:S(2)}) collective-permute-start(bf16[64,1152]{1,0:T(8,128)(2,1)S(1)} %query_merge.3.rest_0_.refs_0_), channel_id=1, source_target_pairs={{0,8},{4,20},{8,0},{12,28},{16,24},{20,4},{24,16},{28,12},{1,9},{5... | collective-permute-start | bytes 442376 | tf_op jit(solution)/shard_map/ppermute | solution.py:42
  25.3 6.6 %collective-permute-start.8 = (bf16[768,128]{1,0:T(8,128)(2,1)S(1)}, bf16[768,128]{1,0:T(8,128)(2,1)S(1)}, u32[]{:S(2)}, u32[]{:S(2)}) collective-permute-start(bf16[768,128]{1,0:T(8,128)(2,1)S(1)} %anchor_relay.6.rest_0_.one_ref), channel_id=1, source_target_pairs={{0,16},{4,12},{8,24},{12,4},{16,0},{20,28},{24,8},{28,20},{1,17},{... | collective-permute-start | bytes 589832 | tf_op jit(solution)/shard_map/ppermute | solution.py:42
  31.9 2.5 %collective-permute-start.12 = (bf16[768,128]{1,0:T(8,128)(2,1)S(1)}, bf16[768,128]{1,0:T(8,128)(2,1)S(1)}, u32[]{:S(2)}, u32[]{:S(2)}) collective-permute-start(bf16[768,128]{1,0:T(8,128)(2,1)S(1)} %anchor_relay.7.rest_0_.first_ref), channel_id=1, source_target_pairs={{0,4},{4,0},{8,12},{12,8},{16,20},{20,16},{24,28},{28,24},{1,5},{5... | collective-permute-start | bytes 589832 | tf_op jit(solution)/shard_map/ppermute | solution.py:42
  32.3 31.7 %collective-permute-start.11 = (bf16[64,1152]{1,0:T(8,128)(2,1)S(1)}, bf16[64,1152]{1,0:T(8,128)(2,1)S(1)}, u32[]{:S(2)}, u32[]{:S(2)}) collective-permute-start(bf16[64,1152]{1,0:T(8,128)(2,1)S(1)} %query_merge.4.rest_0_.refs_0_), channel_id=1, source_target_pairs={{0,16},{4,12},{8,24},{12,4},{16,0},{20,28},{24,8},{28,20},{1,17},{... | collective-permute-start | bytes 442376 | tf_op jit(solution)/shard_map/ppermute | solution.py:42
  33.9 30.5 %collective-permute-start.10 = (bf16[768,128]{1,0:T(8,128)(2,1)S(1)}, bf16[768,128]{1,0:T(8,128)(2,1)S(1)}, u32[]{:S(2)}, u32[]{:S(2)}) collective-permute-start(bf16[768,128]{1,0:T(8,128)(2,1)S(1)} %anchor_relay.8.rest_0_.one_ref), channel_id=1, source_target_pairs={{0,16},{4,12},{8,24},{12,4},{16,0},{20,28},{24,8},{28,20},{1,17},{... | collective-permute-start | bytes 589832 | tf_op jit(solution)/shard_map/ppermute | solution.py:42
  64.3 15.3 %collective-permute-start.14 = (bf16[64,1024]{1,0:T(8,128)(2,1)S(1)}, bf16[64,1024]{1,0:T(8,128)(2,1)S(1)}, u32[]{:S(2)}, u32[]{:S(2)}) collective-permute-start(bf16[64,1024]{1,0:T(8,128)(2,1)S(1)} %query_merge.5.rest_0_.own_ref), channel_id=1, source_target_pairs={{0,4},{4,0},{8,12},{12,8},{16,20},{20,16},{24,28},{28,24},{1,5},{5... | collective-permute-start | bytes 393224 | tf_op jit(solution)/shard_map/ppermute | solution.py:42
  64.4 15.2 %copy-start.1 = (bf16[2048,1024]{1,0:T(8,128)(2,1)S(1)}, bf16[2048,1024]{1,0:T(8,128)(2,1)}, u32[]{:S(2)}) copy-start(bf16[2048,1024]{1,0:T(8,128)(2,1)} %w_ref.1) | copy-start | bytes 12582916
  64.4 32.3 %collective-permute-start.13 = (bf16[768,128]{1,0:T(8,128)(2,1)S(1)}, bf16[768,128]{1,0:T(8,128)(2,1)S(1)}, u32[]{:S(2)}, u32[]{:S(2)}) collective-permute-start(bf16[768,128]{1,0:T(8,128)(2,1)S(1)} %anchor_relay.9.refs_7_.first_ref), channel_id=1, source_target_pairs={{0,4},{4,0},{8,12},{12,8},{16,20},{20,16},{24,28},{28,24},{1,5},{5... | collective-permute-start | bytes 589832 | tf_op jit(solution)/shard_map/ppermute | solution.py:42
  80.5 45.5 %collective-permute-start.15 = (bf16[64,1024]{1,0:T(8,128)(2,1)S(1)}, bf16[64,1024]{1,0:T(8,128)(2,1)S(1)}, u32[]{:S(2)}, u32[]{:S(2)}) collective-permute-start(bf16[64,1024]{1,0:T(8,128)(2,1)S(1)} %query_project.1.rest_0_.refs_7_.refs_8_.one_ref), channel_id=1, source_target_pairs={{0,1},{1,0},{2,3},{3,2},{4,5},{5,4},{6,7},{7,6},{8,9},{9,8},{10,11... | collective-permute-start | bytes 393224 | tf_op jit(solution)/shard_map/ppermute | solution.py:42
  126.0 32.8 %collective-permute-start.16 = (bf16[64,1024]{1,0:T(8,128)(2,1)S(1)}, bf16[64,1024]{1,0:T(8,128)(2,1)S(1)}, u32[]{:S(2)}, u32[]{:S(2)}) collective-permute-start(bf16[64,1024]{1,0:T(8,128)(2,1)S(1)} %query_sum.2.refs_11_.refs_12_.one_ref), channel_id=1, source_target_pairs={{0,2},{1,3},{2,0},{3,1},{4,6},{5,7},{6,4},{7,5},{8,10},{9,11},{10,... | collective-permute-start | bytes 393224 | tf_op jit(solution)/shard_map/ppermute | solution.py:42

commit v11 on v10

--- a/solution.py
+++ b/solution.py
@@ -120,17 +120,15 @@
     )(own, *others, *after)
 
 
-def relay(keep_of, one, two, after=(), split=1):
-    slab, columns = one.shape
-    width = columns // split
+def relay(keep_of, one, two, after=(), kv=0):
+    cols = slice(kv * HD, (kv + 1) * HD)
+    slab = one.shape[0]
 
     def kernel(one_ref, two_ref, *rest):
         keep = keep_of(lax.axis_index("hst"))
-        for j, out_ref in enumerate(rest[-split:]):
-            cols = slice(j * width, (j + 1) * width)
-            choose(keep, take_rows(out_ref, one_ref, slab, cols), take_rows(out_ref, two_ref, slab, cols))
-
-    return small_call(kernel, "anchor_relay", [(slab, width)] * split, (one, two), after)
+        choose(keep, take_rows(rest[-1], one_ref, slab, cols), take_rows(rest[-1], two_ref, slab, cols))
+
+    return small_call(kernel, "anchor_relay", [(slab, HD)], (one, two), after)
 
 
 def add_part(one, two, after=()):
@@ -701,11 +699,17 @@
     value_landed = swap(own_v, "hst", hosts, 1, 1)
     own_keys, own_values = prepare(own_k, own_v, False)
     done = own(0, 2)
-    parts = list(relay(is_even, own_k, value_landed, (done,), kv_local))
-    parts_landed = [swap(x, "hst", hosts, *along[0]) for x in parts]
-    queries = by_chip(query_q, landed, bits, (parts[0],))
+    parts, parts_landed = {}, {}
+
+    def send_off(kv, after):
+        (parts[kv],) = relay(is_even, own_k, value_landed, after, kv)
+        parts_landed[kv] = swap(parts[kv], "hst", hosts, *along[0])
+        return parts[kv]
+
+    done = send_off(0, (done,))
+    done = own(2, 2, (done,))
+    queries = by_chip(query_q, landed, bits, (done,))
     landed = swap(queries, "hst", hosts, 1, 1)
-    done = own(2, 2, (queries,))
     anchor = {}
 
     def pass_on(kv, after):
@@ -718,7 +722,7 @@
         anchor[kv] = held, swap(held, "hst", hosts, 1, 1)
         return held
 
-    keep, give = source_part(lengths, own_keys, own_v, query_kv, queries, landed, q_rows, per_kv, (done,))
+    keep, give = source_part(lengths, own_keys, own_v, query_kv, queries, landed, q_rows, per_kv, ())
     landed = swap(give, "hst", hosts, 1, 1)
     done = own(4, 4, (keep,))
     source = merge_part([keep, landed], False, (done,))
@@ -727,8 +731,8 @@
     done = own(8, 8, (done,))
     source = merge_part([source, landed], False, (done,))
     landed = swap(source, "hst", hosts, *along[1])
-    done = complete(0, (source,))
-    done = pass_on(1, (done,))
+    done = send_off(1, (source,))
+    done = complete(0, (done,))
     anchor[0] = prepare(*anchor[0], True, (done,))
     results = {}
 
@@ -742,17 +746,18 @@
     done = anchors(0, 4, ())
     attended = merge_part([source, landed], True, (done,))
     landed = swap(attended, "hst", hosts, 1, 1)
-    done = complete(1, (attended,))
+    done = pass_on(1, (attended,))
     done = anchors(4, 2, (done,))
     terms = project_part(attended, landed, out_weight, (done,))
-    anchor[1] = prepare(*anchor[1], True, (terms,))
+    done = complete(1, (terms,))
     shares = [[(12, 4, True)], [(6, 2, False), (8, 4, False)]]
     step = 1
     while step < groups:
         landed = swap(terms, "tp", groups, step, step)
         last = False
-        done = terms
         for first, count, last in shares.pop() if shares else ():
+            if first == per_kv:
+                anchor[1] = prepare(*anchor[1], True, (done,))
             done = anchors(first, count, (terms, done), last)
         terms = add_part(terms, landed, () if last else (done,))
         step *= 2

time: 160 us -> 159 us (level)
  no operation moved by 1% of the time
where the time goes in v11:
time: 159 us
  Pallas kernels  142 us (89%)
  starting transfers between devices  14.2 us (9%)
    pallas_call x5, Pallas kernels, anchor_part(): pl.pallas_call(functools.partial(anchor_kernel, first, count, bases, per_...  118 us
    ppermute x17, starting transfers between devices, swap(): lax.ppermute(value, axis, [(i, i ^ (odd if i & 1 else even)) for i in ran...  14.2 us
    pallas_call x1, Pallas kernels, source_part(): pl.pallas_call(functools.partial(source_kernel, per_kv, q_rows, H // KVH)...  11.4 us
    pallas_call x4, Pallas kernels, own_part(): pl.pallas_call(functools.partial(own_kernel, first, count, per_kv), out_s...  7.95 us
  transfers between devices with their start and end apart: 17, of which 2 were waited for; matrix products, arithmetic and copies ran while one was open for 0% of the time, Pallas kernels for 88%

profile of v11, /device:TPU:6, one launch (start us, length us, event | category | flops | bytes accessed | tf_op | source)
XLA Modules:
  0.0 158.6 jit_solution(15358045478965623282)
XLA Ops:
  0.6 1.3 pick_columns.1
  2.1 2.0 %collective-permute-start.2 = (bf16[8,2048]{1,0:T(8,128)(2,1)S(1)}, bf16[8,2048]{1,0:T(8,128)(2,1)S(1)}, u32[]{:S(2)}, u32[]{:S(2)}) collective-permute-start(bf16[8,2048]{1,0:T(8,128)(2,1)S(1)} %copy-done.2), channel_id=1, source_target_pairs={{0,8},{4,12},{8,0},{12,4},{16,24},{20,28},{24,16},{28,20},{1,9},{5... | collective-permute-start | bytes 98312 | tf_op jit(solution)/shard_map/ppermute | solution.py:42
  4.1 1.5 collective-permute-start.3
  5.6 0.4 operands.3
  6.0 1.1 context_own.4.rest_0_.refs_6_
  7.2 1.1 context_own.5.refs_4_.refs_7_
  8.4 0.6 collective-permute-start.7
  9.0 0.7 collective-permute-done.4.landed_ref
  9.8 11.4 %query_source.1 = (bf16[64,1152]{1,0:T(8,128)(2,1)S(1)}, bf16[64,1152]{1,0:T(8,128)(2,1)S(1)}) custom-call(s32[1,8]{1,0:T(1,128)S(1)} %bitcast.1, bf16[512,768]{1,0:T(8,128)(2,1)S(1)} %get-tuple-element.14.k_ref.refs_2_, bf16[768,256]{1,0:T(8,128)(2,1)S(1)} %get-tuple-element.13.second_ref.v_ref, bf16[2,8,1024]{2,1,0:T(8,128)(2,1)S(1)} %copy-done.4, ...), custom_call_target="tpu_custom_call" | custom-call | flops 805306368 | bytes 2097152 | tf_op jit(solution)/shard_map/query_source/pallas_call | solution.py:546
  21.3 1.9 %context_own.6.refs_2_.refs_6_ = f32[768,1024]{1,0:T(8,128)S(1)} custom-call(bf16[768,2048]{1,0:T(8,128)(2,1)S(1)} %copy-done, bf16[512,768]{1,0:T(8,128)(2,1)S(1)} %get-tuple-element.14.k_ref.refs_2_, bf16[768,512]{1,0:T(8,128)(2,1)S(1)} %get-tuple-element.15.v_ref.refs_3_, bf16[64,1152]{1,0:T(8,128)(2,1)S(1)} %get-tuple-element.16.rest_0_.refs_0_), custom_call_target="tpu_custom_call" | custom-call | flops 1610612736 | bytes 2359296 | tf_op jit(solution)/shard_map/context_own/pallas_call | solution.py:239
  23.3 0.3 query_merge.3.rest_0_.refs_0_
  23.6 0.7 collective-permute-start.6
  24.4 1.3 collective-permute-start.10
  25.6 3.8 %context_own.7.refs_2_.refs_6_ = f32[768,2048]{1,0:T(8,128)S(1)} custom-call(bf16[768,2048]{1,0:T(8,128)(2,1)S(1)} %copy-done, bf16[512,768]{1,0:T(8,128)(2,1)S(1)} %get-tuple-element.14.k_ref.refs_2_, bf16[768,512]{1,0:T(8,128)(2,1)S(1)} %get-tuple-element.15.v_ref.refs_3_, bf16[768,128]{1,0:T(8,128)(2,1)S(1)} %anchor_relay.7.rest_0_.one_ref), custom_call_target="tpu_custom_call" | custom-call | flops 3221225472 | bytes 4718592 | tf_op jit(solution)/shard_map/context_own/pallas_call | solution.py:239
  29.5 0.6 collective-permute-done.6.refs_1_
  30.0 0.3 query_merge.4.rest_0_.refs_0_
  30.5 0.3 collective-permute-start.11
  30.8 1.3 collective-permute-start.9
  32.1 0.7 collective-permute-start.8
  33.1 29.5 %context_anchor.5.refs_2_.refs_7_ = bf16[768,512]{1,0:T(8,128)(2,1)S(1)} custom-call(s32[1,8]{1,0:T(1,128)S(1)} %bitcast.2, bf16[768,2048]{1,0:T(8,128)(2,1)S(1)} %copy-done, bf16[512,768]{1,0:T(8,128)(2,1)S(1)} %get-tuple-element.14.k_ref.refs_2_, bf16[768,512]{1,0:T(8,128)(2,1)S(1)} %get-tuple-element.15.v_ref.refs_3_, ...), custom_call_target="tpu_custom_call" | custom-call | flops 2415919104 | bytes 3145728 | tf_op jit(solution)/shard_map/context_anchor/pallas_call | solution.py:387
  62.6 0.3 query_merge.5.rest_0_.own_ref
  62.9 0.5 collective-permute-start.12
  63.5 14.7 %context_anchor.6.rest_0_.refs_8_ = bf16[768,256]{1,0:T(8,128)(2,1)S(1)} custom-call(s32[1,8]{1,0:T(1,128)S(1)} %bitcast.3, bf16[768,2048]{1,0:T(8,128)(2,1)S(1)} %copy-done, bf16[512,768]{1,0:T(8,128)(2,1)S(1)} %get-tuple-element.14.k_ref.refs_2_, bf16[768,512]{1,0:T(8,128)(2,1)S(1)} %get-tuple-element.15.v_ref.refs_3_, ...), custom_call_target="tpu_custom_call" | custom-call | flops 1207959552 | bytes 1572864 | tf_op jit(solution)/shard_map/context_anchor/pallas_call | solution.py:387
  78.2 0.9 query_project.1.rest_0_.refs_7_.one_ref
  79.1 0.5 collective-permute-start.14
  79.6 1.6 collective-permute-start.15
  81.2 14.7 %context_anchor.7.rest_0_.refs_8_.refs_9_ = bf16[768,256]{1,0:T(8,128)(2,1)S(1)} custom-call(s32[1,8]{1,0:T(1,128)S(1)} %bitcast.4, bf16[768,2048]{1,0:T(8,128)(2,1)S(1)} %copy-done, bf16[512,768]{1,0:T(8,128)(2,1)S(1)} %get-tuple-element.14.k_ref.refs_2_, bf16[768,512]{1,0:T(8,128)(2,1)S(1)} %get-tuple-element.15.v_ref.refs_3_, ...), custom_call_target="tpu_custom_call" | custom-call | flops 1207959552 | bytes 1572864 | tf_op jit(solution)/shard_map/context_anchor/pallas_call | solution.py:387
  95.9 0.2 operands.5
  96.1 29.0 %context_anchor.8.rest_0_.refs_10_.refs_12_ = bf16[768,512]{1,0:T(8,128)(2,1)S(1)} custom-call(s32[1,8]{1,0:T(1,128)S(1)} %bitcast.5, bf16[768,2048]{1,0:T(8,128)(2,1)S(1)} %copy-done, bf16[512,768]{1,0:T(8,128)(2,1)S(1)} %get-tuple-element.14.k_ref.refs_2_, bf16[768,512]{1,0:T(8,128)(2,1)S(1)} %get-tuple-element.15.v_ref.refs_3_, ...), custom_call_target="tpu_custom_call" | custom-call | flops 2415919104 | bytes 3145728 | tf_op jit(solution)/shard_map/context_anchor/pallas_call | solution.py:387
  125.2 2.7 %collective-permute-start.16 = (bf16[64,1024]{1,0:T(8,128)(2,1)S(1)}, bf16[64,1024]{1,0:T(8,128)(2,1)S(1)}, u32[]{:S(2)}, u32[]{:S(2)}) collective-permute-start(bf16[64,1024]{1,0:T(8,128)(2,1)S(1)} %query_sum.2.refs_11_.one_ref), channel_id=1, source_target_pairs={{0,2},{1,3},{2,0},{3,1},{4,6},{5,7},{6,4},{7,5},{8,10},{9,11},{10,... | collective-permute-start | bytes 393224 | tf_op jit(solution)/shard_map/ppermute | solution.py:42
  127.8 30.1 %context_anchor.9 = bf16[768,2048]{1,0:T(8,128)(2,1)} custom-call(s32[1,8]{1,0:T(1,128)S(1)} %bitcast.6, bf16[768,2048]{1,0:T(8,128)(2,1)S(1)} %copy-done, bf16[512,768]{1,0:T(8,128)(2,1)S(1)} %get-tuple-element.14.k_ref.refs_2_, bf16[768,512]{1,0:T(8,128)(2,1)S(1)} %get-tuple-element.15.v_ref.refs_3_, bf16[256,768]{1,0:T(8,128)(2,1)S(1)} %get-tuple-element.20.refs_4_, ...), custom_call_target="tpu_custom_call" | custom-call | flops 2415919104 | bytes 3145728 | tf_op jit(solution)/shard_map/context_anchor/pallas_call | solution.py:387
  157.9 0.7 query_sum.3
  (39 shorter events, 1.0 us)
Async XLA Ops:
  0.6 1.4 copy-start.2
  0.6 5.3 %copy-start = (bf16[768,2048]{1,0:T(8,128)(2,1)S(1)}, bf16[768,2048]{1,0:T(8,128)(2,1)}, u32[]{:S(2)}) copy-start(bf16[768,2048]{1,0:T(8,128)(2,1)} %refs_1_.9) | copy-start | bytes 9437188
  2.0 5.1 %collective-permute-start = (bf16[768,256]{1,0:T(8,128)(2,1)S(1)}, bf16[768,256]{1,0:T(8,128)(2,1)S(1)}, u32[]{:S(2)}, u32[]{:S(2)}) collective-permute-start(bf16[768,256]{1,0:T(8,128)(2,1)S(1)} %get-tuple-element.13.second_ref.v_ref), channel_id=1, source_target_pairs={{0,4},{4,0},{8,12},{12,8},{16,20},{20,16},{24,28},{28,24},{1,5},{5... | collective-permute-start | bytes 1179656 | tf_op jit(solution)/shard_map/ppermute | solution.py:42
  2.0 6.2 %collective-permute-start.1 = (bf16[8,2048]{1,0:T(8,128)(2,1)S(1)}, bf16[8,2048]{1,0:T(8,128)(2,1)S(1)}, u32[]{:S(2)}, u32[]{:S(2)}) collective-permute-start(bf16[8,2048]{1,0:T(8,128)(2,1)S(1)} %copy-done.2), channel_id=1, source_target_pairs={{0,24},{4,28},{8,16},{12,20},{16,8},{20,12},{24,0},{28,4},{1,25},{... | collective-permute-start | bytes 98312 | tf_op jit(solution)/shard_map/ppermute | solution.py:42
  2.1 6.2 %collective-permute-start.2 = (bf16[8,2048]{1,0:T(8,128)(2,1)S(1)}, bf16[8,2048]{1,0:T(8,128)(2,1)S(1)}, u32[]{:S(2)}, u32[]{:S(2)}) collective-permute-start(bf16[8,2048]{1,0:T(8,128)(2,1)S(1)} %copy-done.2), channel_id=1, source_target_pairs={{0,8},{4,12},{8,0},{12,4},{16,24},{20,28},{24,16},{28,20},{1,9},{5... | collective-permute-start | bytes 98312 | tf_op jit(solution)/shard_map/ppermute | solution.py:42
  4.1 4.2 %collective-permute-start.3 = (bf16[8,2048]{1,0:T(8,128)(2,1)S(1)}, bf16[8,2048]{1,0:T(8,128)(2,1)S(1)}, u32[]{:S(2)}, u32[]{:S(2)}) collective-permute-start(bf16[8,2048]{1,0:T(8,128)(2,1)S(1)} %copy-done.2), channel_id=1, source_target_pairs={{0,16},{4,20},{8,24},{12,28},{16,0},{20,4},{24,8},{28,12},{1,17},{... | collective-permute-start | bytes 98312 | tf_op jit(solution)/shard_map/ppermute | solution.py:42
  7.1 2.6 %copy-start.3 = (s32[8]{0:T(128)S(1)}, s32[8]{0:T(128)}, u32[]{:S(2)}) copy-start(s32[8]{0:T(128)} %param.8) | copy-start | bytes 100
  7.2 2.6 %copy-start.4 = (bf16[2,8,1024]{2,1,0:T(8,128)(2,1)S(1)}, bf16[2,8,1024]{2,1,0:T(8,128)(2,1)}, u32[]{:S(2)}) copy-start(bf16[2,8,1024]{2,1,0:T(8,128)(2,1)} %self_ref.1) | copy-start | bytes 98308
  8.4 1.4 collective-permute-start.4
  8.4 15.9 %collective-permute-start.7 = (bf16[768,128]{1,0:T(8,128)(2,1)S(1)}, bf16[768,128]{1,0:T(8,128)(2,1)S(1)}, u32[]{:S(2)}, u32[]{:S(2)}) collective-permute-start(bf16[768,128]{1,0:T(8,128)(2,1)S(1)} %anchor_relay.6.rest_0_.one_ref), channel_id=1, source_target_pairs={{0,8},{4,20},{8,0},{12,28},{16,24},{20,4},{24,16},{28,12},{1,9},{5... | collective-permute-start | bytes 589832 | tf_op jit(solution)/shard_map/ppermute | solution.py:42
  21.2 2.1 %collective-permute-start.5 = (bf16[64,1152]{1,0:T(8,128)(2,1)S(1)}, bf16[64,1152]{1,0:T(8,128)(2,1)S(1)}, u32[]{:S(2)}, u32[]{:S(2)}) collective-permute-start(bf16[64,1152]{1,0:T(8,128)(2,1)S(1)} %get-tuple-element.17), channel_id=1, source_target_pairs={{0,4},{4,0},{8,12},{12,8},{16,20},{20,16},{24,28},{28,24},{1,5},{5... | collective-permute-start | bytes 442376 | tf_op jit(solution)/shard_map/ppermute | solution.py:42
  23.6 6.4 %collective-permute-start.6 = (bf16[64,1152]{1,0:T(8,128)(2,1)S(1)}, bf16[64,1152]{1,0:T(8,128)(2,1)S(1)}, u32[]{:S(2)}, u32[]{:S(2)}) collective-permute-start(bf16[64,1152]{1,0:T(8,128)(2,1)S(1)} %query_merge.3.rest_0_.refs_0_), channel_id=1, source_target_pairs={{0,8},{4,20},{8,0},{12,28},{16,24},{20,4},{24,16},{28,12},{1,9},{5... | collective-permute-start | bytes 442376 | tf_op jit(solution)/shard_map/ppermute | solution.py:42
  24.4 6.1 %collective-permute-start.10 = (bf16[768,128]{1,0:T(8,128)(2,1)S(1)}, bf16[768,128]{1,0:T(8,128)(2,1)S(1)}, u32[]{:S(2)}, u32[]{:S(2)}) collective-permute-start(bf16[768,128]{1,0:T(8,128)(2,1)S(1)} %anchor_relay.7.rest_0_.one_ref), channel_id=1, source_target_pairs={{0,16},{4,12},{8,24},{12,4},{16,0},{20,28},{24,8},{28,20},{1,17},{... | collective-permute-start | bytes 589832 | tf_op jit(solution)/shard_map/ppermute | solution.py:42
  30.5 2.4 %collective-permute-start.11 = (bf16[768,128]{1,0:T(8,128)(2,1)S(1)}, bf16[768,128]{1,0:T(8,128)(2,1)S(1)}, u32[]{:S(2)}, u32[]{:S(2)}) collective-permute-start(bf16[768,128]{1,0:T(8,128)(2,1)S(1)} %anchor_relay.9.first_ref.rest_0_), channel_id=1, source_target_pairs={{0,4},{4,0},{8,12},{12,8},{16,20},{20,16},{24,28},{28,24},{1,5},{5... | collective-permute-start | bytes 589832 | tf_op jit(solution)/shard_map/ppermute | solution.py:42
  30.8 31.7 %collective-permute-start.9 = (bf16[64,1152]{1,0:T(8,128)(2,1)S(1)}, bf16[64,1152]{1,0:T(8,128)(2,1)S(1)}, u32[]{:S(2)}, u32[]{:S(2)}) collective-permute-start(bf16[64,1152]{1,0:T(8,128)(2,1)S(1)} %query_merge.4.rest_0_.refs_0_), channel_id=1, source_target_pairs={{0,16},{4,12},{8,24},{12,4},{16,0},{20,28},{24,8},{28,20},{1,17},{... | collective-permute-start | bytes 442376 | tf_op jit(solution)/shard_map/ppermute | solution.py:42
  32.1 30.7 %collective-permute-start.8 = (bf16[768,128]{1,0:T(8,128)(2,1)S(1)}, bf16[768,128]{1,0:T(8,128)(2,1)S(1)}, u32[]{:S(2)}, u32[]{:S(2)}) collective-permute-start(bf16[768,128]{1,0:T(8,128)(2,1)S(1)} %anchor_relay.8.rest_0_.one_ref), channel_id=1, source_target_pairs={{0,8},{4,20},{8,0},{12,28},{16,24},{20,4},{24,16},{28,12},{1,9},{5... | collective-permute-start | bytes 589832 | tf_op jit(solution)/shard_map/ppermute | solution.py:42
  62.9 15.3 %copy-start.1 = (bf16[2048,1024]{1,0:T(8,128)(2,1)S(1)}, bf16[2048,1024]{1,0:T(8,128)(2,1)}, u32[]{:S(2)}) copy-start(bf16[2048,1024]{1,0:T(8,128)(2,1)} %w_ref.1) | copy-start | bytes 12582916
  62.9 16.2 %collective-permute-start.12 = (bf16[768,128]{1,0:T(8,128)(2,1)S(1)}, bf16[768,128]{1,0:T(8,128)(2,1)S(1)}, u32[]{:S(2)}, u32[]{:S(2)}) collective-permute-start(bf16[768,128]{1,0:T(8,128)(2,1)S(1)} %anchor_relay.10.refs_7_.one_ref), channel_id=1, source_target_pairs={{0,16},{4,12},{8,24},{12,4},{16,0},{20,28},{24,8},{28,20},{1,17},{... | collective-permute-start | bytes 589832 | tf_op jit(solution)/shard_map/ppermute | solution.py:42
  63.4 14.8 %collective-permute-start.13 = (bf16[64,1024]{1,0:T(8,128)(2,1)S(1)}, bf16[64,1024]{1,0:T(8,128)(2,1)S(1)}, u32[]{:S(2)}, u32[]{:S(2)}) collective-permute-start(bf16[64,1024]{1,0:T(8,128)(2,1)S(1)} %query_merge.5.rest_0_.own_ref), channel_id=1, source_target_pairs={{0,4},{4,0},{8,12},{12,8},{16,20},{20,16},{24,28},{28,24},{1,5},{5... | collective-permute-start | bytes 393224 | tf_op jit(solution)/shard_map/ppermute | solution.py:42
  79.1 16.8 %collective-permute-start.14 = (bf16[768,128]{1,0:T(8,128)(2,1)S(1)}, bf16[768,128]{1,0:T(8,128)(2,1)S(1)}, u32[]{:S(2)}, u32[]{:S(2)}) collective-permute-start(bf16[768,128]{1,0:T(8,128)(2,1)S(1)} %anchor_relay.11.refs_8_.first_ref), channel_id=1, source_target_pairs={{0,4},{4,0},{8,12},{12,8},{16,20},{20,16},{24,28},{28,24},{1,5},{5... | collective-permute-start | bytes 589832 | tf_op jit(solution)/shard_map/ppermute | solution.py:42
  79.6 45.5 %collective-permute-start.15 = (bf16[64,1024]{1,0:T(8,128)(2,1)S(1)}, bf16[64,1024]{1,0:T(8,128)(2,1)S(1)}, u32[]{:S(2)}, u32[]{:S(2)}) collective-permute-start(bf16[64,1024]{1,0:T(8,128)(2,1)S(1)} %query_project.1.rest_0_.refs_7_.one_ref), channel_id=1, source_target_pairs={{0,1},{1,0},{2,3},{3,2},{4,5},{5,4},{6,7},{7,6},{8,9},{9,8},{10,11... | collective-permute-start | bytes 393224 | tf_op jit(solution)/shard_map/ppermute | solution.py:42
  125.2 32.8 %collective-permute-start.16 = (bf16[64,1024]{1,0:T(8,128)(2,1)S(1)}, bf16[64,1024]{1,0:T(8,128)(2,1)S(1)}, u32[]{:S(2)}, u32[]{:S(2)}) collective-permute-start(bf16[64,1024]{1,0:T(8,128)(2,1)S(1)} %query_sum.2.refs_11_.one_ref), channel_id=1, source_target_pairs={{0,2},{1,3},{2,0},{3,1},{4,6},{5,7},{6,4},{7,5},{8,10},{9,11},{10,... | collective-permute-start | bytes 393224 | tf_op jit(solution)/shard_map/ppermute | solution.py:42

commit v12 on v10

--- a/solution.py
+++ b/solution.py
@@ -79,7 +79,7 @@
         in_specs=[VMEM] * len(inputs) + [ANY] * len(after),
         out_specs=[VMEM] * len(shapes),
         compiler_params=params(),
-        cost_estimate=pl.CostEstimate(flops=0, bytes_accessed=2**20, transcendentals=0),
+        cost_estimate=pl.CostEstimate(flops=0, bytes_accessed=2**14, transcendentals=0),
         name=name,
     )(*inputs, *after)
 
@@ -692,8 +692,10 @@
     def source_first(h):
         return h < 2
 
-    def done_early(h):
-        return (h <= 2) | (h == 5)
+    done_early = (
+        lambda h: (h <= 2) | (h == 5),
+        lambda h: (h <= 1) | (h == 3) | (h == 4),
+    )
 
     bits = (6, 2, 4)
     landed = [swap(query_q, "hst", hosts, x, x) for x in bits]
@@ -702,23 +704,23 @@
     own_keys, own_values = prepare(own_k, own_v, False)
     done = own(0, 2)
     parts = list(relay(is_even, own_k, value_landed, (done,), kv_local))
-    parts_landed = [swap(x, "hst", hosts, *along[0]) for x in parts]
-    queries = by_chip(query_q, landed, bits, (parts[0],))
+    parts_landed = [swap(x, "hst", hosts, *along[kv]) for kv, x in enumerate(parts)]
+    done = own(2, 2, (parts[0],))
+    queries = by_chip(query_q, landed, bits, (done,))
     landed = swap(queries, "hst", hosts, 1, 1)
-    done = own(2, 2, (queries,))
     anchor = {}
 
     def pass_on(kv, after):
         (parts[kv],) = relay(source_first, parts[kv], parts_landed[kv], after)
-        parts_landed[kv] = swap(parts[kv], "hst", hosts, *along[1])
+        parts_landed[kv] = swap(parts[kv], "hst", hosts, *along[1 - kv])
         return parts[kv]
 
     def complete(kv, after):
-        (held,) = relay(done_early, parts[kv], parts_landed[kv], after)
+        (held,) = relay(done_early[kv], parts[kv], parts_landed[kv], after)
         anchor[kv] = held, swap(held, "hst", hosts, 1, 1)
         return held
 
-    keep, give = source_part(lengths, own_keys, own_v, query_kv, queries, landed, q_rows, per_kv, (done,))
+    keep, give = source_part(lengths, own_keys, own_v, query_kv, queries, landed, q_rows, per_kv, ())
     landed = swap(give, "hst", hosts, 1, 1)
     done = own(4, 4, (keep,))
     source = merge_part([keep, landed], False, (done,))
@@ -742,17 +744,18 @@
     done = anchors(0, 4, ())
     attended = merge_part([source, landed], True, (done,))
     landed = swap(attended, "hst", hosts, 1, 1)
-    done = complete(1, (attended,))
-    done = anchors(4, 2, (done,))
+    done = anchors(4, 2, (attended,))
+    done = complete(1, (done,))
     terms = project_part(attended, landed, out_weight, (done,))
-    anchor[1] = prepare(*anchor[1], True, (terms,))
+    done = terms
     shares = [[(12, 4, True)], [(6, 2, False), (8, 4, False)]]
     step = 1
     while step < groups:
         landed = swap(terms, "tp", groups, step, step)
         last = False
-        done = terms
         for first, count, last in shares.pop() if shares else ():
+            if first == per_kv:
+                anchor[1] = prepare(*anchor[1], True, (done,))
             done = anchors(first, count, (terms, done), last)
         terms = add_part(terms, landed, () if last else (done,))
         step *= 2

time: 160 us -> 159 us (level)
  no operation moved by 1% of the time
where the time goes in v12:
time: 159 us
  Pallas kernels  142 us (89%)
  starting transfers between devices  15.2 us (10%)
    pallas_call x5, Pallas kernels, anchor_part(): pl.pallas_call(functools.partial(anchor_kernel, first, count, bases, per_...  118 us
    ppermute x17, starting transfers between devices, swap(): lax.ppermute(value, axis, [(i, i ^ (odd if i & 1 else even)) for i in ran...  15.2 us
    pallas_call x1, Pallas kernels, source_part(): pl.pallas_call(functools.partial(source_kernel, per_kv, q_rows, H // KVH)...  11.4 us
    pallas_call x4, Pallas kernels, own_part(): pl.pallas_call(functools.partial(own_kernel, first, count, per_kv), out_s...  7.95 us
  transfers between devices with their start and end apart: 17, of which 2 were waited for; matrix products, arithmetic and copies ran while one was open for 0% of the time, Pallas kernels for 88%

profile of v12, /device:TPU:6, one launch (start us, length us, event | category | flops | bytes accessed | tf_op | source)
XLA Modules:
  0.0 159.0 jit_solution(16759114485257455917)
XLA Ops:
  0.6 1.3 pick_columns.1
  2.1 2.0 %collective-permute-start.4 = (bf16[8,2048]{1,0:T(8,128)(2,1)S(1)}, bf16[8,2048]{1,0:T(8,128)(2,1)S(1)}, u32[]{:S(2)}, u32[]{:S(2)}) collective-permute-start(bf16[8,2048]{1,0:T(8,128)(2,1)S(1)} %copy-done.2), channel_id=1, source_target_pairs={{0,8},{4,12},{8,0},{12,4},{16,24},{20,28},{24,16},{28,20},{1,9},{5... | collective-permute-start | bytes 98312 | tf_op jit(solution)/shard_map/ppermute | solution.py:42
  4.1 1.5 collective-permute-start.5
  5.6 0.4 operands.3
  6.0 1.1 context_own.4.rest_0_.refs_6_
  7.2 1.1 context_own.5.refs_4_.refs_7_
  8.5 0.6 collective-permute-start.2
  9.1 1.2 collective-permute-start.1
  10.3 11.4 %query_source.1 = (bf16[64,1152]{1,0:T(8,128)(2,1)S(1)}, bf16[64,1152]{1,0:T(8,128)(2,1)S(1)}) custom-call(s32[1,8]{1,0:T(1,128)S(1)} %bitcast.1, bf16[512,768]{1,0:T(8,128)(2,1)S(1)} %get-tuple-element.16.k_ref.refs_2_, bf16[768,256]{1,0:T(8,128)(2,1)S(1)} %get-tuple-element.15.second_ref.v_ref, bf16[2,8,1024]{2,1,0:T(8,128)(2,1)S(1)} %copy-done.4, ...), custom_call_target="tpu_custom_call" | custom-call | flops 805306368 | bytes 2097152 | tf_op jit(solution)/shard_map/query_source/pallas_call | solution.py:548
  21.7 1.9 %context_own.6.refs_2_.refs_6_ = f32[768,1024]{1,0:T(8,128)S(1)} custom-call(bf16[768,2048]{1,0:T(8,128)(2,1)S(1)} %copy-done, bf16[512,768]{1,0:T(8,128)(2,1)S(1)} %get-tuple-element.16.k_ref.refs_2_, bf16[768,512]{1,0:T(8,128)(2,1)S(1)} %get-tuple-element.17.v_ref.refs_3_, bf16[64,1152]{1,0:T(8,128)(2,1)S(1)} %get-tuple-element.20.rest_0_.refs_0_), custom_call_target="tpu_custom_call" | custom-call | flops 1610612736 | bytes 2359296 | tf_op jit(solution)/shard_map/context_own/pallas_call | solution.py:241
  23.7 0.3 query_merge.3.rest_0_.refs_0_
  24.0 1.6 collective-permute-start.9
  25.6 0.9 collective-permute-start.8
  26.5 3.8 %context_own.7.refs_2_.refs_6_ = f32[768,2048]{1,0:T(8,128)S(1)} custom-call(bf16[768,2048]{1,0:T(8,128)(2,1)S(1)} %copy-done, bf16[512,768]{1,0:T(8,128)(2,1)S(1)} %get-tuple-element.16.k_ref.refs_2_, bf16[768,512]{1,0:T(8,128)(2,1)S(1)} %get-tuple-element.17.v_ref.refs_3_, bf16[768,128]{1,0:T(8,128)(2,1)S(1)} %anchor_relay.6.rest_0_.one_ref), custom_call_target="tpu_custom_call" | custom-call | flops 3221225472 | bytes 4718592 | tf_op jit(solution)/shard_map/context_own/pallas_call | solution.py:241
  30.3 0.2 collective-permute-done.9.refs_1_
  30.6 0.3 query_merge.4.rest_0_.refs_0_
  30.9 0.4 collective-permute-done.8.two_ref
  31.5 0.9 collective-permute-start.12
  32.4 1.3 collective-permute-start.10
  33.6 0.2 operands.4
  33.8 29.5 %context_anchor.5.refs_2_.refs_7_ = bf16[768,512]{1,0:T(8,128)(2,1)S(1)} custom-call(s32[1,8]{1,0:T(1,128)S(1)} %bitcast.2, bf16[768,2048]{1,0:T(8,128)(2,1)S(1)} %copy-done, bf16[512,768]{1,0:T(8,128)(2,1)S(1)} %get-tuple-element.16.k_ref.refs_2_, bf16[768,512]{1,0:T(8,128)(2,1)S(1)} %get-tuple-element.17.v_ref.refs_3_, ...), custom_call_target="tpu_custom_call" | custom-call | flops 2415919104 | bytes 3145728 | tf_op jit(solution)/shard_map/context_anchor/pallas_call | solution.py:389
  63.3 0.3 query_merge.5.refs_7_.own_ref
  63.7 14.7 %context_anchor.6.rest_0_.refs_8_ = bf16[768,256]{1,0:T(8,128)(2,1)S(1)} custom-call(s32[1,8]{1,0:T(1,128)S(1)} %bitcast.3, bf16[768,2048]{1,0:T(8,128)(2,1)S(1)} %copy-done, bf16[512,768]{1,0:T(8,128)(2,1)S(1)} %get-tuple-element.16.k_ref.refs_2_, bf16[768,512]{1,0:T(8,128)(2,1)S(1)} %get-tuple-element.17.v_ref.refs_3_, ...), custom_call_target="tpu_custom_call" | custom-call | flops 1207959552 | bytes 1572864 | tf_op jit(solution)/shard_map/context_anchor/pallas_call | solution.py:389
  78.5 0.5 collective-permute-start.13
  79.0 0.9 query_project.1.refs_7_.refs_8_.one_ref
  79.9 1.6 %collective-permute-start.15 = (bf16[64,1024]{1,0:T(8,128)(2,1)S(1)}, bf16[64,1024]{1,0:T(8,128)(2,1)S(1)}, u32[]{:S(2)}, u32[]{:S(2)}) collective-permute-start(bf16[64,1024]{1,0:T(8,128)(2,1)S(1)} %query_project.1.refs_7_.refs_8_.one_ref), channel_id=1, source_target_pairs={{0,1},{1,0},{2,3},{3,2},{4,5},{5,4},{6,7},{7,6},{8,9},{9,8},{10,11... | collective-permute-start | bytes 393224 | tf_op jit(solution)/shard_map/ppermute | solution.py:42
  81.6 14.7 %context_anchor.7.rest_0_.refs_8_.refs_9_ = bf16[768,256]{1,0:T(8,128)(2,1)S(1)} custom-call(s32[1,8]{1,0:T(1,128)S(1)} %bitcast.4, bf16[768,2048]{1,0:T(8,128)(2,1)S(1)} %copy-done, bf16[512,768]{1,0:T(8,128)(2,1)S(1)} %get-tuple-element.16.k_ref.refs_2_, bf16[768,512]{1,0:T(8,128)(2,1)S(1)} %get-tuple-element.17.v_ref.refs_3_, ...), custom_call_target="tpu_custom_call" | custom-call | flops 1207959552 | bytes 1572864 | tf_op jit(solution)/shard_map/context_anchor/pallas_call | solution.py:389
  96.3 0.2 operands.5
  96.5 29.0 %context_anchor.8.rest_0_.refs_10_.refs_12_ = bf16[768,512]{1,0:T(8,128)(2,1)S(1)} custom-call(s32[1,8]{1,0:T(1,128)S(1)} %bitcast.5, bf16[768,2048]{1,0:T(8,128)(2,1)S(1)} %copy-done, bf16[512,768]{1,0:T(8,128)(2,1)S(1)} %get-tuple-element.16.k_ref.refs_2_, bf16[768,512]{1,0:T(8,128)(2,1)S(1)} %get-tuple-element.17.v_ref.refs_3_, ...), custom_call_target="tpu_custom_call" | custom-call | flops 2415919104 | bytes 3145728 | tf_op jit(solution)/shard_map/context_anchor/pallas_call | solution.py:389
  125.5 2.6 %collective-permute-start.16 = (bf16[64,1024]{1,0:T(8,128)(2,1)S(1)}, bf16[64,1024]{1,0:T(8,128)(2,1)S(1)}, u32[]{:S(2)}, u32[]{:S(2)}) collective-permute-start(bf16[64,1024]{1,0:T(8,128)(2,1)S(1)} %query_sum.2.refs_11_.one_ref), channel_id=1, source_target_pairs={{0,2},{1,3},{2,0},{3,1},{4,6},{5,7},{6,4},{7,5},{8,10},{9,11},{10,... | collective-permute-start | bytes 393224 | tf_op jit(solution)/shard_map/ppermute | solution.py:42
  128.2 30.1 %context_anchor.9 = bf16[768,2048]{1,0:T(8,128)(2,1)} custom-call(s32[1,8]{1,0:T(1,128)S(1)} %bitcast.6, bf16[768,2048]{1,0:T(8,128)(2,1)S(1)} %copy-done, bf16[512,768]{1,0:T(8,128)(2,1)S(1)} %get-tuple-element.16.k_ref.refs_2_, bf16[768,512]{1,0:T(8,128)(2,1)S(1)} %get-tuple-element.17.v_ref.refs_3_, bf16[256,768]{1,0:T(8,128)(2,1)S(1)} %get-tuple-element.24.refs_4_, ...), custom_call_target="tpu_custom_call" | custom-call | flops 2415919104 | bytes 3145728 | tf_op jit(solution)/shard_map/context_anchor/pallas_call | solution.py:389
  158.3 0.7 query_sum.3
  (38 shorter events, 0.8 us)
Async XLA Ops:
  0.6 1.4 copy-start.2
  0.6 5.3 %copy-start = (bf16[768,2048]{1,0:T(8,128)(2,1)S(1)}, bf16[768,2048]{1,0:T(8,128)(2,1)}, u32[]{:S(2)}) copy-start(bf16[768,2048]{1,0:T(8,128)(2,1)} %refs_1_.9) | copy-start | bytes 9437188
  2.0 5.1 %collective-permute-start = (bf16[768,256]{1,0:T(8,128)(2,1)S(1)}, bf16[768,256]{1,0:T(8,128)(2,1)S(1)}, u32[]{:S(2)}, u32[]{:S(2)}) collective-permute-start(bf16[768,256]{1,0:T(8,128)(2,1)S(1)} %get-tuple-element.15.second_ref.v_ref), channel_id=1, source_target_pairs={{0,4},{4,0},{8,12},{12,8},{16,20},{20,16},{24,28},{28,24},{1,5},{5... | collective-permute-start | bytes 1179656 | tf_op jit(solution)/shard_map/ppermute | solution.py:42
  2.0 6.3 %collective-permute-start.3 = (bf16[8,2048]{1,0:T(8,128)(2,1)S(1)}, bf16[8,2048]{1,0:T(8,128)(2,1)S(1)}, u32[]{:S(2)}, u32[]{:S(2)}) collective-permute-start(bf16[8,2048]{1,0:T(8,128)(2,1)S(1)} %copy-done.2), channel_id=1, source_target_pairs={{0,24},{4,28},{8,16},{12,20},{16,8},{20,12},{24,0},{28,4},{1,25},{... | collective-permute-start | bytes 98312 | tf_op jit(solution)/shard_map/ppermute | solution.py:42
  2.1 6.2 %collective-permute-start.4 = (bf16[8,2048]{1,0:T(8,128)(2,1)S(1)}, bf16[8,2048]{1,0:T(8,128)(2,1)S(1)}, u32[]{:S(2)}, u32[]{:S(2)}) collective-permute-start(bf16[8,2048]{1,0:T(8,128)(2,1)S(1)} %copy-done.2), channel_id=1, source_target_pairs={{0,8},{4,12},{8,0},{12,4},{16,24},{20,28},{24,16},{28,20},{1,9},{5... | collective-permute-start | bytes 98312 | tf_op jit(solution)/shard_map/ppermute | solution.py:42
  4.1 4.2 %collective-permute-start.5 = (bf16[8,2048]{1,0:T(8,128)(2,1)S(1)}, bf16[8,2048]{1,0:T(8,128)(2,1)S(1)}, u32[]{:S(2)}, u32[]{:S(2)}) collective-permute-start(bf16[8,2048]{1,0:T(8,128)(2,1)S(1)} %copy-done.2), channel_id=1, source_target_pairs={{0,16},{4,20},{8,24},{12,28},{16,0},{20,4},{24,8},{28,12},{1,17},{... | collective-permute-start | bytes 98312 | tf_op jit(solution)/shard_map/ppermute | solution.py:42
  7.2 3.1 %copy-start.3 = (s32[8]{0:T(128)S(1)}, s32[8]{0:T(128)}, u32[]{:S(2)}) copy-start(s32[8]{0:T(128)} %param.8) | copy-start | bytes 100
  7.2 3.1 %copy-start.4 = (bf16[2,8,1024]{2,1,0:T(8,128)(2,1)S(1)}, bf16[2,8,1024]{2,1,0:T(8,128)(2,1)}, u32[]{:S(2)}) copy-start(bf16[2,8,1024]{2,1,0:T(8,128)(2,1)} %self_ref.1) | copy-start | bytes 98308
  8.4 1.9 %collective-permute-start.6 = (bf16[32,2048]{1,0:T(8,128)(2,1)S(1)}, bf16[32,2048]{1,0:T(8,128)(2,1)S(1)}, u32[]{:S(2)}, u32[]{:S(2)}) collective-permute-start(bf16[32,2048]{1,0:T(8,128)(2,1)S(1)} %query_chips.1.known_ref), channel_id=1, source_target_pairs={{0,4},{4,0},{8,12},{12,8},{16,20},{20,16},{24,28},{28,24},{1,5},{5... | collective-permute-start | bytes 393224 | tf_op jit(solution)/shard_map/ppermute | solution.py:42
  8.5 17.1 %collective-permute-start.2 = (bf16[768,128]{1,0:T(8,128)(2,1)S(1)}, bf16[768,128]{1,0:T(8,128)(2,1)S(1)}, u32[]{:S(2)}, u32[]{:S(2)}) collective-permute-start(bf16[768,128]{1,0:T(8,128)(2,1)S(1)} %get-tuple-element.19.rest_0_.one_ref), channel_id=1, source_target_pairs={{0,8},{4,20},{8,0},{12,28},{16,24},{20,4},{24,16},{28,12},{1,9},{5... | collective-permute-start | bytes 589832 | tf_op jit(solution)/shard_map/ppermute | solution.py:42
  9.1 23.3 %collective-permute-start.1 = (bf16[768,128]{1,0:T(8,128)(2,1)S(1)}, bf16[768,128]{1,0:T(8,128)(2,1)S(1)}, u32[]{:S(2)}, u32[]{:S(2)}) collective-permute-start(bf16[768,128]{1,0:T(8,128)(2,1)S(1)} %get-tuple-element.18.one_ref), channel_id=1, source_target_pairs={{0,16},{4,12},{8,24},{12,4},{16,0},{20,28},{24,8},{28,20},{1,17},{... | collective-permute-start | bytes 589832 | tf_op jit(solution)/shard_map/ppermute | solution.py:42
  21.6 2.0 %collective-permute-start.7 = (bf16[64,1152]{1,0:T(8,128)(2,1)S(1)}, bf16[64,1152]{1,0:T(8,128)(2,1)S(1)}, u32[]{:S(2)}, u32[]{:S(2)}) collective-permute-start(bf16[64,1152]{1,0:T(8,128)(2,1)S(1)} %get-tuple-element.21), channel_id=1, source_target_pairs={{0,4},{4,0},{8,12},{12,8},{16,20},{20,16},{24,28},{28,24},{1,5},{5... | collective-permute-start | bytes 442376 | tf_op jit(solution)/shard_map/ppermute | solution.py:42
  24.0 6.6 %collective-permute-start.9 = (bf16[64,1152]{1,0:T(8,128)(2,1)S(1)}, bf16[64,1152]{1,0:T(8,128)(2,1)S(1)}, u32[]{:S(2)}, u32[]{:S(2)}) collective-permute-start(bf16[64,1152]{1,0:T(8,128)(2,1)S(1)} %query_merge.3.rest_0_.refs_0_), channel_id=1, source_target_pairs={{0,8},{4,20},{8,0},{12,28},{16,24},{20,4},{24,16},{28,12},{1,9},{5... | collective-permute-start | bytes 442376 | tf_op jit(solution)/shard_map/ppermute | solution.py:42
  25.6 5.7 %collective-permute-start.8 = (bf16[768,128]{1,0:T(8,128)(2,1)S(1)}, bf16[768,128]{1,0:T(8,128)(2,1)S(1)}, u32[]{:S(2)}, u32[]{:S(2)}) collective-permute-start(bf16[768,128]{1,0:T(8,128)(2,1)S(1)} %anchor_relay.6.rest_0_.one_ref), channel_id=1, source_target_pairs={{0,16},{4,12},{8,24},{12,4},{16,0},{20,28},{24,8},{28,20},{1,17},{... | collective-permute-start | bytes 589832 | tf_op jit(solution)/shard_map/ppermute | solution.py:42
  31.3 2.3 %collective-permute-start.11 = (bf16[768,128]{1,0:T(8,128)(2,1)S(1)}, bf16[768,128]{1,0:T(8,128)(2,1)S(1)}, u32[]{:S(2)}, u32[]{:S(2)}) collective-permute-start(bf16[768,128]{1,0:T(8,128)(2,1)S(1)} %anchor_relay.7.rest_0_.first_ref), channel_id=1, source_target_pairs={{0,4},{4,0},{8,12},{12,8},{16,20},{20,16},{24,28},{28,24},{1,5},{5... | collective-permute-start | bytes 589832 | tf_op jit(solution)/shard_map/ppermute | solution.py:42
  31.5 31.8 %collective-permute-start.12 = (bf16[64,1152]{1,0:T(8,128)(2,1)S(1)}, bf16[64,1152]{1,0:T(8,128)(2,1)S(1)}, u32[]{:S(2)}, u32[]{:S(2)}) collective-permute-start(bf16[64,1152]{1,0:T(8,128)(2,1)S(1)} %query_merge.4.rest_0_.refs_0_), channel_id=1, source_target_pairs={{0,16},{4,12},{8,24},{12,4},{16,0},{20,28},{24,8},{28,20},{1,17},{... | collective-permute-start | bytes 442376 | tf_op jit(solution)/shard_map/ppermute | solution.py:42
  32.4 46.1 %collective-permute-start.10 = (bf16[768,128]{1,0:T(8,128)(2,1)S(1)}, bf16[768,128]{1,0:T(8,128)(2,1)S(1)}, u32[]{:S(2)}, u32[]{:S(2)}) collective-permute-start(bf16[768,128]{1,0:T(8,128)(2,1)S(1)} %anchor_relay.8.rest_0_.one_ref), channel_id=1, source_target_pairs={{0,8},{4,20},{8,0},{12,28},{16,24},{20,4},{24,16},{28,12},{1,9},{5... | collective-permute-start | bytes 589832 | tf_op jit(solution)/shard_map/ppermute | solution.py:42
  63.7 15.4 %copy-start.1 = (bf16[2048,1024]{1,0:T(8,128)(2,1)S(1)}, bf16[2048,1024]{1,0:T(8,128)(2,1)}, u32[]{:S(2)}) copy-start(bf16[2048,1024]{1,0:T(8,128)(2,1)} %w_ref.1) | copy-start | bytes 12582916
  63.7 15.4 %collective-permute-start.14 = (bf16[64,1024]{1,0:T(8,128)(2,1)S(1)}, bf16[64,1024]{1,0:T(8,128)(2,1)S(1)}, u32[]{:S(2)}, u32[]{:S(2)}) collective-permute-start(bf16[64,1024]{1,0:T(8,128)(2,1)S(1)} %query_merge.5.refs_7_.own_ref), channel_id=1, source_target_pairs={{0,4},{4,0},{8,12},{12,8},{16,20},{20,16},{24,28},{28,24},{1,5},{5... | collective-permute-start | bytes 393224 | tf_op jit(solution)/shard_map/ppermute | solution.py:42
  78.5 17.8 %collective-permute-start.13 = (bf16[768,128]{1,0:T(8,128)(2,1)S(1)}, bf16[768,128]{1,0:T(8,128)(2,1)S(1)}, u32[]{:S(2)}, u32[]{:S(2)}) collective-permute-start(bf16[768,128]{1,0:T(8,128)(2,1)S(1)} %anchor_relay.9.rest_0_.first_ref), channel_id=1, source_target_pairs={{0,4},{4,0},{8,12},{12,8},{16,20},{20,16},{24,28},{28,24},{1,5},{5... | collective-permute-start | bytes 589832 | tf_op jit(solution)/shard_map/ppermute | solution.py:42
  79.9 45.5 %collective-permute-start.15 = (bf16[64,1024]{1,0:T(8,128)(2,1)S(1)}, bf16[64,1024]{1,0:T(8,128)(2,1)S(1)}, u32[]{:S(2)}, u32[]{:S(2)}) collective-permute-start(bf16[64,1024]{1,0:T(8,128)(2,1)S(1)} %query_project.1.refs_7_.refs_8_.one_ref), channel_id=1, source_target_pairs={{0,1},{1,0},{2,3},{3,2},{4,5},{5,4},{6,7},{7,6},{8,9},{9,8},{10,11... | collective-permute-start | bytes 393224 | tf_op jit(solution)/shard_map/ppermute | solution.py:42
  125.5 32.8 %collective-permute-start.16 = (bf16[64,1024]{1,0:T(8,128)(2,1)S(1)}, bf16[64,1024]{1,0:T(8,128)(2,1)S(1)}, u32[]{:S(2)}, u32[]{:S(2)}) collective-permute-start(bf16[64,1024]{1,0:T(8,128)(2,1)S(1)} %query_sum.2.refs_11_.one_ref), channel_id=1, source_target_pairs={{0,2},{1,3},{2,0},{3,1},{4,6},{5,7},{6,4},{7,5},{8,10},{9,11},{10,... | collective-permute-start | bytes 393224 | tf_op jit(solution)/shard_map/ppermute | solution.py:42

commit v13 on v11

--- a/solution.py
+++ b/solution.py
@@ -79,7 +79,7 @@
         in_specs=[VMEM] * len(inputs) + [ANY] * len(after),
         out_specs=[VMEM] * len(shapes),
         compiler_params=params(),
-        cost_estimate=pl.CostEstimate(flops=0, bytes_accessed=2**20, transcendentals=0),
+        cost_estimate=pl.CostEstimate(flops=0, bytes_accessed=2**14, transcendentals=0),
         name=name,
     )(*inputs, *after)
 
@@ -371,7 +371,7 @@
     lax.fori_loop(0, heads * (slab // tile), body, 0)
 
 
-def anchor_part(lengths, ctx_q, states, own_k, own_v, anchor, first, count, per_kv, befores=None, after=()):
+def anchor_part(lengths, ctx_q, states, own_k, own_v, anchor, first, count, per_kv, befores=None, after=(), weight=8):
     slab, width = ctx_q.shape
     work = count * slab * slab
     last = befores is not None
@@ -392,7 +392,7 @@
         scratch_shapes=scratch,
         compiler_params=params(),
         cost_estimate=pl.CostEstimate(
-            flops=work * HD * 8, bytes_accessed=count * slab * HD * 8, transcendentals=work
+            flops=work * HD * weight, bytes_accessed=0, transcendentals=0
         ),
         name="context_anchor",
     )(lengths, ctx_q, own_k, own_v, *anchor, *[states[x] for x in bases], *earlier, *after)
@@ -690,8 +690,10 @@
     def source_first(h):
         return h < 2
 
-    def done_early(h):
-        return (h <= 2) | (h == 5)
+    done_early = (
+        lambda h: (h <= 2) | (h == 5),
+        lambda h: (h <= 1) | (h == 3) | (h == 4),
+    )
 
     bits = (6, 2, 4)
     landed = [swap(query_q, "hst", hosts, x, x) for x in bits]
@@ -703,7 +705,7 @@
 
     def send_off(kv, after):
         (parts[kv],) = relay(is_even, own_k, value_landed, after, kv)
-        parts_landed[kv] = swap(parts[kv], "hst", hosts, *along[0])
+        parts_landed[kv] = swap(parts[kv], "hst", hosts, *along[kv])
         return parts[kv]
 
     done = send_off(0, (done,))
@@ -714,42 +716,44 @@
 
     def pass_on(kv, after):
         (parts[kv],) = relay(source_first, parts[kv], parts_landed[kv], after)
-        parts_landed[kv] = swap(parts[kv], "hst", hosts, *along[1])
+        parts_landed[kv] = swap(parts[kv], "hst", hosts, *along[1 - kv])
         return parts[kv]
 
     def complete(kv, after):
-        (held,) = relay(done_early, parts[kv], parts_landed[kv], after)
+        (held,) = relay(done_early[kv], parts[kv], parts_landed[kv], after)
         anchor[kv] = held, swap(held, "hst", hosts, 1, 1)
         return held
 
     keep, give = source_part(lengths, own_keys, own_v, query_kv, queries, landed, q_rows, per_kv, ())
     landed = swap(give, "hst", hosts, 1, 1)
-    done = own(4, 4, (keep,))
+    done = send_off(1, (keep,))
+    done = own(4, 4, (done,))
     source = merge_part([keep, landed], False, (done,))
     landed = swap(source, "hst", hosts, *along[0])
     done = pass_on(0, (source,))
-    done = own(8, 8, (done,))
+    done = own(8, 6, (done,))
     source = merge_part([source, landed], False, (done,))
     landed = swap(source, "hst", hosts, *along[1])
-    done = send_off(1, (source,))
+    done = own(14, 2, (source,))
     done = complete(0, (done,))
+    done = pass_on(1, (done,))
     anchor[0] = prepare(*anchor[0], True, (done,))
     results = {}
 
-    def anchors(first, count, after, last=False):
+    def anchors(first, count, after, last=False, weight=8):
         results[first] = anchor_part(
             lengths, ctx_q, states, own_keys, own_values, anchor[first // per_kv],
-            first, count, per_kv, dict(results) if last else None, after,
+            first, count, per_kv, dict(results) if last else None, after, weight,
         )
         return results[first]
 
-    done = anchors(0, 4, ())
+    done = anchors(0, 4, (), weight=1)
     attended = merge_part([source, landed], True, (done,))
     landed = swap(attended, "hst", hosts, 1, 1)
-    done = pass_on(1, (attended,))
-    done = anchors(4, 2, (done,))
+    done = anchors(4, 2, (attended,))
+    done = complete(1, (done,))
     terms = project_part(attended, landed, out_weight, (done,))
-    done = complete(1, (terms,))
+    done = terms
     shares = [[(12, 4, True)], [(6, 2, False), (8, 4, False)]]
     step = 1
     while step < groups:

time: 159 us -> 161 us (1.013)
  waiting for transfers between devices: 1.33 us -> 2.95 us
    ppermute x17, waiting for transfers between devices: 1.33 us -> 2.95 us  [swap(): lax.ppermute(value, axis, [(i, i ^ (odd if i & 1 else even)) for i in ran...]
    pallas_call x4 -> x5, Pallas kernels: 7.95 us -> 8.22 us  [own_part(): pl.pallas_call(functools.partial(own_kernel, first, count, per_kv), out_s...]
  transfers between devices with their start and end apart: 17 -> 17, of which waited for: 2 -> 3; matrix products, arithmetic and copies ran while one was open for 0% -> 0% of each run, Pallas kernels for 88% -> 88%
where the time goes in v13:
time: 161 us; the launch traced here: 160 us
  Pallas kernels  143 us (89%)
  starting transfers between devices  13.7 us (9%)
  waiting for transfers between devices  2.95 us (2%)
    pallas_call x5, Pallas kernels, anchor_part(): pl.pallas_call(functools.partial(anchor_kernel, first, count, bases, per_...  118 us
    ppermute x17, starting transfers between devices, swap(): lax.ppermute(value, axis, [(i, i ^ (odd if i & 1 else even)) for i in ran...  13.7 us
    pallas_call x1, Pallas kernels, source_part(): pl.pallas_call(functools.partial(source_kernel, per_kv, q_rows, H // KVH)...  11.4 us
    pallas_call x5, Pallas kernels, own_part(): pl.pallas_call(functools.partial(own_kernel, first, count, per_kv), out_s...  8.22 us
  transfers between devices with their start and end apart: 17, of which 3 were waited for; matrix products, arithmetic and copies ran while one was open for 0% of the time, Pallas kernels for 88%

profile of v13, /device:TPU:6, one launch (start us, length us, event | category | flops | bytes accessed | tf_op | source)
XLA Modules:
  0.0 160.4 jit_solution(1632665132132983472)
XLA Ops:
  0.6 1.3 pick_columns.1
  2.1 2.0 %collective-permute-start.2 = (bf16[8,2048]{1,0:T(8,128)(2,1)S(1)}, bf16[8,2048]{1,0:T(8,128)(2,1)S(1)}, u32[]{:S(2)}, u32[]{:S(2)}) collective-permute-start(bf16[8,2048]{1,0:T(8,128)(2,1)S(1)} %copy-done.2), channel_id=1, source_target_pairs={{0,8},{4,12},{8,0},{12,4},{16,24},{20,28},{24,16},{28,20},{1,9},{5... | collective-permute-start | bytes 98312 | tf_op jit(solution)/shard_map/ppermute | solution.py:42
  4.1 1.5 collective-permute-start.3
  5.6 0.4 operands.3
  6.0 1.1 context_own.5.rest_0_.refs_6_
  7.2 1.1 context_own.6.refs_4_.refs_7_
  8.4 0.6 collective-permute-start.6
  9.0 0.7 collective-permute-done.4.landed_ref
  9.8 11.4 %query_source.1 = (bf16[64,1152]{1,0:T(8,128)(2,1)S(1)}, bf16[64,1152]{1,0:T(8,128)(2,1)S(1)}) custom-call(s32[1,8]{1,0:T(1,128)S(1)} %bitcast.1, bf16[512,768]{1,0:T(8,128)(2,1)S(1)} %get-tuple-element.14.k_ref.refs_2_, bf16[768,256]{1,0:T(8,128)(2,1)S(1)} %get-tuple-element.13.second_ref.v_ref, bf16[2,8,1024]{2,1,0:T(8,128)(2,1)S(1)} %copy-done.4, ...), custom_call_target="tpu_custom_call" | custom-call | flops 805306368 | bytes 2097152 | tf_op jit(solution)/shard_map/query_source/pallas_call | solution.py:546
  21.4 1.3 collective-permute-start.5
  22.7 1.9 %context_own.7.refs_2_.refs_6_ = f32[768,1024]{1,0:T(8,128)S(1)} custom-call(bf16[768,2048]{1,0:T(8,128)(2,1)S(1)} %copy-done, bf16[512,768]{1,0:T(8,128)(2,1)S(1)} %get-tuple-element.14.k_ref.refs_2_, bf16[768,512]{1,0:T(8,128)(2,1)S(1)} %get-tuple-element.15.v_ref.refs_3_, bf16[768,128]{1,0:T(8,128)(2,1)S(1)} %anchor_relay.7.rest_0_.one_ref), custom_call_target="tpu_custom_call" | custom-call | flops 1610612736 | bytes 2359296 | tf_op jit(solution)/shard_map/context_own/pallas_call | solution.py:239
  24.6 0.3 query_merge.3.rest_0_.refs_0_
  24.9 0.7 collective-permute-start.9
  25.7 0.9 collective-permute-start.8
  26.6 3.0 %context_own.8.refs_2_.refs_6_ = f32[768,1536]{1,0:T(8,128)S(1)} custom-call(bf16[768,2048]{1,0:T(8,128)(2,1)S(1)} %copy-done, bf16[512,768]{1,0:T(8,128)(2,1)S(1)} %get-tuple-element.14.k_ref.refs_2_, bf16[768,512]{1,0:T(8,128)(2,1)S(1)} %get-tuple-element.15.v_ref.refs_3_, bf16[768,128]{1,0:T(8,128)(2,1)S(1)} %anchor_relay.8.rest_0_.one_ref), custom_call_target="tpu_custom_call" | custom-call | flops 2415919104 | bytes 3538944 | tf_op jit(solution)/shard_map/context_own/pallas_call | solution.py:239
  29.6 2.1 %collective-permute-done.9.refs_1_ = bf16[64,1152]{1,0:T(8,128)(2,1)S(1)} collective-permute-done((bf16[64,1152]{1,0:T(8,128)(2,1)S(1)}, bf16[64,1152]{1,0:T(8,128)(2,1)S(1)}, u32[]{:S(2)}, u32[]{:S(2)}) %collective-permute-start.9) | collective-permute-done | bytes 147488 | tf_op jit(solution)/shard_map/ppermute | solution.py:42
  31.7 0.3 query_merge.4.rest_0_.refs_0_
  32.0 1.1 context_own.9.rest_0_.refs_7_
  33.3 0.9 collective-permute-start.12
  34.2 0.4 collective-permute-start.10
  34.9 29.2 %context_anchor.5.refs_2_.refs_8_ = bf16[768,512]{1,0:T(8,128)(2,1)S(1)} custom-call(s32[1,8]{1,0:T(1,128)S(1)} %bitcast.2, bf16[768,2048]{1,0:T(8,128)(2,1)S(1)} %copy-done, bf16[512,768]{1,0:T(8,128)(2,1)S(1)} %get-tuple-element.14.k_ref.refs_2_, bf16[768,512]{1,0:T(8,128)(2,1)S(1)} %get-tuple-element.15.v_ref.refs_3_, ...), custom_call_target="tpu_custom_call" | custom-call | flops 301989888 | tf_op jit(solution)/shard_map/context_anchor/pallas_call | solution.py:387
  64.1 0.3 query_merge.5.refs_7_.own_ref
  64.7 14.7 %context_anchor.6.rest_0_.refs_9_ = bf16[768,256]{1,0:T(8,128)(2,1)S(1)} custom-call(s32[1,8]{1,0:T(1,128)S(1)} %bitcast.3, bf16[768,2048]{1,0:T(8,128)(2,1)S(1)} %copy-done, bf16[512,768]{1,0:T(8,128)(2,1)S(1)} %get-tuple-element.14.k_ref.refs_2_, bf16[768,512]{1,0:T(8,128)(2,1)S(1)} %get-tuple-element.15.v_ref.refs_3_, ...), custom_call_target="tpu_custom_call" | custom-call | flops 1207959552 | tf_op jit(solution)/shard_map/context_anchor/pallas_call | solution.py:387
  79.4 0.4 collective-permute-start.13
  79.9 0.9 query_project.1.refs_7_.refs_8_.one_ref
  80.7 1.6 %collective-permute-start.15 = (bf16[64,1024]{1,0:T(8,128)(2,1)S(1)}, bf16[64,1024]{1,0:T(8,128)(2,1)S(1)}, u32[]{:S(2)}, u32[]{:S(2)}) collective-permute-start(bf16[64,1024]{1,0:T(8,128)(2,1)S(1)} %query_project.1.refs_7_.refs_8_.one_ref), channel_id=1, source_target_pairs={{0,1},{1,0},{2,3},{3,2},{4,5},{5,4},{6,7},{7,6},{8,9},{9,8},{10,11... | collective-permute-start | bytes 393224 | tf_op jit(solution)/shard_map/ppermute | solution.py:42
  82.4 14.7 %context_anchor.7.rest_0_.refs_8_.refs_10_ = bf16[768,256]{1,0:T(8,128)(2,1)S(1)} custom-call(s32[1,8]{1,0:T(1,128)S(1)} %bitcast.4, bf16[768,2048]{1,0:T(8,128)(2,1)S(1)} %copy-done, bf16[512,768]{1,0:T(8,128)(2,1)S(1)} %get-tuple-element.14.k_ref.refs_2_, bf16[768,512]{1,0:T(8,128)(2,1)S(1)} %get-tuple-element.15.v_ref.refs_3_, ...), custom_call_target="tpu_custom_call" | custom-call | flops 1207959552 | tf_op jit(solution)/shard_map/context_anchor/pallas_call | solution.py:387
  97.1 0.2 operands.5
  97.3 29.5 %context_anchor.8.rest_0_.refs_11_.refs_13_ = bf16[768,512]{1,0:T(8,128)(2,1)S(1)} custom-call(s32[1,8]{1,0:T(1,128)S(1)} %bitcast.5, bf16[768,2048]{1,0:T(8,128)(2,1)S(1)} %copy-done, bf16[512,768]{1,0:T(8,128)(2,1)S(1)} %get-tuple-element.14.k_ref.refs_2_, bf16[768,512]{1,0:T(8,128)(2,1)S(1)} %get-tuple-element.15.v_ref.refs_3_, ...), custom_call_target="tpu_custom_call" | custom-call | flops 2415919104 | tf_op jit(solution)/shard_map/context_anchor/pallas_call | solution.py:387
  126.9 2.7 %collective-permute-start.16 = (bf16[64,1024]{1,0:T(8,128)(2,1)S(1)}, bf16[64,1024]{1,0:T(8,128)(2,1)S(1)}, u32[]{:S(2)}, u32[]{:S(2)}) collective-permute-start(bf16[64,1024]{1,0:T(8,128)(2,1)S(1)} %query_sum.2.refs_12_.one_ref), channel_id=1, source_target_pairs={{0,2},{1,3},{2,0},{3,1},{4,6},{5,7},{6,4},{7,5},{8,10},{9,11},{10,... | collective-permute-start | bytes 393224 | tf_op jit(solution)/shard_map/ppermute | solution.py:42
  129.6 30.1 %context_anchor.9 = bf16[768,2048]{1,0:T(8,128)(2,1)} custom-call(s32[1,8]{1,0:T(1,128)S(1)} %bitcast.6, bf16[768,2048]{1,0:T(8,128)(2,1)S(1)} %copy-done, bf16[512,768]{1,0:T(8,128)(2,1)S(1)} %get-tuple-element.14.k_ref.refs_2_, bf16[768,512]{1,0:T(8,128)(2,1)S(1)} %get-tuple-element.15.v_ref.refs_3_, bf16[256,768]{1,0:T(8,128)(2,1)S(1)} %get-tuple-element.20.refs_4_, ...), custom_call_target="tpu_custom_call" | custom-call | flops 2415919104 | tf_op jit(solution)/shard_map/context_anchor/pallas_call | solution.py:387
  159.7 0.7 query_sum.3
  (40 shorter events, 1.3 us)
Async XLA Ops:
  0.6 1.4 copy-start.2
  0.6 5.3 %copy-start = (bf16[768,2048]{1,0:T(8,128)(2,1)S(1)}, bf16[768,2048]{1,0:T(8,128)(2,1)}, u32[]{:S(2)}) copy-start(bf16[768,2048]{1,0:T(8,128)(2,1)} %refs_1_.9) | copy-start | bytes 9437188
  2.0 5.1 %collective-permute-start = (bf16[768,256]{1,0:T(8,128)(2,1)S(1)}, bf16[768,256]{1,0:T(8,128)(2,1)S(1)}, u32[]{:S(2)}, u32[]{:S(2)}) collective-permute-start(bf16[768,256]{1,0:T(8,128)(2,1)S(1)} %get-tuple-element.13.second_ref.v_ref), channel_id=1, source_target_pairs={{0,4},{4,0},{8,12},{12,8},{16,20},{20,16},{24,28},{28,24},{1,5},{5... | collective-permute-start | bytes 1179656 | tf_op jit(solution)/shard_map/ppermute | solution.py:42
  2.0 6.2 %collective-permute-start.1 = (bf16[8,2048]{1,0:T(8,128)(2,1)S(1)}, bf16[8,2048]{1,0:T(8,128)(2,1)S(1)}, u32[]{:S(2)}, u32[]{:S(2)}) collective-permute-start(bf16[8,2048]{1,0:T(8,128)(2,1)S(1)} %copy-done.2), channel_id=1, source_target_pairs={{0,24},{4,28},{8,16},{12,20},{16,8},{20,12},{24,0},{28,4},{1,25},{... | collective-permute-start | bytes 98312 | tf_op jit(solution)/shard_map/ppermute | solution.py:42
  2.1 6.2 %collective-permute-start.2 = (bf16[8,2048]{1,0:T(8,128)(2,1)S(1)}, bf16[8,2048]{1,0:T(8,128)(2,1)S(1)}, u32[]{:S(2)}, u32[]{:S(2)}) collective-permute-start(bf16[8,2048]{1,0:T(8,128)(2,1)S(1)} %copy-done.2), channel_id=1, source_target_pairs={{0,8},{4,12},{8,0},{12,4},{16,24},{20,28},{24,16},{28,20},{1,9},{5... | collective-permute-start | bytes 98312 | tf_op jit(solution)/shard_map/ppermute | solution.py:42
  4.1 4.2 %collective-permute-start.3 = (bf16[8,2048]{1,0:T(8,128)(2,1)S(1)}, bf16[8,2048]{1,0:T(8,128)(2,1)S(1)}, u32[]{:S(2)}, u32[]{:S(2)}) collective-permute-start(bf16[8,2048]{1,0:T(8,128)(2,1)S(1)} %copy-done.2), channel_id=1, source_target_pairs={{0,16},{4,20},{8,24},{12,28},{16,0},{20,4},{24,8},{28,12},{1,17},{... | collective-permute-start | bytes 98312 | tf_op jit(solution)/shard_map/ppermute | solution.py:42
  7.1 2.6 %copy-start.3 = (s32[8]{0:T(128)S(1)}, s32[8]{0:T(128)}, u32[]{:S(2)}) copy-start(s32[8]{0:T(128)} %param.8) | copy-start | bytes 100
  7.2 2.6 %copy-start.4 = (bf16[2,8,1024]{2,1,0:T(8,128)(2,1)S(1)}, bf16[2,8,1024]{2,1,0:T(8,128)(2,1)}, u32[]{:S(2)}) copy-start(bf16[2,8,1024]{2,1,0:T(8,128)(2,1)} %self_ref.1) | copy-start | bytes 98308
  8.4 1.4 collective-permute-start.4
  8.4 17.2 %collective-permute-start.6 = (bf16[768,128]{1,0:T(8,128)(2,1)S(1)}, bf16[768,128]{1,0:T(8,128)(2,1)S(1)}, u32[]{:S(2)}, u32[]{:S(2)}) collective-permute-start(bf16[768,128]{1,0:T(8,128)(2,1)S(1)} %anchor_relay.6.rest_0_.one_ref), channel_id=1, source_target_pairs={{0,8},{4,20},{8,0},{12,28},{16,24},{20,4},{24,16},{28,12},{1,9},{5... | collective-permute-start | bytes 589832 | tf_op jit(solution)/shard_map/ppermute | solution.py:42
  21.2 3.4 %collective-permute-start.7 = (bf16[64,1152]{1,0:T(8,128)(2,1)S(1)}, bf16[64,1152]{1,0:T(8,128)(2,1)S(1)}, u32[]{:S(2)}, u32[]{:S(2)}) collective-permute-start(bf16[64,1152]{1,0:T(8,128)(2,1)S(1)} %get-tuple-element.17), channel_id=1, source_target_pairs={{0,4},{4,0},{8,12},{12,8},{16,20},{20,16},{24,28},{28,24},{1,5},{5... | collective-permute-start | bytes 442376 | tf_op jit(solution)/shard_map/ppermute | solution.py:42
  21.4 12.7 %collective-permute-start.5 = (bf16[768,128]{1,0:T(8,128)(2,1)S(1)}, bf16[768,128]{1,0:T(8,128)(2,1)S(1)}, u32[]{:S(2)}, u32[]{:S(2)}) collective-permute-start(bf16[768,128]{1,0:T(8,128)(2,1)S(1)} %anchor_relay.7.rest_0_.one_ref), channel_id=1, source_target_pairs={{0,16},{4,12},{8,24},{12,4},{16,0},{20,28},{24,8},{28,20},{1,17},{... | collective-permute-start | bytes 589832 | tf_op jit(solution)/shard_map/ppermute | solution.py:42
  24.9 6.8 %collective-permute-start.9 = (bf16[64,1152]{1,0:T(8,128)(2,1)S(1)}, bf16[64,1152]{1,0:T(8,128)(2,1)S(1)}, u32[]{:S(2)}, u32[]{:S(2)}) collective-permute-start(bf16[64,1152]{1,0:T(8,128)(2,1)S(1)} %query_merge.3.rest_0_.refs_0_), channel_id=1, source_target_pairs={{0,8},{4,20},{8,0},{12,28},{16,24},{20,4},{24,16},{28,12},{1,9},{5... | collective-permute-start | bytes 442376 | tf_op jit(solution)/shard_map/ppermute | solution.py:42
  25.7 7.4 %collective-permute-start.8 = (bf16[768,128]{1,0:T(8,128)(2,1)S(1)}, bf16[768,128]{1,0:T(8,128)(2,1)S(1)}, u32[]{:S(2)}, u32[]{:S(2)}) collective-permute-start(bf16[768,128]{1,0:T(8,128)(2,1)S(1)} %anchor_relay.8.rest_0_.one_ref), channel_id=1, source_target_pairs={{0,16},{4,12},{8,24},{12,4},{16,0},{20,28},{24,8},{28,20},{1,17},{... | collective-permute-start | bytes 589832 | tf_op jit(solution)/shard_map/ppermute | solution.py:42
  33.2 1.5 collective-permute-start.11
  33.3 30.9 %collective-permute-start.12 = (bf16[64,1152]{1,0:T(8,128)(2,1)S(1)}, bf16[64,1152]{1,0:T(8,128)(2,1)S(1)}, u32[]{:S(2)}, u32[]{:S(2)}) collective-permute-start(bf16[64,1152]{1,0:T(8,128)(2,1)S(1)} %query_merge.4.rest_0_.refs_0_), channel_id=1, source_target_pairs={{0,16},{4,12},{8,24},{12,4},{16,0},{20,28},{24,8},{28,20},{1,17},{... | collective-permute-start | bytes 442376 | tf_op jit(solution)/shard_map/ppermute | solution.py:42
  34.2 45.2 %collective-permute-start.10 = (bf16[768,128]{1,0:T(8,128)(2,1)S(1)}, bf16[768,128]{1,0:T(8,128)(2,1)S(1)}, u32[]{:S(2)}, u32[]{:S(2)}) collective-permute-start(bf16[768,128]{1,0:T(8,128)(2,1)S(1)} %anchor_relay.10.rest_0_.one_ref), channel_id=1, source_target_pairs={{0,8},{4,20},{8,0},{12,28},{16,24},{20,4},{24,16},{28,12},{1,9},{5... | collective-permute-start | bytes 589832 | tf_op jit(solution)/shard_map/ppermute | solution.py:42
  64.5 15.4 %copy-start.1 = (bf16[2048,1024]{1,0:T(8,128)(2,1)S(1)}, bf16[2048,1024]{1,0:T(8,128)(2,1)}, u32[]{:S(2)}) copy-start(bf16[2048,1024]{1,0:T(8,128)(2,1)} %w_ref.1) | copy-start | bytes 12582916
  64.5 15.4 %collective-permute-start.14 = (bf16[64,1024]{1,0:T(8,128)(2,1)S(1)}, bf16[64,1024]{1,0:T(8,128)(2,1)S(1)}, u32[]{:S(2)}, u32[]{:S(2)}) collective-permute-start(bf16[64,1024]{1,0:T(8,128)(2,1)S(1)} %query_merge.5.refs_7_.own_ref), channel_id=1, source_target_pairs={{0,4},{4,0},{8,12},{12,8},{16,20},{20,16},{24,28},{28,24},{1,5},{5... | collective-permute-start | bytes 393224 | tf_op jit(solution)/shard_map/ppermute | solution.py:42
  79.4 17.6 %collective-permute-start.13 = (bf16[768,128]{1,0:T(8,128)(2,1)S(1)}, bf16[768,128]{1,0:T(8,128)(2,1)S(1)}, u32[]{:S(2)}, u32[]{:S(2)}) collective-permute-start(bf16[768,128]{1,0:T(8,128)(2,1)S(1)} %anchor_relay.11.rest_0_.first_ref), channel_id=1, source_target_pairs={{0,4},{4,0},{8,12},{12,8},{16,20},{20,16},{24,28},{28,24},{1,5},{5... | collective-permute-start | bytes 589832 | tf_op jit(solution)/shard_map/ppermute | solution.py:42
  80.7 46.1 %collective-permute-start.15 = (bf16[64,1024]{1,0:T(8,128)(2,1)S(1)}, bf16[64,1024]{1,0:T(8,128)(2,1)S(1)}, u32[]{:S(2)}, u32[]{:S(2)}) collective-permute-start(bf16[64,1024]{1,0:T(8,128)(2,1)S(1)} %query_project.1.refs_7_.refs_8_.one_ref), channel_id=1, source_target_pairs={{0,1},{1,0},{2,3},{3,2},{4,5},{5,4},{6,7},{7,6},{8,9},{9,8},{10,11... | collective-permute-start | bytes 393224 | tf_op jit(solution)/shard_map/ppermute | solution.py:42
  126.9 32.8 %collective-permute-start.16 = (bf16[64,1024]{1,0:T(8,128)(2,1)S(1)}, bf16[64,1024]{1,0:T(8,128)(2,1)S(1)}, u32[]{:S(2)}, u32[]{:S(2)}) collective-permute-start(bf16[64,1024]{1,0:T(8,128)(2,1)S(1)} %query_sum.2.refs_12_.one_ref), channel_id=1, source_target_pairs={{0,2},{1,3},{2,0},{3,1},{4,6},{5,7},{6,4},{7,5},{8,10},{9,11},{10,... | collective-permute-start | bytes 393224 | tf_op jit(solution)/shard_map/ppermute | solution.py:42

commit v14 on v11

--- a/solution.py
+++ b/solution.py
@@ -79,7 +79,7 @@
         in_specs=[VMEM] * len(inputs) + [ANY] * len(after),
         out_specs=[VMEM] * len(shapes),
         compiler_params=params(),
-        cost_estimate=pl.CostEstimate(flops=0, bytes_accessed=2**20, transcendentals=0),
+        cost_estimate=pl.CostEstimate(flops=0, bytes_accessed=2**14, transcendentals=0),
         name=name,
     )(*inputs, *after)
 
@@ -261,7 +261,8 @@
     state_refs = refs[6 : 6 + len(bases)]
     earlier = refs[6 + len(bases) : 6 + len(bases) + len(befores)]
     if last:
-        full_ref, out_ref, sems = refs[-3:]
+        full_ref, token_ref, out_ref, sems = refs[-4:]
+        token_ref[...] = jnp.zeros_like(token_ref)
     else:
         out_ref = refs[-1]
     slab = q_ref.shape[0]
@@ -371,7 +372,7 @@
     lax.fori_loop(0, heads * (slab // tile), body, 0)
 
 
-def anchor_part(lengths, ctx_q, states, own_k, own_v, anchor, first, count, per_kv, befores=None, after=()):
+def anchor_part(lengths, ctx_q, states, own_k, own_v, anchor, first, count, per_kv, befores=None, after=(), weight=8):
     slab, width = ctx_q.shape
     work = count * slab * slab
     last = befores is not None
@@ -383,16 +384,17 @@
     scratch = []
     if last:
         scratch = [pltpu.VMEM(results.shape, BF), pltpu.SemaphoreType.DMA((len(earlier) + count,))]
-        results = jax.ShapeDtypeStruct((slab, width), BF)
+        token = jax.ShapeDtypeStruct((8, HD), F32)
+        results = [jax.ShapeDtypeStruct((slab, width), BF), token]
     return pl.pallas_call(
         functools.partial(anchor_kernel, first, count, bases, per_kv, last, places),
         out_shape=results,
         in_specs=[VMEM] * (6 + len(bases) + len(earlier)) + [ANY] * len(after),
-        out_specs=ANY if last else VMEM,
+        out_specs=[ANY, VMEM] if last else VMEM,
         scratch_shapes=scratch,
         compiler_params=params(),
         cost_estimate=pl.CostEstimate(
-            flops=work * HD * 8, bytes_accessed=count * slab * HD * 8, transcendentals=work
+            flops=work * HD * weight, bytes_accessed=0, transcendentals=0
         ),
         name="context_anchor",
     )(lengths, ctx_q, own_k, own_v, *anchor, *[states[x] for x in bases], *earlier, *after)
@@ -652,7 +654,7 @@
     per_kv = min(local_heads, group_size)
     q_rows = query_q.shape[0]
     host = lax.axis_index("hst")
-    fast = hosts == 8 and groups & (groups - 1) == 0
+    fast = hosts == 8 and groups == 4
     fast = fast and q_rows == 8 and local_heads == 16 and per_kv == 8
 
     if not fast:
@@ -673,7 +675,7 @@
                 lengths, ctx_q, {0: state}, own_k, own_v, (anchor[0][cols, :], anchor[1][:, cols]),
                 first, per_kv, per_kv, dict(results) if last else None,
             )
-        return results[first], query_out
+        return results[first][0], query_out
 
     lengths = lengths.reshape(1, hosts)
     states = {}
@@ -731,15 +733,15 @@
     done = own(8, 8, (done,))
     source = merge_part([source, landed], False, (done,))
     landed = swap(source, "hst", hosts, *along[1])
-    done = send_off(1, (source,))
-    done = complete(0, (done,))
+    done = complete(0, (source,))
+    done = send_off(1, (done,))
     anchor[0] = prepare(*anchor[0], True, (done,))
     results = {}
 
-    def anchors(first, count, after, last=False):
+    def anchors(first, count, after, last=False, weight=8):
         results[first] = anchor_part(
             lengths, ctx_q, states, own_keys, own_values, anchor[first // per_kv],
-            first, count, per_kv, dict(results) if last else None, after,
+            first, count, per_kv, dict(results) if last else None, after, weight,
         )
         return results[first]
 
@@ -747,24 +749,22 @@
     attended = merge_part([source, landed], True, (done,))
     landed = swap(attended, "hst", hosts, 1, 1)
     done = pass_on(1, (attended,))
-    done = anchors(4, 2, (done,))
     terms = project_part(attended, landed, out_weight, (done,))
-    done = complete(1, (terms,))
-    shares = [[(12, 4, True)], [(6, 2, False), (8, 4, False)]]
+    done = terms
+    shares = [[(8, 8, True)], [(4, 2, False), (6, 2, False)]]
     step = 1
     while step < groups:
         landed = swap(terms, "tp", groups, step, step)
         last = False
         for first, count, last in shares.pop() if shares else ():
+            if first == 6:
+                done = complete(1, (done,))
             if first == per_kv:
                 anchor[1] = prepare(*anchor[1], True, (done,))
-            done = anchors(first, count, (terms, done), last)
-        terms = add_part(terms, landed, () if last else (done,))
+            done = anchors(first, count, (terms, done), last, 8 if last else 1)
+        terms = add_part(terms, landed, (done[1] if last else done,))
         step *= 2
-    for group in reversed(shares):
-        for first, count, last in group:
-            done = anchors(first, count, (), last)
-    return done, terms
+    return done[0], terms
 
 
 def solution(mesh):

time: 159 us -> 160 us (level)
    pallas_call x5 -> x4, Pallas kernels: 118 us -> 118 us  [anchor_part(): pl.pallas_call(functools.partial(anchor_kernel, first, count, bases, per_...]
  transfers between devices with their start and end apart: 17 -> 17, of which waited for: 2 -> 3; matrix products, arithmetic and copies ran while one was open for 0% -> 0% of each run, Pallas kernels for 88% -> 88%
where the time goes in v14:
time: 160 us
  Pallas kernels  142 us (89%)
  starting transfers between devices  14 us (9%)
  waiting for transfers between devices  2.62 us (2%)
    pallas_call x4, Pallas kernels, anchor_part(): pl.pallas_call(functools.partial(anchor_kernel, first, count, bases, per_...  118 us
    ppermute x17, starting transfers between devices, swap(): lax.ppermute(value, axis, [(i, i ^ (odd if i & 1 else even)) for i in ran...  14 us
    pallas_call x1, Pallas kernels, source_part(): pl.pallas_call(functools.partial(source_kernel, per_kv, q_rows, H // KVH)...  11.4 us
    pallas_call x4, Pallas kernels, own_part(): pl.pallas_call(functools.partial(own_kernel, first, count, per_kv), out_s...  7.93 us
  transfers between devices with their start and end apart: 17, of which 3 were waited for; matrix products, arithmetic and copies ran while one was open for 0% of the time, Pallas kernels for 88%

profile of v14, /device:TPU:6, one launch (start us, length us, event | category | flops | bytes accessed | tf_op | source)
XLA Modules:
  0.0 159.5 jit_solution(9275572007591750017)
XLA Ops:
  0.6 1.3 pick_columns.1
  2.1 2.0 %collective-permute-start.3 = (bf16[8,2048]{1,0:T(8,128)(2,1)S(1)}, bf16[8,2048]{1,0:T(8,128)(2,1)S(1)}, u32[]{:S(2)}, u32[]{:S(2)}) collective-permute-start(bf16[8,2048]{1,0:T(8,128)(2,1)S(1)} %copy-done.2), channel_id=1, source_target_pairs={{0,8},{4,12},{8,0},{12,4},{16,24},{20,28},{24,16},{28,20},{1,9},{5... | collective-permute-start | bytes 98312 | tf_op jit(solution)/shard_map/ppermute | solution.py:42
  4.1 1.5 collective-permute-start.4
  5.6 0.4 operands.3
  6.0 1.1 context_own.4.rest_0_.refs_6_
  7.2 1.1 context_own.5.refs_4_.refs_7_
  8.4 0.6 collective-permute-start.1
  9.0 0.7 collective-permute-done.5.landed_ref
  9.8 11.4 %query_source.1 = (bf16[64,1152]{1,0:T(8,128)(2,1)S(1)}, bf16[64,1152]{1,0:T(8,128)(2,1)S(1)}) custom-call(s32[1,8]{1,0:T(1,128)S(1)} %bitcast.1, bf16[512,768]{1,0:T(8,128)(2,1)S(1)} %get-tuple-element.16.k_ref.refs_2_, bf16[768,256]{1,0:T(8,128)(2,1)S(1)} %get-tuple-element.15.second_ref.v_ref, bf16[2,8,1024]{2,1,0:T(8,128)(2,1)S(1)} %copy-done.4, ...), custom_call_target="tpu_custom_call" | custom-call | flops 805306368 | bytes 2097152 | tf_op jit(solution)/shard_map/query_source/pallas_call | solution.py:548
  21.3 1.9 %context_own.6.refs_2_.refs_6_ = f32[768,1024]{1,0:T(8,128)S(1)} custom-call(bf16[768,2048]{1,0:T(8,128)(2,1)S(1)} %copy-done, bf16[512,768]{1,0:T(8,128)(2,1)S(1)} %get-tuple-element.16.k_ref.refs_2_, bf16[768,512]{1,0:T(8,128)(2,1)S(1)} %get-tuple-element.17.v_ref.refs_3_, bf16[64,1152]{1,0:T(8,128)(2,1)S(1)} %get-tuple-element.18.rest_0_.refs_0_), custom_call_target="tpu_custom_call" | custom-call | flops 1610612736 | bytes 2359296 | tf_op jit(solution)/shard_map/context_own/pallas_call | solution.py:239
  23.2 0.3 query_merge.3.rest_0_.refs_0_
  23.6 0.7 collective-permute-start.8
  24.3 1.3 collective-permute-start.7
  25.6 3.8 %context_own.7.refs_2_.refs_6_ = f32[768,2048]{1,0:T(8,128)S(1)} custom-call(bf16[768,2048]{1,0:T(8,128)(2,1)S(1)} %copy-done, bf16[512,768]{1,0:T(8,128)(2,1)S(1)} %get-tuple-element.16.k_ref.refs_2_, bf16[768,512]{1,0:T(8,128)(2,1)S(1)} %get-tuple-element.17.v_ref.refs_3_, bf16[768,128]{1,0:T(8,128)(2,1)S(1)} %anchor_relay.7.rest_0_.one_ref), custom_call_target="tpu_custom_call" | custom-call | flops 3221225472 | bytes 4718592 | tf_op jit(solution)/shard_map/context_own/pallas_call | solution.py:239
  29.5 0.5 collective-permute-done.8.refs_1_
  30.0 0.3 query_merge.4.rest_0_.refs_0_
  30.4 0.4 collective-permute-start.11
  30.8 1.3 collective-permute-start.10
  32.1 0.8 collective-permute-start.9
  33.2 29.2 %context_anchor.4.refs_2_.refs_7_ = bf16[768,512]{1,0:T(8,128)(2,1)S(1)} custom-call(s32[1,8]{1,0:T(1,128)S(1)} %bitcast.2, bf16[768,2048]{1,0:T(8,128)(2,1)S(1)} %copy-done, bf16[512,768]{1,0:T(8,128)(2,1)S(1)} %get-tuple-element.16.k_ref.refs_2_, bf16[768,512]{1,0:T(8,128)(2,1)S(1)} %get-tuple-element.17.v_ref.refs_3_, ...), custom_call_target="tpu_custom_call" | custom-call | flops 2415919104 | tf_op jit(solution)/shard_map/context_anchor/pallas_call | solution.py:389
  62.4 0.3 query_merge.5.rest_0_.own_ref
  62.8 0.5 collective-permute-start.12
  63.3 1.3 collective-permute-done.13.other_ref
  64.6 0.9 query_project.1.refs_7_.refs_8_.one_ref
  65.5 14.6 %context_anchor.5.rest_0_.refs_8_ = bf16[768,256]{1,0:T(8,128)(2,1)S(1)} custom-call(s32[1,8]{1,0:T(1,128)S(1)} %bitcast.3, bf16[768,2048]{1,0:T(8,128)(2,1)S(1)} %copy-done, bf16[512,768]{1,0:T(8,128)(2,1)S(1)} %get-tuple-element.16.k_ref.refs_2_, bf16[768,512]{1,0:T(8,128)(2,1)S(1)} %get-tuple-element.17.v_ref.refs_3_, ...), custom_call_target="tpu_custom_call" | custom-call | flops 150994944 | tf_op jit(solution)/shard_map/context_anchor/pallas_call | solution.py:389
  80.1 0.2 collective-permute-start.14
  80.3 1.6 collective-permute-start.15
  81.9 14.6 %context_anchor.6.rest_0_.refs_9_.refs_11_ = bf16[768,256]{1,0:T(8,128)(2,1)S(1)} custom-call(s32[1,8]{1,0:T(1,128)S(1)} %bitcast.4, bf16[768,2048]{1,0:T(8,128)(2,1)S(1)} %copy-done, bf16[512,768]{1,0:T(8,128)(2,1)S(1)} %get-tuple-element.16.k_ref.refs_2_, bf16[768,512]{1,0:T(8,128)(2,1)S(1)} %get-tuple-element.17.v_ref.refs_3_, ...), custom_call_target="tpu_custom_call" | custom-call | flops 150994944 | tf_op jit(solution)/shard_map/context_anchor/pallas_call | solution.py:389
  96.5 2.7 %collective-permute-start.16 = (bf16[64,1024]{1,0:T(8,128)(2,1)S(1)}, bf16[64,1024]{1,0:T(8,128)(2,1)S(1)}, u32[]{:S(2)}, u32[]{:S(2)}) collective-permute-start(bf16[64,1024]{1,0:T(8,128)(2,1)S(1)} %query_sum.2.refs_10_.one_ref), channel_id=1, source_target_pairs={{0,2},{1,3},{2,0},{3,1},{4,6},{5,7},{6,4},{7,5},{8,10},{9,11},{10,... | collective-permute-start | bytes 393224 | tf_op jit(solution)/shard_map/ppermute | solution.py:42
  99.2 0.2 operands.5
  99.4 59.4 %context_anchor.7 = (bf16[768,2048]{1,0:T(8,128)(2,1)}, f32[8,128]{1,0:T(8,128)S(1)}) custom-call(s32[1,8]{1,0:T(1,128)S(1)} %bitcast.5, bf16[768,2048]{1,0:T(8,128)(2,1)S(1)} %copy-done, bf16[512,768]{1,0:T(8,128)(2,1)S(1)} %get-tuple-element.16.k_ref.refs_2_, bf16[768,512]{1,0:T(8,128)(2,1)S(1)} %get-tuple-element.17.v_ref.refs_3_, ...), custom_call_target="tpu_custom_call" | custom-call | flops 4831838208 | tf_op jit(solution)/shard_map/context_anchor/pallas_call | solution.py:389
  158.8 0.7 query_sum.3
  (38 shorter events, 1.0 us)
Async XLA Ops:
  0.6 1.4 copy-start.2
  0.6 5.3 %copy-start = (bf16[768,2048]{1,0:T(8,128)(2,1)S(1)}, bf16[768,2048]{1,0:T(8,128)(2,1)}, u32[]{:S(2)}) copy-start(bf16[768,2048]{1,0:T(8,128)(2,1)} %refs_1_.7) | copy-start | bytes 9437188
  2.0 5.1 %collective-permute-start = (bf16[768,256]{1,0:T(8,128)(2,1)S(1)}, bf16[768,256]{1,0:T(8,128)(2,1)S(1)}, u32[]{:S(2)}, u32[]{:S(2)}) collective-permute-start(bf16[768,256]{1,0:T(8,128)(2,1)S(1)} %get-tuple-element.15.second_ref.v_ref), channel_id=1, source_target_pairs={{0,4},{4,0},{8,12},{12,8},{16,20},{20,16},{24,28},{28,24},{1,5},{5... | collective-permute-start | bytes 1179656 | tf_op jit(solution)/shard_map/ppermute | solution.py:42
  2.0 6.2 %collective-permute-start.2 = (bf16[8,2048]{1,0:T(8,128)(2,1)S(1)}, bf16[8,2048]{1,0:T(8,128)(2,1)S(1)}, u32[]{:S(2)}, u32[]{:S(2)}) collective-permute-start(bf16[8,2048]{1,0:T(8,128)(2,1)S(1)} %copy-done.2), channel_id=1, source_target_pairs={{0,24},{4,28},{8,16},{12,20},{16,8},{20,12},{24,0},{28,4},{1,25},{... | collective-permute-start | bytes 98312 | tf_op jit(solution)/shard_map/ppermute | solution.py:42
  2.1 6.1 %collective-permute-start.3 = (bf16[8,2048]{1,0:T(8,128)(2,1)S(1)}, bf16[8,2048]{1,0:T(8,128)(2,1)S(1)}, u32[]{:S(2)}, u32[]{:S(2)}) collective-permute-start(bf16[8,2048]{1,0:T(8,128)(2,1)S(1)} %copy-done.2), channel_id=1, source_target_pairs={{0,8},{4,12},{8,0},{12,4},{16,24},{20,28},{24,16},{28,20},{1,9},{5... | collective-permute-start | bytes 98312 | tf_op jit(solution)/shard_map/ppermute | solution.py:42
  4.1 4.2 %collective-permute-start.4 = (bf16[8,2048]{1,0:T(8,128)(2,1)S(1)}, bf16[8,2048]{1,0:T(8,128)(2,1)S(1)}, u32[]{:S(2)}, u32[]{:S(2)}) collective-permute-start(bf16[8,2048]{1,0:T(8,128)(2,1)S(1)} %copy-done.2), channel_id=1, source_target_pairs={{0,16},{4,20},{8,24},{12,28},{16,0},{20,4},{24,8},{28,12},{1,17},{... | collective-permute-start | bytes 98312 | tf_op jit(solution)/shard_map/ppermute | solution.py:42
  7.1 2.6 %copy-start.3 = (s32[8]{0:T(128)S(1)}, s32[8]{0:T(128)}, u32[]{:S(2)}) copy-start(s32[8]{0:T(128)} %param.8) | copy-start | bytes 100
  7.2 2.6 %copy-start.4 = (bf16[2,8,1024]{2,1,0:T(8,128)(2,1)S(1)}, bf16[2,8,1024]{2,1,0:T(8,128)(2,1)}, u32[]{:S(2)}) copy-start(bf16[2,8,1024]{2,1,0:T(8,128)(2,1)} %self_ref.1) | copy-start | bytes 98308
  8.3 1.4 collective-permute-start.5
  8.4 15.9 %collective-permute-start.1 = (bf16[768,128]{1,0:T(8,128)(2,1)S(1)}, bf16[768,128]{1,0:T(8,128)(2,1)S(1)}, u32[]{:S(2)}, u32[]{:S(2)}) collective-permute-start(bf16[768,128]{1,0:T(8,128)(2,1)S(1)} %anchor_relay.6.rest_0_.one_ref), channel_id=1, source_target_pairs={{0,8},{4,20},{8,0},{12,28},{16,24},{20,4},{24,16},{28,12},{1,9},{5... | collective-permute-start | bytes 589832 | tf_op jit(solution)/shard_map/ppermute | solution.py:42
  21.1 2.1 %collective-permute-start.6 = (bf16[64,1152]{1,0:T(8,128)(2,1)S(1)}, bf16[64,1152]{1,0:T(8,128)(2,1)S(1)}, u32[]{:S(2)}, u32[]{:S(2)}) collective-permute-start(bf16[64,1152]{1,0:T(8,128)(2,1)S(1)} %get-tuple-element.19), channel_id=1, source_target_pairs={{0,4},{4,0},{8,12},{12,8},{16,20},{20,16},{24,28},{28,24},{1,5},{5... | collective-permute-start | bytes 442376 | tf_op jit(solution)/shard_map/ppermute | solution.py:42
  23.6 6.4 %collective-permute-start.8 = (bf16[64,1152]{1,0:T(8,128)(2,1)S(1)}, bf16[64,1152]{1,0:T(8,128)(2,1)S(1)}, u32[]{:S(2)}, u32[]{:S(2)}) collective-permute-start(bf16[64,1152]{1,0:T(8,128)(2,1)S(1)} %query_merge.3.rest_0_.refs_0_), channel_id=1, source_target_pairs={{0,8},{4,20},{8,0},{12,28},{16,24},{20,4},{24,16},{28,12},{1,9},{5... | collective-permute-start | bytes 442376 | tf_op jit(solution)/shard_map/ppermute | solution.py:42
  24.3 6.0 %collective-permute-start.7 = (bf16[768,128]{1,0:T(8,128)(2,1)S(1)}, bf16[768,128]{1,0:T(8,128)(2,1)S(1)}, u32[]{:S(2)}, u32[]{:S(2)}) collective-permute-start(bf16[768,128]{1,0:T(8,128)(2,1)S(1)} %anchor_relay.7.rest_0_.one_ref), channel_id=1, source_target_pairs={{0,16},{4,12},{8,24},{12,4},{16,0},{20,28},{24,8},{28,20},{1,17},{... | collective-permute-start | bytes 589832 | tf_op jit(solution)/shard_map/ppermute | solution.py:42
  30.4 2.6 %collective-permute-start.11 = (bf16[768,128]{1,0:T(8,128)(2,1)S(1)}, bf16[768,128]{1,0:T(8,128)(2,1)S(1)}, u32[]{:S(2)}, u32[]{:S(2)}) collective-permute-start(bf16[768,128]{1,0:T(8,128)(2,1)S(1)} %anchor_relay.8.rest_0_.first_ref), channel_id=1, source_target_pairs={{0,4},{4,0},{8,12},{12,8},{16,20},{20,16},{24,28},{28,24},{1,5},{5... | collective-permute-start | bytes 589832 | tf_op jit(solution)/shard_map/ppermute | solution.py:42
  30.8 31.6 %collective-permute-start.10 = (bf16[64,1152]{1,0:T(8,128)(2,1)S(1)}, bf16[64,1152]{1,0:T(8,128)(2,1)S(1)}, u32[]{:S(2)}, u32[]{:S(2)}) collective-permute-start(bf16[64,1152]{1,0:T(8,128)(2,1)S(1)} %query_merge.4.rest_0_.refs_0_), channel_id=1, source_target_pairs={{0,16},{4,12},{8,24},{12,4},{16,0},{20,28},{24,8},{28,20},{1,17},{... | collective-permute-start | bytes 442376 | tf_op jit(solution)/shard_map/ppermute | solution.py:42
  32.1 30.6 %collective-permute-start.9 = (bf16[768,128]{1,0:T(8,128)(2,1)S(1)}, bf16[768,128]{1,0:T(8,128)(2,1)S(1)}, u32[]{:S(2)}, u32[]{:S(2)}) collective-permute-start(bf16[768,128]{1,0:T(8,128)(2,1)S(1)} %anchor_relay.9.rest_0_.one_ref), channel_id=1, source_target_pairs={{0,8},{4,20},{8,0},{12,28},{16,24},{20,4},{24,16},{28,12},{1,9},{5... | collective-permute-start | bytes 589832 | tf_op jit(solution)/shard_map/ppermute | solution.py:42
  33.2 31.5 %copy-start.1 = (bf16[2048,1024]{1,0:T(8,128)(2,1)S(1)}, bf16[2048,1024]{1,0:T(8,128)(2,1)}, u32[]{:S(2)}) copy-start(bf16[2048,1024]{1,0:T(8,128)(2,1)} %w_ref.1) | copy-start | bytes 12582916
  62.8 17.3 %collective-permute-start.12 = (bf16[768,128]{1,0:T(8,128)(2,1)S(1)}, bf16[768,128]{1,0:T(8,128)(2,1)S(1)}, u32[]{:S(2)}, u32[]{:S(2)}) collective-permute-start(bf16[768,128]{1,0:T(8,128)(2,1)S(1)} %anchor_relay.10.rest_0_.one_ref), channel_id=1, source_target_pairs={{0,16},{4,12},{8,24},{12,4},{16,0},{20,28},{24,8},{28,20},{1,17},{... | collective-permute-start | bytes 589832 | tf_op jit(solution)/shard_map/ppermute | solution.py:42
  63.3 1.3 collective-permute-start.13
  80.1 19.1 %collective-permute-start.14 = (bf16[768,128]{1,0:T(8,128)(2,1)S(1)}, bf16[768,128]{1,0:T(8,128)(2,1)S(1)}, u32[]{:S(2)}, u32[]{:S(2)}) collective-permute-start(bf16[768,128]{1,0:T(8,128)(2,1)S(1)} %anchor_relay.11.refs_8_.first_ref), channel_id=1, source_target_pairs={{0,4},{4,0},{8,12},{12,8},{16,20},{20,16},{24,28},{28,24},{1,5},{5... | collective-permute-start | bytes 589832 | tf_op jit(solution)/shard_map/ppermute | solution.py:42
  80.3 16.2 %collective-permute-start.15 = (bf16[64,1024]{1,0:T(8,128)(2,1)S(1)}, bf16[64,1024]{1,0:T(8,128)(2,1)S(1)}, u32[]{:S(2)}, u32[]{:S(2)}) collective-permute-start(bf16[64,1024]{1,0:T(8,128)(2,1)S(1)} %query_project.1.refs_7_.refs_8_.one_ref), channel_id=1, source_target_pairs={{0,1},{1,0},{2,3},{3,2},{4,5},{5,4},{6,7},{7,6},{8,9},{9,8},{10,11... | collective-permute-start | bytes 393224 | tf_op jit(solution)/shard_map/ppermute | solution.py:42
  96.5 62.3 %collective-permute-start.16 = (bf16[64,1024]{1,0:T(8,128)(2,1)S(1)}, bf16[64,1024]{1,0:T(8,128)(2,1)S(1)}, u32[]{:S(2)}, u32[]{:S(2)}) collective-permute-start(bf16[64,1024]{1,0:T(8,128)(2,1)S(1)} %query_sum.2.refs_10_.one_ref), channel_id=1, source_target_pairs={{0,2},{1,3},{2,0},{3,1},{4,6},{5,7},{6,4},{7,5},{8,10},{9,11},{10,... | collective-permute-start | bytes 393224 | tf_op jit(solution)/shard_map/ppermute | solution.py:42

commit v15 on v12

--- a/solution.py
+++ b/solution.py
@@ -744,11 +744,10 @@
     done = anchors(0, 4, ())
     attended = merge_part([source, landed], True, (done,))
     landed = swap(attended, "hst", hosts, 1, 1)
-    done = anchors(4, 2, (attended,))
-    done = complete(1, (done,))
+    done = complete(1, (attended,))
     terms = project_part(attended, landed, out_weight, (done,))
     done = terms
-    shares = [[(12, 4, True)], [(6, 2, False), (8, 4, False)]]
+    shares = [[(10, 6, True)], [(4, 4, False), (8, 2, False)]]
     step = 1
     while step < groups:
         landed = swap(terms, "tp", groups, step, step)

time: 159 us -> 160 us (level)
    pallas_call x5 -> x4, Pallas kernels: 118 us -> 118 us  [anchor_part(): pl.pallas_call(functools.partial(anchor_kernel, first, count, bases, per_...]
  transfers between devices with their start and end apart: 17 -> 17, of which waited for: 2 -> 3; matrix products, arithmetic and copies ran while one was open for 0% -> 0% of each run, Pallas kernels for 88% -> 88%
where the time goes in v15:
time: 160 us
  Pallas kernels  142 us (89%)
  starting transfers between devices  15.2 us (10%)
    pallas_call x4, Pallas kernels, anchor_part(): pl.pallas_call(functools.partial(anchor_kernel, first, count, bases, per_...  118 us
    ppermute x17, starting transfers between devices, swap(): lax.ppermute(value, axis, [(i, i ^ (odd if i & 1 else even)) for i in ran...  15.2 us
    pallas_call x1, Pallas kernels, source_part(): pl.pallas_call(functools.partial(source_kernel, per_kv, q_rows, H // KVH)...  11.4 us
    pallas_call x4, Pallas kernels, own_part(): pl.pallas_call(functools.partial(own_kernel, first, count, per_kv), out_s...  7.95 us
  transfers between devices with their start and end apart: 17, of which 3 were waited for; matrix products, arithmetic and copies ran while one was open for 0% of the time, Pallas kernels for 88%

profile of v15, /device:TPU:6, one launch (start us, length us, event | category | flops | bytes accessed | tf_op | source)
XLA Modules:
  0.0 160.1 jit_solution(16056353432180586355)
XLA Ops:
  0.6 1.3 pick_columns.1
  2.1 2.0 %collective-permute-start.4 = (bf16[8,2048]{1,0:T(8,128)(2,1)S(1)}, bf16[8,2048]{1,0:T(8,128)(2,1)S(1)}, u32[]{:S(2)}, u32[]{:S(2)}) collective-permute-start(bf16[8,2048]{1,0:T(8,128)(2,1)S(1)} %copy-done.2), channel_id=1, source_target_pairs={{0,8},{4,12},{8,0},{12,4},{16,24},{20,28},{24,16},{28,20},{1,9},{5... | collective-permute-start | bytes 98312 | tf_op jit(solution)/shard_map/ppermute | solution.py:42
  4.1 1.5 collective-permute-start.5
  5.6 0.4 operands.3
  6.0 1.1 context_own.4.rest_0_.refs_6_
  7.2 1.1 context_own.5.refs_4_.refs_7_
  8.5 0.6 collective-permute-start.2
  9.1 1.2 collective-permute-start.1
  10.3 11.4 %query_source.1 = (bf16[64,1152]{1,0:T(8,128)(2,1)S(1)}, bf16[64,1152]{1,0:T(8,128)(2,1)S(1)}) custom-call(s32[1,8]{1,0:T(1,128)S(1)} %bitcast.1, bf16[512,768]{1,0:T(8,128)(2,1)S(1)} %get-tuple-element.16.k_ref.refs_2_, bf16[768,256]{1,0:T(8,128)(2,1)S(1)} %get-tuple-element.15.second_ref.v_ref, bf16[2,8,1024]{2,1,0:T(8,128)(2,1)S(1)} %copy-done.4, ...), custom_call_target="tpu_custom_call" | custom-call | flops 805306368 | bytes 2097152 | tf_op jit(solution)/shard_map/query_source/pallas_call | solution.py:548
  21.7 1.9 %context_own.6.refs_2_.refs_6_ = f32[768,1024]{1,0:T(8,128)S(1)} custom-call(bf16[768,2048]{1,0:T(8,128)(2,1)S(1)} %copy-done, bf16[512,768]{1,0:T(8,128)(2,1)S(1)} %get-tuple-element.16.k_ref.refs_2_, bf16[768,512]{1,0:T(8,128)(2,1)S(1)} %get-tuple-element.17.v_ref.refs_3_, bf16[64,1152]{1,0:T(8,128)(2,1)S(1)} %get-tuple-element.20.rest_0_.refs_0_), custom_call_target="tpu_custom_call" | custom-call | flops 1610612736 | bytes 2359296 | tf_op jit(solution)/shard_map/context_own/pallas_call | solution.py:241
  23.7 0.3 query_merge.3.rest_0_.refs_0_
  24.0 1.6 collective-permute-start.9
  25.6 0.9 collective-permute-start.8
  26.5 3.8 %context_own.7.refs_2_.refs_6_ = f32[768,2048]{1,0:T(8,128)S(1)} custom-call(bf16[768,2048]{1,0:T(8,128)(2,1)S(1)} %copy-done, bf16[512,768]{1,0:T(8,128)(2,1)S(1)} %get-tuple-element.16.k_ref.refs_2_, bf16[768,512]{1,0:T(8,128)(2,1)S(1)} %get-tuple-element.17.v_ref.refs_3_, bf16[768,128]{1,0:T(8,128)(2,1)S(1)} %anchor_relay.6.rest_0_.one_ref), custom_call_target="tpu_custom_call" | custom-call | flops 3221225472 | bytes 4718592 | tf_op jit(solution)/shard_map/context_own/pallas_call | solution.py:241
  30.3 0.2 collective-permute-done.9.refs_1_
  30.6 0.3 query_merge.4.rest_0_.refs_0_
  30.9 0.4 collective-permute-done.8.two_ref
  31.5 0.9 collective-permute-start.11
  32.4 1.3 collective-permute-start.10
  33.6 0.2 operands.4
  33.9 29.5 %context_anchor.4.refs_2_.refs_7_ = bf16[768,512]{1,0:T(8,128)(2,1)S(1)} custom-call(s32[1,8]{1,0:T(1,128)S(1)} %bitcast.2, bf16[768,2048]{1,0:T(8,128)(2,1)S(1)} %copy-done, bf16[512,768]{1,0:T(8,128)(2,1)S(1)} %get-tuple-element.16.k_ref.refs_2_, bf16[768,512]{1,0:T(8,128)(2,1)S(1)} %get-tuple-element.17.v_ref.refs_3_, ...), custom_call_target="tpu_custom_call" | custom-call | flops 2415919104 | bytes 3145728 | tf_op jit(solution)/shard_map/context_anchor/pallas_call | solution.py:389
  63.3 0.3 query_merge.5.rest_0_.own_ref
  63.8 0.5 collective-permute-start.13
  64.3 0.8 collective-permute-done.14.other_ref
  65.1 0.9 query_project.1.refs_7_.refs_8_.one_ref
  66.0 1.6 %collective-permute-start.15 = (bf16[64,1024]{1,0:T(8,128)(2,1)S(1)}, bf16[64,1024]{1,0:T(8,128)(2,1)S(1)}, u32[]{:S(2)}, u32[]{:S(2)}) collective-permute-start(bf16[64,1024]{1,0:T(8,128)(2,1)S(1)} %query_project.1.refs_7_.refs_8_.one_ref), channel_id=1, source_target_pairs={{0,1},{1,0},{2,3},{3,2},{4,5},{5,4},{6,7},{7,6},{8,9},{9,8},{10,11... | collective-permute-start | bytes 393224 | tf_op jit(solution)/shard_map/ppermute | solution.py:42
  67.6 29.0 %context_anchor.5.rest_0_.refs_8_ = bf16[768,512]{1,0:T(8,128)(2,1)S(1)} custom-call(s32[1,8]{1,0:T(1,128)S(1)} %bitcast.3, bf16[768,2048]{1,0:T(8,128)(2,1)S(1)} %copy-done, bf16[512,768]{1,0:T(8,128)(2,1)S(1)} %get-tuple-element.16.k_ref.refs_2_, bf16[768,512]{1,0:T(8,128)(2,1)S(1)} %get-tuple-element.17.v_ref.refs_3_, ...), custom_call_target="tpu_custom_call" | custom-call | flops 2415919104 | bytes 3145728 | tf_op jit(solution)/shard_map/context_anchor/pallas_call | solution.py:389
  96.7 0.2 operands.5
  96.9 14.7 %context_anchor.6.rest_0_.refs_9_.refs_11_ = bf16[768,256]{1,0:T(8,128)(2,1)S(1)} custom-call(s32[1,8]{1,0:T(1,128)S(1)} %bitcast.4, bf16[768,2048]{1,0:T(8,128)(2,1)S(1)} %copy-done, bf16[512,768]{1,0:T(8,128)(2,1)S(1)} %get-tuple-element.16.k_ref.refs_2_, bf16[768,512]{1,0:T(8,128)(2,1)S(1)} %get-tuple-element.17.v_ref.refs_3_, ...), custom_call_target="tpu_custom_call" | custom-call | flops 1207959552 | bytes 1572864 | tf_op jit(solution)/shard_map/context_anchor/pallas_call | solution.py:389
  111.6 2.7 %collective-permute-start.16 = (bf16[64,1024]{1,0:T(8,128)(2,1)S(1)}, bf16[64,1024]{1,0:T(8,128)(2,1)S(1)}, u32[]{:S(2)}, u32[]{:S(2)}) collective-permute-start(bf16[64,1024]{1,0:T(8,128)(2,1)S(1)} %query_sum.2.refs_10_.one_ref), channel_id=1, source_target_pairs={{0,2},{1,3},{2,0},{3,1},{4,6},{5,7},{6,4},{7,5},{8,10},{9,11},{10,... | collective-permute-start | bytes 393224 | tf_op jit(solution)/shard_map/ppermute | solution.py:42
  114.3 45.1 %context_anchor.7 = bf16[768,2048]{1,0:T(8,128)(2,1)} custom-call(s32[1,8]{1,0:T(1,128)S(1)} %bitcast.5, bf16[768,2048]{1,0:T(8,128)(2,1)S(1)} %copy-done, bf16[512,768]{1,0:T(8,128)(2,1)S(1)} %get-tuple-element.16.k_ref.refs_2_, bf16[768,512]{1,0:T(8,128)(2,1)S(1)} %get-tuple-element.17.v_ref.refs_3_, bf16[256,768]{1,0:T(8,128)(2,1)S(1)} %get-tuple-element.24.refs_4_, ...), custom_call_target="tpu_custom_call" | custom-call | flops 3623878656 | bytes 4718592 | tf_op jit(solution)/shard_map/context_anchor/pallas_call | solution.py:389
  159.4 0.7 query_sum.3
  (37 shorter events, 0.8 us)
Async XLA Ops:
  0.6 1.4 copy-start.2
  0.6 5.3 %copy-start = (bf16[768,2048]{1,0:T(8,128)(2,1)S(1)}, bf16[768,2048]{1,0:T(8,128)(2,1)}, u32[]{:S(2)}) copy-start(bf16[768,2048]{1,0:T(8,128)(2,1)} %refs_1_.7) | copy-start | bytes 9437188
  2.0 5.1 %collective-permute-start = (bf16[768,256]{1,0:T(8,128)(2,1)S(1)}, bf16[768,256]{1,0:T(8,128)(2,1)S(1)}, u32[]{:S(2)}, u32[]{:S(2)}) collective-permute-start(bf16[768,256]{1,0:T(8,128)(2,1)S(1)} %get-tuple-element.15.second_ref.v_ref), channel_id=1, source_target_pairs={{0,4},{4,0},{8,12},{12,8},{16,20},{20,16},{24,28},{28,24},{1,5},{5... | collective-permute-start | bytes 1179656 | tf_op jit(solution)/shard_map/ppermute | solution.py:42
  2.0 6.3 %collective-permute-start.3 = (bf16[8,2048]{1,0:T(8,128)(2,1)S(1)}, bf16[8,2048]{1,0:T(8,128)(2,1)S(1)}, u32[]{:S(2)}, u32[]{:S(2)}) collective-permute-start(bf16[8,2048]{1,0:T(8,128)(2,1)S(1)} %copy-done.2), channel_id=1, source_target_pairs={{0,24},{4,28},{8,16},{12,20},{16,8},{20,12},{24,0},{28,4},{1,25},{... | collective-permute-start | bytes 98312 | tf_op jit(solution)/shard_map/ppermute | solution.py:42
  2.1 6.2 %collective-permute-start.4 = (bf16[8,2048]{1,0:T(8,128)(2,1)S(1)}, bf16[8,2048]{1,0:T(8,128)(2,1)S(1)}, u32[]{:S(2)}, u32[]{:S(2)}) collective-permute-start(bf16[8,2048]{1,0:T(8,128)(2,1)S(1)} %copy-done.2), channel_id=1, source_target_pairs={{0,8},{4,12},{8,0},{12,4},{16,24},{20,28},{24,16},{28,20},{1,9},{5... | collective-permute-start | bytes 98312 | tf_op jit(solution)/shard_map/ppermute | solution.py:42
  4.1 4.2 %collective-permute-start.5 = (bf16[8,2048]{1,0:T(8,128)(2,1)S(1)}, bf16[8,2048]{1,0:T(8,128)(2,1)S(1)}, u32[]{:S(2)}, u32[]{:S(2)}) collective-permute-start(bf16[8,2048]{1,0:T(8,128)(2,1)S(1)} %copy-done.2), channel_id=1, source_target_pairs={{0,16},{4,20},{8,24},{12,28},{16,0},{20,4},{24,8},{28,12},{1,17},{... | collective-permute-start | bytes 98312 | tf_op jit(solution)/shard_map/ppermute | solution.py:42
  7.2 3.1 %copy-start.3 = (s32[8]{0:T(128)S(1)}, s32[8]{0:T(128)}, u32[]{:S(2)}) copy-start(s32[8]{0:T(128)} %param.8) | copy-start | bytes 100
  7.2 3.1 %copy-start.4 = (bf16[2,8,1024]{2,1,0:T(8,128)(2,1)S(1)}, bf16[2,8,1024]{2,1,0:T(8,128)(2,1)}, u32[]{:S(2)}) copy-start(bf16[2,8,1024]{2,1,0:T(8,128)(2,1)} %self_ref.1) | copy-start | bytes 98308
  8.4 1.9 %collective-permute-start.6 = (bf16[32,2048]{1,0:T(8,128)(2,1)S(1)}, bf16[32,2048]{1,0:T(8,128)(2,1)S(1)}, u32[]{:S(2)}, u32[]{:S(2)}) collective-permute-start(bf16[32,2048]{1,0:T(8,128)(2,1)S(1)} %query_chips.1.known_ref), channel_id=1, source_target_pairs={{0,4},{4,0},{8,12},{12,8},{16,20},{20,16},{24,28},{28,24},{1,5},{5... | collective-permute-start | bytes 393224 | tf_op jit(solution)/shard_map/ppermute | solution.py:42
  8.5 17.1 %collective-permute-start.2 = (bf16[768,128]{1,0:T(8,128)(2,1)S(1)}, bf16[768,128]{1,0:T(8,128)(2,1)S(1)}, u32[]{:S(2)}, u32[]{:S(2)}) collective-permute-start(bf16[768,128]{1,0:T(8,128)(2,1)S(1)} %get-tuple-element.19.rest_0_.one_ref), channel_id=1, source_target_pairs={{0,8},{4,20},{8,0},{12,28},{16,24},{20,4},{24,16},{28,12},{1,9},{5... | collective-permute-start | bytes 589832 | tf_op jit(solution)/shard_map/ppermute | solution.py:42
  9.1 23.3 %collective-permute-start.1 = (bf16[768,128]{1,0:T(8,128)(2,1)S(1)}, bf16[768,128]{1,0:T(8,128)(2,1)S(1)}, u32[]{:S(2)}, u32[]{:S(2)}) collective-permute-start(bf16[768,128]{1,0:T(8,128)(2,1)S(1)} %get-tuple-element.18.one_ref), channel_id=1, source_target_pairs={{0,16},{4,12},{8,24},{12,4},{16,0},{20,28},{24,8},{28,20},{1,17},{... | collective-permute-start | bytes 589832 | tf_op jit(solution)/shard_map/ppermute | solution.py:42
  21.6 2.0 %collective-permute-start.7 = (bf16[64,1152]{1,0:T(8,128)(2,1)S(1)}, bf16[64,1152]{1,0:T(8,128)(2,1)S(1)}, u32[]{:S(2)}, u32[]{:S(2)}) collective-permute-start(bf16[64,1152]{1,0:T(8,128)(2,1)S(1)} %get-tuple-element.21), channel_id=1, source_target_pairs={{0,4},{4,0},{8,12},{12,8},{16,20},{20,16},{24,28},{28,24},{1,5},{5... | collective-permute-start | bytes 442376 | tf_op jit(solution)/shard_map/ppermute | solution.py:42
  24.0 6.6 %collective-permute-start.9 = (bf16[64,1152]{1,0:T(8,128)(2,1)S(1)}, bf16[64,1152]{1,0:T(8,128)(2,1)S(1)}, u32[]{:S(2)}, u32[]{:S(2)}) collective-permute-start(bf16[64,1152]{1,0:T(8,128)(2,1)S(1)} %query_merge.3.rest_0_.refs_0_), channel_id=1, source_target_pairs={{0,8},{4,20},{8,0},{12,28},{16,24},{20,4},{24,16},{28,12},{1,9},{5... | collective-permute-start | bytes 442376 | tf_op jit(solution)/shard_map/ppermute | solution.py:42
  25.6 5.7 %collective-permute-start.8 = (bf16[768,128]{1,0:T(8,128)(2,1)S(1)}, bf16[768,128]{1,0:T(8,128)(2,1)S(1)}, u32[]{:S(2)}, u32[]{:S(2)}) collective-permute-start(bf16[768,128]{1,0:T(8,128)(2,1)S(1)} %anchor_relay.6.rest_0_.one_ref), channel_id=1, source_target_pairs={{0,16},{4,12},{8,24},{12,4},{16,0},{20,28},{24,8},{28,20},{1,17},{... | collective-permute-start | bytes 589832 | tf_op jit(solution)/shard_map/ppermute | solution.py:42
  31.3 2.3 %collective-permute-start.12 = (bf16[768,128]{1,0:T(8,128)(2,1)S(1)}, bf16[768,128]{1,0:T(8,128)(2,1)S(1)}, u32[]{:S(2)}, u32[]{:S(2)}) collective-permute-start(bf16[768,128]{1,0:T(8,128)(2,1)S(1)} %anchor_relay.7.rest_0_.first_ref), channel_id=1, source_target_pairs={{0,4},{4,0},{8,12},{12,8},{16,20},{20,16},{24,28},{28,24},{1,5},{5... | collective-permute-start | bytes 589832 | tf_op jit(solution)/shard_map/ppermute | solution.py:42
  31.5 31.8 %collective-permute-start.11 = (bf16[64,1152]{1,0:T(8,128)(2,1)S(1)}, bf16[64,1152]{1,0:T(8,128)(2,1)S(1)}, u32[]{:S(2)}, u32[]{:S(2)}) collective-permute-start(bf16[64,1152]{1,0:T(8,128)(2,1)S(1)} %query_merge.4.rest_0_.refs_0_), channel_id=1, source_target_pairs={{0,16},{4,12},{8,24},{12,4},{16,0},{20,28},{24,8},{28,20},{1,17},{... | collective-permute-start | bytes 442376 | tf_op jit(solution)/shard_map/ppermute | solution.py:42
  32.4 31.4 %collective-permute-start.10 = (bf16[768,128]{1,0:T(8,128)(2,1)S(1)}, bf16[768,128]{1,0:T(8,128)(2,1)S(1)}, u32[]{:S(2)}, u32[]{:S(2)}) collective-permute-start(bf16[768,128]{1,0:T(8,128)(2,1)S(1)} %anchor_relay.8.rest_0_.one_ref), channel_id=1, source_target_pairs={{0,8},{4,20},{8,0},{12,28},{16,24},{20,4},{24,16},{28,12},{1,9},{5... | collective-permute-start | bytes 589832 | tf_op jit(solution)/shard_map/ppermute | solution.py:42
  33.8 31.2 %copy-start.1 = (bf16[2048,1024]{1,0:T(8,128)(2,1)S(1)}, bf16[2048,1024]{1,0:T(8,128)(2,1)}, u32[]{:S(2)}) copy-start(bf16[2048,1024]{1,0:T(8,128)(2,1)} %w_ref.1) | copy-start | bytes 12582916
  63.7 1.4 collective-permute-start.14
  63.8 32.9 %collective-permute-start.13 = (bf16[768,128]{1,0:T(8,128)(2,1)S(1)}, bf16[768,128]{1,0:T(8,128)(2,1)S(1)}, u32[]{:S(2)}, u32[]{:S(2)}) collective-permute-start(bf16[768,128]{1,0:T(8,128)(2,1)S(1)} %anchor_relay.9.rest_0_.first_ref), channel_id=1, source_target_pairs={{0,4},{4,0},{8,12},{12,8},{16,20},{20,16},{24,28},{28,24},{1,5},{5... | collective-permute-start | bytes 589832 | tf_op jit(solution)/shard_map/ppermute | solution.py:42
  66.0 45.6 %collective-permute-start.15 = (bf16[64,1024]{1,0:T(8,128)(2,1)S(1)}, bf16[64,1024]{1,0:T(8,128)(2,1)S(1)}, u32[]{:S(2)}, u32[]{:S(2)}) collective-permute-start(bf16[64,1024]{1,0:T(8,128)(2,1)S(1)} %query_project.1.refs_7_.refs_8_.one_ref), channel_id=1, source_target_pairs={{0,1},{1,0},{2,3},{3,2},{4,5},{5,4},{6,7},{7,6},{8,9},{9,8},{10,11... | collective-permute-start | bytes 393224 | tf_op jit(solution)/shard_map/ppermute | solution.py:42
  111.6 47.8 %collective-permute-start.16 = (bf16[64,1024]{1,0:T(8,128)(2,1)S(1)}, bf16[64,1024]{1,0:T(8,128)(2,1)S(1)}, u32[]{:S(2)}, u32[]{:S(2)}) collective-permute-start(bf16[64,1024]{1,0:T(8,128)(2,1)S(1)} %query_sum.2.refs_10_.one_ref), channel_id=1, source_target_pairs={{0,2},{1,3},{2,0},{3,1},{4,6},{5,7},{6,4},{7,5},{8,10},{9,11},{10,... | collective-permute-start | bytes 393224 | tf_op jit(solution)/shard_map/ppermute | solution.py:42

commit v16 on v15

--- a/solution.py
+++ b/solution.py
@@ -741,13 +741,13 @@
         )
         return results[first]
 
-    done = anchors(0, 4, ())
+    done = anchors(0, 6, ())
     attended = merge_part([source, landed], True, (done,))
     landed = swap(attended, "hst", hosts, 1, 1)
     done = complete(1, (attended,))
     terms = project_part(attended, landed, out_weight, (done,))
     done = terms
-    shares = [[(10, 6, True)], [(4, 4, False), (8, 2, False)]]
+    shares = [[(10, 6, True)], [(6, 2, False), (8, 2, False)]]
     step = 1
     while step < groups:
         landed = swap(terms, "tp", groups, step, step)

time: 160 us -> 160 us (level)
  no operation moved by 1% of the time
where the time goes in v16:
time: 160 us
  Pallas kernels  142 us (89%)
  starting transfers between devices  15.2 us (10%)
    pallas_call x4, Pallas kernels, anchor_part(): pl.pallas_call(functools.partial(anchor_kernel, first, count, bases, per_...  118 us
    ppermute x17, starting transfers between devices, swap(): lax.ppermute(value, axis, [(i, i ^ (odd if i & 1 else even)) for i in ran...  15.2 us
    pallas_call x1, Pallas kernels, source_part(): pl.pallas_call(functools.partial(source_kernel, per_kv, q_rows, H // KVH)...  11.4 us
    pallas_call x4, Pallas kernels, own_part(): pl.pallas_call(functools.partial(own_kernel, first, count, per_kv), out_s...  7.95 us
  transfers between devices with their start and end apart: 17, of which 3 were waited for; matrix products, arithmetic and copies ran while one was open for 0% of the time, Pallas kernels for 88%

profile of v16, /device:TPU:6, one launch (start us, length us, event | category | flops | bytes accessed | tf_op | source)
XLA Modules:
  0.0 160.0 jit_solution(1313056313555166102)
XLA Ops:
  0.6 1.3 pick_columns.1
  2.1 2.0 %collective-permute-start.4 = (bf16[8,2048]{1,0:T(8,128)(2,1)S(1)}, bf16[8,2048]{1,0:T(8,128)(2,1)S(1)}, u32[]{:S(2)}, u32[]{:S(2)}) collective-permute-start(bf16[8,2048]{1,0:T(8,128)(2,1)S(1)} %copy-done.2), channel_id=1, source_target_pairs={{0,8},{4,12},{8,0},{12,4},{16,24},{20,28},{24,16},{28,20},{1,9},{5... | collective-permute-start | bytes 98312 | tf_op jit(solution)/shard_map/ppermute | solution.py:42
  4.1 1.5 collective-permute-start.5
  5.6 0.4 operands.3
  6.0 1.1 context_own.4.rest_0_.refs_6_
  7.2 1.1 context_own.5.refs_4_.refs_7_
  8.5 0.6 collective-permute-start.2
  9.1 1.2 collective-permute-start.1
  10.3 11.4 %query_source.1 = (bf16[64,1152]{1,0:T(8,128)(2,1)S(1)}, bf16[64,1152]{1,0:T(8,128)(2,1)S(1)}) custom-call(s32[1,8]{1,0:T(1,128)S(1)} %bitcast.1, bf16[512,768]{1,0:T(8,128)(2,1)S(1)} %get-tuple-element.16.k_ref.refs_2_, bf16[768,256]{1,0:T(8,128)(2,1)S(1)} %get-tuple-element.15.second_ref.v_ref, bf16[2,8,1024]{2,1,0:T(8,128)(2,1)S(1)} %copy-done.4, ...), custom_call_target="tpu_custom_call" | custom-call | flops 805306368 | bytes 2097152 | tf_op jit(solution)/shard_map/query_source/pallas_call | solution.py:548
  21.7 1.9 %context_own.6.refs_2_.refs_8_.refs_6_ = f32[768,1024]{1,0:T(8,128)S(1)} custom-call(bf16[768,2048]{1,0:T(8,128)(2,1)S(1)} %copy-done, bf16[512,768]{1,0:T(8,128)(2,1)S(1)} %get-tuple-element.16.k_ref.refs_2_, bf16[768,512]{1,0:T(8,128)(2,1)S(1)} %get-tuple-element.17.v_ref.refs_3_, bf16[64,1152]{1,0:T(8,128)(2,1)S(1)} %get-tuple-element.20.rest_0_.refs_0_), custom_call_target="tpu_custom_call" | custom-call | flops 1610612736 | bytes 2359296 | tf_op jit(solution)/shard_map/context_own/pallas_call | solution.py:241
  23.7 0.3 query_merge.3.rest_0_.refs_0_
  24.0 1.6 collective-permute-start.9
  25.6 0.9 collective-permute-start.8
  26.5 3.8 %context_own.7.refs_2_.refs_6_ = f32[768,2048]{1,0:T(8,128)S(1)} custom-call(bf16[768,2048]{1,0:T(8,128)(2,1)S(1)} %copy-done, bf16[512,768]{1,0:T(8,128)(2,1)S(1)} %get-tuple-element.16.k_ref.refs_2_, bf16[768,512]{1,0:T(8,128)(2,1)S(1)} %get-tuple-element.17.v_ref.refs_3_, bf16[768,128]{1,0:T(8,128)(2,1)S(1)} %anchor_relay.6.rest_0_.one_ref), custom_call_target="tpu_custom_call" | custom-call | flops 3221225472 | bytes 4718592 | tf_op jit(solution)/shard_map/context_own/pallas_call | solution.py:241
  30.3 0.2 collective-permute-done.9.refs_1_
  30.6 0.3 query_merge.4.rest_0_.refs_0_
  30.9 0.4 collective-permute-done.8.two_ref
  31.5 0.9 collective-permute-start.11
  32.4 1.3 collective-permute-start.10
  33.6 0.2 operands.4
  33.9 43.8 %context_anchor.4.refs_2_.refs_7_ = bf16[768,768]{1,0:T(8,128)(2,1)S(1)} custom-call(s32[1,8]{1,0:T(1,128)S(1)} %bitcast.2, bf16[768,2048]{1,0:T(8,128)(2,1)S(1)} %copy-done, bf16[512,768]{1,0:T(8,128)(2,1)S(1)} %get-tuple-element.16.k_ref.refs_2_, bf16[768,512]{1,0:T(8,128)(2,1)S(1)} %get-tuple-element.17.v_ref.refs_3_, ...), custom_call_target="tpu_custom_call" | custom-call | flops 3623878656 | bytes 4718592 | tf_op jit(solution)/shard_map/context_anchor/pallas_call | solution.py:389
  77.7 0.3 query_merge.5.rest_0_.own_ref
  78.2 0.5 collective-permute-start.13
  78.7 0.8 collective-permute-done.14.other_ref
  79.4 0.9 query_project.1.refs_7_.refs_8_.one_ref
  80.3 1.6 %collective-permute-start.15 = (bf16[64,1024]{1,0:T(8,128)(2,1)S(1)}, bf16[64,1024]{1,0:T(8,128)(2,1)S(1)}, u32[]{:S(2)}, u32[]{:S(2)}) collective-permute-start(bf16[64,1024]{1,0:T(8,128)(2,1)S(1)} %query_project.1.refs_7_.refs_8_.one_ref), channel_id=1, source_target_pairs={{0,1},{1,0},{2,3},{3,2},{4,5},{5,4},{6,7},{7,6},{8,9},{9,8},{10,11... | collective-permute-start | bytes 393224 | tf_op jit(solution)/shard_map/ppermute | solution.py:42
  82.0 14.7 %context_anchor.5.rest_0_.refs_8_ = bf16[768,256]{1,0:T(8,128)(2,1)S(1)} custom-call(s32[1,8]{1,0:T(1,128)S(1)} %bitcast.3, bf16[768,2048]{1,0:T(8,128)(2,1)S(1)} %copy-done, bf16[512,768]{1,0:T(8,128)(2,1)S(1)} %get-tuple-element.16.k_ref.refs_2_, bf16[768,512]{1,0:T(8,128)(2,1)S(1)} %get-tuple-element.17.v_ref.refs_3_, ...), custom_call_target="tpu_custom_call" | custom-call | flops 1207959552 | bytes 1572864 | tf_op jit(solution)/shard_map/context_anchor/pallas_call | solution.py:389
  96.7 0.2 operands.5
  96.9 14.7 %context_anchor.6.rest_0_.refs_9_.refs_11_ = bf16[768,256]{1,0:T(8,128)(2,1)S(1)} custom-call(s32[1,8]{1,0:T(1,128)S(1)} %bitcast.4, bf16[768,2048]{1,0:T(8,128)(2,1)S(1)} %copy-done, bf16[512,768]{1,0:T(8,128)(2,1)S(1)} %get-tuple-element.16.k_ref.refs_2_, bf16[768,512]{1,0:T(8,128)(2,1)S(1)} %get-tuple-element.17.v_ref.refs_3_, ...), custom_call_target="tpu_custom_call" | custom-call | flops 1207959552 | bytes 1572864 | tf_op jit(solution)/shard_map/context_anchor/pallas_call | solution.py:389
  111.6 2.7 %collective-permute-start.16 = (bf16[64,1024]{1,0:T(8,128)(2,1)S(1)}, bf16[64,1024]{1,0:T(8,128)(2,1)S(1)}, u32[]{:S(2)}, u32[]{:S(2)}) collective-permute-start(bf16[64,1024]{1,0:T(8,128)(2,1)S(1)} %query_sum.2.refs_10_.one_ref), channel_id=1, source_target_pairs={{0,2},{1,3},{2,0},{3,1},{4,6},{5,7},{6,4},{7,5},{8,10},{9,11},{10,... | collective-permute-start | bytes 393224 | tf_op jit(solution)/shard_map/ppermute | solution.py:42
  114.3 45.1 %context_anchor.7 = bf16[768,2048]{1,0:T(8,128)(2,1)} custom-call(s32[1,8]{1,0:T(1,128)S(1)} %bitcast.5, bf16[768,2048]{1,0:T(8,128)(2,1)S(1)} %copy-done, bf16[512,768]{1,0:T(8,128)(2,1)S(1)} %get-tuple-element.16.k_ref.refs_2_, bf16[768,512]{1,0:T(8,128)(2,1)S(1)} %get-tuple-element.17.v_ref.refs_3_, bf16[256,768]{1,0:T(8,128)(2,1)S(1)} %get-tuple-element.24.refs_4_, ...), custom_call_target="tpu_custom_call" | custom-call | flops 3623878656 | bytes 4718592 | tf_op jit(solution)/shard_map/context_anchor/pallas_call | solution.py:389
  159.4 0.7 query_sum.3
  (37 shorter events, 0.8 us)
Async XLA Ops:
  0.6 1.4 copy-start.2
  0.6 5.3 %copy-start = (bf16[768,2048]{1,0:T(8,128)(2,1)S(1)}, bf16[768,2048]{1,0:T(8,128)(2,1)}, u32[]{:S(2)}) copy-start(bf16[768,2048]{1,0:T(8,128)(2,1)} %refs_1_.7) | copy-start | bytes 9437188
  2.0 5.1 %collective-permute-start = (bf16[768,256]{1,0:T(8,128)(2,1)S(1)}, bf16[768,256]{1,0:T(8,128)(2,1)S(1)}, u32[]{:S(2)}, u32[]{:S(2)}) collective-permute-start(bf16[768,256]{1,0:T(8,128)(2,1)S(1)} %get-tuple-element.15.second_ref.v_ref), channel_id=1, source_target_pairs={{0,4},{4,0},{8,12},{12,8},{16,20},{20,16},{24,28},{28,24},{1,5},{5... | collective-permute-start | bytes 1179656 | tf_op jit(solution)/shard_map/ppermute | solution.py:42
  2.0 6.3 %collective-permute-start.3 = (bf16[8,2048]{1,0:T(8,128)(2,1)S(1)}, bf16[8,2048]{1,0:T(8,128)(2,1)S(1)}, u32[]{:S(2)}, u32[]{:S(2)}) collective-permute-start(bf16[8,2048]{1,0:T(8,128)(2,1)S(1)} %copy-done.2), channel_id=1, source_target_pairs={{0,24},{4,28},{8,16},{12,20},{16,8},{20,12},{24,0},{28,4},{1,25},{... | collective-permute-start | bytes 98312 | tf_op jit(solution)/shard_map/ppermute | solution.py:42
  2.1 6.2 %collective-permute-start.4 = (bf16[8,2048]{1,0:T(8,128)(2,1)S(1)}, bf16[8,2048]{1,0:T(8,128)(2,1)S(1)}, u32[]{:S(2)}, u32[]{:S(2)}) collective-permute-start(bf16[8,2048]{1,0:T(8,128)(2,1)S(1)} %copy-done.2), channel_id=1, source_target_pairs={{0,8},{4,12},{8,0},{12,4},{16,24},{20,28},{24,16},{28,20},{1,9},{5... | collective-permute-start | bytes 98312 | tf_op jit(solution)/shard_map/ppermute | solution.py:42
  4.1 4.2 %collective-permute-start.5 = (bf16[8,2048]{1,0:T(8,128)(2,1)S(1)}, bf16[8,2048]{1,0:T(8,128)(2,1)S(1)}, u32[]{:S(2)}, u32[]{:S(2)}) collective-permute-start(bf16[8,2048]{1,0:T(8,128)(2,1)S(1)} %copy-done.2), channel_id=1, source_target_pairs={{0,16},{4,20},{8,24},{12,28},{16,0},{20,4},{24,8},{28,12},{1,17},{... | collective-permute-start | bytes 98312 | tf_op jit(solution)/shard_map/ppermute | solution.py:42
  7.2 3.1 %copy-start.3 = (s32[8]{0:T(128)S(1)}, s32[8]{0:T(128)}, u32[]{:S(2)}) copy-start(s32[8]{0:T(128)} %param.8) | copy-start | bytes 100
  7.2 3.1 %copy-start.4 = (bf16[2,8,1024]{2,1,0:T(8,128)(2,1)S(1)}, bf16[2,8,1024]{2,1,0:T(8,128)(2,1)}, u32[]{:S(2)}) copy-start(bf16[2,8,1024]{2,1,0:T(8,128)(2,1)} %self_ref.1) | copy-start | bytes 98308
  8.4 1.9 %collective-permute-start.6 = (bf16[32,2048]{1,0:T(8,128)(2,1)S(1)}, bf16[32,2048]{1,0:T(8,128)(2,1)S(1)}, u32[]{:S(2)}, u32[]{:S(2)}) collective-permute-start(bf16[32,2048]{1,0:T(8,128)(2,1)S(1)} %query_chips.1.known_ref), channel_id=1, source_target_pairs={{0,4},{4,0},{8,12},{12,8},{16,20},{20,16},{24,28},{28,24},{1,5},{5... | collective-permute-start | bytes 393224 | tf_op jit(solution)/shard_map/ppermute | solution.py:42
  8.5 17.1 %collective-permute-start.2 = (bf16[768,128]{1,0:T(8,128)(2,1)S(1)}, bf16[768,128]{1,0:T(8,128)(2,1)S(1)}, u32[]{:S(2)}, u32[]{:S(2)}) collective-permute-start(bf16[768,128]{1,0:T(8,128)(2,1)S(1)} %get-tuple-element.19.rest_0_.one_ref), channel_id=1, source_target_pairs={{0,8},{4,20},{8,0},{12,28},{16,24},{20,4},{24,16},{28,12},{1,9},{5... | collective-permute-start | bytes 589832 | tf_op jit(solution)/shard_map/ppermute | solution.py:42
  9.1 23.3 %collective-permute-start.1 = (bf16[768,128]{1,0:T(8,128)(2,1)S(1)}, bf16[768,128]{1,0:T(8,128)(2,1)S(1)}, u32[]{:S(2)}, u32[]{:S(2)}) collective-permute-start(bf16[768,128]{1,0:T(8,128)(2,1)S(1)} %get-tuple-element.18.one_ref), channel_id=1, source_target_pairs={{0,16},{4,12},{8,24},{12,4},{16,0},{20,28},{24,8},{28,20},{1,17},{... | collective-permute-start | bytes 589832 | tf_op jit(solution)/shard_map/ppermute | solution.py:42
  21.6 2.0 %collective-permute-start.7 = (bf16[64,1152]{1,0:T(8,128)(2,1)S(1)}, bf16[64,1152]{1,0:T(8,128)(2,1)S(1)}, u32[]{:S(2)}, u32[]{:S(2)}) collective-permute-start(bf16[64,1152]{1,0:T(8,128)(2,1)S(1)} %get-tuple-element.21), channel_id=1, source_target_pairs={{0,4},{4,0},{8,12},{12,8},{16,20},{20,16},{24,28},{28,24},{1,5},{5... | collective-permute-start | bytes 442376 | tf_op jit(solution)/shard_map/ppermute | solution.py:42
  24.0 6.6 %collective-permute-start.9 = (bf16[64,1152]{1,0:T(8,128)(2,1)S(1)}, bf16[64,1152]{1,0:T(8,128)(2,1)S(1)}, u32[]{:S(2)}, u32[]{:S(2)}) collective-permute-start(bf16[64,1152]{1,0:T(8,128)(2,1)S(1)} %query_merge.3.rest_0_.refs_0_), channel_id=1, source_target_pairs={{0,8},{4,20},{8,0},{12,28},{16,24},{20,4},{24,16},{28,12},{1,9},{5... | collective-permute-start | bytes 442376 | tf_op jit(solution)/shard_map/ppermute | solution.py:42
  25.6 5.7 %collective-permute-start.8 = (bf16[768,128]{1,0:T(8,128)(2,1)S(1)}, bf16[768,128]{1,0:T(8,128)(2,1)S(1)}, u32[]{:S(2)}, u32[]{:S(2)}) collective-permute-start(bf16[768,128]{1,0:T(8,128)(2,1)S(1)} %anchor_relay.6.rest_0_.one_ref), channel_id=1, source_target_pairs={{0,16},{4,12},{8,24},{12,4},{16,0},{20,28},{24,8},{28,20},{1,17},{... | collective-permute-start | bytes 589832 | tf_op jit(solution)/shard_map/ppermute | solution.py:42
  31.3 2.3 %collective-permute-start.12 = (bf16[768,128]{1,0:T(8,128)(2,1)S(1)}, bf16[768,128]{1,0:T(8,128)(2,1)S(1)}, u32[]{:S(2)}, u32[]{:S(2)}) collective-permute-start(bf16[768,128]{1,0:T(8,128)(2,1)S(1)} %anchor_relay.7.rest_0_.first_ref), channel_id=1, source_target_pairs={{0,4},{4,0},{8,12},{12,8},{16,20},{20,16},{24,28},{28,24},{1,5},{5... | collective-permute-start | bytes 589832 | tf_op jit(solution)/shard_map/ppermute | solution.py:42
  31.5 46.2 %collective-permute-start.11 = (bf16[64,1152]{1,0:T(8,128)(2,1)S(1)}, bf16[64,1152]{1,0:T(8,128)(2,1)S(1)}, u32[]{:S(2)}, u32[]{:S(2)}) collective-permute-start(bf16[64,1152]{1,0:T(8,128)(2,1)S(1)} %query_merge.4.rest_0_.refs_0_), channel_id=1, source_target_pairs={{0,16},{4,12},{8,24},{12,4},{16,0},{20,28},{24,8},{28,20},{1,17},{... | collective-permute-start | bytes 442376 | tf_op jit(solution)/shard_map/ppermute | solution.py:42
  32.4 45.7 %collective-permute-start.10 = (bf16[768,128]{1,0:T(8,128)(2,1)S(1)}, bf16[768,128]{1,0:T(8,128)(2,1)S(1)}, u32[]{:S(2)}, u32[]{:S(2)}) collective-permute-start(bf16[768,128]{1,0:T(8,128)(2,1)S(1)} %anchor_relay.8.rest_0_.one_ref), channel_id=1, source_target_pairs={{0,8},{4,20},{8,0},{12,28},{16,24},{20,4},{24,16},{28,12},{1,9},{5... | collective-permute-start | bytes 589832 | tf_op jit(solution)/shard_map/ppermute | solution.py:42
  33.8 45.6 %copy-start.1 = (bf16[2048,1024]{1,0:T(8,128)(2,1)S(1)}, bf16[2048,1024]{1,0:T(8,128)(2,1)}, u32[]{:S(2)}) copy-start(bf16[2048,1024]{1,0:T(8,128)(2,1)} %w_ref.1) | copy-start | bytes 12582916
  78.0 1.4 collective-permute-start.14
  78.2 18.5 %collective-permute-start.13 = (bf16[768,128]{1,0:T(8,128)(2,1)S(1)}, bf16[768,128]{1,0:T(8,128)(2,1)S(1)}, u32[]{:S(2)}, u32[]{:S(2)}) collective-permute-start(bf16[768,128]{1,0:T(8,128)(2,1)S(1)} %anchor_relay.9.rest_0_.first_ref), channel_id=1, source_target_pairs={{0,4},{4,0},{8,12},{12,8},{16,20},{20,16},{24,28},{28,24},{1,5},{5... | collective-permute-start | bytes 589832 | tf_op jit(solution)/shard_map/ppermute | solution.py:42
  80.3 31.3 %collective-permute-start.15 = (bf16[64,1024]{1,0:T(8,128)(2,1)S(1)}, bf16[64,1024]{1,0:T(8,128)(2,1)S(1)}, u32[]{:S(2)}, u32[]{:S(2)}) collective-permute-start(bf16[64,1024]{1,0:T(8,128)(2,1)S(1)} %query_project.1.refs_7_.refs_8_.one_ref), channel_id=1, source_target_pairs={{0,1},{1,0},{2,3},{3,2},{4,5},{5,4},{6,7},{7,6},{8,9},{9,8},{10,11... | collective-permute-start | bytes 393224 | tf_op jit(solution)/shard_map/ppermute | solution.py:42
  111.6 47.7 %collective-permute-start.16 = (bf16[64,1024]{1,0:T(8,128)(2,1)S(1)}, bf16[64,1024]{1,0:T(8,128)(2,1)S(1)}, u32[]{:S(2)}, u32[]{:S(2)}) collective-permute-start(bf16[64,1024]{1,0:T(8,128)(2,1)S(1)} %query_sum.2.refs_10_.one_ref), channel_id=1, source_target_pairs={{0,2},{1,3},{2,0},{3,1},{4,6},{5,7},{6,4},{7,5},{8,10},{9,11},{10,... | collective-permute-start | bytes 393224 | tf_op jit(solution)/shard_map/ppermute | solution.py:42
